TPU v7x, 512 devices: a whole 4x8x8 slice. The times are simulated.
512 devices in a mesh: ctx: 64 (over y, x, core), head: 8 (over z).
Axes of the slice: x: 4, y: 8, z: 8, core: 2. Of those that a mesh axis runs over, the one named last changes fastest.
Arguments:
- queries: bfloat16 [4096, 12288], P(('ctx', 'head')), may hold values from -8 to 8
- latent: bfloat16 [4096, 512], P(('ctx', 'head')), may hold values from -6 to 6
- rope_key: bfloat16 [4096, 64], P(('ctx', 'head')), may hold values from -8 to 8
- w_uk: bfloat16 [64, 512, 128], P('head'), may hold values from -0.25 to 0.25
- w_uv: bfloat16 [64, 512, 128], P('head'), may hold values from -0.25 to 0.25
- block_order: int32 [128], replicated, may hold values from 0 to 127, each once
Outputs:
- out: bfloat16 [4096, 8192], P(('ctx', 'head'))
Inputs may be any that keep to these rules, and one draw needn't show every extreme that they name: `block_order`: each of 0 to 127 appears once.
All inputs are finite; a program needn't handle non-finite values.
Results may differ from a plain program's by a relative error of at most 0.009.
Values may be sent and summed in bfloat16 or wider, within the bound.
No kernel may reach another device: no remote copies, remote signals or barrier semaphores. Data moves between devices by JAX's collectives and lax.ppermute only.
A program may use at most 64 MiB of HBM per device.

v0:
```python
import math

import jax
import jax.numpy as jnp
from jax import lax
from jax.sharding import PartitionSpec as P

HALF = 32
DL = 512
DR = 64
DN = 128
DV = 128


FLOOR_SCORE = -1e30


def lookup(values, wanted):
    slot_ids = jnp.arange(values.shape[0], dtype=jnp.int32)
    chosen = jnp.where(slot_ids[None, :] == wanted[:, None], values[None, :], 0)
    return jnp.sum(chosen, axis=1)


def update(state, q_pair, k_rows, q_pos, k_info, local_heads, score_scale):
    row_max, row_total, weighted = state
    q_lat, q_rope = q_pair
    k_lat, k_rope = k_rows
    k_pos, k_valid = k_info
    scores = jnp.einsum("rl,ul->ru", q_lat, k_lat, preferred_element_type=jnp.float32)
    scores = scores + jnp.einsum("rd,ud->ru", q_rope, k_rope, preferred_element_type=jnp.float32)
    scores = scores * score_scale
    visible = k_valid[None, :] & (k_pos[None, :] <= q_pos[:, None])
    visible = jnp.repeat(visible, local_heads, axis=0)
    new_max = jnp.maximum(row_max, jnp.max(jnp.where(visible, scores, FLOOR_SCORE), axis=1))
    exponent = jnp.where(visible, jnp.exp(scores - new_max[:, None]), 0.0)
    shrink = jnp.exp(row_max - new_max)
    row_total = row_total * shrink + jnp.sum(exponent, axis=1)
    weighted = weighted * shrink[:, None] + jnp.dot(
        exponent.astype(jnp.bfloat16), k_lat, preferred_element_type=jnp.float32
    )
    return (new_max, row_total, weighted)


def maybe_update(any_visible, state, q_pair, k_rows, q_pos, k_info, local_heads, score_scale):

    def compute(current):
        return update(current, q_pair, k_rows, q_pos, k_info, local_heads, score_scale)

    def unchanged(current):
        return current

    return lax.cond(any_visible, compute, unchanged, state)


def on_device(queries, latent, rope_key, w_uk, w_uv, block_order):
    half_rows = HALF
    score_scale = (DN + DR) ** (-0.5)
    ctx_index = lax.axis_index("ctx")
    q_span = lax.all_to_all(queries, "head", split_axis=1, concat_axis=0, tiled=True)
    local_heads = q_span.shape[1] // (DN + DR)
    own_blocks = lookup(block_order, jnp.stack([2 * ctx_index, 2 * ctx_index + 1]))
    own_second = q_span[half_rows:]
    second_block = own_blocks[1]
    q_rows = jnp.concatenate([q_span[:half_rows], own_second], axis=0).reshape(
        2 * half_rows, local_heads, DN + DR
    )
    q_lat = jnp.einsum(
        "thd,hld->thl", q_rows[:, :, :DN], w_uk, preferred_element_type=jnp.float32
    ).astype(jnp.bfloat16)
    q_rope = q_rows[:, :, DN:]
    query_blocks = [own_blocks[0], second_block]
    queries_of = []
    for half_index in range(2):
        q_pos = query_blocks[half_index] * half_rows + jnp.arange(half_rows, dtype=jnp.int32)
        lat_part = q_lat[half_index * half_rows : (half_index + 1) * half_rows].reshape(
            half_rows * local_heads, DL
        )
        rope_part = q_rope[half_index * half_rows : (half_index + 1) * half_rows].reshape(
            half_rows * local_heads, DR
        )
        queries_of.append(((lat_part, rope_part), q_pos))
    state_rows = half_rows * local_heads
    fresh_state = (
        jnp.full((state_rows,), FLOOR_SCORE, jnp.float32),
        jnp.zeros((state_rows,), jnp.float32),
        jnp.zeros((state_rows, DL), jnp.float32),
    )
    span_lat, span_rope = (
        lax.all_gather(latent, "head", axis=0, tiled=True),
        lax.all_gather(rope_key, "head", axis=0, tiled=True),
    )
    seg_lat = lax.all_gather(span_lat, "ctx", axis=0, tiled=True)
    seg_rope = lax.all_gather(span_rope, "ctx", axis=0, tiled=True)
    row_count = seg_lat.shape[0]
    sub_rows = math.gcd(row_count, 512)
    all_index = jnp.arange(row_count, dtype=jnp.int32)
    seg_pos = lookup(block_order, all_index // half_rows) * half_rows + all_index % half_rows
    k_valid = jnp.ones((sub_rows,), jnp.bool_)

    def advance(step_index, states):
        offset = step_index * sub_rows
        k_lat = lax.dynamic_slice_in_dim(seg_lat, offset, sub_rows, 0)
        k_rope = lax.dynamic_slice_in_dim(seg_rope, offset, sub_rows, 0)
        k_pos = lax.dynamic_slice_in_dim(seg_pos, offset, sub_rows, 0)
        results = []
        for half_index in range(2):
            q_pair, q_pos = queries_of[half_index]
            any_visible = jnp.min(k_pos) <= q_pos[half_rows - 1]
            results.append(
                maybe_update(
                    any_visible,
                    states[half_index],
                    q_pair,
                    (k_lat, k_rope),
                    q_pos,
                    (k_pos, k_valid),
                    local_heads,
                    score_scale,
                )
            )
        return tuple(results)

    states = lax.fori_loop(0, row_count // sub_rows, advance, (fresh_state, fresh_state))
    finished = []
    for half_index in range(2):
        row_max, row_total, weighted = states[half_index]
        o_lat = (
            (weighted / row_total[:, None]).astype(jnp.bfloat16).reshape(half_rows, local_heads, DL)
        )
        projected = jnp.einsum("thl,hlv->thv", o_lat, w_uv, preferred_element_type=jnp.float32)
        finished.append(projected.astype(jnp.bfloat16).reshape(half_rows, local_heads * DV))
    first_out = finished[0]
    second_out = finished[1]
    out_span = jnp.concatenate([first_out, second_out], axis=0)
    return lax.all_to_all(out_span, "head", split_axis=0, concat_axis=1, tiled=True)


def solution(mesh):
    in_specs = (
        P(("ctx", "head"), None),
        P(("ctx", "head"), None),
        P(("ctx", "head"), None),
        P("head", None, None),
        P("head", None, None),
        P(),
    )
    out_specs = P(("ctx", "head"), None)
    return jax.shard_map(
        on_device, mesh=mesh, in_specs=in_specs, out_specs=out_specs, check_vma=False
    )
```

profile of v0, /device:TPU:1, one launch (start us, length us, event | category | flops | bytes accessed | tf_op | source)
XLA Modules:
  0.0 228.5 jit_solution(13813577660906284217)
XLA Ops:
  6.5 27.7 %all_gather.12 = bf16[64,512]{1,0:T(8,128)(2,1)} all-gather(bf16[8,512]{1,0:T(8,128)(2,1)} %param.13), channel_id=1, replica_groups=mesh['ctx'=64,'head'=8] {'head'}, dimensions={0}, use_global_device_ids=true | all-gather | bytes 73728 | tf_op jit(solution)/shard_map/all_gather | solution.py:89
  34.3 3.9 %all-to-all-start = ((bf16[8,8,1536]{2,0,1:T(8,128)(2,1)}), bf16[8,8,1536]{2,0,1:T(8,128)(2,1)S(1)}, u32[]{:S(2)}, u32[]{:S(2)}) async-start(bf16[8,8,1536]{2,0,1:T(8,128)(2,1)} %bitcast.80), calls=%async_computation | async-start | bytes 393216 | tf_op jit(solution)/shard_map/all_to_all | solution.py:59
  38.2 19.4 %all_gather.14 = bf16[64,64]{1,0:T(8,128)(2,1)S(1)} all-gather(bf16[8,64]{1,0:T(8,128)(2,1)} %param.14), channel_id=1, replica_groups=mesh['ctx'=64,'head'=8] {'head'}, dimensions={0}, use_global_device_ids=true | all-gather | bytes 9216 | tf_op jit(solution)/shard_map/all_gather | solution.py:90
  57.7 0.8 fusion.34
  58.5 68.3 %all_gather.15 = bf16[4096,64]{1,0:T(8,128)(2,1)} all-gather(bf16[64,64]{1,0:T(8,128)(2,1)S(1)} %all_gather.14), channel_id=1, replica_groups=mesh['ctx'=64,'head'=8] {'ctx'}, dimensions={0}, use_global_device_ids=true | all-gather | bytes 532480 | tf_op jit(solution)/shard_map/all_gather | solution.py:93
  126.8 1.9 select_reduce_fusion
  132.3 74.6 %while.23 = (s32[]{:T(128)}, f32[256]{0:T(256)S(1)}, f32[256]{0:T(256)S(1)}, f32[256,512]{1,0:T(8,128)S(1)}, f32[256]{0:T(256)S(1)}, /*index=5*/f32[256]{0:T(256...) while((s32[]{:T(128)}, f32[256]{0:T(256)S(1)}, ...), condition=%wide.region_12.13_spmd, body=%wide.region_2.12_spmd.sunk | while | flops 573605376 | bytes 11510567 | solution.py:123
  132.3 0.7 fusion.56
  134.8 1.1 constant_dynamic-slice_fusion.4
  135.9 0.9 constant_dynamic-slice_fusion.5
  136.8 1.5 conditional.4
  140.1 1.5 conditional.5
  141.6 0.7 fusion.56
  144.1 1.1 constant_dynamic-slice_fusion.4
  145.2 0.9 constant_dynamic-slice_fusion.5
  146.1 1.5 conditional.4
  149.4 1.5 conditional.5
  150.9 0.7 fusion.56
  153.4 1.1 constant_dynamic-slice_fusion.4
  154.5 0.9 constant_dynamic-slice_fusion.5
  155.4 1.5 conditional.4
  158.7 1.5 conditional.5
  160.3 0.7 fusion.56
  162.8 1.1 constant_dynamic-slice_fusion.4
  163.8 0.9 constant_dynamic-slice_fusion.5
  164.8 1.5 conditional.4
  168.1 1.5 conditional.5
  169.6 0.7 fusion.56
  172.1 1.1 constant_dynamic-slice_fusion.4
  173.2 0.9 constant_dynamic-slice_fusion.5
  174.1 1.5 conditional.4
  177.4 1.5 conditional.5
  181.4 1.1 constant_dynamic-slice_fusion.4
  182.5 0.9 constant_dynamic-slice_fusion.5
  183.4 1.5 conditional.4
  186.7 1.5 conditional.5
  188.2 0.7 fusion.56
  190.7 1.1 constant_dynamic-slice_fusion.4
  191.8 0.9 constant_dynamic-slice_fusion.5
  192.7 1.5 conditional.4
  196.0 1.5 conditional.5
  197.6 0.7 fusion.56
  200.1 1.1 constant_dynamic-slice_fusion.4
  201.1 0.9 constant_dynamic-slice_fusion.5
  202.1 1.5 conditional.4
  205.4 1.5 conditional.5
  207.0 1.6 fusion.20
  209.1 11.8 %all_to_all.35 = bf16[8,8,1024]{2,1,0:T(8,128)(2,1)S(1)} all-to-all(bf16[8,8,1024]{2,1,0:T(8,128)(2,1)S(1)} %maximum_bitcast_fusion), channel_id=1, replica_groups=mesh['ctx'=64,'head'=8] {'head'}, dimensions={0} | all-to-all | bytes 262144 | tf_op jit(solution)/shard_map/all_to_all | solution.py:135
  (180 shorter events, 36.6 us)
Async XLA Ops:
  6.5 124.7 %copy-start = (bf16[8,512,128]{2,1,0:T(8,128)(2,1)S(1)}, bf16[8,512,128]{2,1,0:T(8,128)(2,1)}, u32[]{:S(2)}) copy-start(bf16[8,512,128]{2,1,0:T(8,128)(2,1)} %param.15) | copy-start | bytes 3145732
  6.5 125.5 %all-gather.2.cloned.1.call-start = ((), (), s32[]{:S(2)}) async-start(), calls=%async_computation.2 | async-start | bytes 4259840 | tf_op jit(solution)/shard_map/all_gather | solution.py:92
  34.3 96.5 %all-to-all-start = ((bf16[8,8,1536]{2,0,1:T(8,128)(2,1)}), bf16[8,8,1536]{2,0,1:T(8,128)(2,1)S(1)}, u32[]{:S(2)}, u32[]{:S(2)}) async-start(bf16[8,8,1536]{2,0,1:T(8,128)(2,1)} %bitcast.80), calls=%async_computation | async-start | bytes 393216 | tf_op jit(solution)/shard_map/all_to_all | solution.py:59
  206.9 1.9 copy-start.1
Sparse Core Ops, SparseCore 0:
  34.4 90.0 all-gather.1
where the time goes:
time: 230 us; the launch traced here: 228 us
  blocking collectives  127 us (55%)
  local copies, waits for them, and re-layouts  27.6 us (12%)
  loops' own time  20.3 us (9%)
  matrix products  19.7 us (9%)
  between operations  15 us (7%)
  other arithmetic  14.7 us (6%)
  starting transfers between devices  3.92 us (2%)
    all_gather x1, blocking collectives, on_device(): seg_rope = lax.all_gather(span_rope, 'ctx', axis=0, tiled=True)  68.3 us
    all_gather x1, blocking collectives, on_device(): lax.all_gather(latent, 'head', axis=0, tiled=True)  27.7 us
    another operation x1, loops' own time, on_device(): lax.fori_loop(0, row_count // sub_rows, advance, (fresh_state, fresh_state))  19.5 us
    all_gather x1, blocking collectives, on_device(): lax.all_gather(rope_key, 'head', axis=0, tiled=True)  19.4 us
    all_to_all x1, blocking collectives, on_device(): lax.all_to_all(out_span, 'head', split_axis=0, concat_axis=1, tiled=True)  11.8 us
    slice x16, local copies, waits for them, and re-layouts, advance(): any_visible = jnp.min(k_pos) <= q_pos[half_rows - 1]  9.37 us
    dynamic_slice x8, local copies, waits for them, and re-layouts, advance(): k_lat = lax.dynamic_slice_in_dim(seg_lat, offset, sub_rows, 0)  8.67 us
    dynamic_slice x8, local copies, waits for them, and re-layouts, advance(): k_rope = lax.dynamic_slice_in_dim(seg_rope, offset, sub_rows, 0)  7.36 us
  transfers between devices with their start and end apart: 2, of which 0 were waited for; matrix products, arithmetic and copies ran while one was open for 2% of the time, Pallas kernels for 0%

commit v1 on v0

v1 whole, which is shorter than its diff:
```python
import functools

import jax
import jax.numpy as jnp
from jax import lax
from jax.experimental import pallas as pl
from jax.experimental.pallas import tpu as pltpu
from jax.sharding import PartitionSpec as P

HALF = 32
DL = 512
DR = 64
DN = 128
DV = 128
DQ = DN + DR
WIDE = 640
STAT = 128
NX = 4
NY = 8
NZ = 8
HEADS = 8
SPAN = 64
FLOOR_SCORE = -1e30
LOG2E = 1.4426950408889634
SCALE2 = DQ ** (-0.5) * LOG2E


def ctx_of(y, x, core):
    return ((y % NY) * NX + (x % NX)) * 2 + core


def along_x(step):
    return [
        (ctx_of(y, x, c), ctx_of(y, x + step, c))
        for y in range(NY)
        for x in range(NX)
        for c in range(2)
    ]


CORE_SWAP = [(i, i ^ 1) for i in range(NX * NY * 2)]
Y_GROUPS = [[ctx_of(y, x, c) for y in range(NY)] for x in range(NX) for c in range(2)]


def attend_kernel(place_ref, order_ref, q0, q1, q2, q3, kv_own, kv_sib, w_uk, w_uv, out_ref, keys, qs, mask, stat):
    me = place_ref[0]
    core = me % 2
    x = (me // 2) % NX
    y = me // (2 * NX)
    rows = NX * SPAN
    key_count = 2 * NY * SPAN
    keys[: NY * SPAN] = kv_own[...]
    keys[NY * SPAN :] = kv_sib[...]
    lane = lax.broadcasted_iota(jnp.int32, (1, key_count), 1)
    key_pos = lane % HALF
    for side in range(2):
        side_core = core if side == 0 else 1 - core
        for yy in range(NY):
            slot = (yy * NX + x) * 2 + side_core
            for half in range(2):
                which = (side * NY + yy) * 2 + half
                key_pos = key_pos + jnp.where(lane // HALF == which, order_ref[2 * slot + half] * HALF, 0)
    row = lax.broadcasted_iota(jnp.int32, (rows, 1), 0)
    q_pos = row % HALF
    for step in range(NX):
        slot = (y * NX + (x - step + NX) % NX) * 2 + core
        for half in range(2):
            q_pos = q_pos + jnp.where(row // HALF == 2 * step + half, order_ref[2 * slot + half] * HALF, 0)
    mask[...] = jnp.where(key_pos <= q_pos, 0.0, FLOOR_SCORE)
    for step, q in enumerate((q0, q1, q2, q3)):
        for h in range(HEADS):
            here = slice(step * SPAN, (step + 1) * SPAN)
            qs[h, here, :DN] = q[:, h * DQ : h * DQ + DN]
            qs[h, here, DN : DN + DR] = q[:, h * DQ + DN : (h + 1) * DQ]
            qs[h, here, DN + DR :] = jnp.zeros((SPAN, DR), jnp.bfloat16)
    stat[...] = jnp.zeros_like(stat)
    lanes = lax.broadcasted_iota(jnp.int32, (rows, STAT), 1)

    def head(h, carry):
        q_lat = lax.dot_general(
            qs[h, :, :DN], w_uk[h], (((1,), (1,)), ((), ())), preferred_element_type=jnp.float32
        ).astype(jnp.bfloat16)
        q_all = jnp.concatenate([q_lat, qs[h, :, DN:]], axis=1)
        scores = lax.dot_general(
            q_all, keys[...], (((1,), (1,)), ((), ())), preferred_element_type=jnp.float32
        )
        scores = scores * SCALE2 + mask[...]
        top = jnp.max(scores, axis=1, keepdims=True)
        weight = jnp.exp2(scores - top)
        total = jnp.sum(weight, axis=1, keepdims=True)
        lat = jnp.dot(weight.astype(jnp.bfloat16), keys[:, :DL], preferred_element_type=jnp.float32)
        o_lat = (lat / total).astype(jnp.bfloat16)
        proj = jnp.dot(o_lat, w_uv[h], preferred_element_type=jnp.float32).astype(jnp.bfloat16)
        for step in range(NX):
            out_ref[step, :, pl.ds(pl.multiple_of(h * DV, DV), DV)] = proj[step * SPAN : (step + 1) * SPAN]
        level = top + jnp.log2(total)
        stat[...] = jnp.where(lanes % HEADS == h, level, stat[...])
        return carry

    lax.fori_loop(0, HEADS, head, 0)
    level = stat[...]
    high = level.astype(jnp.bfloat16)
    rest = level - high.astype(jnp.float32)
    middle = rest.astype(jnp.bfloat16)
    low = (rest - middle.astype(jnp.float32)).astype(jnp.bfloat16)
    part = lanes // HEADS
    packed = jnp.where(
        part == 0,
        high.astype(jnp.float32),
        jnp.where(part == 1, middle.astype(jnp.float32), jnp.where(part == 2, low.astype(jnp.float32), 0.0)),
    ).astype(jnp.bfloat16)
    for step in range(NX):
        out_ref[step, :, HEADS * DV :] = packed[step * SPAN : (step + 1) * SPAN]


def attend(place, order, qs, kv_own, kv_sib, w_uk, w_uv):
    vmem = pl.BlockSpec(memory_space=pltpu.VMEM)
    smem = pl.BlockSpec(memory_space=pltpu.SMEM)
    rows = NX * SPAN
    key_count = 2 * NY * SPAN
    return pl.pallas_call(
        attend_kernel,
        out_shape=jax.ShapeDtypeStruct((NX, SPAN, HEADS * DV + STAT), jnp.bfloat16),
        in_specs=[smem, smem] + [vmem] * 8,
        out_specs=vmem,
        scratch_shapes=[
            pltpu.VMEM((key_count, WIDE), jnp.bfloat16),
            pltpu.VMEM((HEADS, rows, DN + 2 * DR), jnp.bfloat16),
            pltpu.VMEM((rows, key_count), jnp.float32),
            pltpu.VMEM((rows, STAT), jnp.float32),
        ],
        compiler_params=pltpu.CompilerParams(vmem_limit_bytes=32 * 1024 * 1024),
        cost_estimate=pl.CostEstimate(flops=6_000_000_000, bytes_accessed=5_000_000, transcendentals=2_000_000),
    )(place, order, *qs, kv_own, kv_sib, w_uk, w_uv)


def merge_kernel(p0, p1, p2, p3, out_ref):
    parts = (p0, p1, p2, p3)
    levels = []
    for p in parts:
        pieces = p[:, HEADS * DV :].astype(jnp.float32)
        levels.append(pieces[:, :HEADS] + pieces[:, HEADS : 2 * HEADS] + pieces[:, 2 * HEADS : 3 * HEADS])
    top = functools.reduce(jnp.maximum, levels)
    shares = [jnp.exp2(level - top) for level in levels]
    whole = functools.reduce(jnp.add, shares)
    shares = [share / whole for share in shares]
    for h in range(HEADS):
        cols = slice(h * DV, (h + 1) * DV)
        acc = jnp.zeros((SPAN, DV), jnp.float32)
        for p, share in zip(parts, shares):
            acc = acc + share[:, h : h + 1] * p[:, cols].astype(jnp.float32)
        out_ref[:, cols] = acc.astype(jnp.bfloat16)


def merge(parts):
    vmem = pl.BlockSpec(memory_space=pltpu.VMEM)
    return pl.pallas_call(
        merge_kernel,
        out_shape=jax.ShapeDtypeStruct((SPAN, HEADS * DV), jnp.bfloat16),
        in_specs=[vmem] * NX,
        out_specs=vmem,
        cost_estimate=pl.CostEstimate(flops=1_000_000, bytes_accessed=800_000, transcendentals=2000),
    )(*parts)


def copies(value, count):
    return jnp.broadcast_to(value[None], (count,) + value.shape)


def on_device(queries, latent, rope_key, w_uk, w_uv, block_order):
    place = lax.axis_index("ctx").astype(jnp.int32).reshape(1)
    kv = jnp.concatenate([latent, rope_key, jnp.zeros_like(rope_key)], axis=1)
    kv = lax.all_to_all(copies(kv, NZ), "head", split_axis=0, concat_axis=0, tiled=True)
    kv = kv.reshape(SPAN, WIDE)
    kv = lax.all_to_all(
        copies(kv, NY), "ctx", split_axis=0, concat_axis=0, tiled=True, axis_index_groups=Y_GROUPS
    )
    kv_own = kv.reshape(NY * SPAN, WIDE)
    kv_sib = lax.ppermute(kv_own, "ctx", CORE_SWAP)
    q_own = lax.all_to_all(queries, "head", split_axis=1, concat_axis=0, tiled=True)
    qs = [q_own] + [lax.ppermute(q_own, "ctx", along_x(step)) for step in range(1, NX)]
    partial = attend(place, block_order, qs, kv_own, kv_sib, w_uk, w_uv)
    parts = [partial[0]] + [lax.ppermute(partial[step], "ctx", along_x(-step)) for step in range(1, NX)]
    merged = merge(parts)
    return lax.all_to_all(merged, "head", split_axis=0, concat_axis=1, tiled=True)


def solution(mesh):
    in_specs = (
        P(("ctx", "head"), None),
        P(("ctx", "head"), None),
        P(("ctx", "head"), None),
        P("head", None, None),
        P("head", None, None),
        P(),
    )
    out_specs = P(("ctx", "head"), None)
    return jax.shard_map(
        on_device, mesh=mesh, in_specs=in_specs, out_specs=out_specs, check_vma=False
    )
```

time: 230 us -> 125 us (0.54)
  the two profiles are of different devices: /device:TPU:1 before, /device:TPU:6 now
where the time goes in v1:
time: 125 us; the launch traced here: 124 us
  blocking collectives  71 us (57%)
  starting transfers between devices  20.9 us (17%)
  Pallas kernels  14.8 us (12%)
  waiting for transfers between devices  14 us (11%)
  local copies, waits for them, and re-layouts  2.77 us (2%)
    all_to_all x1, blocking collectives, on_device(): lax.all_to_all(copies(kv, NY), 'ctx', split_axis=0, concat_axis=0, tiled=...  26 us
    all_to_all x1, blocking collectives, on_device(): lax.all_to_all(copies(kv, NZ), 'head', split_axis=0, concat_axis=0, tiled...  18.8 us
    all_to_all x1, blocking collectives, on_device(): lax.all_to_all(queries, 'head', split_axis=1, concat_axis=0, tiled=True)  13.8 us
    pallas_call x1, Pallas kernels, attend(): pl.pallas_call(attend_kernel, out_shape=jax.ShapeDtypeStruct((NX, SPAN, H...  12.6 us
    all_to_all x1, blocking collectives, on_device(): lax.all_to_all(merged, 'head', split_axis=0, concat_axis=1, tiled=True)  12.3 us
    ppermute x3, starting transfers between devices, on_device(): lax.ppermute(q_own, 'ctx', along_x(step))  9.75 us
    ppermute x3, starting transfers between devices, on_device(): lax.ppermute(partial[step], 'ctx', along_x(-step))  9.25 us
    ppermute x3, waiting for transfers between devices, on_device(): lax.ppermute(partial[step], 'ctx', along_x(-step))  7.14 us
  transfers between devices with their start and end apart: 7, of which 5 were waited for; matrix products, arithmetic and copies ran while one was open for 0% of the time, Pallas kernels for 0%

profile of v1, /device:TPU:6, one launch (start us, length us, event | category | flops | bytes accessed | tf_op | source)
XLA Modules:
  0.0 124.3 jit_solution(10326671698014712888)
XLA Ops:
  0.0 0.0 copy-start.7
  0.0 0.1 pad.2.clone
  0.1 0.6 copy-done.7
  0.7 0.7 maximum_maximum_fusion
  1.4 0.0 copy-start.3
  1.4 18.8 %all_to_all.48 = bf16[8,8,640]{2,1,0:T(8,128)(2,1)S(1)} all-to-all(bf16[8,8,640]{2,1,0:T(8,128)(2,1)S(1)} %broadcast_in_dim.17), channel_id=1, replica_groups=mesh['ctx'=64,'head'=8] {'head'}, dimensions={0} | all-to-all | bytes 163840 | tf_op jit(solution)/shard_map/all_to_all | solution.py:173
  20.2 0.0 copy-start
  20.2 0.0 copy-start.1
  20.2 0.1 broadcast_in_dim.19
  20.3 26.0 %all_to_all.49 = bf16[8,64,640]{2,1,0:T(8,128)(2,1)S(1)} all-to-all(bf16[8,64,640]{2,1,0:T(8,128)(2,1)S(1)} %broadcast_in_dim.19), channel_id=1, replica_groups={{0,64,128,192,256,320,384,448},{8,72,136,200,264,328,392,456},{16,80,14..., dimensions={0} | all-to-all | bytes 1310720 | tf_op jit(solution)/shard_map/all_to_all | solution.py:175
  46.3 1.9 %collective-permute-start.3 = (bf16[512,640]{1,0:T(8,128)(2,1)S(1)}, bf16[512,640]{1,0:T(8,128)(2,1)}, u32[]{:S(2)}, u32[]{:S(2)}) collective-permute-start(bf16[512,640]{1,0:T(8,128)(2,1)S(1)} %bitcast.19), channel_id=1, source_target_pairs={{0,8},{8,0},{16,24},{24,16},{32,40},{40,32},{48,56},{56,48},{64,72... | collective-permute-start | bytes 1966088 | tf_op jit(solution)/shard_map/ppermute | solution.py:179
  48.2 0.0 copy-done.3
  48.2 13.8 %all_to_all.50 = bf16[8,8,1536]{2,0,1:T(8,128)(2,1)S(1)} all-to-all(bf16[8,8,1536]{2,0,1:T(8,128)(2,1)S(1)} %bitcast.28), channel_id=1, replica_groups=mesh['ctx'=64,'head'=8] {'head'}, dimensions={1} | all-to-all | bytes 393216 | tf_op jit(solution)/shard_map/all_to_all | solution.py:180
  62.0 2.7 %collective-permute-start.2 = (bf16[64,1536]{1,0:T(8,128)(2,1)S(1)}, bf16[64,1536]{1,0:T(8,128)(2,1)S(1)}, u32[]{:S(2)}, u32[]{:S(2)}) collective-permute-start(bf16[64,1536]{1,0:T(8,128)(2,1)S(1)} %bitcast.21), channel_id=1, source_target_pairs={{0,48},{8,56},{16,0},{24,8},{32,16},{40,24},{48,32},{56,40},{64,11... | collective-permute-start | bytes 589832 | tf_op jit(solution)/shard_map/ppermute | solution.py:181
  64.7 3.0 %collective-permute-start.1 = (bf16[64,1536]{1,0:T(8,128)(2,1)S(1)}, bf16[64,1536]{1,0:T(8,128)(2,1)S(1)}, u32[]{:S(2)}, u32[]{:S(2)}) collective-permute-start(bf16[64,1536]{1,0:T(8,128)(2,1)S(1)} %bitcast.22), channel_id=1, source_target_pairs={{0,32},{8,40},{16,48},{24,56},{32,0},{40,8},{48,16},{56,24},{64,96... | collective-permute-start | bytes 589832 | tf_op jit(solution)/shard_map/ppermute | solution.py:181
  67.8 4.0 %collective-permute-start = (bf16[64,1536]{1,0:T(8,128)(2,1)S(1)}, bf16[64,1536]{1,0:T(8,128)(2,1)S(1)}, u32[]{:S(2)}, u32[]{:S(2)}) collective-permute-start(bf16[64,1536]{1,0:T(8,128)(2,1)S(1)} %bitcast.23), channel_id=1, source_target_pairs={{0,16},{8,24},{16,32},{24,40},{32,48},{40,56},{48,0},{56,8},{64,80... | collective-permute-start | bytes 589832 | tf_op jit(solution)/shard_map/ppermute | solution.py:181
  71.8 0.0 copy-start.2
  71.8 4.4 %collective-permute-done.2.q3 = bf16[64,1536]{1,0:T(8,128)(2,1)S(1)} collective-permute-done((bf16[64,1536]{1,0:T(8,128)(2,1)S(1)}, bf16[64,1536]{1,0:T(8,128)(2,1)S(1)}, u32[]{:S(2)}, u32[]{:S(2)}) %collective-permute-start.2) | collective-permute-done | bytes 196640 | tf_op jit(solution)/shard_map/ppermute | solution.py:181
  76.2 0.0 collective-permute-done.1.q2
  76.2 2.5 %collective-permute-done.q1 = bf16[64,1536]{1,0:T(8,128)(2,1)S(1)} collective-permute-done((bf16[64,1536]{1,0:T(8,128)(2,1)S(1)}, bf16[64,1536]{1,0:T(8,128)(2,1)S(1)}, u32[]{:S(2)}, u32[]{:S(2)}) %collective-permute-start) | collective-permute-done | bytes 196640 | tf_op jit(solution)/shard_map/ppermute | solution.py:181
  78.7 0.0 collective-permute-done.3.kv_sib
  78.7 0.0 copy-done
  78.7 0.0 copy-done.1
  78.7 0.0 copy-done.2
  78.7 12.6 %shard_map.64 = bf16[4,64,1152]{2,1,0:T(8,128)(2,1)S(1)} custom-call(s32[1]{0:T(128)} %bitcast.place_ref, s32[128]{0:T(128)S(1)} %copy-done.2, bf16[64,1536]{1,0:T(8,128)(2,1)S(1)} %bitcast.24, bf16[64,1536]{1,0:T(8,128)(2,1)S(1)} %collective-permute-done.q1, bf16[64,1536]{1,0:T(8,128)(2,1)S(1)} %collective-permute-done.1.q2, ...), custom_call_target="tpu_custom_call" | custom-call | flops 6000000000 | bytes 5000000 | tf_op jit(solution)/shard_map/pallas_call | solution.py:121
  91.3 0.7 slice_bitcast_fusion
  92.0 4.6 %collective-permute-start.6 = (bf16[64,1152]{1,0:T(8,128)(2,1)S(1)}, bf16[64,1152]{1,0:T(8,128)(2,1)S(1)}, u32[]{:S(2)}, u32[]{:S(2)}) collective-permute-start(bf16[64,1152]{1,0:T(8,128)(2,1)S(1)} %get-tuple-element.5), channel_id=1, source_target_pairs={{0,16},{8,24},{16,32},{24,40},{32,48},{40,56},{48,0},{56,8},{64,80... | collective-permute-start | bytes 442376 | tf_op jit(solution)/shard_map/ppermute | solution.py:183
  96.6 2.1 %collective-permute-start.5 = (bf16[64,1152]{1,0:T(8,128)(2,1)S(1)}, bf16[64,1152]{1,0:T(8,128)(2,1)S(1)}, u32[]{:S(2)}, u32[]{:S(2)}) collective-permute-start(bf16[64,1152]{1,0:T(8,128)(2,1)S(1)} %get-tuple-element.6), channel_id=1, source_target_pairs={{0,32},{8,40},{16,48},{24,56},{32,0},{40,8},{48,16},{56,24},{64,96... | collective-permute-start | bytes 442376 | tf_op jit(solution)/shard_map/ppermute | solution.py:183
  98.7 2.6 %collective-permute-start.4 = (bf16[64,1152]{1,0:T(8,128)(2,1)S(1)}, bf16[64,1152]{1,0:T(8,128)(2,1)S(1)}, u32[]{:S(2)}, u32[]{:S(2)}) collective-permute-start(bf16[64,1152]{1,0:T(8,128)(2,1)S(1)} %get-tuple-element.7), channel_id=1, source_target_pairs={{0,48},{8,56},{16,0},{24,8},{32,16},{40,24},{48,32},{56,40},{64,11... | collective-permute-start | bytes 442376 | tf_op jit(solution)/shard_map/ppermute | solution.py:183
  101.3 1.6 %collective-permute-done.6.p3 = bf16[64,1152]{1,0:T(8,128)(2,1)S(1)} collective-permute-done((bf16[64,1152]{1,0:T(8,128)(2,1)S(1)}, bf16[64,1152]{1,0:T(8,128)(2,1)S(1)}, u32[]{:S(2)}, u32[]{:S(2)}) %collective-permute-start.6) | collective-permute-done | bytes 147488 | tf_op jit(solution)/shard_map/ppermute | solution.py:183
  102.8 0.0 copy-start.4
  102.8 3.7 %collective-permute-done.5.p2 = bf16[64,1152]{1,0:T(8,128)(2,1)S(1)} collective-permute-done((bf16[64,1152]{1,0:T(8,128)(2,1)S(1)}, bf16[64,1152]{1,0:T(8,128)(2,1)S(1)}, u32[]{:S(2)}, u32[]{:S(2)}) %collective-permute-start.5) | collective-permute-done | bytes 147488 | tf_op jit(solution)/shard_map/ppermute | solution.py:183
  106.6 0.0 copy-start.5
  106.6 1.9 %collective-permute-done.4.p1 = bf16[64,1152]{1,0:T(8,128)(2,1)S(1)} collective-permute-done((bf16[64,1152]{1,0:T(8,128)(2,1)S(1)}, bf16[64,1152]{1,0:T(8,128)(2,1)S(1)}, u32[]{:S(2)}, u32[]{:S(2)}) %collective-permute-start.4) | collective-permute-done | bytes 147488 | tf_op jit(solution)/shard_map/ppermute | solution.py:183
  108.4 0.0 copy-start.6
  108.4 0.0 copy-done.4
  108.4 0.0 copy-done.5
  108.4 0.6 copy-done.6
  109.1 2.3 %shard_map.65 = bf16[64,1024]{1,0:T(8,128)(2,1)} custom-call(bf16[64,1152]{1,0:T(8,128)(2,1)} %get-tuple-element.8.p0, bf16[64,1152]{1,0:T(8,128)(2,1)} %copy-done.6, bf16[64,1152]{1,0:T(8,128)(2,1)} %copy-done.5, bf16[64,1152]{1,0:T(8,128)(2,1)} %copy-done.4), custom_call_target="tpu_custom_call" | custom-call | flops 1000000 | bytes 800000 | tf_op jit(solution)/shard_map/pallas_call | solution.py:157
  111.3 12.3 %all_to_all.51 = bf16[8,8,1024]{2,1,0:T(8,128)(2,1)S(1)} all-to-all(bf16[8,8,1024]{2,1,0:T(8,128)(2,1)} %bitcast.26), channel_id=1, replica_groups=mesh['ctx'=64,'head'=8] {'head'}, dimensions={0} | all-to-all | bytes 262144 | tf_op jit(solution)/shard_map/all_to_all | solution.py:185
  123.7 0.7 copy.8
  (2 shorter events, 0.0 us)
Async XLA Ops:
  0.0 0.7 copy-start.7
  1.4 46.8 %copy-start.3 = (bf16[8,12288]{1,0:T(8,128)(2,1)S(1)}, bf16[8,12288]{1,0:T(8,128)(2,1)}, u32[]{:S(2)}) copy-start(bf16[8,12288]{1,0:T(8,128)(2,1)} %param.6) | copy-start | bytes 589828
  20.2 58.5 %copy-start = (bf16[8,512,128]{2,1,0:T(8,128)(2,1)S(1)}, bf16[8,512,128]{2,1,0:T(8,128)(2,1)}, u32[]{:S(2)}) copy-start(bf16[8,512,128]{2,1,0:T(8,128)(2,1)} %w_uk.1) | copy-start | bytes 3145732
  20.2 58.5 %copy-start.1 = (bf16[8,512,128]{2,1,0:T(8,128)(2,1)S(1)}, bf16[8,512,128]{2,1,0:T(8,128)(2,1)}, u32[]{:S(2)}) copy-start(bf16[8,512,128]{2,1,0:T(8,128)(2,1)} %w_uv.1) | copy-start | bytes 3145732
  46.3 32.4 %collective-permute-start.3 = (bf16[512,640]{1,0:T(8,128)(2,1)S(1)}, bf16[512,640]{1,0:T(8,128)(2,1)}, u32[]{:S(2)}, u32[]{:S(2)}) collective-permute-start(bf16[512,640]{1,0:T(8,128)(2,1)S(1)} %bitcast.19), channel_id=1, source_target_pairs={{0,8},{8,0},{16,24},{24,16},{32,40},{40,32},{48,56},{56,48},{64,72... | collective-permute-start | bytes 1966088 | tf_op jit(solution)/shard_map/ppermute | solution.py:179
  62.0 14.2 %collective-permute-start.2 = (bf16[64,1536]{1,0:T(8,128)(2,1)S(1)}, bf16[64,1536]{1,0:T(8,128)(2,1)S(1)}, u32[]{:S(2)}, u32[]{:S(2)}) collective-permute-start(bf16[64,1536]{1,0:T(8,128)(2,1)S(1)} %bitcast.21), channel_id=1, source_target_pairs={{0,48},{8,56},{16,0},{24,8},{32,16},{40,24},{48,32},{56,40},{64,11... | collective-permute-start | bytes 589832 | tf_op jit(solution)/shard_map/ppermute | solution.py:181
  64.7 11.5 %collective-permute-start.1 = (bf16[64,1536]{1,0:T(8,128)(2,1)S(1)}, bf16[64,1536]{1,0:T(8,128)(2,1)S(1)}, u32[]{:S(2)}, u32[]{:S(2)}) collective-permute-start(bf16[64,1536]{1,0:T(8,128)(2,1)S(1)} %bitcast.22), channel_id=1, source_target_pairs={{0,32},{8,40},{16,48},{24,56},{32,0},{40,8},{48,16},{56,24},{64,96... | collective-permute-start | bytes 589832 | tf_op jit(solution)/shard_map/ppermute | solution.py:181
  67.8 10.9 %collective-permute-start = (bf16[64,1536]{1,0:T(8,128)(2,1)S(1)}, bf16[64,1536]{1,0:T(8,128)(2,1)S(1)}, u32[]{:S(2)}, u32[]{:S(2)}) collective-permute-start(bf16[64,1536]{1,0:T(8,128)(2,1)S(1)} %bitcast.23), channel_id=1, source_target_pairs={{0,16},{8,24},{16,32},{24,40},{32,48},{40,56},{48,0},{56,8},{64,80... | collective-permute-start | bytes 589832 | tf_op jit(solution)/shard_map/ppermute | solution.py:181
  71.8 6.9 %copy-start.2 = (s32[128]{0:T(128)S(1)}, s32[128]{0:T(128)}, u32[]{:S(2)}) copy-start(s32[128]{0:T(128)} %order_ref.1) | copy-start | bytes 1540
  92.0 10.8 %collective-permute-start.6 = (bf16[64,1152]{1,0:T(8,128)(2,1)S(1)}, bf16[64,1152]{1,0:T(8,128)(2,1)S(1)}, u32[]{:S(2)}, u32[]{:S(2)}) collective-permute-start(bf16[64,1152]{1,0:T(8,128)(2,1)S(1)} %get-tuple-element.5), channel_id=1, source_target_pairs={{0,16},{8,24},{16,32},{24,40},{32,48},{40,56},{48,0},{56,8},{64,80... | collective-permute-start | bytes 442376 | tf_op jit(solution)/shard_map/ppermute | solution.py:183
  96.6 10.0 %collective-permute-start.5 = (bf16[64,1152]{1,0:T(8,128)(2,1)S(1)}, bf16[64,1152]{1,0:T(8,128)(2,1)S(1)}, u32[]{:S(2)}, u32[]{:S(2)}) collective-permute-start(bf16[64,1152]{1,0:T(8,128)(2,1)S(1)} %get-tuple-element.6), channel_id=1, source_target_pairs={{0,32},{8,40},{16,48},{24,56},{32,0},{40,8},{48,16},{56,24},{64,96... | collective-permute-start | bytes 442376 | tf_op jit(solution)/shard_map/ppermute | solution.py:183
  98.7 9.7 %collective-permute-start.4 = (bf16[64,1152]{1,0:T(8,128)(2,1)S(1)}, bf16[64,1152]{1,0:T(8,128)(2,1)S(1)}, u32[]{:S(2)}, u32[]{:S(2)}) collective-permute-start(bf16[64,1152]{1,0:T(8,128)(2,1)S(1)} %get-tuple-element.7), channel_id=1, source_target_pairs={{0,48},{8,56},{16,0},{24,8},{32,16},{40,24},{48,32},{56,40},{64,11... | collective-permute-start | bytes 442376 | tf_op jit(solution)/shard_map/ppermute | solution.py:183
  102.8 5.6 %copy-start.4 = (bf16[64,1152]{1,0:T(8,128)(2,1)}, bf16[64,1152]{1,0:T(8,128)(2,1)S(1)}, u32[]{:S(2)}) copy-start(bf16[64,1152]{1,0:T(8,128)(2,1)S(1)} %collective-permute-done.6.p3) | copy-start | bytes 442372
  106.6 1.9 %copy-start.5 = (bf16[64,1152]{1,0:T(8,128)(2,1)}, bf16[64,1152]{1,0:T(8,128)(2,1)S(1)}, u32[]{:S(2)}) copy-start(bf16[64,1152]{1,0:T(8,128)(2,1)S(1)} %collective-permute-done.5.p2) | copy-start | bytes 442372
  108.4 0.6 copy-start.6

commit v2 on v1

v2 whole, which is shorter than its diff:
```python
import functools

import jax
import jax.numpy as jnp
from jax import lax
from jax.experimental import pallas as pl
from jax.experimental.pallas import tpu as pltpu
from jax.sharding import PartitionSpec as P

HALF = 32
DL = 512
DR = 64
DN = 128
DV = 128
DQ = DN + DR
WIDE = 640
STAT = 128
EXTRA = 128
NX = 4
NY = 8
NZ = 8
HEADS = 8
SPAN = 64
FLOOR_SCORE = -1e30
LOG2E = 1.4426950408889634
SCALE2 = DQ ** (-0.5) * LOG2E


def ctx_of(y, x, core):
    return ((y % NY) * NX + (x % NX)) * 2 + core


def along_x(step):
    return [
        (ctx_of(y, x, c), ctx_of(y, x + step, c))
        for y in range(NY)
        for x in range(NX)
        for c in range(2)
    ]


CORE_SWAP = [(i, i ^ 1) for i in range(NX * NY * 2)]
Y_GROUPS = [[ctx_of(y, x, c) for y in range(NY)] for x in range(NX) for c in range(2)]


def prepare_kernel(place_ref, order_ref, q0, q1, q2, q3, w_uk, out_ref, nope):
    me = place_ref[0]
    core = me % 2
    x = (me // 2) % NX
    y = me // (2 * NX)
    blocks = 2 * NY * SPAN // HALF
    lane = lax.broadcasted_iota(jnp.int32, (HALF, EXTRA), 1)
    token = lax.broadcasted_iota(jnp.int32, (HALF, EXTRA), 0)
    key_block = jnp.zeros((HALF, EXTRA), jnp.int32)
    for which in range(blocks):
        side_core = core if which < blocks // 2 else 1 - core
        slot = (((which // 2) % NY) * NX + x) * 2 + side_core
        key_block = jnp.where(lane == which, order_ref[2 * slot + which % 2], key_block)
    for step, q in enumerate((q0, q1, q2, q3)):
        slot = (y * NX + (x - step + NX) % NX) * 2 + core
        here = slice(step * SPAN, (step + 1) * SPAN)
        floors = []
        for half in range(2):
            ahead = (lane < blocks) & (key_block > order_ref[2 * slot + half])
            if step == 0:
                own = lane - blocks - half * HALF
                ahead = ahead | ((own >= 0) & (own < HALF) & (own > token))
            floors.append(jnp.where(ahead, FLOOR_SCORE, 0.0))
        floor = jnp.concatenate(floors, axis=0).astype(jnp.bfloat16)
        for h in range(HEADS):
            nope[h, here] = q[:, h * DQ : h * DQ + DN]
            out_ref[h, here, DL : DL + DR] = q[:, h * DQ + DN : (h + 1) * DQ]
            out_ref[h, here, DL + DR : WIDE] = jnp.zeros((SPAN, DR), jnp.bfloat16)
            out_ref[h, here, WIDE:] = floor
    for h in range(HEADS):
        out_ref[h, :, :DL] = lax.dot_general(
            nope[h], w_uk[h], (((1,), (1,)), ((), ())), preferred_element_type=jnp.float32
        ).astype(jnp.bfloat16)


def prepare(place, order, qs, w_uk):
    vmem = pl.BlockSpec(memory_space=pltpu.VMEM)
    smem = pl.BlockSpec(memory_space=pltpu.SMEM)
    rows = NX * SPAN
    return pl.pallas_call(
        prepare_kernel,
        out_shape=jax.ShapeDtypeStruct((HEADS, rows, WIDE + EXTRA), jnp.bfloat16),
        in_specs=[smem, smem] + [vmem] * 5,
        out_specs=vmem,
        scratch_shapes=[pltpu.VMEM((HEADS, rows, DN), jnp.bfloat16)],
        compiler_params=pltpu.CompilerParams(vmem_limit_bytes=16 * 1024 * 1024),
        cost_estimate=pl.CostEstimate(flops=4_000_000_000, bytes_accessed=6_000_000, transcendentals=0),
    )(place, order, *qs, w_uk)


def attend_kernel(place_ref, q_ref, kv_own, kv_sib, w_uv, out0, out1, out2, out3, keys, stat):
    outs = (out0, out1, out2, out3)
    y = place_ref[0] // (2 * NX)
    rows = NX * SPAN
    key_count = 2 * NY * SPAN
    blocks = key_count // HALF
    keys[: NY * SPAN, :WIDE] = kv_own[...]
    keys[NY * SPAN :, :WIDE] = kv_sib[...]
    key = lax.broadcasted_iota(jnp.int32, (key_count, EXTRA), 0)
    col = lax.broadcasted_iota(jnp.int32, (key_count, EXTRA), 1)
    own_first = 2 * y
    own_col = blocks + key - own_first * HALF
    in_own = (key // HALF == own_first) | (key // HALF == own_first + 1)
    ones = (col == key // HALF) | (in_own & (col == own_col))
    keys[:, WIDE:] = jnp.where(ones, 1.0, 0.0).astype(jnp.bfloat16)
    stat[...] = jnp.zeros_like(stat)
    lanes = lax.broadcasted_iota(jnp.int32, (rows, STAT), 1)

    def pair(p, carry):
        heads = [2 * p, 2 * p + 1]
        scores = [
            lax.dot_general(q_ref[h], keys[...], (((1,), (1,)), ((), ())), preferred_element_type=jnp.float32)
            for h in heads
        ]
        levels = []
        for h, s in zip(heads, scores):
            top = jnp.max(s, axis=1, keepdims=True)
            weight = jnp.exp2((s - top) * SCALE2)
            total = jnp.sum(weight, axis=1, keepdims=True)
            lat = jnp.dot(weight.astype(jnp.bfloat16), keys[:, :DL], preferred_element_type=jnp.float32)
            o_lat = (lat * (1.0 / total)).astype(jnp.bfloat16)
            proj = jnp.dot(o_lat, w_uv[h], preferred_element_type=jnp.float32).astype(jnp.bfloat16)
            for step in range(NX):
                outs[step][:, pl.ds(pl.multiple_of(h * DV, DV), DV)] = proj[step * SPAN : (step + 1) * SPAN]
            levels.append(top * SCALE2 + jnp.log2(total))
        held = stat[...]
        for h, level in zip(heads, levels):
            held = jnp.where(lanes % HEADS == h, level, held)
        stat[...] = held
        return carry

    lax.fori_loop(0, HEADS // 2, pair, 0)
    level = stat[...]
    high = level.astype(jnp.bfloat16)
    rest = level - high.astype(jnp.float32)
    middle = rest.astype(jnp.bfloat16)
    low = (rest - middle.astype(jnp.float32)).astype(jnp.bfloat16)
    part = lanes // HEADS
    packed = jnp.where(
        part == 0,
        high.astype(jnp.float32),
        jnp.where(part == 1, middle.astype(jnp.float32), jnp.where(part == 2, low.astype(jnp.float32), 0.0)),
    ).astype(jnp.bfloat16)
    for step in range(NX):
        outs[step][:, HEADS * DV :] = packed[step * SPAN : (step + 1) * SPAN]


def attend(place, q_all, kv_own, kv_sib, w_uv):
    vmem = pl.BlockSpec(memory_space=pltpu.VMEM)
    smem = pl.BlockSpec(memory_space=pltpu.SMEM)
    rows = NX * SPAN
    key_count = 2 * NY * SPAN
    return pl.pallas_call(
        attend_kernel,
        out_shape=[jax.ShapeDtypeStruct((SPAN, HEADS * DV + STAT), jnp.bfloat16)] * NX,
        in_specs=[smem] + [vmem] * 4,
        out_specs=[vmem] * NX,
        scratch_shapes=[
            pltpu.VMEM((key_count, WIDE + EXTRA), jnp.bfloat16),
            pltpu.VMEM((rows, STAT), jnp.float32),
        ],
        compiler_params=pltpu.CompilerParams(vmem_limit_bytes=24 * 1024 * 1024),
        cost_estimate=pl.CostEstimate(flops=6_000_000_000, bytes_accessed=5_000_000, transcendentals=2_000_000),
    )(place, q_all, kv_own, kv_sib, w_uv)


def merge_kernel(p0, p1, p2, p3, out_ref):
    parts = (p0, p1, p2, p3)
    levels = []
    for p in parts:
        pieces = p[:, HEADS * DV :].astype(jnp.float32)
        levels.append(pieces[:, :HEADS] + pieces[:, HEADS : 2 * HEADS] + pieces[:, 2 * HEADS : 3 * HEADS])
    top = functools.reduce(jnp.maximum, levels)
    shares = [jnp.exp2(level - top) for level in levels]
    whole = functools.reduce(jnp.add, shares)
    shares = [share / whole for share in shares]
    for h in range(HEADS):
        cols = slice(h * DV, (h + 1) * DV)
        acc = jnp.zeros((SPAN, DV), jnp.float32)
        for p, share in zip(parts, shares):
            acc = acc + share[:, h : h + 1] * p[:, cols].astype(jnp.float32)
        out_ref[:, cols] = acc.astype(jnp.bfloat16)


def merge(parts):
    vmem = pl.BlockSpec(memory_space=pltpu.VMEM)
    return pl.pallas_call(
        merge_kernel,
        out_shape=jax.ShapeDtypeStruct((SPAN, HEADS * DV), jnp.bfloat16),
        in_specs=[vmem] * NX,
        out_specs=vmem,
        cost_estimate=pl.CostEstimate(flops=1_000_000, bytes_accessed=800_000, transcendentals=2000),
    )(*parts)


def copies(value, count):
    return jnp.broadcast_to(value[None], (count,) + value.shape)


def on_device(queries, latent, rope_key, w_uk, w_uv, block_order):
    place = lax.axis_index("ctx").astype(jnp.int32).reshape(1)
    kv = jnp.concatenate([latent, rope_key, jnp.zeros_like(rope_key)], axis=1)
    both = jnp.concatenate([queries.reshape(8, NZ, HEADS * DQ).swapaxes(0, 1), copies(kv, NZ)], axis=2)
    both = lax.all_to_all(both, "head", split_axis=0, concat_axis=0, tiled=True).reshape(SPAN, HEADS * DQ + WIDE)
    q_own = both[:, : HEADS * DQ]
    kv = lax.all_to_all(
        copies(both[:, HEADS * DQ :], NY), "ctx", split_axis=0, concat_axis=0, tiled=True, axis_index_groups=Y_GROUPS
    )
    kv_own = kv.reshape(NY * SPAN, WIDE)
    kv_sib = lax.ppermute(kv_own, "ctx", CORE_SWAP)
    qs = [q_own] + [lax.ppermute(q_own, "ctx", along_x(step)) for step in range(1, NX)]
    q_all = prepare(place, block_order, qs, w_uk)
    partial = attend(place, q_all, kv_own, kv_sib, w_uv)
    parts = [partial[0]] + [lax.ppermute(partial[step], "ctx", along_x(-step)) for step in range(1, NX)]
    merged = merge(parts)
    return lax.all_to_all(merged, "head", split_axis=0, concat_axis=1, tiled=True)


def solution(mesh):
    in_specs = (
        P(("ctx", "head"), None),
        P(("ctx", "head"), None),
        P(("ctx", "head"), None),
        P("head", None, None),
        P("head", None, None),
        P(),
    )
    out_specs = P(("ctx", "head"), None)
    return jax.shard_map(
        on_device, mesh=mesh, in_specs=in_specs, out_specs=out_specs, check_vma=False
    )
```

time: 125 us -> 111 us (0.89)
  the two profiles are of different devices: /device:TPU:6 before, /device:TPU:8 now
where the time goes in v2:
time: 111 us; the launch traced here: 110 us
  blocking collectives  59 us (53%)
  starting transfers between devices  23.5 us (21%)
  waiting for transfers between devices  12.2 us (11%)
  Pallas kernels  11.6 us (10%)
  local copies, waits for them, and re-layouts  2.14 us (2%)
  other arithmetic  1.75 us (2%)
    all_to_all x1, blocking collectives, on_device(): lax.all_to_all(copies(both[:, HEADS * DQ:], NY), 'ctx', split_axis=0, con...  24.3 us
    all_to_all x1, blocking collectives, on_device(): lax.all_to_all(both, 'head', split_axis=0, concat_axis=0, tiled=True)  22.3 us
    all_to_all x1, blocking collectives, on_device(): lax.all_to_all(merged, 'head', split_axis=0, concat_axis=1, tiled=True)  12.4 us
    ppermute x3, starting transfers between devices, on_device(): lax.ppermute(q_own, 'ctx', along_x(step))  11.4 us
    ppermute x3, starting transfers between devices, on_device(): lax.ppermute(partial[step], 'ctx', along_x(-step))  10.2 us
    pallas_call x1, Pallas kernels, attend(): pl.pallas_call(attend_kernel, out_shape=[jax.ShapeDtypeStruct((SPAN, HEAD...  7.89 us
    ppermute x3, waiting for transfers between devices, on_device(): lax.ppermute(partial[step], 'ctx', along_x(-step))  6.46 us
    ppermute x3, waiting for transfers between devices, on_device(): lax.ppermute(q_own, 'ctx', along_x(step))  5.7 us
  transfers between devices with their start and end apart: 7, of which 4 were waited for; matrix products, arithmetic and copies ran while one was open for 0% of the time, Pallas kernels for 1%

profile of v2, /device:TPU:8, one launch (start us, length us, event | category | flops | bytes accessed | tf_op | source)
XLA Modules:
  0.0 110.4 jit_solution(16831078787492728981)
XLA Ops:
  0.0 0.0 copy-start.3
  0.0 0.0 copy-start.1
  0.0 0.1 pad.4.clone
  0.1 0.8 maximum_maximum_fusion
  0.9 0.9 pad_maximum_fusion
  1.8 22.3 %all_to_all.29 = bf16[8,8,2176]{2,1,0:T(8,128)(2,1)S(1)} all-to-all(bf16[8,8,2176]{2,1,0:T(8,128)(2,1)S(1)} %pad_maximum_fusion), channel_id=1, replica_groups=mesh['ctx'=64,'head'=8] {'head'}, dimensions={0} | all-to-all | bytes 557056 | tf_op jit(solution)/shard_map/all_to_all | solution.py:209
  24.2 0.1 broadcast_in_dim.8
  24.3 24.3 %all_to_all.30 = bf16[8,64,640]{2,1,0:T(8,128)(2,1)S(1)} all-to-all(bf16[8,64,640]{2,1,0:T(8,128)(2,1)S(1)} %broadcast_in_dim.8), channel_id=1, replica_groups={{0,64,128,192,256,320,384,448},{8,72,136,200,264,328,392,456},{16,80,14..., dimensions={0} | all-to-all | bytes 1310720 | tf_op jit(solution)/shard_map/all_to_all | solution.py:211
  48.5 1.9 %collective-permute-start.3 = (bf16[512,640]{1,0:T(8,128)(2,1)S(1)}, bf16[512,640]{1,0:T(8,128)(2,1)S(1)}, u32[]{:S(2)}, u32[]{:S(2)}) collective-permute-start(bf16[512,640]{1,0:T(8,128)(2,1)S(1)} %bitcast.10), channel_id=1, source_target_pairs={{0,8},{8,0},{16,24},{24,16},{32,40},{40,32},{48,56},{56,48},{64,72... | collective-permute-start | bytes 1966088 | tf_op jit(solution)/shard_map/ppermute | solution.py:215
  50.5 3.4 %collective-permute-start = (bf16[64,1536]{1,0:T(8,128)(2,1)S(1)}, bf16[64,1536]{1,0:T(8,128)(2,1)S(1)}, u32[]{:S(2)}, u32[]{:S(2)}) collective-permute-start(bf16[64,1536]{1,0:T(8,128)(2,1)S(1)} %slice.8.q0), channel_id=1, source_target_pairs={{0,16},{8,24},{16,32},{24,40},{32,48},{40,56},{48,0},{56,8},{64,80... | collective-permute-start | bytes 589832 | tf_op jit(solution)/shard_map/ppermute | solution.py:216
  53.9 4.6 %collective-permute-start.1 = (bf16[64,1536]{1,0:T(8,128)(2,1)S(1)}, bf16[64,1536]{1,0:T(8,128)(2,1)S(1)}, u32[]{:S(2)}, u32[]{:S(2)}) collective-permute-start(bf16[64,1536]{1,0:T(8,128)(2,1)S(1)} %slice.8.q0), channel_id=1, source_target_pairs={{0,32},{8,40},{16,48},{24,56},{32,0},{40,8},{48,16},{56,24},{64,96... | collective-permute-start | bytes 589832 | tf_op jit(solution)/shard_map/ppermute | solution.py:216
  58.5 3.3 %collective-permute-start.2 = (bf16[64,1536]{1,0:T(8,128)(2,1)S(1)}, bf16[64,1536]{1,0:T(8,128)(2,1)S(1)}, u32[]{:S(2)}, u32[]{:S(2)}) collective-permute-start(bf16[64,1536]{1,0:T(8,128)(2,1)S(1)} %slice.8.q0), channel_id=1, source_target_pairs={{0,48},{8,56},{16,0},{24,8},{32,16},{40,24},{48,32},{56,40},{64,11... | collective-permute-start | bytes 589832 | tf_op jit(solution)/shard_map/ppermute | solution.py:216
  61.9 0.0 collective-permute-done.q1
  61.9 4.2 %collective-permute-done.1.q2 = bf16[64,1536]{1,0:T(8,128)(2,1)S(1)} collective-permute-done((bf16[64,1536]{1,0:T(8,128)(2,1)S(1)}, bf16[64,1536]{1,0:T(8,128)(2,1)S(1)}, u32[]{:S(2)}, u32[]{:S(2)}) %collective-permute-start.1) | collective-permute-done | bytes 196640 | tf_op jit(solution)/shard_map/ppermute | solution.py:216
  66.1 1.5 %collective-permute-done.2.q3 = bf16[64,1536]{1,0:T(8,128)(2,1)S(1)} collective-permute-done((bf16[64,1536]{1,0:T(8,128)(2,1)S(1)}, bf16[64,1536]{1,0:T(8,128)(2,1)S(1)}, u32[]{:S(2)}, u32[]{:S(2)}) %collective-permute-start.2) | collective-permute-done | bytes 196640 | tf_op jit(solution)/shard_map/ppermute | solution.py:216
  67.6 0.0 copy-done.3
  67.6 0.0 copy-done.1
  67.6 0.0 copy-start.2
  67.6 1.5 %shard_map.64.q_ref = bf16[8,256,768]{2,1,0:T(8,128)(2,1)S(1)} custom-call(s32[1]{0:T(128)} %bitcast.place_ref, s32[128]{0:T(128)S(1)} %copy-done.3, bf16[64,1536]{1,0:T(8,128)(2,1)S(1)} %slice.8.q0, bf16[64,1536]{1,0:T(8,128)(2,1)S(1)} %collective-permute-done.q1, bf16[64,1536]{1,0:T(8,128)(2,1)S(1)} %collective-permute-done.1.q2, ...), custom_call_target="tpu_custom_call" | custom-call | flops 4000000000 | bytes 6000000 | tf_op jit(solution)/shard_map/pallas_call | solution.py:85
  69.1 0.0 collective-permute-done.3.kv_sib
  69.1 0.0 copy-done.2
  69.1 7.9 %shard_map.65 = (bf16[64,1152]{1,0:T(8,128)(2,1)S(1)}, bf16[64,1152]{1,0:T(8,128)(2,1)S(1)}, bf16[64,1152]{1,0:T(8,128)(2,1)S(1)}, bf16[64,1152]{1,0:T(8,128)(2,1)S(1)}) custom-call(s32[1]{0:T(128)} %bitcast.place_ref, bf16[8,256,768]{2,1,0:T(8,128)(2,1)S(1)} %shard_map.64.q_ref, bf16[512,640]{1,0:T(8,128)(2,1)S(1)} %bitcast.11, ...), custom_call_target="tpu_custom_call" | custom-call | flops 6000000000 | bytes 5000000 | tf_op jit(solution)/shard_map/pallas_call | solution.py:158
  77.0 0.0 copy-start
  77.0 0.7 copy-done
  77.7 4.6 %collective-permute-start.4 = (bf16[64,1152]{1,0:T(8,128)(2,1)S(1)}, bf16[64,1152]{1,0:T(8,128)(2,1)S(1)}, u32[]{:S(2)}, u32[]{:S(2)}) collective-permute-start(bf16[64,1152]{1,0:T(8,128)(2,1)S(1)} %get-tuple-element.10), channel_id=1, source_target_pairs={{0,48},{8,56},{16,0},{24,8},{32,16},{40,24},{48,32},{56,40},{64,11... | collective-permute-start | bytes 442376 | tf_op jit(solution)/shard_map/ppermute | solution.py:219
  82.2 3.7 %collective-permute-start.5 = (bf16[64,1152]{1,0:T(8,128)(2,1)S(1)}, bf16[64,1152]{1,0:T(8,128)(2,1)S(1)}, u32[]{:S(2)}, u32[]{:S(2)}) collective-permute-start(bf16[64,1152]{1,0:T(8,128)(2,1)S(1)} %get-tuple-element.11), channel_id=1, source_target_pairs={{0,32},{8,40},{16,48},{24,56},{32,0},{40,8},{48,16},{56,24},{64,96... | collective-permute-start | bytes 442376 | tf_op jit(solution)/shard_map/ppermute | solution.py:219
  86.0 1.9 %collective-permute-start.6 = (bf16[64,1152]{1,0:T(8,128)(2,1)S(1)}, bf16[64,1152]{1,0:T(8,128)(2,1)S(1)}, u32[]{:S(2)}, u32[]{:S(2)}) collective-permute-start(bf16[64,1152]{1,0:T(8,128)(2,1)S(1)} %get-tuple-element.12), channel_id=1, source_target_pairs={{0,16},{8,24},{16,32},{24,40},{32,48},{40,56},{48,0},{56,8},{64,80... | collective-permute-start | bytes 442376 | tf_op jit(solution)/shard_map/ppermute | solution.py:219
  87.9 0.0 collective-permute-done.4.p1
  87.9 0.0 copy-start.4
  87.9 3.4 %collective-permute-done.5.p2 = bf16[64,1152]{1,0:T(8,128)(2,1)S(1)} collective-permute-done((bf16[64,1152]{1,0:T(8,128)(2,1)S(1)}, bf16[64,1152]{1,0:T(8,128)(2,1)S(1)}, u32[]{:S(2)}, u32[]{:S(2)}) %collective-permute-start.5) | collective-permute-done | bytes 147488 | tf_op jit(solution)/shard_map/ppermute | solution.py:219
  91.3 0.0 copy-start.5
  91.3 3.1 %collective-permute-done.6.p3 = bf16[64,1152]{1,0:T(8,128)(2,1)S(1)} collective-permute-done((bf16[64,1152]{1,0:T(8,128)(2,1)S(1)}, bf16[64,1152]{1,0:T(8,128)(2,1)S(1)}, u32[]{:S(2)}, u32[]{:S(2)}) %collective-permute-start.6) | collective-permute-done | bytes 147488 | tf_op jit(solution)/shard_map/ppermute | solution.py:219
  94.4 0.0 copy-start.6
  94.4 0.0 copy-done.4
  94.4 0.0 copy-done.5
  94.4 0.6 copy-done.6
  95.0 2.3 %shard_map.66 = bf16[64,1024]{1,0:T(8,128)(2,1)} custom-call(bf16[64,1152]{1,0:T(8,128)(2,1)} %copy-done, bf16[64,1152]{1,0:T(8,128)(2,1)} %copy-done.4, bf16[64,1152]{1,0:T(8,128)(2,1)} %copy-done.5, bf16[64,1152]{1,0:T(8,128)(2,1)} %copy-done.6), custom_call_target="tpu_custom_call" | custom-call | flops 1000000 | bytes 800000 | tf_op jit(solution)/shard_map/pallas_call | solution.py:192
  97.3 12.4 %all_to_all.31 = bf16[8,8,1024]{2,1,0:T(8,128)(2,1)S(1)} all-to-all(bf16[8,8,1024]{2,1,0:T(8,128)(2,1)} %bitcast.15), channel_id=1, replica_groups=mesh['ctx'=64,'head'=8] {'head'}, dimensions={0} | all-to-all | bytes 262144 | tf_op jit(solution)/shard_map/all_to_all | solution.py:221
  109.7 0.7 copy.8
  (4 shorter events, 0.0 us)
Async XLA Ops:
  0.0 67.6 %copy-start.3 = (s32[128]{0:T(128)S(1)}, s32[128]{0:T(128)}, u32[]{:S(2)}) copy-start(s32[128]{0:T(128)} %order_ref.1) | copy-start | bytes 1540
  0.0 67.6 %copy-start.1 = (bf16[8,512,128]{2,1,0:T(8,128)(2,1)S(1)}, bf16[8,512,128]{2,1,0:T(8,128)(2,1)}, u32[]{:S(2)}) copy-start(bf16[8,512,128]{2,1,0:T(8,128)(2,1)} %w_uk.1) | copy-start | bytes 3145732
  48.5 20.5 %collective-permute-start.3 = (bf16[512,640]{1,0:T(8,128)(2,1)S(1)}, bf16[512,640]{1,0:T(8,128)(2,1)S(1)}, u32[]{:S(2)}, u32[]{:S(2)}) collective-permute-start(bf16[512,640]{1,0:T(8,128)(2,1)S(1)} %bitcast.10), channel_id=1, source_target_pairs={{0,8},{8,0},{16,24},{24,16},{32,40},{40,32},{48,56},{56,48},{64,72... | collective-permute-start | bytes 1966088 | tf_op jit(solution)/shard_map/ppermute | solution.py:215
  50.5 11.4 %collective-permute-start = (bf16[64,1536]{1,0:T(8,128)(2,1)S(1)}, bf16[64,1536]{1,0:T(8,128)(2,1)S(1)}, u32[]{:S(2)}, u32[]{:S(2)}) collective-permute-start(bf16[64,1536]{1,0:T(8,128)(2,1)S(1)} %slice.8.q0), channel_id=1, source_target_pairs={{0,16},{8,24},{16,32},{24,40},{32,48},{40,56},{48,0},{56,8},{64,80... | collective-permute-start | bytes 589832 | tf_op jit(solution)/shard_map/ppermute | solution.py:216
  53.9 12.2 %collective-permute-start.1 = (bf16[64,1536]{1,0:T(8,128)(2,1)S(1)}, bf16[64,1536]{1,0:T(8,128)(2,1)S(1)}, u32[]{:S(2)}, u32[]{:S(2)}) collective-permute-start(bf16[64,1536]{1,0:T(8,128)(2,1)S(1)} %slice.8.q0), channel_id=1, source_target_pairs={{0,32},{8,40},{16,48},{24,56},{32,0},{40,8},{48,16},{56,24},{64,96... | collective-permute-start | bytes 589832 | tf_op jit(solution)/shard_map/ppermute | solution.py:216
  58.5 9.1 %collective-permute-start.2 = (bf16[64,1536]{1,0:T(8,128)(2,1)S(1)}, bf16[64,1536]{1,0:T(8,128)(2,1)S(1)}, u32[]{:S(2)}, u32[]{:S(2)}) collective-permute-start(bf16[64,1536]{1,0:T(8,128)(2,1)S(1)} %slice.8.q0), channel_id=1, source_target_pairs={{0,48},{8,56},{16,0},{24,8},{32,16},{40,24},{48,32},{56,40},{64,11... | collective-permute-start | bytes 589832 | tf_op jit(solution)/shard_map/ppermute | solution.py:216
  67.6 1.5 %copy-start.2 = (bf16[8,512,128]{2,1,0:T(8,128)(2,1)S(1)}, bf16[8,512,128]{2,1,0:T(8,128)(2,1)}, u32[]{:S(2)}) copy-start(bf16[8,512,128]{2,1,0:T(8,128)(2,1)} %w_uv.1) | copy-start | bytes 3145732
  77.0 0.7 copy-start
  77.7 10.2 %collective-permute-start.4 = (bf16[64,1152]{1,0:T(8,128)(2,1)S(1)}, bf16[64,1152]{1,0:T(8,128)(2,1)S(1)}, u32[]{:S(2)}, u32[]{:S(2)}) collective-permute-start(bf16[64,1152]{1,0:T(8,128)(2,1)S(1)} %get-tuple-element.10), channel_id=1, source_target_pairs={{0,48},{8,56},{16,0},{24,8},{32,16},{40,24},{48,32},{56,40},{64,11... | collective-permute-start | bytes 442376 | tf_op jit(solution)/shard_map/ppermute | solution.py:219
  82.2 9.1 %collective-permute-start.5 = (bf16[64,1152]{1,0:T(8,128)(2,1)S(1)}, bf16[64,1152]{1,0:T(8,128)(2,1)S(1)}, u32[]{:S(2)}, u32[]{:S(2)}) collective-permute-start(bf16[64,1152]{1,0:T(8,128)(2,1)S(1)} %get-tuple-element.11), channel_id=1, source_target_pairs={{0,32},{8,40},{16,48},{24,56},{32,0},{40,8},{48,16},{56,24},{64,96... | collective-permute-start | bytes 442376 | tf_op jit(solution)/shard_map/ppermute | solution.py:219
  86.0 8.4 %collective-permute-start.6 = (bf16[64,1152]{1,0:T(8,128)(2,1)S(1)}, bf16[64,1152]{1,0:T(8,128)(2,1)S(1)}, u32[]{:S(2)}, u32[]{:S(2)}) collective-permute-start(bf16[64,1152]{1,0:T(8,128)(2,1)S(1)} %get-tuple-element.12), channel_id=1, source_target_pairs={{0,16},{8,24},{16,32},{24,40},{32,48},{40,56},{48,0},{56,8},{64,80... | collective-permute-start | bytes 442376 | tf_op jit(solution)/shard_map/ppermute | solution.py:219
  87.9 6.5 %copy-start.4 = (bf16[64,1152]{1,0:T(8,128)(2,1)}, bf16[64,1152]{1,0:T(8,128)(2,1)S(1)}, u32[]{:S(2)}) copy-start(bf16[64,1152]{1,0:T(8,128)(2,1)S(1)} %collective-permute-done.4.p1) | copy-start | bytes 442372
  91.3 3.1 %copy-start.5 = (bf16[64,1152]{1,0:T(8,128)(2,1)}, bf16[64,1152]{1,0:T(8,128)(2,1)S(1)}, u32[]{:S(2)}) copy-start(bf16[64,1152]{1,0:T(8,128)(2,1)S(1)} %collective-permute-done.5.p2) | copy-start | bytes 442372
  94.4 0.7 copy-start.6

commit v3 on v2

v3 whole, which is shorter than its diff:
```python
import functools

import jax
import jax.numpy as jnp
from jax import lax
from jax.experimental import pallas as pl
from jax.experimental.pallas import tpu as pltpu
from jax.sharding import PartitionSpec as P

HALF = 32
DL = 512
DR = 64
DN = 128
DV = 128
DQ = DN + DR
WIDE = 640
STAT = 128
EXTRA = 128
NX = 4
NY = 8
NZ = 8
HEADS = 8
SPAN = 64
LANES = 128
PACKED = DL // LANES * SPAN + HALF
FLOOR_SCORE = -1e30
LOG2E = 1.4426950408889634
SCALE2 = DQ ** (-0.5) * LOG2E


def ctx_of(y, x, core):
    return ((y % NY) * NX + (x % NX)) * 2 + core


def along_x(step):
    return [
        (ctx_of(y, x, c), ctx_of(y, x + step, c))
        for y in range(NY)
        for x in range(NX)
        for c in range(2)
    ]


CORE_SWAP = [(i, i ^ 1) for i in range(NX * NY * 2)]
XZ_GROUPS = [
    [ctx_of(y, x, c) * NZ + z for x in range(NX) for z in range(NZ)] for y in range(NY) for c in range(2)
]
Y_GROUPS = [[ctx_of(y, x, c) for y in range(NY)] for x in range(NX) for c in range(2)]


def pack_kernel(both_ref, q_ref, kv_ref):
    q_ref[...] = both_ref[:, : HEADS * DQ]
    rope = both_ref[:, HEADS * DQ + DL : HEADS * DQ + DL + DR]
    for to in range(NY):
        for j in range(DL // LANES):
            col = HEADS * DQ + j * LANES
            kv_ref[to, j * SPAN : (j + 1) * SPAN] = both_ref[:, col : col + LANES]
        kv_ref[to, PACKED - HALF :, :DR] = rope[:HALF]
        kv_ref[to, PACKED - HALF :, DR:] = rope[HALF:]


def pack(both):
    vmem = pl.BlockSpec(memory_space=pltpu.VMEM)
    return pl.pallas_call(
        pack_kernel,
        out_shape=[
            jax.ShapeDtypeStruct((SPAN, HEADS * DQ), jnp.bfloat16),
            jax.ShapeDtypeStruct((NY, PACKED, LANES), jnp.bfloat16),
        ],
        in_specs=[vmem],
        out_specs=[vmem] * 2,
        compiler_params=pltpu.CompilerParams(vmem_limit_bytes=8 * 1024 * 1024),
        cost_estimate=pl.CostEstimate(flops=4_000_000_000, bytes_accessed=1_000_000, transcendentals=0),
    )(both)


def prepare_kernel(info_ref, q0, q1, q2, q3, w_uk, out_ref, nope):
    me = info_ref[0]
    core = me % 2
    x = (me // 2) % NX
    y = me // (2 * NX)
    blocks = 2 * NY * SPAN // HALF
    lane = lax.broadcasted_iota(jnp.int32, (HALF, EXTRA), 1)
    token = lax.broadcasted_iota(jnp.int32, (HALF, EXTRA), 0)
    key_block = jnp.zeros((HALF, EXTRA), jnp.int32)
    for which in range(blocks):
        side_core = core if which < blocks // 2 else 1 - core
        slot = (((which // 2) % NY) * NX + x) * 2 + side_core
        key_block = jnp.where(lane == which, info_ref[1 + 2 * slot + which % 2], key_block)
    for step, q in enumerate((q0, q1, q2, q3)):
        slot = (y * NX + (x - step + NX) % NX) * 2 + core
        here = slice(step * SPAN, (step + 1) * SPAN)
        floors = []
        for half in range(2):
            ahead = (lane < blocks) & (key_block > info_ref[1 + 2 * slot + half])
            if step == 0:
                own = lane - blocks - half * HALF
                ahead = ahead | ((own >= 0) & (own < HALF) & (own > token))
            floors.append(jnp.where(ahead, FLOOR_SCORE, 0.0))
        floor = jnp.concatenate(floors, axis=0).astype(jnp.bfloat16)
        for h in range(HEADS):
            nope[h, here] = q[:, h * DQ : h * DQ + DN]
            out_ref[h, here, DL : DL + DR] = q[:, h * DQ + DN : (h + 1) * DQ]
            out_ref[h, here, DL + DR : WIDE] = jnp.zeros((SPAN, DR), jnp.bfloat16)
            out_ref[h, here, WIDE:] = floor
    for h in range(HEADS):
        out_ref[h, :, :DL] = lax.dot_general(
            nope[h], w_uk[h], (((1,), (1,)), ((), ())), preferred_element_type=jnp.float32
        ).astype(jnp.bfloat16)


def prepare(info, qs, w_uk):
    vmem = pl.BlockSpec(memory_space=pltpu.VMEM)
    smem = pl.BlockSpec(memory_space=pltpu.SMEM)
    rows = NX * SPAN
    return pl.pallas_call(
        prepare_kernel,
        out_shape=jax.ShapeDtypeStruct((HEADS, rows, WIDE + EXTRA), jnp.bfloat16),
        in_specs=[smem] + [vmem] * 5,
        out_specs=vmem,
        scratch_shapes=[pltpu.VMEM((HEADS, rows, DN), jnp.bfloat16)],
        compiler_params=pltpu.CompilerParams(vmem_limit_bytes=16 * 1024 * 1024),
        cost_estimate=pl.CostEstimate(flops=4_000_000_000, bytes_accessed=6_000_000, transcendentals=0),
    )(info, *qs, w_uk)


def fill_keys(keys, kv, first, own_block):
    count = NY * SPAN
    blocks = 2 * count // HALF
    for b in range(NY):
        here = slice(b * SPAN, (b + 1) * SPAN)
        for j in range(DL // LANES):
            keys[here, j * LANES : (j + 1) * LANES] = kv[b, j * SPAN : (j + 1) * SPAN]
        keys[b * SPAN : b * SPAN + HALF, DL : DL + DR] = kv[b, PACKED - HALF :, :DR]
        keys[b * SPAN + HALF : (b + 1) * SPAN, DL : DL + DR] = kv[b, PACKED - HALF :, DR:]
    keys[:, DL + DR : WIDE] = jnp.zeros((count, WIDE - DL - DR), jnp.bfloat16)
    key = lax.broadcasted_iota(jnp.int32, (count, EXTRA), 0)
    col = lax.broadcasted_iota(jnp.int32, (count, EXTRA), 1)
    ones = col == key // HALF + first
    if own_block is not None:
        in_own = (key // HALF == own_block) | (key // HALF == own_block + 1)
        ones = ones | (in_own & (col == blocks + key - own_block * HALF))
    keys[:, WIDE:] = jnp.where(ones, 1.0, 0.0).astype(jnp.bfloat16)


def scores_of(q, keys):
    return lax.dot_general(q, keys[...], (((1,), (1,)), ((), ())), preferred_element_type=jnp.float32)


def own_kernel(place_ref, q_ref, kv, lat_ref, top_ref, total_ref, keys):
    y = place_ref[0] // (2 * NX)
    rows = NX * SPAN
    fill_keys(keys, kv, 0, 2 * y)

    def pair(p, carry):
        heads = [2 * p, 2 * p + 1]
        scores = [scores_of(q_ref[h], keys) for h in heads]
        for h, s in zip(heads, scores):
            top = jnp.max(s, axis=1, keepdims=True)
            weight = jnp.exp2((s - top) * SCALE2)
            total = jnp.sum(weight, axis=1, keepdims=True)
            lat_ref[h] = jnp.dot(weight.astype(jnp.bfloat16), keys[:, :DL], preferred_element_type=jnp.float32)
            top_ref[h] = jnp.broadcast_to(top, (rows, STAT))
            total_ref[h] = jnp.broadcast_to(total, (rows, STAT))
        return carry

    lax.fori_loop(0, HEADS // 2, pair, 0)


def attend_own(place, q_all, kv):
    vmem = pl.BlockSpec(memory_space=pltpu.VMEM)
    smem = pl.BlockSpec(memory_space=pltpu.SMEM)
    rows = NX * SPAN
    return pl.pallas_call(
        own_kernel,
        out_shape=[
            jax.ShapeDtypeStruct((HEADS, rows, DL), jnp.float32),
            jax.ShapeDtypeStruct((HEADS, rows, STAT), jnp.float32),
            jax.ShapeDtypeStruct((HEADS, rows, STAT), jnp.float32),
        ],
        in_specs=[smem] + [vmem] * 2,
        out_specs=[vmem] * 3,
        scratch_shapes=[pltpu.VMEM((NY * SPAN, WIDE + EXTRA), jnp.bfloat16)],
        compiler_params=pltpu.CompilerParams(vmem_limit_bytes=20 * 1024 * 1024),
        cost_estimate=pl.CostEstimate(flops=20_000_000_000, bytes_accessed=5_000_000, transcendentals=1_000_000),
    )(place, q_all, kv)


def other_kernel(place_ref, q_ref, kv, lat_ref, top_ref, total_ref, w_uv, out_ref, keys, stat):
    x = (place_ref[0] // 2) % NX
    rows = NX * SPAN
    fill_keys(keys, kv, NY * SPAN // HALF, None)
    stat[...] = jnp.zeros_like(stat)
    lanes = lax.broadcasted_iota(jnp.int32, (rows, STAT), 1)

    def pair(p, carry):
        heads = [2 * p, 2 * p + 1]
        scores = [scores_of(q_ref[h], keys) for h in heads]
        levels = []
        for h, s in zip(heads, scores):
            old_top = top_ref[h, :, :1]
            old_total = total_ref[h, :, :1]
            top = jnp.maximum(old_top, jnp.max(s, axis=1, keepdims=True))
            shrink = jnp.exp2((old_top - top) * SCALE2)
            weight = jnp.exp2((s - top) * SCALE2)
            total = old_total * shrink + jnp.sum(weight, axis=1, keepdims=True)
            lat = jnp.dot(weight.astype(jnp.bfloat16), keys[:, :DL], preferred_element_type=jnp.float32)
            share = 1.0 / total
            o_lat = (lat * share + lat_ref[h] * (shrink * share)).astype(jnp.bfloat16)
            proj = jnp.dot(o_lat, w_uv[h], preferred_element_type=jnp.float32).astype(jnp.bfloat16)
            for step in range(NX):
                to = (x + NX - step) % NX
                out_ref[to, :, pl.ds(pl.multiple_of(h * DV, DV), DV)] = proj[step * SPAN : (step + 1) * SPAN]
            levels.append(top * SCALE2 + jnp.log2(total))
        held = stat[...]
        for h, level in zip(heads, levels):
            held = jnp.where(lanes % HEADS == h, level, held)
        stat[...] = held
        return carry

    lax.fori_loop(0, HEADS // 2, pair, 0)
    level = stat[...]
    high = level.astype(jnp.bfloat16)
    rest = level - high.astype(jnp.float32)
    middle = rest.astype(jnp.bfloat16)
    low = (rest - middle.astype(jnp.float32)).astype(jnp.bfloat16)
    part = lanes // HEADS
    packed = jnp.where(
        part == 0,
        high.astype(jnp.float32),
        jnp.where(part == 1, middle.astype(jnp.float32), jnp.where(part == 2, low.astype(jnp.float32), 0.0)),
    ).astype(jnp.bfloat16)
    for step in range(NX):
        to = (x + NX - step) % NX
        out_ref[to, :, HEADS * DV :] = packed[step * SPAN : (step + 1) * SPAN]


def attend_other(place, q_all, kv, state, w_uv):
    vmem = pl.BlockSpec(memory_space=pltpu.VMEM)
    smem = pl.BlockSpec(memory_space=pltpu.SMEM)
    rows = NX * SPAN
    return pl.pallas_call(
        other_kernel,
        out_shape=jax.ShapeDtypeStruct((NX, SPAN, HEADS * DV + STAT), jnp.bfloat16),
        in_specs=[smem] + [vmem] * 6,
        out_specs=vmem,
        scratch_shapes=[
            pltpu.VMEM((NY * SPAN, WIDE + EXTRA), jnp.bfloat16),
            pltpu.VMEM((rows, STAT), jnp.float32),
        ],
        compiler_params=pltpu.CompilerParams(vmem_limit_bytes=20 * 1024 * 1024),
        cost_estimate=pl.CostEstimate(flops=4_000_000_000, bytes_accessed=5_000_000, transcendentals=1_000_000),
    )(place, q_all, kv, *state, w_uv)


def merge_kernel(p_ref, out_ref):
    for z in range(NZ):
        levels = []
        for x in range(NX):
            pieces = p_ref[x, z, :, HEADS * DV :].astype(jnp.float32)
            levels.append(pieces[:, :HEADS] + pieces[:, HEADS : 2 * HEADS] + pieces[:, 2 * HEADS : 3 * HEADS])
        top = functools.reduce(jnp.maximum, levels)
        shares = [jnp.exp2(level - top) for level in levels]
        whole = functools.reduce(jnp.add, shares)
        shares = [share / whole for share in shares]
        for h in range(HEADS):
            acc = jnp.zeros((SPAN // NZ, DV), jnp.float32)
            for x in range(NX):
                acc = acc + shares[x][:, h : h + 1] * p_ref[x, z, :, h * DV : (h + 1) * DV].astype(jnp.float32)
            out_ref[:, (z * HEADS + h) * DV : (z * HEADS + h + 1) * DV] = acc.astype(jnp.bfloat16)


def merge(parts):
    vmem = pl.BlockSpec(memory_space=pltpu.VMEM)
    return pl.pallas_call(
        merge_kernel,
        out_shape=jax.ShapeDtypeStruct((SPAN // NZ, NZ * HEADS * DV), jnp.bfloat16),
        in_specs=[vmem],
        out_specs=vmem,
        cost_estimate=pl.CostEstimate(flops=1_000_000, bytes_accessed=800_000, transcendentals=2000),
    )(parts)


def copies(value, count):
    return jnp.broadcast_to(value[None], (count,) + value.shape)


def on_device(queries, latent, rope_key, w_uk, w_uv, block_order):
    place = lax.axis_index("ctx").astype(jnp.int32).reshape(1)
    info = jnp.concatenate([place, block_order])
    kv = jnp.concatenate([latent, rope_key, jnp.zeros_like(rope_key)], axis=1)
    both = jnp.concatenate([queries.reshape(8, NZ, HEADS * DQ).swapaxes(0, 1), copies(kv, NZ)], axis=2)
    both = lax.all_to_all(both, "head", split_axis=0, concat_axis=0, tiled=True).reshape(SPAN, HEADS * DQ + WIDE)
    q_own, kv = pack(both)
    kv_own = lax.all_to_all(kv, "ctx", split_axis=0, concat_axis=0, tiled=True, axis_index_groups=Y_GROUPS)
    kv_sib = lax.ppermute(kv_own, "ctx", CORE_SWAP)
    qs = [q_own] + [lax.ppermute(q_own, "ctx", along_x(step)) for step in range(1, NX)]
    q_all = prepare(info, qs, w_uk)
    state = attend_own(place, q_all, kv_own)
    partial = attend_other(place, q_all, kv_sib, state, w_uv)
    rows = SPAN // NZ
    partial = partial.reshape(NX * NZ, rows, HEADS * DV + STAT)
    parts = lax.all_to_all(
        partial, ("ctx", "head"), split_axis=0, concat_axis=0, tiled=True, axis_index_groups=XZ_GROUPS
    )
    return merge(parts.reshape(NX, NZ, rows, HEADS * DV + STAT))


def solution(mesh):
    in_specs = (
        P(("ctx", "head"), None),
        P(("ctx", "head"), None),
        P(("ctx", "head"), None),
        P("head", None, None),
        P("head", None, None),
        P(),
    )
    out_specs = P(("ctx", "head"), None)
    return jax.shard_map(
        on_device, mesh=mesh, in_specs=in_specs, out_specs=out_specs, check_vma=False
    )
```

time: 111 us -> 92.5 us (0.83)
  the two profiles are of different devices: /device:TPU:8 before, /device:TPU:72 now
where the time goes in v3:
time: 92.5 us; the launch traced here: 92 us
  blocking collectives  45.6 us (49%)
  starting transfers between devices  19.7 us (21%)
  Pallas kernels  15.3 us (17%)
  waiting for transfers between devices  5.89 us (6%)
  local copies, waits for them, and re-layouts  3.6 us (4%)
  other arithmetic  1.75 us (2%)
    all_to_all x1, blocking collectives, on_device(): lax.all_to_all(partial, ('ctx', 'head'), split_axis=0, concat_axis=0, til...  25.1 us
    all_to_all x1, blocking collectives, on_device(): lax.all_to_all(both, 'head', split_axis=0, concat_axis=0, tiled=True)  20.5 us
    ppermute x3, starting transfers between devices, on_device(): lax.ppermute(q_own, 'ctx', along_x(step))  10.2 us
    all_to_all x1, starting transfers between devices, on_device(): lax.all_to_all(kv, 'ctx', split_axis=0, concat_axis=0, tiled=True, axis_i...  7.55 us
    pallas_call x1, Pallas kernels, attend_other(): pl.pallas_call(other_kernel, out_shape=jax.ShapeDtypeStruct((NX, SPAN, HE...  6.33 us
    ppermute x3, waiting for transfers between devices, on_device(): lax.ppermute(q_own, 'ctx', along_x(step))  5.88 us
    pallas_call x1, Pallas kernels, attend_own(): pl.pallas_call(own_kernel, out_shape=[jax.ShapeDtypeStruct((HEADS, rows,...  3.82 us
    unnamed x10, local copies, waits for them, and re-layouts  3.51 us
  transfers between devices with their start and end apart: 5, of which 2 were waited for; matrix products, arithmetic and copies ran while one was open for 0% of the time, Pallas kernels for 6%

profile of v3, /device:TPU:72, one launch (start us, length us, event | category | flops | bytes accessed | tf_op | source)
XLA Modules:
  0.0 92.0 jit_solution(4733346070078945856)
XLA Ops:
  0.0 0.1 pad.4.clone
  0.1 0.7 maximum_maximum_fusion
  0.8 0.9 %pad_maximum_fusion = bf16[8,8,2176]{2,1,0:T(8,128)(2,1)S(1)} fusion(bf16[8,8,640]{2,1,0:T(8,128)(2,1)S(1)} %broadcast_in_dim.10, bf16[8,8,1536]{2,1,0:T(8,128)(2,1)} %bitcast.10), kind=kLoop, calls=%fused_computation | loop fusion | flops 557056 | bytes 557056 | tf_op jit(solution)/shard_map/concatenate | solution.py:292
  1.8 20.5 %all_to_all.15 = bf16[8,8,2176]{2,1,0:T(8,128)(2,1)S(1)} all-to-all(bf16[8,8,2176]{2,1,0:T(8,128)(2,1)S(1)} %pad_maximum_fusion), channel_id=1, replica_groups=mesh['ctx'=64,'head'=8] {'head'}, dimensions={0} | all-to-all | bytes 557056 | tf_op jit(solution)/shard_map/all_to_all | solution.py:293
  22.3 0.0 copy-start.4
  22.3 0.0 copy-start
  22.3 0.9 shard_map.64
  23.2 7.5 %all-to-all-start.1 = ((bf16[8,288,128]{2,1,0:T(8,128)(2,1)}), bf16[8,288,128]{2,1,0:T(8,128)(2,1)S(1)}, u32[]{:S(2)}, u32[]{:S(2)}) async-start(bf16[8,288,128]{2,1,0:T(8,128)(2,1)} %get-tuple-element.11), calls=%async_computation.1 | async-start | bytes 1179648 | tf_op jit(solution)/shard_map/all_to_all | solution.py:295
  30.8 4.7 %collective-permute-start.2 = (bf16[64,1536]{1,0:T(8,128)(2,1)S(1)}, bf16[64,1536]{1,0:T(8,128)(2,1)S(1)}, u32[]{:S(2)}, u32[]{:S(2)}) collective-permute-start(bf16[64,1536]{1,0:T(8,128)(2,1)S(1)} %get-tuple-element.10.q0), channel_id=1, source_target_pairs={{0,48},{8,56},{16,0},{24,8},{32,16},{40,24},{48,32},{56,40},{64,11... | collective-permute-start | bytes 589832 | tf_op jit(solution)/shard_map/ppermute | solution.py:297
  35.4 2.7 %collective-permute-start.1 = (bf16[64,1536]{1,0:T(8,128)(2,1)S(1)}, bf16[64,1536]{1,0:T(8,128)(2,1)S(1)}, u32[]{:S(2)}, u32[]{:S(2)}) collective-permute-start(bf16[64,1536]{1,0:T(8,128)(2,1)S(1)} %get-tuple-element.10.q0), channel_id=1, source_target_pairs={{0,32},{8,40},{16,48},{24,56},{32,0},{40,8},{48,16},{56,24},{64,96... | collective-permute-start | bytes 589832 | tf_op jit(solution)/shard_map/ppermute | solution.py:297
  38.1 2.8 %collective-permute-start = (bf16[64,1536]{1,0:T(8,128)(2,1)S(1)}, bf16[64,1536]{1,0:T(8,128)(2,1)S(1)}, u32[]{:S(2)}, u32[]{:S(2)}) collective-permute-start(bf16[64,1536]{1,0:T(8,128)(2,1)S(1)} %get-tuple-element.10.q0), channel_id=1, source_target_pairs={{0,16},{8,24},{16,32},{24,40},{32,48},{40,56},{48,0},{56,8},{64,80... | collective-permute-start | bytes 589832 | tf_op jit(solution)/shard_map/ppermute | solution.py:297
  41.0 0.0 copy-done.4
  41.0 0.1 pad_add_fusion.info_ref
  41.0 0.0 collective-permute-done.2.q3
  41.0 3.5 %collective-permute-done.1.q2 = bf16[64,1536]{1,0:T(8,128)(2,1)S(1)} collective-permute-done((bf16[64,1536]{1,0:T(8,128)(2,1)S(1)}, bf16[64,1536]{1,0:T(8,128)(2,1)S(1)}, u32[]{:S(2)}, u32[]{:S(2)}) %collective-permute-start.1) | collective-permute-done | bytes 196640 | tf_op jit(solution)/shard_map/ppermute | solution.py:297
  44.5 2.4 %collective-permute-done.q1 = bf16[64,1536]{1,0:T(8,128)(2,1)S(1)} collective-permute-done((bf16[64,1536]{1,0:T(8,128)(2,1)S(1)}, bf16[64,1536]{1,0:T(8,128)(2,1)S(1)}, u32[]{:S(2)}, u32[]{:S(2)}) %collective-permute-start) | collective-permute-done | bytes 196640 | tf_op jit(solution)/shard_map/ppermute | solution.py:297
  46.9 0.0 copy-done
  46.9 1.5 %shard_map.65.q_ref = bf16[8,256,768]{2,1,0:T(8,128)(2,1)S(1)} custom-call(s32[129]{0:T(256)S(1)} %pad_add_fusion.info_ref, bf16[64,1536]{1,0:T(8,128)(2,1)S(1)} %get-tuple-element.10.q0, bf16[64,1536]{1,0:T(8,128)(2,1)S(1)} %collective-permute-done.q1, bf16[64,1536]{1,0:T(8,128)(2,1)S(1)} %collective-permute-done.1.q2, ...), custom_call_target="tpu_custom_call" | custom-call | flops 4000000000 | bytes 6000000 | tf_op jit(solution)/shard_map/pallas_call | solution.py:116
  48.4 0.0 copy-start.2
  48.4 1.6 %copy-done.2 = bf16[8,256,768]{2,1,0:T(8,128)(2,1)} copy-done((bf16[8,256,768]{2,1,0:T(8,128)(2,1)}, bf16[8,256,768]{2,1,0:T(8,128)(2,1)S(1)}, u32[]{:S(2)}) %copy-start.2) | copy-done | bytes 3145752
  50.0 0.0 copy-start.1
  50.0 0.0 all-to-all-done.1.kv
  50.0 2.0 %collective-permute-start.3 = (bf16[8,288,128]{2,1,0:T(8,128)(2,1)S(1)}, bf16[8,288,128]{2,1,0:T(8,128)(2,1)S(1)}, u32[]{:S(2)}, u32[]{:S(2)}) collective-permute-start(bf16[8,288,128]{2,1,0:T(8,128)(2,1)S(1)} %all-to-all-done.1.kv), channel_id=1, source_target_pairs={{0,8},{8,0},{16,24},{24,16},{32,40},{40,32},{48,56},{56,48},{64,72... | collective-permute-start | bytes 1769480 | tf_op jit(solution)/shard_map/ppermute | solution.py:296
  52.1 0.0 copy-start.3
  52.1 1.9 %copy-done.3 = bf16[8,256,768]{2,1,0:T(8,128)(2,1)S(1)} copy-done((bf16[8,256,768]{2,1,0:T(8,128)(2,1)S(1)}, bf16[8,256,768]{2,1,0:T(8,128)(2,1)}, u32[]{:S(2)}) %copy-start.3) | copy-done | bytes 3145752
  54.0 3.8 %shard_map.66 = (f32[8,256,512]{2,1,0:T(8,128)S(1)}, f32[8,256,128]{2,1,0:T(8,128)S(1)}, f32[8,256,128]{2,1,0:T(8,128)S(1)}) custom-call(s32[1]{0:T(128)} %bitcast.place_ref, bf16[8,256,768]{2,1,0:T(8,128)(2,1)S(1)} %copy-done.3, bf16[8,288,128]{2,1,0:T(8,128)(2,1)S(1)} %all-to-all-done.1.kv), custom_call_target="tpu_custom_call" | custom-call | flops 20000000000 | bytes 5000000 | tf_op jit(solution)/shard_map/pallas_call | solution.py:174
  57.8 0.0 collective-permute-done.3.kv
  57.8 0.0 copy-done.1
  57.8 6.3 %shard_map.67 = bf16[4,64,1152]{2,1,0:T(8,128)(2,1)S(1)} custom-call(s32[1]{0:T(128)} %bitcast.place_ref, bf16[8,256,768]{2,1,0:T(8,128)(2,1)S(1)} %copy-done.3, bf16[8,288,128]{2,1,0:T(8,128)(2,1)S(1)} %collective-permute-done.3.kv, f32[8,256,512]{2,1,0:T(8,128)S(1)} %get-tuple-element.12.lat_ref, f32[8,256,128]{2,1,0:T(8,128)S(1)} %get-tuple-element.13.top_ref, ...), custom_call_target="tpu_custom_call" | custom-call | flops 4000000000 | bytes 5000000 | tf_op jit(solution)/shard_map/pallas_call | solution.py:242
  64.2 25.1 %all_to_all.16 = bf16[32,8,1152]{2,1,0:T(8,128)(2,1)} all-to-all(bf16[32,8,1152]{2,1,0:T(8,128)(2,1)S(1)} %bitcast.7), channel_id=1, replica_groups={{0,1,2,3,4,5,6,7,16,17,18,19,20,21,22,23,32,33,34,35,36,37,38,39,48,49,..., dimensions={0} | all-to-all | bytes 1179648 | tf_op jit(solution)/shard_map/all_to_all | solution.py:303
  89.2 2.8 %shard_map.68 = bf16[8,8192]{1,0:T(8,128)(2,1)} custom-call(bf16[4,8,8,1152]{3,2,1,0:T(8,128)(2,1)} %bitcast.9), custom_call_target="tpu_custom_call" | custom-call | flops 1000000 | bytes 800000 | tf_op jit(solution)/shard_map/pallas_call | solution.py:275
  (2 shorter events, 0.0 us)
Async XLA Ops:
  22.3 18.7 %copy-start.4 = (s32[128]{0:T(128)S(1)}, s32[128]{0:T(128)}, u32[]{:S(2)}) copy-start(s32[128]{0:T(128)} %param.11) | copy-start | bytes 1540
  22.3 24.6 %copy-start = (bf16[8,512,128]{2,1,0:T(8,128)(2,1)S(1)}, bf16[8,512,128]{2,1,0:T(8,128)(2,1)}, u32[]{:S(2)}) copy-start(bf16[8,512,128]{2,1,0:T(8,128)(2,1)} %w_uk.1) | copy-start | bytes 3145732
  23.2 26.8 %all-to-all-start.1 = ((bf16[8,288,128]{2,1,0:T(8,128)(2,1)}), bf16[8,288,128]{2,1,0:T(8,128)(2,1)S(1)}, u32[]{:S(2)}, u32[]{:S(2)}) async-start(bf16[8,288,128]{2,1,0:T(8,128)(2,1)} %get-tuple-element.11), calls=%async_computation.1 | async-start | bytes 1179648 | tf_op jit(solution)/shard_map/all_to_all | solution.py:295
  30.8 10.3 %collective-permute-start.2 = (bf16[64,1536]{1,0:T(8,128)(2,1)S(1)}, bf16[64,1536]{1,0:T(8,128)(2,1)S(1)}, u32[]{:S(2)}, u32[]{:S(2)}) collective-permute-start(bf16[64,1536]{1,0:T(8,128)(2,1)S(1)} %get-tuple-element.10.q0), channel_id=1, source_target_pairs={{0,48},{8,56},{16,0},{24,8},{32,16},{40,24},{48,32},{56,40},{64,11... | collective-permute-start | bytes 589832 | tf_op jit(solution)/shard_map/ppermute | solution.py:297
  35.4 9.1 %collective-permute-start.1 = (bf16[64,1536]{1,0:T(8,128)(2,1)S(1)}, bf16[64,1536]{1,0:T(8,128)(2,1)S(1)}, u32[]{:S(2)}, u32[]{:S(2)}) collective-permute-start(bf16[64,1536]{1,0:T(8,128)(2,1)S(1)} %get-tuple-element.10.q0), channel_id=1, source_target_pairs={{0,32},{8,40},{16,48},{24,56},{32,0},{40,8},{48,16},{56,24},{64,96... | collective-permute-start | bytes 589832 | tf_op jit(solution)/shard_map/ppermute | solution.py:297
  38.1 8.8 %collective-permute-start = (bf16[64,1536]{1,0:T(8,128)(2,1)S(1)}, bf16[64,1536]{1,0:T(8,128)(2,1)S(1)}, u32[]{:S(2)}, u32[]{:S(2)}) collective-permute-start(bf16[64,1536]{1,0:T(8,128)(2,1)S(1)} %get-tuple-element.10.q0), channel_id=1, source_target_pairs={{0,16},{8,24},{16,32},{24,40},{32,48},{40,56},{48,0},{56,8},{64,80... | collective-permute-start | bytes 589832 | tf_op jit(solution)/shard_map/ppermute | solution.py:297
  48.4 1.6 %copy-start.2 = (bf16[8,256,768]{2,1,0:T(8,128)(2,1)}, bf16[8,256,768]{2,1,0:T(8,128)(2,1)S(1)}, u32[]{:S(2)}) copy-start(bf16[8,256,768]{2,1,0:T(8,128)(2,1)S(1)} %shard_map.65.q_ref) | copy-start | bytes 9437188
  50.0 7.8 %copy-start.1 = (bf16[8,512,128]{2,1,0:T(8,128)(2,1)S(1)}, bf16[8,512,128]{2,1,0:T(8,128)(2,1)}, u32[]{:S(2)}) copy-start(bf16[8,512,128]{2,1,0:T(8,128)(2,1)} %w_uv.1) | copy-start | bytes 3145732
  50.0 7.8 %collective-permute-start.3 = (bf16[8,288,128]{2,1,0:T(8,128)(2,1)S(1)}, bf16[8,288,128]{2,1,0:T(8,128)(2,1)S(1)}, u32[]{:S(2)}, u32[]{:S(2)}) collective-permute-start(bf16[8,288,128]{2,1,0:T(8,128)(2,1)S(1)} %all-to-all-done.1.kv), channel_id=1, source_target_pairs={{0,8},{8,0},{16,24},{24,16},{32,40},{40,32},{48,56},{56,48},{64,72... | collective-permute-start | bytes 1769480 | tf_op jit(solution)/shard_map/ppermute | solution.py:296
  52.1 1.9 %copy-start.3 = (bf16[8,256,768]{2,1,0:T(8,128)(2,1)S(1)}, bf16[8,256,768]{2,1,0:T(8,128)(2,1)}, u32[]{:S(2)}) copy-start(bf16[8,256,768]{2,1,0:T(8,128)(2,1)} %copy-done.2) | copy-start | bytes 9437188

commit v4 on v3

v4 whole, which is shorter than its diff:
```python
import functools

import jax
import jax.numpy as jnp
from jax import lax
from jax.experimental import pallas as pl
from jax.experimental.pallas import tpu as pltpu
from jax.sharding import PartitionSpec as P

HALF = 32
DL = 512
DR = 64
DN = 128
DV = 128
DQ = DN + DR
WIDE = 640
STAT = 128
EXTRA = 128
NX = 4
NY = 8
NZ = 8
HEADS = 8
SPAN = 64
LANES = 128
PACKED = DL // LANES * SPAN + HALF
FLOOR_SCORE = -1e30
LOG2E = 1.4426950408889634
SCALE2 = DQ ** (-0.5) * LOG2E


def ctx_of(y, x, core):
    return ((y % NY) * NX + (x % NX)) * 2 + core


def along_x(step):
    return [
        (ctx_of(y, x, c), ctx_of(y, x + step, c))
        for y in range(NY)
        for x in range(NX)
        for c in range(2)
    ]


CORE_SWAP = [(i, i ^ 1) for i in range(NX * NY * 2)]
XZ_GROUPS = [
    [ctx_of(y, x, c) * NZ + z for x in range(NX) for z in range(NZ)] for y in range(NY) for c in range(2)
]
Y_GROUPS = [[ctx_of(y, x, c) for y in range(NY)] for x in range(NX) for c in range(2)]


def spread_kernel(q_ref, lat_ref, rope_ref, out_ref):
    end = HEADS * DQ
    for z in range(NZ):
        out_ref[z, :, :end] = q_ref[:, z * end : (z + 1) * end]
        out_ref[z, :, end : end + DL] = lat_ref[...]
        out_ref[z, :, end + DL : end + DL + DR] = rope_ref[...]
        out_ref[z, :, end + DL + DR :] = jnp.zeros_like(rope_ref)


def spread(queries, latent, rope_key):
    vmem = pl.BlockSpec(memory_space=pltpu.VMEM)
    return pl.pallas_call(
        spread_kernel,
        out_shape=jax.ShapeDtypeStruct((NZ, SPAN // NZ, HEADS * DQ + WIDE), jnp.bfloat16),
        in_specs=[vmem] * 3,
        out_specs=vmem,
        compiler_params=pltpu.CompilerParams(vmem_limit_bytes=60 * 1024 * 1024),
        cost_estimate=pl.CostEstimate(flops=1_000_000, bytes_accessed=500_000, transcendentals=0),
    )(queries, latent, rope_key)


def pack_kernel(both_ref, q_ref, kv_ref):
    q_ref[...] = both_ref[:, : HEADS * DQ]
    rope = both_ref[:, HEADS * DQ + DL : HEADS * DQ + DL + DR]
    for to in range(NY):
        for j in range(DL // LANES):
            col = HEADS * DQ + j * LANES
            kv_ref[to, j * SPAN : (j + 1) * SPAN] = both_ref[:, col : col + LANES]
        kv_ref[to, PACKED - HALF :, :DR] = rope[:HALF]
        kv_ref[to, PACKED - HALF :, DR:] = rope[HALF:]


def pack(both):
    vmem = pl.BlockSpec(memory_space=pltpu.VMEM)
    return pl.pallas_call(
        pack_kernel,
        out_shape=[
            jax.ShapeDtypeStruct((SPAN, HEADS * DQ), jnp.bfloat16),
            jax.ShapeDtypeStruct((NY, PACKED, LANES), jnp.bfloat16),
        ],
        in_specs=[vmem],
        out_specs=[vmem] * 2,
        compiler_params=pltpu.CompilerParams(vmem_limit_bytes=8 * 1024 * 1024),
        cost_estimate=pl.CostEstimate(flops=4_000_000_000, bytes_accessed=1_000_000, transcendentals=0),
    )(both)


def fill_keys(keys, kv, first, own_block):
    count = NY * SPAN
    blocks = 2 * count // HALF
    for b in range(NY):
        here = slice(b * SPAN, (b + 1) * SPAN)
        for j in range(DL // LANES):
            keys[here, j * LANES : (j + 1) * LANES] = kv[b, j * SPAN : (j + 1) * SPAN]
        keys[b * SPAN : b * SPAN + HALF, DL : DL + DR] = kv[b, PACKED - HALF :, :DR]
        keys[b * SPAN + HALF : (b + 1) * SPAN, DL : DL + DR] = kv[b, PACKED - HALF :, DR:]
    keys[:, DL + DR : WIDE] = jnp.zeros((count, WIDE - DL - DR), jnp.bfloat16)
    key = lax.broadcasted_iota(jnp.int32, (count, EXTRA), 0)
    col = lax.broadcasted_iota(jnp.int32, (count, EXTRA), 1)
    ones = col == key // HALF + first
    if own_block is not None:
        in_own = (key // HALF == own_block) | (key // HALF == own_block + 1)
        ones = ones | (in_own & (col == blocks + key - own_block * HALF))
    keys[:, WIDE:] = jnp.where(ones, 1.0, 0.0).astype(jnp.bfloat16)


def pair_scores(q_ref, keys, p):
    q = q_ref[2 * p : 2 * p + 2].reshape(2 * NX * SPAN, WIDE + EXTRA)
    return lax.dot_general(q, keys[...], (((1,), (1,)), ((), ())), preferred_element_type=jnp.float32)


def wide(value, count):
    return jnp.concatenate([value] * count, axis=1)


def floors_of(info_ref):
    me = info_ref[0]
    core = me % 2
    x = (me // 2) % NX
    y = me // (2 * NX)
    blocks = 2 * NY * SPAN // HALF
    lane = lax.broadcasted_iota(jnp.int32, (HALF, EXTRA), 1)
    token = lax.broadcasted_iota(jnp.int32, (HALF, EXTRA), 0)
    key_block = jnp.zeros((HALF, EXTRA), jnp.int32)
    for which in range(blocks):
        side_core = core if which < blocks // 2 else 1 - core
        slot = (((which // 2) % NY) * NX + x) * 2 + side_core
        key_block = jnp.where(lane == which, info_ref[1 + 2 * slot + which % 2], key_block)
    floors = []
    for step in range(NX):
        slot = (y * NX + (x - step + NX) % NX) * 2 + core
        for half in range(2):
            ahead = (lane < blocks) & (key_block > info_ref[1 + 2 * slot + half])
            if step == 0:
                own = lane - blocks - half * HALF
                ahead = ahead | ((own >= 0) & (own < HALF) & (own > token))
            floors.append(jnp.where(ahead, FLOOR_SCORE, 0.0))
    return jnp.concatenate(floors, axis=0).astype(jnp.bfloat16)


def own_kernel(info_ref, q0, q1, q2, q3, w_uk, kv, q_ref, lat_ref, top_ref, total_ref, keys):
    y = info_ref[0] // (2 * NX)
    rows = NX * SPAN
    floor = floors_of(info_ref)
    none = jnp.zeros((rows, WIDE - DL - DR), jnp.bfloat16)

    def fill_queries(h):
        here = slice(h * DQ, (h + 1) * DQ)
        q = jnp.concatenate([q0[:, here], q1[:, here], q2[:, here], q3[:, here]], axis=0)
        q_lat = lax.dot_general(
            q[:, :DN], w_uk[h], (((1,), (1,)), ((), ())), preferred_element_type=jnp.float32
        )
        q_ref[h, :, :DL] = q_lat.astype(jnp.bfloat16)
        q_ref[h, :, DL : DL + DR] = q[:, DN:]
        q_ref[h, :, DL + DR : WIDE] = none
        q_ref[h, :, WIDE:] = floor

    fill_queries(0)
    fill_queries(1)
    fill_keys(keys, kv, 0, 2 * y)
    ahead = pair_scores(q_ref, keys, 0)
    for p in range(HEADS // 2):
        s = ahead
        if p + 1 < HEADS // 2:
            fill_queries(2 * p + 2)
            fill_queries(2 * p + 3)
            ahead = pair_scores(q_ref, keys, p + 1)
        top = jnp.max(s, axis=1, keepdims=True)
        weight = jnp.exp2((s - top) * SCALE2)
        total = jnp.sum(weight, axis=1, keepdims=True)
        lat = jnp.dot(weight.astype(jnp.bfloat16), keys[:, :DL], preferred_element_type=jnp.float32)
        pair = slice(2 * p, 2 * p + 2)
        lat_ref[pair] = lat.reshape(2, rows, DL)
        top_ref[pair] = jnp.broadcast_to(top, (2 * rows, STAT)).reshape(2, rows, STAT)
        total_ref[pair] = jnp.broadcast_to(total, (2 * rows, STAT)).reshape(2, rows, STAT)


def attend_own(info, qs, w_uk, kv):
    vmem = pl.BlockSpec(memory_space=pltpu.VMEM)
    smem = pl.BlockSpec(memory_space=pltpu.SMEM)
    rows = NX * SPAN
    return pl.pallas_call(
        own_kernel,
        out_shape=[
            jax.ShapeDtypeStruct((HEADS, rows, WIDE + EXTRA), jnp.bfloat16),
            jax.ShapeDtypeStruct((HEADS, rows, DL), jnp.float32),
            jax.ShapeDtypeStruct((HEADS, rows, STAT), jnp.float32),
            jax.ShapeDtypeStruct((HEADS, rows, STAT), jnp.float32),
        ],
        in_specs=[smem] + [vmem] * 6,
        out_specs=[vmem] * 4,
        scratch_shapes=[pltpu.VMEM((NY * SPAN, WIDE + EXTRA), jnp.bfloat16)],
        compiler_params=pltpu.CompilerParams(vmem_limit_bytes=20 * 1024 * 1024),
        cost_estimate=pl.CostEstimate(flops=6_000_000_000, bytes_accessed=5_000_000, transcendentals=1_000_000),
    )(info, *qs, w_uk, kv)


def other_kernel(place_ref, q_ref, kv, lat_ref, top_ref, total_ref, w_uv, out_ref, keys):
    x = (place_ref[0] // 2) % NX
    rows = NX * SPAN
    fill_keys(keys, kv, NY * SPAN // HALF, None)
    lanes = lax.broadcasted_iota(jnp.int32, (rows, STAT), 1)
    level = jnp.zeros((rows, STAT), jnp.float32)
    ahead = pair_scores(q_ref, keys, 0)
    for p in range(HEADS // 2):
        s = ahead
        if p + 1 < HEADS // 2:
            ahead = pair_scores(q_ref, keys, p + 1)
        pair = slice(2 * p, 2 * p + 2)
        old_top = top_ref[pair].reshape(2 * rows, STAT)
        old_total = total_ref[pair].reshape(2 * rows, STAT)
        top = jnp.maximum(old_top, jnp.max(s, axis=1, keepdims=True))
        shrink = jnp.exp2((old_top - top) * SCALE2)
        weight = jnp.exp2((s - wide(top, NY * SPAN // STAT)) * SCALE2)
        total = old_total * shrink + jnp.sum(weight, axis=1, keepdims=True)
        lat = jnp.dot(weight.astype(jnp.bfloat16), keys[:, :DL], preferred_element_type=jnp.float32)
        share = 1.0 / total
        old_lat = lat_ref[pair].reshape(2 * rows, DL)
        o_lat = (lat * wide(share, DL // STAT) + old_lat * wide(shrink * share, DL // STAT)).astype(jnp.bfloat16)
        here = top * SCALE2 + jnp.log2(total)
        for i in range(2):
            h = 2 * p + i
            proj = jnp.dot(o_lat[i * rows : (i + 1) * rows], w_uv[h], preferred_element_type=jnp.float32)
            proj = proj.astype(jnp.bfloat16)
            for step in range(NX):
                to = (x + NX - step) % NX
                out_ref[to, :, h * DV : (h + 1) * DV] = proj[step * SPAN : (step + 1) * SPAN]
            level = jnp.where(lanes % HEADS == h, here[i * rows : (i + 1) * rows], level)
    high = level.astype(jnp.bfloat16)
    rest = level - high.astype(jnp.float32)
    middle = rest.astype(jnp.bfloat16)
    low = (rest - middle.astype(jnp.float32)).astype(jnp.bfloat16)
    part = lanes // HEADS
    packed = jnp.where(
        part == 0,
        high.astype(jnp.float32),
        jnp.where(part == 1, middle.astype(jnp.float32), jnp.where(part == 2, low.astype(jnp.float32), 0.0)),
    ).astype(jnp.bfloat16)
    for step in range(NX):
        to = (x + NX - step) % NX
        out_ref[to, :, HEADS * DV :] = packed[step * SPAN : (step + 1) * SPAN]


def attend_other(place, q_all, kv, state, w_uv):
    vmem = pl.BlockSpec(memory_space=pltpu.VMEM)
    smem = pl.BlockSpec(memory_space=pltpu.SMEM)
    rows = NX * SPAN
    return pl.pallas_call(
        other_kernel,
        out_shape=jax.ShapeDtypeStruct((NX, SPAN, HEADS * DV + STAT), jnp.bfloat16),
        in_specs=[smem] + [vmem] * 6,
        out_specs=vmem,
        scratch_shapes=[pltpu.VMEM((NY * SPAN, WIDE + EXTRA), jnp.bfloat16)],
        compiler_params=pltpu.CompilerParams(vmem_limit_bytes=20 * 1024 * 1024),
        cost_estimate=pl.CostEstimate(flops=4_000_000_000, bytes_accessed=5_000_000, transcendentals=1_000_000),
    )(place, q_all, kv, *state, w_uv)


def merge_kernel(p_ref, out_ref):
    levels = []
    for x in range(NX):
        pieces = p_ref[x, :, :, HEADS * DV :].astype(jnp.float32).reshape(SPAN, STAT)
        rest = pltpu.roll(pieces, STAT - HEADS, 1) + pltpu.roll(pieces, STAT - 2 * HEADS, 1)
        levels.append(pieces + rest)
    top = functools.reduce(jnp.maximum, levels)
    shares = [jnp.exp2(level - top) for level in levels]
    whole = functools.reduce(jnp.add, shares)
    shares = [share / whole for share in shares]
    tokens = SPAN // NZ
    for z in range(NZ):
        here = slice(z * tokens, (z + 1) * tokens)
        for h in range(HEADS):
            acc = jnp.zeros((tokens, DV), jnp.float32)
            for x in range(NX):
                acc = acc + shares[x][here, h : h + 1] * p_ref[x, z, :, h * DV : (h + 1) * DV].astype(jnp.float32)
            out_ref[:, (z * HEADS + h) * DV : (z * HEADS + h + 1) * DV] = acc.astype(jnp.bfloat16)


def merge(parts):
    vmem = pl.BlockSpec(memory_space=pltpu.VMEM)
    return pl.pallas_call(
        merge_kernel,
        out_shape=jax.ShapeDtypeStruct((SPAN // NZ, NZ * HEADS * DV), jnp.bfloat16),
        in_specs=[vmem],
        out_specs=vmem,
        compiler_params=pltpu.CompilerParams(vmem_limit_bytes=8 * 1024 * 1024),
        cost_estimate=pl.CostEstimate(flops=1_000_000, bytes_accessed=800_000, transcendentals=2000),
    )(parts)


def on_device(queries, latent, rope_key, w_uk, w_uv, block_order):
    place = lax.axis_index("ctx").astype(jnp.int32).reshape(1)
    info = jnp.concatenate([place, block_order])
    both = spread(queries, latent, rope_key)
    both = lax.all_to_all(both, "head", split_axis=0, concat_axis=0, tiled=True).reshape(SPAN, HEADS * DQ + WIDE)
    q_own, kv = pack(both)
    kv_own = lax.all_to_all(kv, "ctx", split_axis=0, concat_axis=0, tiled=True, axis_index_groups=Y_GROUPS)
    kv_sib = lax.ppermute(kv_own, "ctx", CORE_SWAP)
    qs = [q_own] + [lax.ppermute(q_own, "ctx", along_x(step)) for step in range(1, NX)]
    q_all, *state = attend_own(info, qs, w_uk, kv_own)
    partial = attend_other(place, q_all, kv_sib, state, w_uv)
    rows = SPAN // NZ
    partial = partial.reshape(NX * NZ, rows, HEADS * DV + STAT)
    parts = lax.all_to_all(
        partial, ("ctx", "head"), split_axis=0, concat_axis=0, tiled=True, axis_index_groups=XZ_GROUPS
    )
    return merge(parts.reshape(NX, NZ, rows, HEADS * DV + STAT))


def solution(mesh):
    in_specs = (
        P(("ctx", "head"), None),
        P(("ctx", "head"), None),
        P(("ctx", "head"), None),
        P("head", None, None),
        P("head", None, None),
        P(),
    )
    out_specs = P(("ctx", "head"), None)
    return jax.shard_map(
        on_device, mesh=mesh, in_specs=in_specs, out_specs=out_specs, check_vma=False
    )
```

time: 92.5 us -> 86.3 us (0.933)
  the two profiles are of different devices: /device:TPU:72 before, /device:TPU:64 now
where the time goes in v4:
time: 86.3 us; the launch traced here: 85.8 us
  blocking collectives  48.3 us (56%)
  starting transfers between devices  20.4 us (24%)
  Pallas kernels  12.2 us (14%)
  waiting for transfers between devices  4.81 us (6%)
    all_to_all x1, blocking collectives, on_device(): lax.all_to_all(partial, ('ctx', 'head'), split_axis=0, concat_axis=0, til...  27.6 us
    all_to_all x1, blocking collectives, on_device(): lax.all_to_all(both, 'head', split_axis=0, concat_axis=0, tiled=True)  20.7 us
    ppermute x3, starting transfers between devices, on_device(): lax.ppermute(q_own, 'ctx', along_x(step))  11.4 us
    all_to_all x1, starting transfers between devices, on_device(): lax.all_to_all(kv, 'ctx', split_axis=0, concat_axis=0, tiled=True, axis_i...  7.1 us
    all_to_all x1, waiting for transfers between devices, on_device(): lax.all_to_all(kv, 'ctx', split_axis=0, concat_axis=0, tiled=True, axis_i...  4.79 us
    pallas_call x1, Pallas kernels, attend_own(): pl.pallas_call(own_kernel, out_shape=[jax.ShapeDtypeStruct((HEADS, rows,...  4.29 us
    pallas_call x1, Pallas kernels, attend_other(): pl.pallas_call(other_kernel, out_shape=jax.ShapeDtypeStruct((NX, SPAN, HE...  4.07 us
    ppermute x1, starting transfers between devices, on_device(): kv_sib = lax.ppermute(kv_own, 'ctx', CORE_SWAP)  1.91 us
  transfers between devices with their start and end apart: 5, of which 1 were waited for; matrix products, arithmetic and copies ran while one was open for 0% of the time, Pallas kernels for 5%

profile of v4, /device:TPU:64, one launch (start us, length us, event | category | flops | bytes accessed | tf_op | source)
XLA Modules:
  0.0 85.8 jit_solution(14781436390738507437)
XLA Ops:
  0.0 1.7 %shard_map.64 = bf16[8,8,2176]{2,1,0:T(8,128)(2,1)} custom-call(bf16[8,12288]{1,0:T(8,128)(2,1)} %q_ref.1, bf16[8,512]{1,0:T(8,128)(2,1)} %lat_ref.1, bf16[8,64]{1,0:T(8,128)(2,1)} %rope_ref.1), custom_call_target="tpu_custom_call" | custom-call | flops 1000000 | bytes 500000 | tf_op jit(solution)/shard_map/pallas_call | solution.py:62
  1.7 20.7 %all_to_all.15 = bf16[8,8,2176]{2,1,0:T(8,128)(2,1)S(1)} all-to-all(bf16[8,8,2176]{2,1,0:T(8,128)(2,1)} %shard_map.64), channel_id=1, replica_groups=mesh['ctx'=64,'head'=8] {'head'}, dimensions={0} | all-to-all | bytes 557056 | tf_op jit(solution)/shard_map/all_to_all | solution.py:305
  22.4 0.0 copy-start.2
  22.4 0.0 copy-start
  22.4 0.9 %shard_map.65 = (bf16[64,1536]{1,0:T(8,128)(2,1)S(1)}, bf16[8,288,128]{2,1,0:T(8,128)(2,1)}) custom-call(bf16[64,2176]{1,0:T(8,128)(2,1)S(1)} %bitcast.6), custom_call_target="tpu_custom_call" | custom-call | flops 4000000000 | bytes 1000000 | tf_op jit(solution)/shard_map/pallas_call | solution.py:85
  23.3 7.1 %all-to-all-start.1 = ((bf16[8,288,128]{2,1,0:T(8,128)(2,1)}), bf16[8,288,128]{2,1,0:T(8,128)(2,1)S(1)}, u32[]{:S(2)}, u32[]{:S(2)}) async-start(bf16[8,288,128]{2,1,0:T(8,128)(2,1)} %get-tuple-element.12), calls=%async_computation.1 | async-start | bytes 1179648 | tf_op jit(solution)/shard_map/all_to_all | solution.py:307
  30.4 3.4 %collective-permute-start = (bf16[64,1536]{1,0:T(8,128)(2,1)S(1)}, bf16[64,1536]{1,0:T(8,128)(2,1)S(1)}, u32[]{:S(2)}, u32[]{:S(2)}) collective-permute-start(bf16[64,1536]{1,0:T(8,128)(2,1)S(1)} %get-tuple-element.11.q0), channel_id=1, source_target_pairs={{0,16},{8,24},{16,32},{24,40},{32,48},{40,56},{48,0},{56,8},{64,80... | collective-permute-start | bytes 589832 | tf_op jit(solution)/shard_map/ppermute | solution.py:309
  33.8 4.6 %collective-permute-start.1 = (bf16[64,1536]{1,0:T(8,128)(2,1)S(1)}, bf16[64,1536]{1,0:T(8,128)(2,1)S(1)}, u32[]{:S(2)}, u32[]{:S(2)}) collective-permute-start(bf16[64,1536]{1,0:T(8,128)(2,1)S(1)} %get-tuple-element.11.q0), channel_id=1, source_target_pairs={{0,32},{8,40},{16,48},{24,56},{32,0},{40,8},{48,16},{56,24},{64,96... | collective-permute-start | bytes 589832 | tf_op jit(solution)/shard_map/ppermute | solution.py:309
  38.5 3.3 %collective-permute-start.2 = (bf16[64,1536]{1,0:T(8,128)(2,1)S(1)}, bf16[64,1536]{1,0:T(8,128)(2,1)S(1)}, u32[]{:S(2)}, u32[]{:S(2)}) collective-permute-start(bf16[64,1536]{1,0:T(8,128)(2,1)S(1)} %get-tuple-element.11.q0), channel_id=1, source_target_pairs={{0,48},{8,56},{16,0},{24,8},{32,16},{40,24},{48,32},{56,40},{64,11... | collective-permute-start | bytes 589832 | tf_op jit(solution)/shard_map/ppermute | solution.py:309
  41.8 4.8 %all-to-all-done.1.kv = bf16[8,288,128]{2,1,0:T(8,128)(2,1)S(1)} async-done(((bf16[8,288,128]{2,1,0:T(8,128)(2,1)}), bf16[8,288,128]{2,1,0:T(8,128)(2,1)S(1)}, u32[]{:S(2)}, u32[]{:S(2)}) %all-to-all-start.1) | async-done | bytes 589856 | tf_op jit(solution)/shard_map/all_to_all | solution.py:307
  46.6 1.9 %collective-permute-start.3 = (bf16[8,288,128]{2,1,0:T(8,128)(2,1)S(1)}, bf16[8,288,128]{2,1,0:T(8,128)(2,1)S(1)}, u32[]{:S(2)}, u32[]{:S(2)}) collective-permute-start(bf16[8,288,128]{2,1,0:T(8,128)(2,1)S(1)} %all-to-all-done.1.kv), channel_id=1, source_target_pairs={{0,8},{8,0},{16,24},{24,16},{32,40},{40,32},{48,56},{56,48},{64,72... | collective-permute-start | bytes 1769480 | tf_op jit(solution)/shard_map/ppermute | solution.py:308
  48.5 0.0 copy-done.2
  48.5 0.1 pad_add_fusion.info_ref
  48.6 0.0 copy-start.1
  48.6 0.0 collective-permute-done.q1
  48.6 0.0 collective-permute-done.1.q2
  48.6 0.0 collective-permute-done.2.q3
  48.6 0.0 copy-done
  48.7 4.3 %shard_map.66 = (bf16[8,256,768]{2,1,0:T(8,128)(2,1)S(1)}, f32[8,256,512]{2,1,0:T(8,128)S(1)}, f32[8,256,128]{2,1,0:T(8,128)S(1)}, f32[8,256,128]{2,1,0:T(8,128)S(1)}) custom-call(s32[129]{0:T(256)S(1)} %pad_add_fusion.info_ref, bf16[64,1536]{1,0:T(8,128)(2,1)S(1)} %get-tuple-element.11.q0, bf16[64,1536]{1,0:T(8,128)(2,1)S(1)} %collective-permute-done.q1, ...), custom_call_target="tpu_custom_call" | custom-call | flops 6000000000 | bytes 5000000 | tf_op jit(solution)/shard_map/pallas_call | solution.py:192
  52.9 0.0 collective-permute-done.3.kv
  53.0 0.0 copy-done.1
  53.0 4.1 %shard_map.67 = bf16[4,64,1152]{2,1,0:T(8,128)(2,1)S(1)} custom-call(s32[1]{0:T(128)} %bitcast.place_ref, bf16[8,256,768]{2,1,0:T(8,128)(2,1)S(1)} %get-tuple-element.13.q_ref, bf16[8,288,128]{2,1,0:T(8,128)(2,1)S(1)} %collective-permute-done.3.kv, f32[8,256,512]{2,1,0:T(8,128)S(1)} %get-tuple-element.14.lat_ref, ...), custom_call_target="tpu_custom_call" | custom-call | flops 4000000000 | bytes 5000000 | tf_op jit(solution)/shard_map/pallas_call | solution.py:258
  57.0 27.6 %all_to_all.16 = bf16[32,8,1152]{2,1,0:T(8,128)(2,1)S(1)} all-to-all(bf16[32,8,1152]{2,1,0:T(8,128)(2,1)S(1)} %bitcast.5), channel_id=1, replica_groups={{0,1,2,3,4,5,6,7,16,17,18,19,20,21,22,23,32,33,34,35,36,37,38,39,48,49,..., dimensions={0} | all-to-all | bytes 1179648 | tf_op jit(solution)/shard_map/all_to_all | solution.py:314
  84.6 1.2 %shard_map.68 = bf16[8,8192]{1,0:T(8,128)(2,1)} custom-call(bf16[4,8,8,1152]{3,2,1,0:T(8,128)(2,1)S(1)} %bitcast.4), custom_call_target="tpu_custom_call" | custom-call | flops 1000000 | bytes 800000 | tf_op jit(solution)/shard_map/pallas_call | solution.py:291
Async XLA Ops:
  22.4 26.1 %copy-start.2 = (s32[128]{0:T(128)S(1)}, s32[128]{0:T(128)}, u32[]{:S(2)}) copy-start(s32[128]{0:T(128)} %param.11) | copy-start | bytes 1540
  22.4 26.2 %copy-start = (bf16[8,512,128]{2,1,0:T(8,128)(2,1)S(1)}, bf16[8,512,128]{2,1,0:T(8,128)(2,1)}, u32[]{:S(2)}) copy-start(bf16[8,512,128]{2,1,0:T(8,128)(2,1)} %w_uk.1) | copy-start | bytes 3145732
  23.3 23.3 %all-to-all-start.1 = ((bf16[8,288,128]{2,1,0:T(8,128)(2,1)}), bf16[8,288,128]{2,1,0:T(8,128)(2,1)S(1)}, u32[]{:S(2)}, u32[]{:S(2)}) async-start(bf16[8,288,128]{2,1,0:T(8,128)(2,1)} %get-tuple-element.12), calls=%async_computation.1 | async-start | bytes 1179648 | tf_op jit(solution)/shard_map/all_to_all | solution.py:307
  30.4 18.2 %collective-permute-start = (bf16[64,1536]{1,0:T(8,128)(2,1)S(1)}, bf16[64,1536]{1,0:T(8,128)(2,1)S(1)}, u32[]{:S(2)}, u32[]{:S(2)}) collective-permute-start(bf16[64,1536]{1,0:T(8,128)(2,1)S(1)} %get-tuple-element.11.q0), channel_id=1, source_target_pairs={{0,16},{8,24},{16,32},{24,40},{32,48},{40,56},{48,0},{56,8},{64,80... | collective-permute-start | bytes 589832 | tf_op jit(solution)/shard_map/ppermute | solution.py:309
  33.8 14.8 %collective-permute-start.1 = (bf16[64,1536]{1,0:T(8,128)(2,1)S(1)}, bf16[64,1536]{1,0:T(8,128)(2,1)S(1)}, u32[]{:S(2)}, u32[]{:S(2)}) collective-permute-start(bf16[64,1536]{1,0:T(8,128)(2,1)S(1)} %get-tuple-element.11.q0), channel_id=1, source_target_pairs={{0,32},{8,40},{16,48},{24,56},{32,0},{40,8},{48,16},{56,24},{64,96... | collective-permute-start | bytes 589832 | tf_op jit(solution)/shard_map/ppermute | solution.py:309
  38.5 10.2 %collective-permute-start.2 = (bf16[64,1536]{1,0:T(8,128)(2,1)S(1)}, bf16[64,1536]{1,0:T(8,128)(2,1)S(1)}, u32[]{:S(2)}, u32[]{:S(2)}) collective-permute-start(bf16[64,1536]{1,0:T(8,128)(2,1)S(1)} %get-tuple-element.11.q0), channel_id=1, source_target_pairs={{0,48},{8,56},{16,0},{24,8},{32,16},{40,24},{48,32},{56,40},{64,11... | collective-permute-start | bytes 589832 | tf_op jit(solution)/shard_map/ppermute | solution.py:309
  46.6 6.3 %collective-permute-start.3 = (bf16[8,288,128]{2,1,0:T(8,128)(2,1)S(1)}, bf16[8,288,128]{2,1,0:T(8,128)(2,1)S(1)}, u32[]{:S(2)}, u32[]{:S(2)}) collective-permute-start(bf16[8,288,128]{2,1,0:T(8,128)(2,1)S(1)} %all-to-all-done.1.kv), channel_id=1, source_target_pairs={{0,8},{8,0},{16,24},{24,16},{32,40},{40,32},{48,56},{56,48},{64,72... | collective-permute-start | bytes 1769480 | tf_op jit(solution)/shard_map/ppermute | solution.py:308
  48.6 4.3 %copy-start.1 = (bf16[8,512,128]{2,1,0:T(8,128)(2,1)S(1)}, bf16[8,512,128]{2,1,0:T(8,128)(2,1)}, u32[]{:S(2)}) copy-start(bf16[8,512,128]{2,1,0:T(8,128)(2,1)} %w_uv.1) | copy-start | bytes 3145732

commit v5 on v4

--- a/solution.py
+++ b/solution.py
@@ -22,7 +22,10 @@
 HEADS = 8
 SPAN = 64
 LANES = 128
-PACKED = DL // LANES * SPAN + HALF
+PACKED = DL // LANES * HALF + HALF // 2
+PIECE = NY * HALF
+PIECES = 4
+BLOCKS = PIECES * NY
 FLOOR_SCORE = -1e30
 LOG2E = 1.4426950408889634
 SCALE2 = DQ ** (-0.5) * LOG2E
@@ -41,6 +44,7 @@
     ]
 
 
+Z_SWAP = [(i, i ^ 1) for i in range(NZ)]
 CORE_SWAP = [(i, i ^ 1) for i in range(NX * NY * 2)]
 XZ_GROUPS = [
     [ctx_of(y, x, c) * NZ + z for x in range(NX) for z in range(NZ)] for y in range(NY) for c in range(2)
@@ -69,48 +73,48 @@
     )(queries, latent, rope_key)
 
 
-def pack_kernel(both_ref, q_ref, kv_ref):
+def pack_kernel(info_ref, both_ref, q_ref, kv_ref):
     q_ref[...] = both_ref[:, : HEADS * DQ]
-    rope = both_ref[:, HEADS * DQ + DL : HEADS * DQ + DL + DR]
+    rows = pl.ds(pl.multiple_of(info_ref[1] * HALF, HALF), HALF)
+    kept = both_ref[rows, HEADS * DQ : HEADS * DQ + DL + DR]
     for to in range(NY):
         for j in range(DL // LANES):
-            col = HEADS * DQ + j * LANES
-            kv_ref[to, j * SPAN : (j + 1) * SPAN] = both_ref[:, col : col + LANES]
-        kv_ref[to, PACKED - HALF :, :DR] = rope[:HALF]
-        kv_ref[to, PACKED - HALF :, DR:] = rope[HALF:]
-
-
-def pack(both):
-    vmem = pl.BlockSpec(memory_space=pltpu.VMEM)
+            kv_ref[to, j * HALF : (j + 1) * HALF] = kept[:, j * LANES : (j + 1) * LANES]
+        kv_ref[to, DL // LANES * HALF :, :DR] = kept[: HALF // 2, DL:]
+        kv_ref[to, DL // LANES * HALF :, DR:] = kept[HALF // 2 :, DL:]
+
+
+def pack(info, both):
+    vmem = pl.BlockSpec(memory_space=pltpu.VMEM)
+    smem = pl.BlockSpec(memory_space=pltpu.SMEM)
     return pl.pallas_call(
         pack_kernel,
         out_shape=[
             jax.ShapeDtypeStruct((SPAN, HEADS * DQ), jnp.bfloat16),
             jax.ShapeDtypeStruct((NY, PACKED, LANES), jnp.bfloat16),
         ],
-        in_specs=[vmem],
+        in_specs=[smem, vmem],
         out_specs=[vmem] * 2,
         compiler_params=pltpu.CompilerParams(vmem_limit_bytes=8 * 1024 * 1024),
         cost_estimate=pl.CostEstimate(flops=4_000_000_000, bytes_accessed=1_000_000, transcendentals=0),
-    )(both)
-
-
-def fill_keys(keys, kv, first, own_block):
-    count = NY * SPAN
-    blocks = 2 * count // HALF
+    )(info, both)
+
+
+def fill_keys(keys, kv, piece, info_ref):
+    lat_rows = DL // LANES * HALF
     for b in range(NY):
-        here = slice(b * SPAN, (b + 1) * SPAN)
+        here = slice(b * HALF, (b + 1) * HALF)
         for j in range(DL // LANES):
-            keys[here, j * LANES : (j + 1) * LANES] = kv[b, j * SPAN : (j + 1) * SPAN]
-        keys[b * SPAN : b * SPAN + HALF, DL : DL + DR] = kv[b, PACKED - HALF :, :DR]
-        keys[b * SPAN + HALF : (b + 1) * SPAN, DL : DL + DR] = kv[b, PACKED - HALF :, DR:]
-    keys[:, DL + DR : WIDE] = jnp.zeros((count, WIDE - DL - DR), jnp.bfloat16)
-    key = lax.broadcasted_iota(jnp.int32, (count, EXTRA), 0)
-    col = lax.broadcasted_iota(jnp.int32, (count, EXTRA), 1)
-    ones = col == key // HALF + first
-    if own_block is not None:
-        in_own = (key // HALF == own_block) | (key // HALF == own_block + 1)
-        ones = ones | (in_own & (col == blocks + key - own_block * HALF))
+            keys[here, j * LANES : (j + 1) * LANES] = kv[b, j * HALF : (j + 1) * HALF]
+        keys[b * HALF : b * HALF + HALF // 2, DL : DL + DR] = kv[b, lat_rows:, :DR]
+        keys[b * HALF + HALF // 2 : (b + 1) * HALF, DL : DL + DR] = kv[b, lat_rows:, DR:]
+    keys[:, DL + DR : WIDE] = jnp.zeros((PIECE, WIDE - DL - DR), jnp.bfloat16)
+    key = lax.broadcasted_iota(jnp.int32, (PIECE, EXTRA), 0)
+    col = lax.broadcasted_iota(jnp.int32, (PIECE, EXTRA), 1)
+    ones = col == key // HALF + piece * NY
+    if piece % 2 == 0:
+        y = info_ref[0] // (2 * NX)
+        ones = ones | ((key // HALF == y) & (col == BLOCKS + piece // 2 * HALF + key - y * HALF))
     keys[:, WIDE:] = jnp.where(ones, 1.0, 0.0).astype(jnp.bfloat16)
 
 
@@ -124,32 +128,32 @@
 
 
 def floors_of(info_ref):
-    me = info_ref[0]
+    me, parity = info_ref[0], info_ref[1]
     core = me % 2
     x = (me // 2) % NX
     y = me // (2 * NX)
-    blocks = 2 * NY * SPAN // HALF
     lane = lax.broadcasted_iota(jnp.int32, (HALF, EXTRA), 1)
     token = lax.broadcasted_iota(jnp.int32, (HALF, EXTRA), 0)
     key_block = jnp.zeros((HALF, EXTRA), jnp.int32)
-    for which in range(blocks):
-        side_core = core if which < blocks // 2 else 1 - core
-        slot = (((which // 2) % NY) * NX + x) * 2 + side_core
-        key_block = jnp.where(lane == which, info_ref[1 + 2 * slot + which % 2], key_block)
+    for which in range(BLOCKS):
+        piece = which // NY
+        key_core = (core + piece) % 2
+        key_half = (parity + piece // 2) % 2
+        slot = ((which % NY) * NX + x) * 2 + key_core
+        key_block = jnp.where(lane == which, info_ref[2 + 2 * slot + key_half], key_block)
     floors = []
     for step in range(NX):
         slot = (y * NX + (x - step + NX) % NX) * 2 + core
         for half in range(2):
-            ahead = (lane < blocks) & (key_block > info_ref[1 + 2 * slot + half])
+            ahead = (lane < BLOCKS) & (key_block > info_ref[2 + 2 * slot + half])
             if step == 0:
-                own = lane - blocks - half * HALF
+                own = lane - BLOCKS - (parity + half) % 2 * HALF
                 ahead = ahead | ((own >= 0) & (own < HALF) & (own > token))
             floors.append(jnp.where(ahead, FLOOR_SCORE, 0.0))
     return jnp.concatenate(floors, axis=0).astype(jnp.bfloat16)
 
 
-def own_kernel(info_ref, q0, q1, q2, q3, w_uk, kv, q_ref, lat_ref, top_ref, total_ref, keys):
-    y = info_ref[0] // (2 * NX)
+def first_kernel(info_ref, q0, q1, q2, q3, w_uk, kv, q_ref, lat_ref, top_ref, total_ref, keys):
     rows = NX * SPAN
     floor = floors_of(info_ref)
     none = jnp.zeros((rows, WIDE - DL - DR), jnp.bfloat16)
@@ -167,7 +171,7 @@
 
     fill_queries(0)
     fill_queries(1)
-    fill_keys(keys, kv, 0, 2 * y)
+    fill_keys(keys, kv, 0, info_ref)
     ahead = pair_scores(q_ref, keys, 0)
     for p in range(HEADS // 2):
         s = ahead
@@ -185,12 +189,12 @@
         total_ref[pair] = jnp.broadcast_to(total, (2 * rows, STAT)).reshape(2, rows, STAT)
 
 
-def attend_own(info, qs, w_uk, kv):
+def attend_first(info, qs, w_uk, kv):
     vmem = pl.BlockSpec(memory_space=pltpu.VMEM)
     smem = pl.BlockSpec(memory_space=pltpu.SMEM)
     rows = NX * SPAN
     return pl.pallas_call(
-        own_kernel,
+        first_kernel,
         out_shape=[
             jax.ShapeDtypeStruct((HEADS, rows, WIDE + EXTRA), jnp.bfloat16),
             jax.ShapeDtypeStruct((HEADS, rows, DL), jnp.float32),
@@ -199,16 +203,61 @@
         ],
         in_specs=[smem] + [vmem] * 6,
         out_specs=[vmem] * 4,
-        scratch_shapes=[pltpu.VMEM((NY * SPAN, WIDE + EXTRA), jnp.bfloat16)],
+        scratch_shapes=[pltpu.VMEM((PIECE, WIDE + EXTRA), jnp.bfloat16)],
         compiler_params=pltpu.CompilerParams(vmem_limit_bytes=20 * 1024 * 1024),
         cost_estimate=pl.CostEstimate(flops=6_000_000_000, bytes_accessed=5_000_000, transcendentals=1_000_000),
     )(info, *qs, w_uk, kv)
 
 
-def other_kernel(place_ref, q_ref, kv, lat_ref, top_ref, total_ref, w_uv, out_ref, keys):
-    x = (place_ref[0] // 2) % NX
-    rows = NX * SPAN
-    fill_keys(keys, kv, NY * SPAN // HALF, None)
+def advance(s, keys, lat_ref, top_ref, total_ref, pair):
+    rows = 2 * NX * SPAN
+    old_top = top_ref[pair].reshape(rows, STAT)
+    top = jnp.maximum(old_top, jnp.max(s, axis=1, keepdims=True))
+    shrink = jnp.exp2((old_top - top) * SCALE2)
+    weight = jnp.exp2((s - wide(top, PIECE // STAT)) * SCALE2)
+    total = total_ref[pair].reshape(rows, STAT) * shrink + jnp.sum(weight, axis=1, keepdims=True)
+    lat = jnp.dot(weight.astype(jnp.bfloat16), keys[:, :DL], preferred_element_type=jnp.float32)
+    return top, total, shrink, lat, lat_ref[pair].reshape(rows, DL)
+
+
+def middle_kernel(piece, info_ref, q_ref, kv, old_lat, old_top, old_total, lat_ref, top_ref, total_ref, keys):
+    rows = NX * SPAN
+    fill_keys(keys, kv, piece, info_ref)
+    ahead = pair_scores(q_ref, keys, 0)
+    for p in range(HEADS // 2):
+        s = ahead
+        if p + 1 < HEADS // 2:
+            ahead = pair_scores(q_ref, keys, p + 1)
+        pair = slice(2 * p, 2 * p + 2)
+        top, total, shrink, lat, held = advance(s, keys, old_lat, old_top, old_total, pair)
+        lat_ref[pair] = (lat + held * wide(shrink, DL // STAT)).reshape(2, rows, DL)
+        top_ref[pair] = top.reshape(2, rows, STAT)
+        total_ref[pair] = total.reshape(2, rows, STAT)
+
+
+def attend_middle(piece, info, q_all, kv, state):
+    vmem = pl.BlockSpec(memory_space=pltpu.VMEM)
+    smem = pl.BlockSpec(memory_space=pltpu.SMEM)
+    rows = NX * SPAN
+    return pl.pallas_call(
+        functools.partial(middle_kernel, piece),
+        out_shape=[
+            jax.ShapeDtypeStruct((HEADS, rows, DL), jnp.float32),
+            jax.ShapeDtypeStruct((HEADS, rows, STAT), jnp.float32),
+            jax.ShapeDtypeStruct((HEADS, rows, STAT), jnp.float32),
+        ],
+        in_specs=[smem] + [vmem] * 5,
+        out_specs=[vmem] * 3,
+        scratch_shapes=[pltpu.VMEM((PIECE, WIDE + EXTRA), jnp.bfloat16)],
+        compiler_params=pltpu.CompilerParams(vmem_limit_bytes=16 * 1024 * 1024),
+        cost_estimate=pl.CostEstimate(flops=2_500_000_000, bytes_accessed=5_000_000, transcendentals=500_000),
+    )(info, q_all, kv, *state)
+
+
+def last_kernel(info_ref, q_ref, kv, old_lat, old_top, old_total, w_uv, out_ref, keys):
+    x = (info_ref[0] // 2) % NX
+    rows = NX * SPAN
+    fill_keys(keys, kv, PIECES - 1, info_ref)
     lanes = lax.broadcasted_iota(jnp.int32, (rows, STAT), 1)
     level = jnp.zeros((rows, STAT), jnp.float32)
     ahead = pair_scores(q_ref, keys, 0)
@@ -217,16 +266,9 @@
         if p + 1 < HEADS // 2:
             ahead = pair_scores(q_ref, keys, p + 1)
         pair = slice(2 * p, 2 * p + 2)
-        old_top = top_ref[pair].reshape(2 * rows, STAT)
-        old_total = total_ref[pair].reshape(2 * rows, STAT)
-        top = jnp.maximum(old_top, jnp.max(s, axis=1, keepdims=True))
-        shrink = jnp.exp2((old_top - top) * SCALE2)
-        weight = jnp.exp2((s - wide(top, NY * SPAN // STAT)) * SCALE2)
-        total = old_total * shrink + jnp.sum(weight, axis=1, keepdims=True)
-        lat = jnp.dot(weight.astype(jnp.bfloat16), keys[:, :DL], preferred_element_type=jnp.float32)
+        top, total, shrink, lat, held = advance(s, keys, old_lat, old_top, old_total, pair)
         share = 1.0 / total
-        old_lat = lat_ref[pair].reshape(2 * rows, DL)
-        o_lat = (lat * wide(share, DL // STAT) + old_lat * wide(shrink * share, DL // STAT)).astype(jnp.bfloat16)
+        o_lat = (lat * wide(share, DL // STAT) + held * wide(shrink * share, DL // STAT)).astype(jnp.bfloat16)
         here = top * SCALE2 + jnp.log2(total)
         for i in range(2):
             h = 2 * p + i
@@ -251,19 +293,19 @@
         out_ref[to, :, HEADS * DV :] = packed[step * SPAN : (step + 1) * SPAN]
 
 
-def attend_other(place, q_all, kv, state, w_uv):
+def attend_last(info, q_all, kv, state, w_uv):
     vmem = pl.BlockSpec(memory_space=pltpu.VMEM)
     smem = pl.BlockSpec(memory_space=pltpu.SMEM)
     rows = NX * SPAN
     return pl.pallas_call(
-        other_kernel,
+        last_kernel,
         out_shape=jax.ShapeDtypeStruct((NX, SPAN, HEADS * DV + STAT), jnp.bfloat16),
         in_specs=[smem] + [vmem] * 6,
         out_specs=vmem,
-        scratch_shapes=[pltpu.VMEM((NY * SPAN, WIDE + EXTRA), jnp.bfloat16)],
+        scratch_shapes=[pltpu.VMEM((PIECE, WIDE + EXTRA), jnp.bfloat16)],
         compiler_params=pltpu.CompilerParams(vmem_limit_bytes=20 * 1024 * 1024),
         cost_estimate=pl.CostEstimate(flops=4_000_000_000, bytes_accessed=5_000_000, transcendentals=1_000_000),
-    )(place, q_all, kv, *state, w_uv)
+    )(info, q_all, kv, *state, w_uv)
 
 
 def merge_kernel(p_ref, out_ref):
@@ -299,16 +341,20 @@
 
 
 def on_device(queries, latent, rope_key, w_uk, w_uv, block_order):
-    place = lax.axis_index("ctx").astype(jnp.int32).reshape(1)
+    place = jnp.stack([lax.axis_index("ctx"), lax.axis_index("head") % 2]).astype(jnp.int32)
     info = jnp.concatenate([place, block_order])
     both = spread(queries, latent, rope_key)
     both = lax.all_to_all(both, "head", split_axis=0, concat_axis=0, tiled=True).reshape(SPAN, HEADS * DQ + WIDE)
-    q_own, kv = pack(both)
-    kv_own = lax.all_to_all(kv, "ctx", split_axis=0, concat_axis=0, tiled=True, axis_index_groups=Y_GROUPS)
-    kv_sib = lax.ppermute(kv_own, "ctx", CORE_SWAP)
+    q_own, kv = pack(info, both)
+    near = lax.all_to_all(kv, "ctx", split_axis=0, concat_axis=0, tiled=True, axis_index_groups=Y_GROUPS)
+    far = lax.ppermute(near, "head", Z_SWAP)
+    near_core = lax.ppermute(near, "ctx", CORE_SWAP)
+    far_core = lax.ppermute(far, "ctx", CORE_SWAP)
     qs = [q_own] + [lax.ppermute(q_own, "ctx", along_x(step)) for step in range(1, NX)]
-    q_all, *state = attend_own(info, qs, w_uk, kv_own)
-    partial = attend_other(place, q_all, kv_sib, state, w_uv)
+    q_all, *state = attend_first(info, qs, w_uk, near)
+    state = attend_middle(1, info, q_all, near_core, state)
+    state = attend_middle(2, info, q_all, far, state)
+    partial = attend_last(info, q_all, far_core, state, w_uv)
     rows = SPAN // NZ
     partial = partial.reshape(NX * NZ, rows, HEADS * DV + STAT)
     parts = lax.all_to_all(

time: 86.3 us -> 93.4 us (1.082)
  blocking collectives: 48.3 us -> 25.8 us
  starting transfers between devices: 20.4 us -> 35.6 us
  waiting for transfers between devices: 4.81 us -> 15 us
  Pallas kernels: 12.2 us -> 15.5 us
    all_to_all x1 -> x0, blocking collectives: 20.7 us -> none  [on_device(): lax.all_to_all(both, 'head', split_axis=0, concat_axis=0, tiled=True)]
    all_to_all x0 -> x1, waiting for transfers between devices: none -> 10 us  [on_device(): lax.all_to_all(both, 'head', split_axis=0, concat_axis=0, tiled=True)]
    all_to_all x0 -> x1, starting transfers between devices: none -> 9.96 us  [on_device(): lax.all_to_all(both, 'head', split_axis=0, concat_axis=0, tiled=True)]
    ppermute x1 -> x3, starting transfers between devices: 1.91 us -> 7.2 us  [the longest x1 3.37 us: on_device(): far = lax.ppermute(near, 'head', Z_SWAP)]
    ppermute x1 -> x3, waiting for transfers between devices: 0.01 us -> 4.94 us  [the longest x1 4.94 us: on_device(): far = lax.ppermute(near, 'head', Z_SWAP)]
    all_to_all x1, waiting for transfers between devices: 4.79 us -> 0.01 us  [on_device(): lax.all_to_all(kv, 'ctx', split_axis=0, concat_axis=0, tiled=True, axis_i...]
    pallas_call x2 -> x4, Pallas kernels: 8.35 us -> 11.3 us  [the longest x2 5.14 us: attend_middle(): pl.pallas_call(functools.partial(middle_kernel, piece), out_shape=[jax.Sh...]
    all_to_all x1, blocking collectives: 27.6 us -> 25.8 us  [on_device(): lax.all_to_all(partial, ('ctx', 'head'), split_axis=0, concat_axis=0, til...]
  transfers between devices with their start and end apart: 5 -> 8, of which waited for: 1 -> 2; matrix products, arithmetic and copies ran while one was open for 0% -> 1% of each run, Pallas kernels for 5% -> 9%
where the time goes in v5:
time: 93.4 us; the launch traced here: 92.9 us
  starting transfers between devices  35.6 us (38%)
  blocking collectives  25.8 us (28%)
  Pallas kernels  15.5 us (17%)
  waiting for transfers between devices  15 us (16%)
    all_to_all x1, blocking collectives, on_device(): lax.all_to_all(partial, ('ctx', 'head'), split_axis=0, concat_axis=0, til...  25.8 us
    ppermute x3, starting transfers between devices, on_device(): lax.ppermute(q_own, 'ctx', along_x(step))  11.4 us
    all_to_all x1, waiting for transfers between devices, on_device(): lax.all_to_all(both, 'head', split_axis=0, concat_axis=0, tiled=True)  10 us
    all_to_all x1, starting transfers between devices, on_device(): lax.all_to_all(both, 'head', split_axis=0, concat_axis=0, tiled=True)  9.96 us
    all_to_all x1, starting transfers between devices, on_device(): lax.all_to_all(kv, 'ctx', split_axis=0, concat_axis=0, tiled=True, axis_i...  7.1 us
    pallas_call x2, Pallas kernels, attend_middle(): pl.pallas_call(functools.partial(middle_kernel, piece), out_shape=[jax.Sh...  5.14 us
    ppermute x1, waiting for transfers between devices, on_device(): far = lax.ppermute(near, 'head', Z_SWAP)  4.94 us
    ppermute x1, starting transfers between devices, on_device(): far = lax.ppermute(near, 'head', Z_SWAP)  3.37 us
  transfers between devices with their start and end apart: 8, of which 2 were waited for; matrix products, arithmetic and copies ran while one was open for 1% of the time, Pallas kernels for 9%

profile of v5, /device:TPU:64, one launch (start us, length us, event | category | flops | bytes accessed | tf_op | source)
XLA Modules:
  0.0 92.9 jit_solution(1358984838091740182)
XLA Ops:
  0.0 1.7 %shard_map.64 = bf16[8,8,2176]{2,1,0:T(8,128)(2,1)} custom-call(bf16[8,12288]{1,0:T(8,128)(2,1)} %q_ref.1, bf16[8,512]{1,0:T(8,128)(2,1)} %lat_ref.1, bf16[8,64]{1,0:T(8,128)(2,1)} %rope_ref.1), custom_call_target="tpu_custom_call" | custom-call | flops 1000000 | bytes 500000 | tf_op jit(solution)/shard_map/pallas_call | solution.py:66
  1.7 10.0 %all-to-all-start = ((bf16[8,8,2176]{2,1,0:T(8,128)(2,1)}), bf16[8,8,2176]{2,1,0:T(8,128)(2,1)S(1)}, u32[]{:S(2)}, u32[]{:S(2)}) async-start(bf16[8,8,2176]{2,1,0:T(8,128)(2,1)} %shard_map.64), calls=%async_computation | async-start | bytes 557056 | tf_op jit(solution)/shard_map/all_to_all | solution.py:347
  11.6 0.7 pad_add_fusion.info_ref
  12.4 10.0 %all-to-all-done = bf16[8,8,2176]{2,1,0:T(8,128)(2,1)S(1)} async-done(((bf16[8,8,2176]{2,1,0:T(8,128)(2,1)}), bf16[8,8,2176]{2,1,0:T(8,128)(2,1)S(1)}, u32[]{:S(2)}, u32[]{:S(2)}) %all-to-all-start) | async-done | bytes 278560 | tf_op jit(solution)/shard_map/all_to_all | solution.py:347
  22.4 0.0 copy-start
  22.4 1.3 %shard_map.65 = (bf16[64,1536]{1,0:T(8,128)(2,1)S(1)}, bf16[8,144,128]{2,1,0:T(8,128)(2,1)}) custom-call(s32[130]{0:T(256)S(1)} %pad_add_fusion.info_ref, bf16[64,2176]{1,0:T(8,128)(2,1)S(1)} %bitcast.7), custom_call_target="tpu_custom_call" | custom-call | flops 4000000000 | bytes 1000000 | tf_op jit(solution)/shard_map/pallas_call | solution.py:90
  23.7 7.1 %all-to-all-start.1 = ((bf16[8,144,128]{2,1,0:T(8,128)(2,1)}), bf16[8,144,128]{2,1,0:T(8,128)(2,1)S(1)}, u32[]{:S(2)}, u32[]{:S(2)}) async-start(bf16[8,144,128]{2,1,0:T(8,128)(2,1)} %get-tuple-element.18), calls=%async_computation.1 | async-start | bytes 589824 | tf_op jit(solution)/shard_map/all_to_all | solution.py:349
  30.8 3.4 %collective-permute-start = (bf16[64,1536]{1,0:T(8,128)(2,1)S(1)}, bf16[64,1536]{1,0:T(8,128)(2,1)S(1)}, u32[]{:S(2)}, u32[]{:S(2)}) collective-permute-start(bf16[64,1536]{1,0:T(8,128)(2,1)S(1)} %get-tuple-element.17.q0), channel_id=1, source_target_pairs={{0,16},{8,24},{16,32},{24,40},{32,48},{40,56},{48,0},{56,8},{64,80... | collective-permute-start | bytes 589832 | tf_op jit(solution)/shard_map/ppermute | solution.py:353
  34.2 4.6 %collective-permute-start.1 = (bf16[64,1536]{1,0:T(8,128)(2,1)S(1)}, bf16[64,1536]{1,0:T(8,128)(2,1)S(1)}, u32[]{:S(2)}, u32[]{:S(2)}) collective-permute-start(bf16[64,1536]{1,0:T(8,128)(2,1)S(1)} %get-tuple-element.17.q0), channel_id=1, source_target_pairs={{0,32},{8,40},{16,48},{24,56},{32,0},{40,8},{48,16},{56,24},{64,96... | collective-permute-start | bytes 589832 | tf_op jit(solution)/shard_map/ppermute | solution.py:353
  38.9 3.3 %collective-permute-start.2 = (bf16[64,1536]{1,0:T(8,128)(2,1)S(1)}, bf16[64,1536]{1,0:T(8,128)(2,1)S(1)}, u32[]{:S(2)}, u32[]{:S(2)}) collective-permute-start(bf16[64,1536]{1,0:T(8,128)(2,1)S(1)} %get-tuple-element.17.q0), channel_id=1, source_target_pairs={{0,48},{8,56},{16,0},{24,8},{32,16},{40,24},{48,32},{56,40},{64,11... | collective-permute-start | bytes 589832 | tf_op jit(solution)/shard_map/ppermute | solution.py:353
  42.2 0.0 all-to-all-done.1.kv
  42.2 1.9 %collective-permute-start.5 = (bf16[8,144,128]{2,1,0:T(8,128)(2,1)S(1)}, bf16[8,144,128]{2,1,0:T(8,128)(2,1)S(1)}, u32[]{:S(2)}, u32[]{:S(2)}) collective-permute-start(bf16[8,144,128]{2,1,0:T(8,128)(2,1)S(1)} %all-to-all-done.1.kv), channel_id=1, source_target_pairs={{0,8},{8,0},{16,24},{24,16},{32,40},{40,32},{48,56},{56,48},{64,72... | collective-permute-start | bytes 884744 | tf_op jit(solution)/shard_map/ppermute | solution.py:351
  44.2 3.4 %collective-permute-start.3 = (bf16[8,144,128]{2,1,0:T(8,128)(2,1)S(1)}, bf16[8,144,128]{2,1,0:T(8,128)(2,1)S(1)}, u32[]{:S(2)}, u32[]{:S(2)}) collective-permute-start(bf16[8,144,128]{2,1,0:T(8,128)(2,1)S(1)} %all-to-all-done.1.kv), channel_id=1, source_target_pairs={{0,1},{1,0},{2,3},{3,2},{4,5},{5,4},{6,7},{7,6},{8,9},{9,8},{10,11... | collective-permute-start | bytes 884744 | tf_op jit(solution)/shard_map/ppermute | solution.py:350
  47.5 0.0 collective-permute-done.q1
  47.6 0.0 collective-permute-done.1.q2
  47.6 0.0 collective-permute-done.2.q3
  47.6 0.0 copy-done
  47.6 2.9 %shard_map.66 = (bf16[8,256,768]{2,1,0:T(8,128)(2,1)S(1)}, f32[8,256,512]{2,1,0:T(8,128)S(1)}, f32[8,256,128]{2,1,0:T(8,128)S(1)}, f32[8,256,128]{2,1,0:T(8,128)S(1)}) custom-call(s32[130]{0:T(256)S(1)} %pad_add_fusion.info_ref, bf16[64,1536]{1,0:T(8,128)(2,1)S(1)} %get-tuple-element.17.q0, bf16[64,1536]{1,0:T(8,128)(2,1)S(1)} %collective-permute-done.q1, ...), custom_call_target="tpu_custom_call" | custom-call | flops 6000000000 | bytes 5000000 | tf_op jit(solution)/shard_map/pallas_call | solution.py:196
  50.5 4.9 %collective-permute-done.3.kv = bf16[8,144,128]{2,1,0:T(8,128)(2,1)S(1)} collective-permute-done((bf16[8,144,128]{2,1,0:T(8,128)(2,1)S(1)}, bf16[8,144,128]{2,1,0:T(8,128)(2,1)S(1)}, u32[]{:S(2)}, u32[]{:S(2)}) %collective-permute-start.3) | collective-permute-done | bytes 294944 | tf_op jit(solution)/shard_map/ppermute | solution.py:350
  55.5 1.9 %collective-permute-start.4 = (bf16[8,144,128]{2,1,0:T(8,128)(2,1)S(1)}, bf16[8,144,128]{2,1,0:T(8,128)(2,1)S(1)}, u32[]{:S(2)}, u32[]{:S(2)}) collective-permute-start(bf16[8,144,128]{2,1,0:T(8,128)(2,1)S(1)} %collective-permute-done.3.kv), channel_id=1, source_target_pairs={{0,8},{8,0},{16,24},{24,16},{32,40},{40,32},{48,56},{56,48},{64,72... | collective-permute-start | bytes 884744 | tf_op jit(solution)/shard_map/ppermute | solution.py:352
  57.4 0.0 collective-permute-done.5.kv
  57.4 2.6 %shard_map.67 = (f32[8,256,512]{2,1,0:T(8,128)S(1)}, f32[8,256,128]{2,1,0:T(8,128)S(1)}, f32[8,256,128]{2,1,0:T(8,128)S(1)}) custom-call(s32[130]{0:T(256)S(1)} %pad_add_fusion.info_ref, bf16[8,256,768]{2,1,0:T(8,128)(2,1)S(1)} %get-tuple-element.19.q_ref, bf16[8,144,128]{2,1,0:T(8,128)(2,1)S(1)} %collective-permute-done.5.kv, ...), custom_call_target="tpu_custom_call" | custom-call | flops 2500000000 | bytes 5000000 | tf_op jit(solution)/shard_map/pallas_call | solution.py:242
  60.0 0.0 copy-start.1
  60.0 2.6 %shard_map.68 = (f32[8,256,512]{2,1,0:T(8,128)S(1)}, f32[8,256,128]{2,1,0:T(8,128)S(1)}, f32[8,256,128]{2,1,0:T(8,128)S(1)}) custom-call(s32[130]{0:T(256)S(1)} %pad_add_fusion.info_ref, bf16[8,256,768]{2,1,0:T(8,128)(2,1)S(1)} %get-tuple-element.19.q_ref, bf16[8,144,128]{2,1,0:T(8,128)(2,1)S(1)} %collective-permute-done.3.kv, ...), custom_call_target="tpu_custom_call" | custom-call | flops 2500000000 | bytes 5000000 | tf_op jit(solution)/shard_map/pallas_call | solution.py:242
  62.6 0.0 collective-permute-done.4.kv
  62.6 0.0 copy-done.1
  62.6 3.2 %shard_map.69 = bf16[4,64,1152]{2,1,0:T(8,128)(2,1)S(1)} custom-call(s32[130]{0:T(256)S(1)} %pad_add_fusion.info_ref, bf16[8,256,768]{2,1,0:T(8,128)(2,1)S(1)} %get-tuple-element.19.q_ref, bf16[8,144,128]{2,1,0:T(8,128)(2,1)S(1)} %collective-permute-done.4.kv, f32[8,256,512]{2,1,0:T(8,128)S(1)} %get-tuple-element.26.old_lat, ...), custom_call_target="tpu_custom_call" | custom-call | flops 4000000000 | bytes 5000000 | tf_op jit(solution)/shard_map/pallas_call | solution.py:300
  65.8 25.8 %all_to_all.15 = bf16[32,8,1152]{2,1,0:T(8,128)(2,1)S(1)} all-to-all(bf16[32,8,1152]{2,1,0:T(8,128)(2,1)S(1)} %bitcast.6), channel_id=1, replica_groups={{0,1,2,3,4,5,6,7,16,17,18,19,20,21,22,23,32,33,34,35,36,37,38,39,48,49,..., dimensions={0} | all-to-all | bytes 1179648 | tf_op jit(solution)/shard_map/all_to_all | solution.py:360
  91.7 1.2 %shard_map.70 = bf16[8,8192]{1,0:T(8,128)(2,1)} custom-call(bf16[4,8,8,1152]{3,2,1,0:T(8,128)(2,1)S(1)} %bitcast.5), custom_call_target="tpu_custom_call" | custom-call | flops 1000000 | bytes 800000 | tf_op jit(solution)/shard_map/pallas_call | solution.py:333
Async XLA Ops:
  1.7 20.7 %all-to-all-start = ((bf16[8,8,2176]{2,1,0:T(8,128)(2,1)}), bf16[8,8,2176]{2,1,0:T(8,128)(2,1)S(1)}, u32[]{:S(2)}, u32[]{:S(2)}) async-start(bf16[8,8,2176]{2,1,0:T(8,128)(2,1)} %shard_map.64), calls=%async_computation | async-start | bytes 557056 | tf_op jit(solution)/shard_map/all_to_all | solution.py:347
  22.4 25.2 %copy-start = (bf16[8,512,128]{2,1,0:T(8,128)(2,1)S(1)}, bf16[8,512,128]{2,1,0:T(8,128)(2,1)}, u32[]{:S(2)}) copy-start(bf16[8,512,128]{2,1,0:T(8,128)(2,1)} %w_uk.1) | copy-start | bytes 3145732
  23.7 18.5 %all-to-all-start.1 = ((bf16[8,144,128]{2,1,0:T(8,128)(2,1)}), bf16[8,144,128]{2,1,0:T(8,128)(2,1)S(1)}, u32[]{:S(2)}, u32[]{:S(2)}) async-start(bf16[8,144,128]{2,1,0:T(8,128)(2,1)} %get-tuple-element.18), calls=%async_computation.1 | async-start | bytes 589824 | tf_op jit(solution)/shard_map/all_to_all | solution.py:349
  30.8 16.7 %collective-permute-start = (bf16[64,1536]{1,0:T(8,128)(2,1)S(1)}, bf16[64,1536]{1,0:T(8,128)(2,1)S(1)}, u32[]{:S(2)}, u32[]{:S(2)}) collective-permute-start(bf16[64,1536]{1,0:T(8,128)(2,1)S(1)} %get-tuple-element.17.q0), channel_id=1, source_target_pairs={{0,16},{8,24},{16,32},{24,40},{32,48},{40,56},{48,0},{56,8},{64,80... | collective-permute-start | bytes 589832 | tf_op jit(solution)/shard_map/ppermute | solution.py:353
  34.2 13.3 %collective-permute-start.1 = (bf16[64,1536]{1,0:T(8,128)(2,1)S(1)}, bf16[64,1536]{1,0:T(8,128)(2,1)S(1)}, u32[]{:S(2)}, u32[]{:S(2)}) collective-permute-start(bf16[64,1536]{1,0:T(8,128)(2,1)S(1)} %get-tuple-element.17.q0), channel_id=1, source_target_pairs={{0,32},{8,40},{16,48},{24,56},{32,0},{40,8},{48,16},{56,24},{64,96... | collective-permute-start | bytes 589832 | tf_op jit(solution)/shard_map/ppermute | solution.py:353
  38.9 8.7 %collective-permute-start.2 = (bf16[64,1536]{1,0:T(8,128)(2,1)S(1)}, bf16[64,1536]{1,0:T(8,128)(2,1)S(1)}, u32[]{:S(2)}, u32[]{:S(2)}) collective-permute-start(bf16[64,1536]{1,0:T(8,128)(2,1)S(1)} %get-tuple-element.17.q0), channel_id=1, source_target_pairs={{0,48},{8,56},{16,0},{24,8},{32,16},{40,24},{48,32},{56,40},{64,11... | collective-permute-start | bytes 589832 | tf_op jit(solution)/shard_map/ppermute | solution.py:353
  42.2 15.2 %collective-permute-start.5 = (bf16[8,144,128]{2,1,0:T(8,128)(2,1)S(1)}, bf16[8,144,128]{2,1,0:T(8,128)(2,1)S(1)}, u32[]{:S(2)}, u32[]{:S(2)}) collective-permute-start(bf16[8,144,128]{2,1,0:T(8,128)(2,1)S(1)} %all-to-all-done.1.kv), channel_id=1, source_target_pairs={{0,8},{8,0},{16,24},{24,16},{32,40},{40,32},{48,56},{56,48},{64,72... | collective-permute-start | bytes 884744 | tf_op jit(solution)/shard_map/ppermute | solution.py:351
  44.2 11.3 %collective-permute-start.3 = (bf16[8,144,128]{2,1,0:T(8,128)(2,1)S(1)}, bf16[8,144,128]{2,1,0:T(8,128)(2,1)S(1)}, u32[]{:S(2)}, u32[]{:S(2)}) collective-permute-start(bf16[8,144,128]{2,1,0:T(8,128)(2,1)S(1)} %all-to-all-done.1.kv), channel_id=1, source_target_pairs={{0,1},{1,0},{2,3},{3,2},{4,5},{5,4},{6,7},{7,6},{8,9},{9,8},{10,11... | collective-permute-start | bytes 884744 | tf_op jit(solution)/shard_map/ppermute | solution.py:350
  55.5 7.1 %collective-permute-start.4 = (bf16[8,144,128]{2,1,0:T(8,128)(2,1)S(1)}, bf16[8,144,128]{2,1,0:T(8,128)(2,1)S(1)}, u32[]{:S(2)}, u32[]{:S(2)}) collective-permute-start(bf16[8,144,128]{2,1,0:T(8,128)(2,1)S(1)} %collective-permute-done.3.kv), channel_id=1, source_target_pairs={{0,8},{8,0},{16,24},{24,16},{32,40},{40,32},{48,56},{56,48},{64,72... | collective-permute-start | bytes 884744 | tf_op jit(solution)/shard_map/ppermute | solution.py:352
  60.0 2.6 %copy-start.1 = (bf16[8,512,128]{2,1,0:T(8,128)(2,1)S(1)}, bf16[8,512,128]{2,1,0:T(8,128)(2,1)}, u32[]{:S(2)}) copy-start(bf16[8,512,128]{2,1,0:T(8,128)(2,1)} %w_uv.1) | copy-start | bytes 3145732

commit v6 on v4

--- a/solution.py
+++ b/solution.py
@@ -28,24 +28,12 @@
 SCALE2 = DQ ** (-0.5) * LOG2E
 
 
-def ctx_of(y, x, core):
-    return ((y % NY) * NX + (x % NX)) * 2 + core
-
-
 def along_x(step):
-    return [
-        (ctx_of(y, x, c), ctx_of(y, x + step, c))
-        for y in range(NY)
-        for x in range(NX)
-        for c in range(2)
-    ]
-
-
-CORE_SWAP = [(i, i ^ 1) for i in range(NX * NY * 2)]
-XZ_GROUPS = [
-    [ctx_of(y, x, c) * NZ + z for x in range(NX) for z in range(NZ)] for y in range(NY) for c in range(2)
-]
-Y_GROUPS = [[ctx_of(y, x, c) for y in range(NY)] for x in range(NX) for c in range(2)]
+    return [(x, (x + step) % NX) for x in range(NX)]
+
+
+CORE_SWAP = [(0, 1), (1, 0)]
+CTX = ("y", "x", "core")
 
 
 def spread_kernel(q_ref, lat_ref, rope_ref, out_ref):
@@ -299,34 +287,24 @@
 
 
 def on_device(queries, latent, rope_key, w_uk, w_uv, block_order):
-    place = lax.axis_index("ctx").astype(jnp.int32).reshape(1)
+    place = lax.axis_index(CTX).astype(jnp.int32).reshape(1)
     info = jnp.concatenate([place, block_order])
     both = spread(queries, latent, rope_key)
-    both = lax.all_to_all(both, "head", split_axis=0, concat_axis=0, tiled=True).reshape(SPAN, HEADS * DQ + WIDE)
+    both = lax.all_to_all(both, "z", split_axis=0, concat_axis=0, tiled=True).reshape(SPAN, HEADS * DQ + WIDE)
     q_own, kv = pack(both)
-    kv_own = lax.all_to_all(kv, "ctx", split_axis=0, concat_axis=0, tiled=True, axis_index_groups=Y_GROUPS)
-    kv_sib = lax.ppermute(kv_own, "ctx", CORE_SWAP)
-    qs = [q_own] + [lax.ppermute(q_own, "ctx", along_x(step)) for step in range(1, NX)]
+    kv_own = lax.all_to_all(kv, "y", split_axis=0, concat_axis=0, tiled=True)
+    kv_sib = lax.ppermute(kv_own, "core", CORE_SWAP)
+    qs = [q_own] + [lax.ppermute(q_own, "x", along_x(step)) for step in range(1, NX)]
     q_all, *state = attend_own(info, qs, w_uk, kv_own)
     partial = attend_other(place, q_all, kv_sib, state, w_uv)
     rows = SPAN // NZ
     partial = partial.reshape(NX * NZ, rows, HEADS * DV + STAT)
-    parts = lax.all_to_all(
-        partial, ("ctx", "head"), split_axis=0, concat_axis=0, tiled=True, axis_index_groups=XZ_GROUPS
-    )
+    parts = lax.all_to_all(partial, ("x", "z"), split_axis=0, concat_axis=0, tiled=True)
     return merge(parts.reshape(NX, NZ, rows, HEADS * DV + STAT))
 
 
 def solution(mesh):
-    in_specs = (
-        P(("ctx", "head"), None),
-        P(("ctx", "head"), None),
-        P(("ctx", "head"), None),
-        P("head", None, None),
-        P("head", None, None),
-        P(),
-    )
-    out_specs = P(("ctx", "head"), None)
-    return jax.shard_map(
-        on_device, mesh=mesh, in_specs=in_specs, out_specs=out_specs, check_vma=False
-    )
+    fine = jax.sharding.Mesh(mesh.devices.reshape(NY, NX, 2, NZ), ("y", "x", "core", "z"))
+    tokens = P(("y", "x", "core", "z"), None)
+    in_specs = (tokens, tokens, tokens, P("z", None, None), P("z", None, None), P())
+    return jax.shard_map(on_device, mesh=fine, in_specs=in_specs, out_specs=tokens, check_vma=False)

time: 86.3 us -> 86.2 us (level)
  no operation moved by 1% of the time
where the time goes in v6:
time: 86.2 us; the launch traced here: 85.8 us
  blocking collectives  48.3 us (56%)
  starting transfers between devices  20.4 us (24%)
  Pallas kernels  12.2 us (14%)
  waiting for transfers between devices  4.8 us (6%)
    all_to_all x1, blocking collectives, on_device(): lax.all_to_all(partial, ('x', 'z'), split_axis=0, concat_axis=0, tiled=True)  27.6 us
    all_to_all x1, blocking collectives, on_device(): lax.all_to_all(both, 'z', split_axis=0, concat_axis=0, tiled=True)  20.7 us
    ppermute x3, starting transfers between devices, on_device(): lax.ppermute(q_own, 'x', along_x(step))  11.4 us
    all_to_all x1, starting transfers between devices, on_device(): kv_own = lax.all_to_all(kv, 'y', split_axis=0, concat_axis=0, tiled=True)  7.1 us
    all_to_all x1, waiting for transfers between devices, on_device(): kv_own = lax.all_to_all(kv, 'y', split_axis=0, concat_axis=0, tiled=True)  4.79 us
    pallas_call x1, Pallas kernels, attend_own(): pl.pallas_call(own_kernel, out_shape=[jax.ShapeDtypeStruct((HEADS, rows,...  4.28 us
    pallas_call x1, Pallas kernels, attend_other(): pl.pallas_call(other_kernel, out_shape=jax.ShapeDtypeStruct((NX, SPAN, HE...  4.07 us
    ppermute x1, starting transfers between devices, on_device(): kv_sib = lax.ppermute(kv_own, 'core', CORE_SWAP)  1.91 us
  transfers between devices with their start and end apart: 5, of which 1 were waited for; matrix products, arithmetic and copies ran while one was open for 0% of the time, Pallas kernels for 5%

profile of v6, /device:TPU:64, one launch (start us, length us, event | category | flops | bytes accessed | tf_op | source)
XLA Modules:
  0.0 85.8 jit_solution(10514003006079024513)
XLA Ops:
  0.0 1.7 %shard_map.64 = bf16[8,8,2176]{2,1,0:T(8,128)(2,1)} custom-call(bf16[8,12288]{1,0:T(8,128)(2,1)} %q_ref.1, bf16[8,512]{1,0:T(8,128)(2,1)} %lat_ref.1, bf16[8,64]{1,0:T(8,128)(2,1)} %rope_ref.1), custom_call_target="tpu_custom_call" | custom-call | flops 1000000 | bytes 500000 | tf_op jit(solution)/shard_map/pallas_call | solution.py:50
  1.7 20.7 %all_to_all.15 = bf16[8,8,2176]{2,1,0:T(8,128)(2,1)S(1)} all-to-all(bf16[8,8,2176]{2,1,0:T(8,128)(2,1)} %shard_map.64), channel_id=1, replica_groups=mesh['y'=8,'x'=4,'core'=2,'z'=8] {'z'}, dimensions={0} | all-to-all | bytes 557056 | tf_op jit(solution)/shard_map/all_to_all | solution.py:293
  22.4 0.0 copy-start.2
  22.4 0.0 copy-start
  22.4 0.9 %shard_map.65 = (bf16[64,1536]{1,0:T(8,128)(2,1)S(1)}, bf16[8,288,128]{2,1,0:T(8,128)(2,1)}) custom-call(bf16[64,2176]{1,0:T(8,128)(2,1)S(1)} %bitcast.6), custom_call_target="tpu_custom_call" | custom-call | flops 4000000000 | bytes 1000000 | tf_op jit(solution)/shard_map/pallas_call | solution.py:73
  23.3 7.1 %all-to-all-start.1 = ((bf16[8,288,128]{2,1,0:T(8,128)(2,1)}), bf16[8,288,128]{2,1,0:T(8,128)(2,1)S(1)}, u32[]{:S(2)}, u32[]{:S(2)}) async-start(bf16[8,288,128]{2,1,0:T(8,128)(2,1)} %get-tuple-element.12), calls=%async_computation.1 | async-start | bytes 1179648 | tf_op jit(solution)/shard_map/all_to_all | solution.py:295
  30.4 3.4 %collective-permute-start = (bf16[64,1536]{1,0:T(8,128)(2,1)S(1)}, bf16[64,1536]{1,0:T(8,128)(2,1)S(1)}, u32[]{:S(2)}, u32[]{:S(2)}) collective-permute-start(bf16[64,1536]{1,0:T(8,128)(2,1)S(1)} %get-tuple-element.11.q0), channel_id=1, source_target_pairs={{0,16},{16,32},{32,48},{48,0},{1,17},{17,33},{33,49},{49,1},{2,18}... | collective-permute-start | bytes 589832 | tf_op jit(solution)/shard_map/ppermute | solution.py:297
  33.8 4.6 %collective-permute-start.1 = (bf16[64,1536]{1,0:T(8,128)(2,1)S(1)}, bf16[64,1536]{1,0:T(8,128)(2,1)S(1)}, u32[]{:S(2)}, u32[]{:S(2)}) collective-permute-start(bf16[64,1536]{1,0:T(8,128)(2,1)S(1)} %get-tuple-element.11.q0), channel_id=1, source_target_pairs={{0,32},{16,48},{32,0},{48,16},{1,33},{17,49},{33,1},{49,17},{2,34}... | collective-permute-start | bytes 589832 | tf_op jit(solution)/shard_map/ppermute | solution.py:297
  38.5 3.3 %collective-permute-start.2 = (bf16[64,1536]{1,0:T(8,128)(2,1)S(1)}, bf16[64,1536]{1,0:T(8,128)(2,1)S(1)}, u32[]{:S(2)}, u32[]{:S(2)}) collective-permute-start(bf16[64,1536]{1,0:T(8,128)(2,1)S(1)} %get-tuple-element.11.q0), channel_id=1, source_target_pairs={{0,48},{16,0},{32,16},{48,32},{1,49},{17,1},{33,17},{49,33},{2,50}... | collective-permute-start | bytes 589832 | tf_op jit(solution)/shard_map/ppermute | solution.py:297
  41.8 4.8 %all-to-all-done.1.kv = bf16[8,288,128]{2,1,0:T(8,128)(2,1)S(1)} async-done(((bf16[8,288,128]{2,1,0:T(8,128)(2,1)}), bf16[8,288,128]{2,1,0:T(8,128)(2,1)S(1)}, u32[]{:S(2)}, u32[]{:S(2)}) %all-to-all-start.1) | async-done | bytes 589856 | tf_op jit(solution)/shard_map/all_to_all | solution.py:295
  46.6 1.9 %collective-permute-start.3 = (bf16[8,288,128]{2,1,0:T(8,128)(2,1)S(1)}, bf16[8,288,128]{2,1,0:T(8,128)(2,1)S(1)}, u32[]{:S(2)}, u32[]{:S(2)}) collective-permute-start(bf16[8,288,128]{2,1,0:T(8,128)(2,1)S(1)} %all-to-all-done.1.kv), channel_id=1, source_target_pairs={{0,8},{8,0},{1,9},{9,1},{2,10},{10,2},{3,11},{11,3},{4,12},{12,4},... | collective-permute-start | bytes 1769480 | tf_op jit(solution)/shard_map/ppermute | solution.py:296
  48.5 0.0 copy-done.2
  48.5 0.1 pad_add_fusion.info_ref
  48.6 0.0 copy-start.1
  48.6 0.0 collective-permute-done.q1
  48.6 0.0 collective-permute-done.1.q2
  48.6 0.0 collective-permute-done.2.q3
  48.6 0.0 copy-done
  48.7 4.3 %shard_map.66 = (bf16[8,256,768]{2,1,0:T(8,128)(2,1)S(1)}, f32[8,256,512]{2,1,0:T(8,128)S(1)}, f32[8,256,128]{2,1,0:T(8,128)S(1)}, f32[8,256,128]{2,1,0:T(8,128)S(1)}) custom-call(s32[129]{0:T(256)S(1)} %pad_add_fusion.info_ref, bf16[64,1536]{1,0:T(8,128)(2,1)S(1)} %get-tuple-element.11.q0, bf16[64,1536]{1,0:T(8,128)(2,1)S(1)} %collective-permute-done.q1, ...), custom_call_target="tpu_custom_call" | custom-call | flops 6000000000 | bytes 5000000 | tf_op jit(solution)/shard_map/pallas_call | solution.py:180
  52.9 0.0 collective-permute-done.3.kv
  53.0 0.0 copy-done.1
  53.0 4.1 %shard_map.67 = bf16[4,64,1152]{2,1,0:T(8,128)(2,1)S(1)} custom-call(s32[1]{0:T(128)} %bitcast.place_ref, bf16[8,256,768]{2,1,0:T(8,128)(2,1)S(1)} %get-tuple-element.13.q_ref, bf16[8,288,128]{2,1,0:T(8,128)(2,1)S(1)} %collective-permute-done.3.kv, f32[8,256,512]{2,1,0:T(8,128)S(1)} %get-tuple-element.14.lat_ref, ...), custom_call_target="tpu_custom_call" | custom-call | flops 4000000000 | bytes 5000000 | tf_op jit(solution)/shard_map/pallas_call | solution.py:246
  57.0 27.6 %all_to_all.16 = bf16[32,8,1152]{2,1,0:T(8,128)(2,1)S(1)} all-to-all(bf16[32,8,1152]{2,1,0:T(8,128)(2,1)S(1)} %bitcast.5), channel_id=1, replica_groups=mesh['y'=8,'x'=4,'core'=2,'z'=8] {'x','z'}, dimensions={0} | all-to-all | bytes 1179648 | tf_op jit(solution)/shard_map/all_to_all | solution.py:302
  84.6 1.2 %shard_map.68 = bf16[8,8192]{1,0:T(8,128)(2,1)} custom-call(bf16[4,8,8,1152]{3,2,1,0:T(8,128)(2,1)S(1)} %bitcast.4), custom_call_target="tpu_custom_call" | custom-call | flops 1000000 | bytes 800000 | tf_op jit(solution)/shard_map/pallas_call | solution.py:279
Async XLA Ops:
  22.4 26.1 %copy-start.2 = (s32[128]{0:T(128)S(1)}, s32[128]{0:T(128)}, u32[]{:S(2)}) copy-start(s32[128]{0:T(128)} %param.11) | copy-start | bytes 1540
  22.4 26.2 %copy-start = (bf16[8,512,128]{2,1,0:T(8,128)(2,1)S(1)}, bf16[8,512,128]{2,1,0:T(8,128)(2,1)}, u32[]{:S(2)}) copy-start(bf16[8,512,128]{2,1,0:T(8,128)(2,1)} %w_uk.1) | copy-start | bytes 3145732
  23.3 23.3 %all-to-all-start.1 = ((bf16[8,288,128]{2,1,0:T(8,128)(2,1)}), bf16[8,288,128]{2,1,0:T(8,128)(2,1)S(1)}, u32[]{:S(2)}, u32[]{:S(2)}) async-start(bf16[8,288,128]{2,1,0:T(8,128)(2,1)} %get-tuple-element.12), calls=%async_computation.1 | async-start | bytes 1179648 | tf_op jit(solution)/shard_map/all_to_all | solution.py:295
  30.4 18.2 %collective-permute-start = (bf16[64,1536]{1,0:T(8,128)(2,1)S(1)}, bf16[64,1536]{1,0:T(8,128)(2,1)S(1)}, u32[]{:S(2)}, u32[]{:S(2)}) collective-permute-start(bf16[64,1536]{1,0:T(8,128)(2,1)S(1)} %get-tuple-element.11.q0), channel_id=1, source_target_pairs={{0,16},{16,32},{32,48},{48,0},{1,17},{17,33},{33,49},{49,1},{2,18}... | collective-permute-start | bytes 589832 | tf_op jit(solution)/shard_map/ppermute | solution.py:297
  33.8 14.8 %collective-permute-start.1 = (bf16[64,1536]{1,0:T(8,128)(2,1)S(1)}, bf16[64,1536]{1,0:T(8,128)(2,1)S(1)}, u32[]{:S(2)}, u32[]{:S(2)}) collective-permute-start(bf16[64,1536]{1,0:T(8,128)(2,1)S(1)} %get-tuple-element.11.q0), channel_id=1, source_target_pairs={{0,32},{16,48},{32,0},{48,16},{1,33},{17,49},{33,1},{49,17},{2,34}... | collective-permute-start | bytes 589832 | tf_op jit(solution)/shard_map/ppermute | solution.py:297
  38.5 10.2 %collective-permute-start.2 = (bf16[64,1536]{1,0:T(8,128)(2,1)S(1)}, bf16[64,1536]{1,0:T(8,128)(2,1)S(1)}, u32[]{:S(2)}, u32[]{:S(2)}) collective-permute-start(bf16[64,1536]{1,0:T(8,128)(2,1)S(1)} %get-tuple-element.11.q0), channel_id=1, source_target_pairs={{0,48},{16,0},{32,16},{48,32},{1,49},{17,1},{33,17},{49,33},{2,50}... | collective-permute-start | bytes 589832 | tf_op jit(solution)/shard_map/ppermute | solution.py:297
  46.6 6.3 %collective-permute-start.3 = (bf16[8,288,128]{2,1,0:T(8,128)(2,1)S(1)}, bf16[8,288,128]{2,1,0:T(8,128)(2,1)S(1)}, u32[]{:S(2)}, u32[]{:S(2)}) collective-permute-start(bf16[8,288,128]{2,1,0:T(8,128)(2,1)S(1)} %all-to-all-done.1.kv), channel_id=1, source_target_pairs={{0,8},{8,0},{1,9},{9,1},{2,10},{10,2},{3,11},{11,3},{4,12},{12,4},... | collective-permute-start | bytes 1769480 | tf_op jit(solution)/shard_map/ppermute | solution.py:296
  48.6 4.3 %copy-start.1 = (bf16[8,512,128]{2,1,0:T(8,128)(2,1)S(1)}, bf16[8,512,128]{2,1,0:T(8,128)(2,1)}, u32[]{:S(2)}) copy-start(bf16[8,512,128]{2,1,0:T(8,128)(2,1)} %w_uv.1) | copy-start | bytes 3145732

commit v7 on v6

--- a/solution.py
+++ b/solution.py
@@ -38,7 +38,7 @@
 
 def spread_kernel(q_ref, lat_ref, rope_ref, out_ref):
     end = HEADS * DQ
-    for z in range(NZ):
+    for z in range(out_ref.shape[0]):
         out_ref[z, :, :end] = q_ref[:, z * end : (z + 1) * end]
         out_ref[z, :, end : end + DL] = lat_ref[...]
         out_ref[z, :, end + DL : end + DL + DR] = rope_ref[...]
@@ -46,12 +46,19 @@
 
 
 def spread(queries, latent, rope_key):
-    vmem = pl.BlockSpec(memory_space=pltpu.VMEM)
+    tokens = SPAN // NZ
+    steps = 4
+    each = NZ // steps
     return pl.pallas_call(
         spread_kernel,
-        out_shape=jax.ShapeDtypeStruct((NZ, SPAN // NZ, HEADS * DQ + WIDE), jnp.bfloat16),
-        in_specs=[vmem] * 3,
-        out_specs=vmem,
+        grid=(steps,),
+        out_shape=jax.ShapeDtypeStruct((NZ, tokens, HEADS * DQ + WIDE), jnp.bfloat16),
+        in_specs=[
+            pl.BlockSpec((tokens, each * HEADS * DQ), lambda i: (0, i)),
+            pl.BlockSpec((tokens, DL), lambda i: (0, 0)),
+            pl.BlockSpec((tokens, DR), lambda i: (0, 0)),
+        ],
+        out_specs=pl.BlockSpec((each, tokens, HEADS * DQ + WIDE), lambda i: (i, 0, 0)),
         compiler_params=pltpu.CompilerParams(vmem_limit_bytes=60 * 1024 * 1024),
         cost_estimate=pl.CostEstimate(flops=1_000_000, bytes_accessed=500_000, transcendentals=0),
     )(queries, latent, rope_key)
@@ -102,9 +109,26 @@
     keys[:, WIDE:] = jnp.where(ones, 1.0, 0.0).astype(jnp.bfloat16)
 
 
-def pair_scores(q_ref, keys, p):
-    q = q_ref[2 * p : 2 * p + 2].reshape(2 * NX * SPAN, WIDE + EXTRA)
+def pair_scores(q_ref, floor, keys, p):
+    rows = NX * SPAN
+    q = jnp.concatenate(
+        [q_ref[2 * p : 2 * p + 2].reshape(2 * rows, WIDE), jnp.concatenate([floor, floor], axis=0)], axis=1
+    )
     return lax.dot_general(q, keys[...], (((1,), (1,)), ((), ())), preferred_element_type=jnp.float32)
+
+
+def pair_values(keys, w_uv, p):
+    w = jnp.concatenate([w_uv[2 * p], w_uv[2 * p + 1]], axis=1)
+    return jnp.dot(keys[:, :DL], w, preferred_element_type=jnp.float32).astype(jnp.bfloat16)
+
+
+def weigh(weight, values):
+    rows = NX * SPAN
+    weight = weight.astype(jnp.bfloat16)
+    return [
+        jnp.dot(weight[i * rows : (i + 1) * rows], values[:, i * DV : (i + 1) * DV], preferred_element_type=jnp.float32)
+        for i in range(2)
+    ]
 
 
 def wide(value, count):
@@ -136,10 +160,11 @@
     return jnp.concatenate(floors, axis=0).astype(jnp.bfloat16)
 
 
-def own_kernel(info_ref, q0, q1, q2, q3, w_uk, kv, q_ref, lat_ref, top_ref, total_ref, keys):
+def own_kernel(info_ref, q0, q1, q2, q3, w_uk, w_uv, kv, q_ref, floor_ref, sum_ref, top_ref, total_ref, keys):
     y = info_ref[0] // (2 * NX)
     rows = NX * SPAN
     floor = floors_of(info_ref)
+    floor_ref[...] = floor
     none = jnp.zeros((rows, WIDE - DL - DR), jnp.bfloat16)
 
     def fill_queries(h):
@@ -151,59 +176,63 @@
         q_ref[h, :, :DL] = q_lat.astype(jnp.bfloat16)
         q_ref[h, :, DL : DL + DR] = q[:, DN:]
         q_ref[h, :, DL + DR : WIDE] = none
-        q_ref[h, :, WIDE:] = floor
 
     fill_queries(0)
     fill_queries(1)
     fill_keys(keys, kv, 0, 2 * y)
-    ahead = pair_scores(q_ref, keys, 0)
+    ahead = pair_scores(q_ref, floor, keys, 0)
     for p in range(HEADS // 2):
         s = ahead
+        values = pair_values(keys, w_uv, p)
         if p + 1 < HEADS // 2:
             fill_queries(2 * p + 2)
             fill_queries(2 * p + 3)
-            ahead = pair_scores(q_ref, keys, p + 1)
+            ahead = pair_scores(q_ref, floor, keys, p + 1)
         top = jnp.max(s, axis=1, keepdims=True)
         weight = jnp.exp2((s - top) * SCALE2)
         total = jnp.sum(weight, axis=1, keepdims=True)
-        lat = jnp.dot(weight.astype(jnp.bfloat16), keys[:, :DL], preferred_element_type=jnp.float32)
+        sums = weigh(weight, values)
+        for i in range(2):
+            sum_ref[2 * p + i] = sums[i]
         pair = slice(2 * p, 2 * p + 2)
-        lat_ref[pair] = lat.reshape(2, rows, DL)
         top_ref[pair] = jnp.broadcast_to(top, (2 * rows, STAT)).reshape(2, rows, STAT)
         total_ref[pair] = jnp.broadcast_to(total, (2 * rows, STAT)).reshape(2, rows, STAT)
 
 
-def attend_own(info, qs, w_uk, kv):
+def attend_own(info, qs, w_uk, w_uv, kv):
     vmem = pl.BlockSpec(memory_space=pltpu.VMEM)
     smem = pl.BlockSpec(memory_space=pltpu.SMEM)
     rows = NX * SPAN
     return pl.pallas_call(
         own_kernel,
         out_shape=[
-            jax.ShapeDtypeStruct((HEADS, rows, WIDE + EXTRA), jnp.bfloat16),
-            jax.ShapeDtypeStruct((HEADS, rows, DL), jnp.float32),
+            jax.ShapeDtypeStruct((HEADS, rows, WIDE), jnp.bfloat16),
+            jax.ShapeDtypeStruct((rows, EXTRA), jnp.bfloat16),
+            jax.ShapeDtypeStruct((HEADS, rows, DV), jnp.float32),
             jax.ShapeDtypeStruct((HEADS, rows, STAT), jnp.float32),
             jax.ShapeDtypeStruct((HEADS, rows, STAT), jnp.float32),
         ],
-        in_specs=[smem] + [vmem] * 6,
-        out_specs=[vmem] * 4,
+        in_specs=[smem] + [vmem] * 7,
+        out_specs=[vmem] * 5,
         scratch_shapes=[pltpu.VMEM((NY * SPAN, WIDE + EXTRA), jnp.bfloat16)],
         compiler_params=pltpu.CompilerParams(vmem_limit_bytes=20 * 1024 * 1024),
         cost_estimate=pl.CostEstimate(flops=6_000_000_000, bytes_accessed=5_000_000, transcendentals=1_000_000),
-    )(info, *qs, w_uk, kv)
-
-
-def other_kernel(place_ref, q_ref, kv, lat_ref, top_ref, total_ref, w_uv, out_ref, keys):
+    )(info, *qs, w_uk, w_uv, kv)
+
+
+def other_kernel(place_ref, q_ref, floor_ref, kv, sum_ref, top_ref, total_ref, w_uv, out_ref, keys):
     x = (place_ref[0] // 2) % NX
     rows = NX * SPAN
+    floor = floor_ref[...]
     fill_keys(keys, kv, NY * SPAN // HALF, None)
     lanes = lax.broadcasted_iota(jnp.int32, (rows, STAT), 1)
     level = jnp.zeros((rows, STAT), jnp.float32)
-    ahead = pair_scores(q_ref, keys, 0)
+    ahead = pair_scores(q_ref, floor, keys, 0)
     for p in range(HEADS // 2):
         s = ahead
+        values = pair_values(keys, w_uv, p)
         if p + 1 < HEADS // 2:
-            ahead = pair_scores(q_ref, keys, p + 1)
+            ahead = pair_scores(q_ref, floor, keys, p + 1)
         pair = slice(2 * p, 2 * p + 2)
         old_top = top_ref[pair].reshape(2 * rows, STAT)
         old_total = total_ref[pair].reshape(2 * rows, STAT)
@@ -211,19 +240,17 @@
         shrink = jnp.exp2((old_top - top) * SCALE2)
         weight = jnp.exp2((s - wide(top, NY * SPAN // STAT)) * SCALE2)
         total = old_total * shrink + jnp.sum(weight, axis=1, keepdims=True)
-        lat = jnp.dot(weight.astype(jnp.bfloat16), keys[:, :DL], preferred_element_type=jnp.float32)
+        sums = weigh(weight, values)
         share = 1.0 / total
-        old_lat = lat_ref[pair].reshape(2 * rows, DL)
-        o_lat = (lat * wide(share, DL // STAT) + old_lat * wide(shrink * share, DL // STAT)).astype(jnp.bfloat16)
         here = top * SCALE2 + jnp.log2(total)
         for i in range(2):
             h = 2 * p + i
-            proj = jnp.dot(o_lat[i * rows : (i + 1) * rows], w_uv[h], preferred_element_type=jnp.float32)
-            proj = proj.astype(jnp.bfloat16)
+            mine = slice(i * rows, (i + 1) * rows)
+            value = ((sums[i] + sum_ref[h] * shrink[mine]) * share[mine]).astype(jnp.bfloat16)
             for step in range(NX):
                 to = (x + NX - step) % NX
-                out_ref[to, :, h * DV : (h + 1) * DV] = proj[step * SPAN : (step + 1) * SPAN]
-            level = jnp.where(lanes % HEADS == h, here[i * rows : (i + 1) * rows], level)
+                out_ref[to, :, h * DV : (h + 1) * DV] = value[step * SPAN : (step + 1) * SPAN]
+            level = jnp.where(lanes % HEADS == h, here[mine], level)
     high = level.astype(jnp.bfloat16)
     rest = level - high.astype(jnp.float32)
     middle = rest.astype(jnp.bfloat16)
@@ -239,19 +266,19 @@
         out_ref[to, :, HEADS * DV :] = packed[step * SPAN : (step + 1) * SPAN]
 
 
-def attend_other(place, q_all, kv, state, w_uv):
+def attend_other(place, q_all, floor, kv, state, w_uv):
     vmem = pl.BlockSpec(memory_space=pltpu.VMEM)
     smem = pl.BlockSpec(memory_space=pltpu.SMEM)
     rows = NX * SPAN
     return pl.pallas_call(
         other_kernel,
         out_shape=jax.ShapeDtypeStruct((NX, SPAN, HEADS * DV + STAT), jnp.bfloat16),
-        in_specs=[smem] + [vmem] * 6,
+        in_specs=[smem] + [vmem] * 7,
         out_specs=vmem,
         scratch_shapes=[pltpu.VMEM((NY * SPAN, WIDE + EXTRA), jnp.bfloat16)],
         compiler_params=pltpu.CompilerParams(vmem_limit_bytes=20 * 1024 * 1024),
         cost_estimate=pl.CostEstimate(flops=4_000_000_000, bytes_accessed=5_000_000, transcendentals=1_000_000),
-    )(place, q_all, kv, *state, w_uv)
+    )(place, q_all, floor, kv, *state, w_uv)
 
 
 def merge_kernel(p_ref, out_ref):
@@ -295,8 +322,8 @@
     kv_own = lax.all_to_all(kv, "y", split_axis=0, concat_axis=0, tiled=True)
     kv_sib = lax.ppermute(kv_own, "core", CORE_SWAP)
     qs = [q_own] + [lax.ppermute(q_own, "x", along_x(step)) for step in range(1, NX)]
-    q_all, *state = attend_own(info, qs, w_uk, kv_own)
-    partial = attend_other(place, q_all, kv_sib, state, w_uv)
+    q_all, floor, *state = attend_own(info, qs, w_uk, w_uv, kv_own)
+    partial = attend_other(place, q_all, floor, kv_sib, state, w_uv)
     rows = SPAN // NZ
     partial = partial.reshape(NX * NZ, rows, HEADS * DV + STAT)
     parts = lax.all_to_all(partial, ("x", "z"), split_axis=0, concat_axis=0, tiled=True)

time: 86.2 us -> 87.4 us (1.014)
  Pallas kernels: 12.2 us -> 13.2 us
    pallas_call x1, Pallas kernels: 1.68 us -> 2.86 us  [spread(): pl.pallas_call(spread_kernel, grid=(steps,), out_shape=jax.ShapeDtypeStru...]
where the time goes in v7:
time: 87.4 us; the launch traced here: 86.8 us
  blocking collectives  48.3 us (55%)
  starting transfers between devices  20.4 us (23%)
  Pallas kernels  13.2 us (15%)
  waiting for transfers between devices  4.8 us (5%)
    all_to_all x1, blocking collectives, on_device(): lax.all_to_all(partial, ('x', 'z'), split_axis=0, concat_axis=0, tiled=True)  27.6 us
    all_to_all x1, blocking collectives, on_device(): lax.all_to_all(both, 'z', split_axis=0, concat_axis=0, tiled=True)  20.7 us
    ppermute x3, starting transfers between devices, on_device(): lax.ppermute(q_own, 'x', along_x(step))  11.4 us
    all_to_all x1, starting transfers between devices, on_device(): kv_own = lax.all_to_all(kv, 'y', split_axis=0, concat_axis=0, tiled=True)  7.1 us
    all_to_all x1, waiting for transfers between devices, on_device(): kv_own = lax.all_to_all(kv, 'y', split_axis=0, concat_axis=0, tiled=True)  4.79 us
    pallas_call x1, Pallas kernels, attend_own(): pl.pallas_call(own_kernel, out_shape=[jax.ShapeDtypeStruct((HEADS, rows,...  4.59 us
    pallas_call x1, Pallas kernels, attend_other(): pl.pallas_call(other_kernel, out_shape=jax.ShapeDtypeStruct((NX, SPAN, HE...  3.57 us
    pallas_call x1, Pallas kernels, spread(): pl.pallas_call(spread_kernel, grid=(steps,), out_shape=jax.ShapeDtypeStru...  2.86 us
  transfers between devices with their start and end apart: 5, of which 1 were waited for; matrix products, arithmetic and copies ran while one was open for 0% of the time, Pallas kernels for 5%

profile of v7, /device:TPU:64, one launch (start us, length us, event | category | flops | bytes accessed | tf_op | source)
XLA Modules:
  0.0 86.8 jit_solution(11690628752086723800)
XLA Ops:
  0.0 2.9 %shard_map.64 = bf16[8,8,2176]{2,1,0:T(8,128)(2,1)} custom-call(bf16[8,12288]{1,0:T(8,128)(2,1)} %q_ref.1, bf16[8,512]{1,0:T(8,128)(2,1)} %lat_ref.1, bf16[8,64]{1,0:T(8,128)(2,1)} %rope_ref.1), custom_call_target="tpu_custom_call" | custom-call | flops 1000000 | bytes 500000 | tf_op jit(solution)/shard_map/pallas_call | solution.py:52
  2.9 20.7 %all_to_all.15 = bf16[8,8,2176]{2,1,0:T(8,128)(2,1)S(1)} all-to-all(bf16[8,8,2176]{2,1,0:T(8,128)(2,1)} %shard_map.64), channel_id=1, replica_groups=mesh['y'=8,'x'=4,'core'=2,'z'=8] {'z'}, dimensions={0} | all-to-all | bytes 557056 | tf_op jit(solution)/shard_map/all_to_all | solution.py:320
  23.6 0.0 copy-start.2
  23.6 0.0 copy-start
  23.6 0.0 copy-start.1
  23.6 0.9 %shard_map.65 = (bf16[64,1536]{1,0:T(8,128)(2,1)S(1)}, bf16[8,288,128]{2,1,0:T(8,128)(2,1)}) custom-call(bf16[64,2176]{1,0:T(8,128)(2,1)S(1)} %bitcast.6), custom_call_target="tpu_custom_call" | custom-call | flops 4000000000 | bytes 1000000 | tf_op jit(solution)/shard_map/pallas_call | solution.py:80
  24.5 7.1 %all-to-all-start.1 = ((bf16[8,288,128]{2,1,0:T(8,128)(2,1)}), bf16[8,288,128]{2,1,0:T(8,128)(2,1)S(1)}, u32[]{:S(2)}, u32[]{:S(2)}) async-start(bf16[8,288,128]{2,1,0:T(8,128)(2,1)} %get-tuple-element.13), calls=%async_computation.1 | async-start | bytes 1179648 | tf_op jit(solution)/shard_map/all_to_all | solution.py:322
  31.6 3.4 %collective-permute-start = (bf16[64,1536]{1,0:T(8,128)(2,1)S(1)}, bf16[64,1536]{1,0:T(8,128)(2,1)S(1)}, u32[]{:S(2)}, u32[]{:S(2)}) collective-permute-start(bf16[64,1536]{1,0:T(8,128)(2,1)S(1)} %get-tuple-element.12.q0), channel_id=1, source_target_pairs={{0,16},{16,32},{32,48},{48,0},{1,17},{17,33},{33,49},{49,1},{2,18}... | collective-permute-start | bytes 589832 | tf_op jit(solution)/shard_map/ppermute | solution.py:324
  35.0 4.6 %collective-permute-start.1 = (bf16[64,1536]{1,0:T(8,128)(2,1)S(1)}, bf16[64,1536]{1,0:T(8,128)(2,1)S(1)}, u32[]{:S(2)}, u32[]{:S(2)}) collective-permute-start(bf16[64,1536]{1,0:T(8,128)(2,1)S(1)} %get-tuple-element.12.q0), channel_id=1, source_target_pairs={{0,32},{16,48},{32,0},{48,16},{1,33},{17,49},{33,1},{49,17},{2,34}... | collective-permute-start | bytes 589832 | tf_op jit(solution)/shard_map/ppermute | solution.py:324
  39.7 3.3 %collective-permute-start.2 = (bf16[64,1536]{1,0:T(8,128)(2,1)S(1)}, bf16[64,1536]{1,0:T(8,128)(2,1)S(1)}, u32[]{:S(2)}, u32[]{:S(2)}) collective-permute-start(bf16[64,1536]{1,0:T(8,128)(2,1)S(1)} %get-tuple-element.12.q0), channel_id=1, source_target_pairs={{0,48},{16,0},{32,16},{48,32},{1,49},{17,1},{33,17},{49,33},{2,50}... | collective-permute-start | bytes 589832 | tf_op jit(solution)/shard_map/ppermute | solution.py:324
  43.0 4.8 %all-to-all-done.1.kv = bf16[8,288,128]{2,1,0:T(8,128)(2,1)S(1)} async-done(((bf16[8,288,128]{2,1,0:T(8,128)(2,1)}), bf16[8,288,128]{2,1,0:T(8,128)(2,1)S(1)}, u32[]{:S(2)}, u32[]{:S(2)}) %all-to-all-start.1) | async-done | bytes 589856 | tf_op jit(solution)/shard_map/all_to_all | solution.py:322
  47.8 1.9 %collective-permute-start.3 = (bf16[8,288,128]{2,1,0:T(8,128)(2,1)S(1)}, bf16[8,288,128]{2,1,0:T(8,128)(2,1)S(1)}, u32[]{:S(2)}, u32[]{:S(2)}) collective-permute-start(bf16[8,288,128]{2,1,0:T(8,128)(2,1)S(1)} %all-to-all-done.1.kv), channel_id=1, source_target_pairs={{0,8},{8,0},{1,9},{9,1},{2,10},{10,2},{3,11},{11,3},{4,12},{12,4},... | collective-permute-start | bytes 1769480 | tf_op jit(solution)/shard_map/ppermute | solution.py:323
  49.7 0.0 copy-done.2
  49.7 0.1 pad_add_fusion.info_ref
  49.8 0.0 collective-permute-done.q1
  49.8 0.0 collective-permute-done.1.q2
  49.8 0.0 collective-permute-done.2.q3
  49.8 0.0 copy-done
  49.8 0.0 copy-done.1
  49.8 4.6 %shard_map.66 = (bf16[8,256,640]{2,1,0:T(8,128)(2,1)S(1)}, bf16[256,128]{1,0:T(8,128)(2,1)S(1)}, f32[8,256,128]{2,1,0:T(8,128)S(1)}, f32[8,256,128]{2,1,0:T(8,128)S(1)}, f32[8,256,128]{2,1,0:T(8,128)S(1)}) custom-call(s32[129]{0:T(256)S(1)} %pad_add_fusion.info_ref, bf16[64,1536]{1,0:T(8,128)(2,1)S(1)} %get-tuple-element.12.q0, ...), custom_call_target="tpu_custom_call" | custom-call | flops 6000000000 | bytes 5000000 | tf_op jit(solution)/shard_map/pallas_call | solution.py:206
  54.4 0.0 collective-permute-done.3.kv
  54.4 3.6 %shard_map.67 = bf16[4,64,1152]{2,1,0:T(8,128)(2,1)S(1)} custom-call(s32[1]{0:T(128)} %bitcast.place_ref, bf16[8,256,640]{2,1,0:T(8,128)(2,1)S(1)} %get-tuple-element.14.q_ref, bf16[256,128]{1,0:T(8,128)(2,1)S(1)} %get-tuple-element.15.floor_ref, bf16[8,288,128]{2,1,0:T(8,128)(2,1)S(1)} %collective-permute-done.3.kv, ...), custom_call_target="tpu_custom_call" | custom-call | flops 4000000000 | bytes 5000000 | tf_op jit(solution)/shard_map/pallas_call | solution.py:273
  58.0 27.6 %all_to_all.16 = bf16[32,8,1152]{2,1,0:T(8,128)(2,1)S(1)} all-to-all(bf16[32,8,1152]{2,1,0:T(8,128)(2,1)S(1)} %bitcast.5), channel_id=1, replica_groups=mesh['y'=8,'x'=4,'core'=2,'z'=8] {'x','z'}, dimensions={0} | all-to-all | bytes 1179648 | tf_op jit(solution)/shard_map/all_to_all | solution.py:329
  85.6 1.2 %shard_map.68 = bf16[8,8192]{1,0:T(8,128)(2,1)} custom-call(bf16[4,8,8,1152]{3,2,1,0:T(8,128)(2,1)S(1)} %bitcast.4), custom_call_target="tpu_custom_call" | custom-call | flops 1000000 | bytes 800000 | tf_op jit(solution)/shard_map/pallas_call | solution.py:306
Async XLA Ops:
  23.6 26.1 %copy-start.2 = (s32[128]{0:T(128)S(1)}, s32[128]{0:T(128)}, u32[]{:S(2)}) copy-start(s32[128]{0:T(128)} %param.11) | copy-start | bytes 1540
  23.6 26.2 %copy-start = (bf16[8,512,128]{2,1,0:T(8,128)(2,1)S(1)}, bf16[8,512,128]{2,1,0:T(8,128)(2,1)}, u32[]{:S(2)}) copy-start(bf16[8,512,128]{2,1,0:T(8,128)(2,1)} %w_uk.1) | copy-start | bytes 3145732
  23.6 26.2 %copy-start.1 = (bf16[8,512,128]{2,1,0:T(8,128)(2,1)S(1)}, bf16[8,512,128]{2,1,0:T(8,128)(2,1)}, u32[]{:S(2)}) copy-start(bf16[8,512,128]{2,1,0:T(8,128)(2,1)} %w_uv.3) | copy-start | bytes 3145732
  24.5 23.3 %all-to-all-start.1 = ((bf16[8,288,128]{2,1,0:T(8,128)(2,1)}), bf16[8,288,128]{2,1,0:T(8,128)(2,1)S(1)}, u32[]{:S(2)}, u32[]{:S(2)}) async-start(bf16[8,288,128]{2,1,0:T(8,128)(2,1)} %get-tuple-element.13), calls=%async_computation.1 | async-start | bytes 1179648 | tf_op jit(solution)/shard_map/all_to_all | solution.py:322
  31.6 18.2 %collective-permute-start = (bf16[64,1536]{1,0:T(8,128)(2,1)S(1)}, bf16[64,1536]{1,0:T(8,128)(2,1)S(1)}, u32[]{:S(2)}, u32[]{:S(2)}) collective-permute-start(bf16[64,1536]{1,0:T(8,128)(2,1)S(1)} %get-tuple-element.12.q0), channel_id=1, source_target_pairs={{0,16},{16,32},{32,48},{48,0},{1,17},{17,33},{33,49},{49,1},{2,18}... | collective-permute-start | bytes 589832 | tf_op jit(solution)/shard_map/ppermute | solution.py:324
  35.0 14.8 %collective-permute-start.1 = (bf16[64,1536]{1,0:T(8,128)(2,1)S(1)}, bf16[64,1536]{1,0:T(8,128)(2,1)S(1)}, u32[]{:S(2)}, u32[]{:S(2)}) collective-permute-start(bf16[64,1536]{1,0:T(8,128)(2,1)S(1)} %get-tuple-element.12.q0), channel_id=1, source_target_pairs={{0,32},{16,48},{32,0},{48,16},{1,33},{17,49},{33,1},{49,17},{2,34}... | collective-permute-start | bytes 589832 | tf_op jit(solution)/shard_map/ppermute | solution.py:324
  39.7 10.2 %collective-permute-start.2 = (bf16[64,1536]{1,0:T(8,128)(2,1)S(1)}, bf16[64,1536]{1,0:T(8,128)(2,1)S(1)}, u32[]{:S(2)}, u32[]{:S(2)}) collective-permute-start(bf16[64,1536]{1,0:T(8,128)(2,1)S(1)} %get-tuple-element.12.q0), channel_id=1, source_target_pairs={{0,48},{16,0},{32,16},{48,32},{1,49},{17,1},{33,17},{49,33},{2,50}... | collective-permute-start | bytes 589832 | tf_op jit(solution)/shard_map/ppermute | solution.py:324
  47.8 6.6 %collective-permute-start.3 = (bf16[8,288,128]{2,1,0:T(8,128)(2,1)S(1)}, bf16[8,288,128]{2,1,0:T(8,128)(2,1)S(1)}, u32[]{:S(2)}, u32[]{:S(2)}) collective-permute-start(bf16[8,288,128]{2,1,0:T(8,128)(2,1)S(1)} %all-to-all-done.1.kv), channel_id=1, source_target_pairs={{0,8},{8,0},{1,9},{9,1},{2,10},{10,2},{3,11},{11,3},{4,12},{12,4},... | collective-permute-start | bytes 1769480 | tf_op jit(solution)/shard_map/ppermute | solution.py:323

commit v8 on v7

--- a/solution.py
+++ b/solution.py
@@ -38,7 +38,7 @@
 
 def spread_kernel(q_ref, lat_ref, rope_ref, out_ref):
     end = HEADS * DQ
-    for z in range(out_ref.shape[0]):
+    for z in range(NZ):
         out_ref[z, :, :end] = q_ref[:, z * end : (z + 1) * end]
         out_ref[z, :, end : end + DL] = lat_ref[...]
         out_ref[z, :, end + DL : end + DL + DR] = rope_ref[...]
@@ -46,25 +46,19 @@
 
 
 def spread(queries, latent, rope_key):
-    tokens = SPAN // NZ
-    steps = 4
-    each = NZ // steps
+    vmem = pl.BlockSpec(memory_space=pltpu.VMEM)
     return pl.pallas_call(
         spread_kernel,
-        grid=(steps,),
-        out_shape=jax.ShapeDtypeStruct((NZ, tokens, HEADS * DQ + WIDE), jnp.bfloat16),
-        in_specs=[
-            pl.BlockSpec((tokens, each * HEADS * DQ), lambda i: (0, i)),
-            pl.BlockSpec((tokens, DL), lambda i: (0, 0)),
-            pl.BlockSpec((tokens, DR), lambda i: (0, 0)),
-        ],
-        out_specs=pl.BlockSpec((each, tokens, HEADS * DQ + WIDE), lambda i: (i, 0, 0)),
+        out_shape=jax.ShapeDtypeStruct((NZ, SPAN // NZ, HEADS * DQ + WIDE), jnp.bfloat16),
+        in_specs=[vmem] * 3,
+        out_specs=vmem,
         compiler_params=pltpu.CompilerParams(vmem_limit_bytes=60 * 1024 * 1024),
         cost_estimate=pl.CostEstimate(flops=1_000_000, bytes_accessed=500_000, transcendentals=0),
     )(queries, latent, rope_key)
 
 
-def pack_kernel(both_ref, q_ref, kv_ref):
+def pack_kernel(both_ref, floor_ref, q_ref, kv_ref):
+    del floor_ref
     q_ref[...] = both_ref[:, : HEADS * DQ]
     rope = both_ref[:, HEADS * DQ + DL : HEADS * DQ + DL + DR]
     for to in range(NY):
@@ -75,7 +69,7 @@
         kv_ref[to, PACKED - HALF :, DR:] = rope[HALF:]
 
 
-def pack(both):
+def pack(both, floor):
     vmem = pl.BlockSpec(memory_space=pltpu.VMEM)
     return pl.pallas_call(
         pack_kernel,
@@ -83,11 +77,11 @@
             jax.ShapeDtypeStruct((SPAN, HEADS * DQ), jnp.bfloat16),
             jax.ShapeDtypeStruct((NY, PACKED, LANES), jnp.bfloat16),
         ],
-        in_specs=[vmem],
+        in_specs=[vmem] + [pl.BlockSpec(memory_space=pl.ANY)],
         out_specs=[vmem] * 2,
         compiler_params=pltpu.CompilerParams(vmem_limit_bytes=8 * 1024 * 1024),
         cost_estimate=pl.CostEstimate(flops=4_000_000_000, bytes_accessed=1_000_000, transcendentals=0),
-    )(both)
+    )(both, floor)
 
 
 def fill_keys(keys, kv, first, own_block):
@@ -160,11 +154,26 @@
     return jnp.concatenate(floors, axis=0).astype(jnp.bfloat16)
 
 
-def own_kernel(info_ref, q0, q1, q2, q3, w_uk, w_uv, kv, q_ref, floor_ref, sum_ref, top_ref, total_ref, keys):
-    y = info_ref[0] // (2 * NX)
-    rows = NX * SPAN
-    floor = floors_of(info_ref)
-    floor_ref[...] = floor
+def floor_kernel(info_ref, floor_ref):
+    floor_ref[...] = floors_of(info_ref)
+
+
+def make_floor(info):
+    vmem = pl.BlockSpec(memory_space=pltpu.VMEM)
+    smem = pl.BlockSpec(memory_space=pltpu.SMEM)
+    return pl.pallas_call(
+        floor_kernel,
+        out_shape=jax.ShapeDtypeStruct((NX * SPAN, EXTRA), jnp.bfloat16),
+        in_specs=[smem],
+        out_specs=vmem,
+        compiler_params=pltpu.CompilerParams(vmem_limit_bytes=8 * 1024 * 1024),
+        cost_estimate=pl.CostEstimate(flops=4_000_000_000, bytes_accessed=500_000, transcendentals=0),
+    )(info)
+
+
+def own_kernel(place_ref, q0, q1, q2, q3, w_uk, w_uv, kv, floor_ref, q_ref, sum_ref, top_ref, total_ref, keys):
+    rows = NX * SPAN
+    floor = floor_ref[...]
     none = jnp.zeros((rows, WIDE - DL - DR), jnp.bfloat16)
 
     def fill_queries(h):
@@ -179,7 +188,7 @@
 
     fill_queries(0)
     fill_queries(1)
-    fill_keys(keys, kv, 0, 2 * y)
+    fill_keys(keys, kv, 0, place_ref[0] // (2 * NX) * 2)
     ahead = pair_scores(q_ref, floor, keys, 0)
     for p in range(HEADS // 2):
         s = ahead
@@ -199,7 +208,7 @@
         total_ref[pair] = jnp.broadcast_to(total, (2 * rows, STAT)).reshape(2, rows, STAT)
 
 
-def attend_own(info, qs, w_uk, w_uv, kv):
+def attend_own(place, qs, w_uk, w_uv, kv, floor):
     vmem = pl.BlockSpec(memory_space=pltpu.VMEM)
     smem = pl.BlockSpec(memory_space=pltpu.SMEM)
     rows = NX * SPAN
@@ -207,17 +216,16 @@
         own_kernel,
         out_shape=[
             jax.ShapeDtypeStruct((HEADS, rows, WIDE), jnp.bfloat16),
-            jax.ShapeDtypeStruct((rows, EXTRA), jnp.bfloat16),
             jax.ShapeDtypeStruct((HEADS, rows, DV), jnp.float32),
             jax.ShapeDtypeStruct((HEADS, rows, STAT), jnp.float32),
             jax.ShapeDtypeStruct((HEADS, rows, STAT), jnp.float32),
         ],
-        in_specs=[smem] + [vmem] * 7,
-        out_specs=[vmem] * 5,
+        in_specs=[smem] + [vmem] * 8,
+        out_specs=[vmem] * 4,
         scratch_shapes=[pltpu.VMEM((NY * SPAN, WIDE + EXTRA), jnp.bfloat16)],
         compiler_params=pltpu.CompilerParams(vmem_limit_bytes=20 * 1024 * 1024),
         cost_estimate=pl.CostEstimate(flops=6_000_000_000, bytes_accessed=5_000_000, transcendentals=1_000_000),
-    )(info, *qs, w_uk, w_uv, kv)
+    )(place, *qs, w_uk, w_uv, kv, floor)
 
 
 def other_kernel(place_ref, q_ref, floor_ref, kv, sum_ref, top_ref, total_ref, w_uv, out_ref, keys):
@@ -281,7 +289,7 @@
     )(place, q_all, floor, kv, *state, w_uv)
 
 
-def merge_kernel(p_ref, out_ref):
+def merge_kernel(p_ref, out_ref, held, sems):
     levels = []
     for x in range(NX):
         pieces = p_ref[x, :, :, HEADS * DV :].astype(jnp.float32).reshape(SPAN, STAT)
@@ -292,13 +300,19 @@
     whole = functools.reduce(jnp.add, shares)
     shares = [share / whole for share in shares]
     tokens = SPAN // NZ
+    moves = []
     for z in range(NZ):
         here = slice(z * tokens, (z + 1) * tokens)
         for h in range(HEADS):
             acc = jnp.zeros((tokens, DV), jnp.float32)
             for x in range(NX):
                 acc = acc + shares[x][here, h : h + 1] * p_ref[x, z, :, h * DV : (h + 1) * DV].astype(jnp.float32)
-            out_ref[:, (z * HEADS + h) * DV : (z * HEADS + h + 1) * DV] = acc.astype(jnp.bfloat16)
+            held[:, (z * HEADS + h) * DV : (z * HEADS + h + 1) * DV] = acc.astype(jnp.bfloat16)
+        cols = slice(z * HEADS * DV, (z + 1) * HEADS * DV)
+        moves.append(pltpu.make_async_copy(held.at[:, cols], out_ref.at[:, cols], sems.at[z]))
+        moves[-1].start()
+    for move in moves:
+        move.wait()
 
 
 def merge(parts):
@@ -307,7 +321,11 @@
         merge_kernel,
         out_shape=jax.ShapeDtypeStruct((SPAN // NZ, NZ * HEADS * DV), jnp.bfloat16),
         in_specs=[vmem],
-        out_specs=vmem,
+        out_specs=pl.BlockSpec(memory_space=pl.ANY),
+        scratch_shapes=[
+            pltpu.VMEM((SPAN // NZ, NZ * HEADS * DV), jnp.bfloat16),
+            pltpu.SemaphoreType.DMA((NZ,)),
+        ],
         compiler_params=pltpu.CompilerParams(vmem_limit_bytes=8 * 1024 * 1024),
         cost_estimate=pl.CostEstimate(flops=1_000_000, bytes_accessed=800_000, transcendentals=2000),
     )(parts)
@@ -315,14 +333,14 @@
 
 def on_device(queries, latent, rope_key, w_uk, w_uv, block_order):
     place = lax.axis_index(CTX).astype(jnp.int32).reshape(1)
-    info = jnp.concatenate([place, block_order])
+    floor = make_floor(jnp.concatenate([place, block_order]))
     both = spread(queries, latent, rope_key)
     both = lax.all_to_all(both, "z", split_axis=0, concat_axis=0, tiled=True).reshape(SPAN, HEADS * DQ + WIDE)
-    q_own, kv = pack(both)
+    q_own, kv = pack(both, floor)
     kv_own = lax.all_to_all(kv, "y", split_axis=0, concat_axis=0, tiled=True)
     kv_sib = lax.ppermute(kv_own, "core", CORE_SWAP)
     qs = [q_own] + [lax.ppermute(q_own, "x", along_x(step)) for step in range(1, NX)]
-    q_all, floor, *state = attend_own(info, qs, w_uk, w_uv, kv_own)
+    q_all, *state = attend_own(place, qs, w_uk, w_uv, kv_own, floor)
     partial = attend_other(place, q_all, floor, kv_sib, state, w_uv)
     rows = SPAN // NZ
     partial = partial.reshape(NX * NZ, rows, HEADS * DV + STAT)

time: 87.4 us -> 85.5 us (0.978)
  blocking collectives: 48.3 us -> 27.3 us
  starting transfers between devices: 20.4 us -> 30.3 us
  waiting for transfers between devices: 4.8 us -> 14.2 us
  Pallas kernels: 13.2 us -> 12.3 us
    all_to_all x1 -> x0, blocking collectives: 20.7 us -> none  [on_device(): lax.all_to_all(both, 'z', split_axis=0, concat_axis=0, tiled=True)]
    all_to_all x0 -> x1, starting transfers between devices: none -> 9.96 us  [on_device(): lax.all_to_all(both, 'z', split_axis=0, concat_axis=0, tiled=True)]
    all_to_all x0 -> x1, waiting for transfers between devices: none -> 9.42 us  [on_device(): lax.all_to_all(both, 'z', split_axis=0, concat_axis=0, tiled=True)]
    pallas_call x1 -> x2, Pallas kernels: 2.86 us -> 2.29 us  [the longest x1 1.67 us: spread(): pl.pallas_call(spread_kernel, out_shape=jax.ShapeDtypeStruct((NZ, SPAN //...]
  transfers between devices with their start and end apart: 5 -> 6, of which waited for: 1 -> 2; matrix products, arithmetic and copies ran while one was open for 0% -> 1% of each run, Pallas kernels for 5% -> 5%
where the time goes in v8:
time: 85.5 us; the launch traced here: 85.1 us
  starting transfers between devices  30.3 us (35%)
  blocking collectives  27.3 us (32%)
  waiting for transfers between devices  14.2 us (17%)
  Pallas kernels  12.3 us (14%)
    all_to_all x1, blocking collectives, on_device(): lax.all_to_all(partial, ('x', 'z'), split_axis=0, concat_axis=0, tiled=True)  27.3 us
    ppermute x3, starting transfers between devices, on_device(): lax.ppermute(q_own, 'x', along_x(step))  11.4 us
    all_to_all x1, starting transfers between devices, on_device(): lax.all_to_all(both, 'z', split_axis=0, concat_axis=0, tiled=True)  9.96 us
    all_to_all x1, waiting for transfers between devices, on_device(): lax.all_to_all(both, 'z', split_axis=0, concat_axis=0, tiled=True)  9.42 us
    all_to_all x1, starting transfers between devices, on_device(): kv_own = lax.all_to_all(kv, 'y', split_axis=0, concat_axis=0, tiled=True)  7.1 us
    all_to_all x1, waiting for transfers between devices, on_device(): kv_own = lax.all_to_all(kv, 'y', split_axis=0, concat_axis=0, tiled=True)  4.8 us
    pallas_call x1, Pallas kernels, attend_own(): pl.pallas_call(own_kernel, out_shape=[jax.ShapeDtypeStruct((HEADS, rows,...  4.05 us
    pallas_call x1, Pallas kernels, attend_other(): pl.pallas_call(other_kernel, out_shape=jax.ShapeDtypeStruct((NX, SPAN, HE...  3.82 us
  transfers between devices with their start and end apart: 6, of which 2 were waited for; matrix products, arithmetic and copies ran while one was open for 1% of the time, Pallas kernels for 5%

profile of v8, /device:TPU:64, one launch (start us, length us, event | category | flops | bytes accessed | tf_op | source)
XLA Modules:
  0.0 85.1 jit_solution(17343223343180753678)
XLA Ops:
  0.0 1.7 %shard_map.64 = bf16[8,8,2176]{2,1,0:T(8,128)(2,1)} custom-call(bf16[8,12288]{1,0:T(8,128)(2,1)} %q_ref.1, bf16[8,512]{1,0:T(8,128)(2,1)} %lat_ref.1, bf16[8,64]{1,0:T(8,128)(2,1)} %rope_ref.1), custom_call_target="tpu_custom_call" | custom-call | flops 1000000 | bytes 500000 | tf_op jit(solution)/shard_map/pallas_call | solution.py:50
  1.7 10.0 %all-to-all-start = ((bf16[8,8,2176]{2,1,0:T(8,128)(2,1)}), bf16[8,8,2176]{2,1,0:T(8,128)(2,1)S(1)}, u32[]{:S(2)}, u32[]{:S(2)}) async-start(bf16[8,8,2176]{2,1,0:T(8,128)(2,1)} %shard_map.64), calls=%async_computation | async-start | bytes 557056 | tf_op jit(solution)/shard_map/all_to_all | solution.py:338
  11.6 0.7 pad_add_fusion.info_ref
  12.4 0.6 shard_map.65.floor_ref
  13.0 9.4 %all-to-all-done = bf16[8,8,2176]{2,1,0:T(8,128)(2,1)S(1)} async-done(((bf16[8,8,2176]{2,1,0:T(8,128)(2,1)}), bf16[8,8,2176]{2,1,0:T(8,128)(2,1)S(1)}, u32[]{:S(2)}, u32[]{:S(2)}) %all-to-all-start) | async-done | bytes 278560 | tf_op jit(solution)/shard_map/all_to_all | solution.py:338
  22.4 0.0 copy-start
  22.4 0.0 copy-start.1
  22.4 0.9 %shard_map.66 = (bf16[64,1536]{1,0:T(8,128)(2,1)S(1)}, bf16[8,288,128]{2,1,0:T(8,128)(2,1)}) custom-call(bf16[64,2176]{1,0:T(8,128)(2,1)S(1)} %bitcast.6, bf16[256,128]{1,0:T(8,128)(2,1)S(1)} %shard_map.65.floor_ref), custom_call_target="tpu_custom_call" | custom-call | flops 4000000000 | bytes 1000000 | tf_op jit(solution)/shard_map/pallas_call | solution.py:74
  23.3 7.1 %all-to-all-start.1 = ((bf16[8,288,128]{2,1,0:T(8,128)(2,1)}), bf16[8,288,128]{2,1,0:T(8,128)(2,1)S(1)}, u32[]{:S(2)}, u32[]{:S(2)}) async-start(bf16[8,288,128]{2,1,0:T(8,128)(2,1)} %get-tuple-element.12), calls=%async_computation.1 | async-start | bytes 1179648 | tf_op jit(solution)/shard_map/all_to_all | solution.py:340
  30.4 3.4 %collective-permute-start = (bf16[64,1536]{1,0:T(8,128)(2,1)S(1)}, bf16[64,1536]{1,0:T(8,128)(2,1)S(1)}, u32[]{:S(2)}, u32[]{:S(2)}) collective-permute-start(bf16[64,1536]{1,0:T(8,128)(2,1)S(1)} %get-tuple-element.11.q0), channel_id=1, source_target_pairs={{0,16},{16,32},{32,48},{48,0},{1,17},{17,33},{33,49},{49,1},{2,18}... | collective-permute-start | bytes 589832 | tf_op jit(solution)/shard_map/ppermute | solution.py:342
  33.8 4.6 %collective-permute-start.1 = (bf16[64,1536]{1,0:T(8,128)(2,1)S(1)}, bf16[64,1536]{1,0:T(8,128)(2,1)S(1)}, u32[]{:S(2)}, u32[]{:S(2)}) collective-permute-start(bf16[64,1536]{1,0:T(8,128)(2,1)S(1)} %get-tuple-element.11.q0), channel_id=1, source_target_pairs={{0,32},{16,48},{32,0},{48,16},{1,33},{17,49},{33,1},{49,17},{2,34}... | collective-permute-start | bytes 589832 | tf_op jit(solution)/shard_map/ppermute | solution.py:342
  38.5 3.3 %collective-permute-start.2 = (bf16[64,1536]{1,0:T(8,128)(2,1)S(1)}, bf16[64,1536]{1,0:T(8,128)(2,1)S(1)}, u32[]{:S(2)}, u32[]{:S(2)}) collective-permute-start(bf16[64,1536]{1,0:T(8,128)(2,1)S(1)} %get-tuple-element.11.q0), channel_id=1, source_target_pairs={{0,48},{16,0},{32,16},{48,32},{1,49},{17,1},{33,17},{49,33},{2,50}... | collective-permute-start | bytes 589832 | tf_op jit(solution)/shard_map/ppermute | solution.py:342
  41.8 4.8 %all-to-all-done.1.kv = bf16[8,288,128]{2,1,0:T(8,128)(2,1)S(1)} async-done(((bf16[8,288,128]{2,1,0:T(8,128)(2,1)}), bf16[8,288,128]{2,1,0:T(8,128)(2,1)S(1)}, u32[]{:S(2)}, u32[]{:S(2)}) %all-to-all-start.1) | async-done | bytes 589856 | tf_op jit(solution)/shard_map/all_to_all | solution.py:340
  46.6 1.9 %collective-permute-start.3 = (bf16[8,288,128]{2,1,0:T(8,128)(2,1)S(1)}, bf16[8,288,128]{2,1,0:T(8,128)(2,1)S(1)}, u32[]{:S(2)}, u32[]{:S(2)}) collective-permute-start(bf16[8,288,128]{2,1,0:T(8,128)(2,1)S(1)} %all-to-all-done.1.kv), channel_id=1, source_target_pairs={{0,8},{8,0},{1,9},{9,1},{2,10},{10,2},{3,11},{11,3},{4,12},{12,4},... | collective-permute-start | bytes 1769480 | tf_op jit(solution)/shard_map/ppermute | solution.py:341
  48.5 0.0 collective-permute-done.q1
  48.5 0.0 collective-permute-done.1.q2
  48.6 0.0 collective-permute-done.2.q3
  48.6 0.0 copy-done
  48.6 0.0 copy-done.1
  48.6 4.0 %shard_map.67 = (bf16[8,256,640]{2,1,0:T(8,128)(2,1)S(1)}, f32[8,256,128]{2,1,0:T(8,128)S(1)}, f32[8,256,128]{2,1,0:T(8,128)S(1)}, f32[8,256,128]{2,1,0:T(8,128)S(1)}) custom-call(s32[1]{0:T(128)} %bitcast.place_ref, bf16[64,1536]{1,0:T(8,128)(2,1)S(1)} %get-tuple-element.11.q0, bf16[64,1536]{1,0:T(8,128)(2,1)S(1)} %collective-permute-done.q1, ...), custom_call_target="tpu_custom_call" | custom-call | flops 6000000000 | bytes 5000000 | tf_op jit(solution)/shard_map/pallas_call | solution.py:215
  52.6 0.0 collective-permute-done.3.kv
  52.6 3.8 %shard_map.68 = bf16[4,64,1152]{2,1,0:T(8,128)(2,1)S(1)} custom-call(s32[1]{0:T(128)} %bitcast.place_ref, bf16[8,256,640]{2,1,0:T(8,128)(2,1)S(1)} %get-tuple-element.13.q_ref, bf16[256,128]{1,0:T(8,128)(2,1)S(1)} %shard_map.65.floor_ref, bf16[8,288,128]{2,1,0:T(8,128)(2,1)S(1)} %collective-permute-done.3.kv, f32[8,256,128]{2,1,0:T(8,128)S(1)} %get-tuple-element.14.sum_ref, ...), custom_call_target="tpu_custom_call" | custom-call | flops 4000000000 | bytes 5000000 | tf_op jit(solution)/shard_map/pallas_call | solution.py:281
  56.5 27.3 %all_to_all.15 = bf16[32,8,1152]{2,1,0:T(8,128)(2,1)S(1)} all-to-all(bf16[32,8,1152]{2,1,0:T(8,128)(2,1)S(1)} %bitcast.5), channel_id=1, replica_groups=mesh['y'=8,'x'=4,'core'=2,'z'=8] {'x','z'}, dimensions={0} | all-to-all | bytes 1179648 | tf_op jit(solution)/shard_map/all_to_all | solution.py:347
  83.8 1.2 %shard_map.69 = bf16[8,8192]{1,0:T(8,128)(2,1)} custom-call(bf16[4,8,8,1152]{3,2,1,0:T(8,128)(2,1)S(1)} %bitcast.4), custom_call_target="tpu_custom_call" | custom-call | flops 1000000 | bytes 800000 | tf_op jit(solution)/shard_map/pallas_call | solution.py:320
Async XLA Ops:
  1.7 20.7 %all-to-all-start = ((bf16[8,8,2176]{2,1,0:T(8,128)(2,1)}), bf16[8,8,2176]{2,1,0:T(8,128)(2,1)S(1)}, u32[]{:S(2)}, u32[]{:S(2)}) async-start(bf16[8,8,2176]{2,1,0:T(8,128)(2,1)} %shard_map.64), calls=%async_computation | async-start | bytes 557056 | tf_op jit(solution)/shard_map/all_to_all | solution.py:338
  22.4 26.2 %copy-start = (bf16[8,512,128]{2,1,0:T(8,128)(2,1)S(1)}, bf16[8,512,128]{2,1,0:T(8,128)(2,1)}, u32[]{:S(2)}) copy-start(bf16[8,512,128]{2,1,0:T(8,128)(2,1)} %w_uk.1) | copy-start | bytes 3145732
  22.4 26.2 %copy-start.1 = (bf16[8,512,128]{2,1,0:T(8,128)(2,1)S(1)}, bf16[8,512,128]{2,1,0:T(8,128)(2,1)}, u32[]{:S(2)}) copy-start(bf16[8,512,128]{2,1,0:T(8,128)(2,1)} %w_uv.3) | copy-start | bytes 3145732
  23.3 23.3 %all-to-all-start.1 = ((bf16[8,288,128]{2,1,0:T(8,128)(2,1)}), bf16[8,288,128]{2,1,0:T(8,128)(2,1)S(1)}, u32[]{:S(2)}, u32[]{:S(2)}) async-start(bf16[8,288,128]{2,1,0:T(8,128)(2,1)} %get-tuple-element.12), calls=%async_computation.1 | async-start | bytes 1179648 | tf_op jit(solution)/shard_map/all_to_all | solution.py:340
  30.4 18.1 %collective-permute-start = (bf16[64,1536]{1,0:T(8,128)(2,1)S(1)}, bf16[64,1536]{1,0:T(8,128)(2,1)S(1)}, u32[]{:S(2)}, u32[]{:S(2)}) collective-permute-start(bf16[64,1536]{1,0:T(8,128)(2,1)S(1)} %get-tuple-element.11.q0), channel_id=1, source_target_pairs={{0,16},{16,32},{32,48},{48,0},{1,17},{17,33},{33,49},{49,1},{2,18}... | collective-permute-start | bytes 589832 | tf_op jit(solution)/shard_map/ppermute | solution.py:342
  33.8 14.7 %collective-permute-start.1 = (bf16[64,1536]{1,0:T(8,128)(2,1)S(1)}, bf16[64,1536]{1,0:T(8,128)(2,1)S(1)}, u32[]{:S(2)}, u32[]{:S(2)}) collective-permute-start(bf16[64,1536]{1,0:T(8,128)(2,1)S(1)} %get-tuple-element.11.q0), channel_id=1, source_target_pairs={{0,32},{16,48},{32,0},{48,16},{1,33},{17,49},{33,1},{49,17},{2,34}... | collective-permute-start | bytes 589832 | tf_op jit(solution)/shard_map/ppermute | solution.py:342
  38.5 10.1 %collective-permute-start.2 = (bf16[64,1536]{1,0:T(8,128)(2,1)S(1)}, bf16[64,1536]{1,0:T(8,128)(2,1)S(1)}, u32[]{:S(2)}, u32[]{:S(2)}) collective-permute-start(bf16[64,1536]{1,0:T(8,128)(2,1)S(1)} %get-tuple-element.11.q0), channel_id=1, source_target_pairs={{0,48},{16,0},{32,16},{48,32},{1,49},{17,1},{33,17},{49,33},{2,50}... | collective-permute-start | bytes 589832 | tf_op jit(solution)/shard_map/ppermute | solution.py:342
  46.6 6.0 %collective-permute-start.3 = (bf16[8,288,128]{2,1,0:T(8,128)(2,1)S(1)}, bf16[8,288,128]{2,1,0:T(8,128)(2,1)S(1)}, u32[]{:S(2)}, u32[]{:S(2)}) collective-permute-start(bf16[8,288,128]{2,1,0:T(8,128)(2,1)S(1)} %all-to-all-done.1.kv), channel_id=1, source_target_pairs={{0,8},{8,0},{1,9},{9,1},{2,10},{10,2},{3,11},{11,3},{4,12},{12,4},... | collective-permute-start | bytes 1769480 | tf_op jit(solution)/shard_map/ppermute | solution.py:341

commit v9 on v8

--- a/solution.py
+++ b/solution.py
@@ -36,49 +36,78 @@
 CTX = ("y", "x", "core")
 
 
-def spread_kernel(q_ref, lat_ref, rope_ref, out_ref):
+def spread_kernel(q_ref, lat_ref, rope_ref, out_ref, lat, rope, held, sems):
     end = HEADS * DQ
+    fetches = [
+        pltpu.make_async_copy(lat_ref, lat, sems.at[2 * NZ]),
+        pltpu.make_async_copy(rope_ref, rope, sems.at[2 * NZ + 1]),
+    ]
+    parts = [
+        pltpu.make_async_copy(q_ref.at[:, z * end : (z + 1) * end], held.at[z, :, :end], sems.at[z]) for z in range(NZ)
+    ]
+    for copy in fetches + parts:
+        copy.start()
+    for copy in fetches:
+        copy.wait()
     for z in range(NZ):
-        out_ref[z, :, :end] = q_ref[:, z * end : (z + 1) * end]
-        out_ref[z, :, end : end + DL] = lat_ref[...]
-        out_ref[z, :, end + DL : end + DL + DR] = rope_ref[...]
-        out_ref[z, :, end + DL + DR :] = jnp.zeros_like(rope_ref)
+        held[z, :, end : end + DL] = lat[...]
+        held[z, :, end + DL : end + DL + DR] = rope[...]
+        held[z, :, end + DL + DR :] = jnp.zeros_like(rope)
+    moves = [pltpu.make_async_copy(held.at[z], out_ref.at[z], sems.at[NZ + z]) for z in range(NZ)]
+    for z in range(NZ):
+        parts[z].wait()
+        moves[z].start()
+    for move in moves:
+        move.wait()
 
 
 def spread(queries, latent, rope_key):
-    vmem = pl.BlockSpec(memory_space=pltpu.VMEM)
+    hbm = pl.BlockSpec(memory_space=pl.ANY)
+    shape = (NZ, SPAN // NZ, HEADS * DQ + WIDE)
     return pl.pallas_call(
         spread_kernel,
-        out_shape=jax.ShapeDtypeStruct((NZ, SPAN // NZ, HEADS * DQ + WIDE), jnp.bfloat16),
-        in_specs=[vmem] * 3,
-        out_specs=vmem,
+        out_shape=jax.ShapeDtypeStruct(shape, jnp.bfloat16),
+        in_specs=[hbm] * 3,
+        out_specs=hbm,
+        scratch_shapes=[
+            pltpu.VMEM(latent.shape, jnp.bfloat16),
+            pltpu.VMEM(rope_key.shape, jnp.bfloat16),
+            pltpu.VMEM(shape, jnp.bfloat16),
+            pltpu.SemaphoreType.DMA((2 * NZ + 2,)),
+        ],
         compiler_params=pltpu.CompilerParams(vmem_limit_bytes=60 * 1024 * 1024),
         cost_estimate=pl.CostEstimate(flops=1_000_000, bytes_accessed=500_000, transcendentals=0),
     )(queries, latent, rope_key)
 
 
-def pack_kernel(both_ref, floor_ref, q_ref, kv_ref):
+def pack_kernel(both_ref, floor_ref, q_ref, kv_ref, block, sems):
     del floor_ref
+    for j in range(DL // LANES):
+        col = HEADS * DQ + j * LANES
+        block[j * SPAN : (j + 1) * SPAN] = both_ref[:, col : col + LANES]
+    rope = both_ref[:, HEADS * DQ + DL : HEADS * DQ + DL + DR]
+    block[PACKED - HALF :, :DR] = rope[:HALF]
+    block[PACKED - HALF :, DR:] = rope[HALF:]
+    moves = [pltpu.make_async_copy(block, kv_ref.at[to], sems.at[to]) for to in range(NY)]
+    for move in moves:
+        move.start()
     q_ref[...] = both_ref[:, : HEADS * DQ]
-    rope = both_ref[:, HEADS * DQ + DL : HEADS * DQ + DL + DR]
-    for to in range(NY):
-        for j in range(DL // LANES):
-            col = HEADS * DQ + j * LANES
-            kv_ref[to, j * SPAN : (j + 1) * SPAN] = both_ref[:, col : col + LANES]
-        kv_ref[to, PACKED - HALF :, :DR] = rope[:HALF]
-        kv_ref[to, PACKED - HALF :, DR:] = rope[HALF:]
+    for move in moves:
+        move.wait()
 
 
 def pack(both, floor):
     vmem = pl.BlockSpec(memory_space=pltpu.VMEM)
+    hbm = pl.BlockSpec(memory_space=pl.ANY)
     return pl.pallas_call(
         pack_kernel,
         out_shape=[
             jax.ShapeDtypeStruct((SPAN, HEADS * DQ), jnp.bfloat16),
             jax.ShapeDtypeStruct((NY, PACKED, LANES), jnp.bfloat16),
         ],
-        in_specs=[vmem] + [pl.BlockSpec(memory_space=pl.ANY)],
-        out_specs=[vmem] * 2,
+        in_specs=[vmem, hbm],
+        out_specs=[vmem, hbm],
+        scratch_shapes=[pltpu.VMEM((PACKED, LANES), jnp.bfloat16), pltpu.SemaphoreType.DMA((NY,))],
         compiler_params=pltpu.CompilerParams(vmem_limit_bytes=8 * 1024 * 1024),
         cost_estimate=pl.CostEstimate(flops=4_000_000_000, bytes_accessed=1_000_000, transcendentals=0),
     )(both, floor)
@@ -228,6 +257,11 @@
     )(place, *qs, w_uk, w_uv, kv, floor)
 
 
+def head_scores(q_ref, floor, keys, h):
+    q = jnp.concatenate([q_ref[h], floor], axis=1)
+    return lax.dot_general(q, keys[...], (((1,), (1,)), ((), ())), preferred_element_type=jnp.float32)
+
+
 def other_kernel(place_ref, q_ref, floor_ref, kv, sum_ref, top_ref, total_ref, w_uv, out_ref, keys):
     x = (place_ref[0] // 2) % NX
     rows = NX * SPAN
@@ -235,30 +269,25 @@
     fill_keys(keys, kv, NY * SPAN // HALF, None)
     lanes = lax.broadcasted_iota(jnp.int32, (rows, STAT), 1)
     level = jnp.zeros((rows, STAT), jnp.float32)
-    ahead = pair_scores(q_ref, floor, keys, 0)
-    for p in range(HEADS // 2):
+    ahead = head_scores(q_ref, floor, keys, 0)
+    for h in range(HEADS):
         s = ahead
-        values = pair_values(keys, w_uv, p)
-        if p + 1 < HEADS // 2:
-            ahead = pair_scores(q_ref, floor, keys, p + 1)
-        pair = slice(2 * p, 2 * p + 2)
-        old_top = top_ref[pair].reshape(2 * rows, STAT)
-        old_total = total_ref[pair].reshape(2 * rows, STAT)
+        if h % 2 == 0:
+            values = pair_values(keys, w_uv, h // 2)
+        if h + 1 < HEADS:
+            ahead = head_scores(q_ref, floor, keys, h + 1)
+        old_top = top_ref[h]
         top = jnp.maximum(old_top, jnp.max(s, axis=1, keepdims=True))
         shrink = jnp.exp2((old_top - top) * SCALE2)
         weight = jnp.exp2((s - wide(top, NY * SPAN // STAT)) * SCALE2)
-        total = old_total * shrink + jnp.sum(weight, axis=1, keepdims=True)
-        sums = weigh(weight, values)
-        share = 1.0 / total
-        here = top * SCALE2 + jnp.log2(total)
-        for i in range(2):
-            h = 2 * p + i
-            mine = slice(i * rows, (i + 1) * rows)
-            value = ((sums[i] + sum_ref[h] * shrink[mine]) * share[mine]).astype(jnp.bfloat16)
-            for step in range(NX):
-                to = (x + NX - step) % NX
-                out_ref[to, :, h * DV : (h + 1) * DV] = value[step * SPAN : (step + 1) * SPAN]
-            level = jnp.where(lanes % HEADS == h, here[mine], level)
+        total = total_ref[h] * shrink + jnp.sum(weight, axis=1, keepdims=True)
+        value = values[:, h % 2 * DV : (h % 2 + 1) * DV]
+        sums = jnp.dot(weight.astype(jnp.bfloat16), value, preferred_element_type=jnp.float32)
+        out = ((sums + sum_ref[h] * shrink) * (1.0 / total)).astype(jnp.bfloat16)
+        for step in range(NX):
+            to = (x + NX - step) % NX
+            out_ref[to, :, h * DV : (h + 1) * DV] = out[step * SPAN : (step + 1) * SPAN]
+        level = jnp.where(lanes % HEADS == h, top * SCALE2 + jnp.log2(total), level)
     high = level.astype(jnp.bfloat16)
     rest = level - high.astype(jnp.float32)
     middle = rest.astype(jnp.bfloat16)

time: 85.5 us -> 85.6 us (level)
  no operation moved by 1% of the time
where the time goes in v9:
time: 85.6 us; the launch traced here: 85.1 us
  starting transfers between devices  30.4 us (36%)
  blocking collectives  27.3 us (32%)
  waiting for transfers between devices  14.2 us (17%)
  Pallas kernels  12.3 us (14%)
    all_to_all x1, blocking collectives, on_device(): lax.all_to_all(partial, ('x', 'z'), split_axis=0, concat_axis=0, tiled=True)  27.3 us
    ppermute x3, starting transfers between devices, on_device(): lax.ppermute(q_own, 'x', along_x(step))  11.4 us
    all_to_all x1, starting transfers between devices, on_device(): lax.all_to_all(both, 'z', split_axis=0, concat_axis=0, tiled=True)  9.98 us
    all_to_all x1, waiting for transfers between devices, on_device(): lax.all_to_all(both, 'z', split_axis=0, concat_axis=0, tiled=True)  9.42 us
    all_to_all x1, starting transfers between devices, on_device(): kv_own = lax.all_to_all(kv, 'y', split_axis=0, concat_axis=0, tiled=True)  7.11 us
    all_to_all x1, waiting for transfers between devices, on_device(): kv_own = lax.all_to_all(kv, 'y', split_axis=0, concat_axis=0, tiled=True)  4.8 us
    pallas_call x1, Pallas kernels, attend_own(): pl.pallas_call(own_kernel, out_shape=[jax.ShapeDtypeStruct((HEADS, rows,...  4.05 us
    pallas_call x1, Pallas kernels, attend_other(): pl.pallas_call(other_kernel, out_shape=jax.ShapeDtypeStruct((NX, SPAN, HE...  3.78 us
  transfers between devices with their start and end apart: 6, of which 2 were waited for; matrix products, arithmetic and copies ran while one was open for 1% of the time, Pallas kernels for 5%

profile of v9, /device:TPU:64, one launch (start us, length us, event | category | flops | bytes accessed | tf_op | source)
XLA Modules:
  0.0 85.1 jit_solution(15460483062110435070)
XLA Ops:
  0.0 1.7 %shard_map.64 = bf16[8,8,2176]{2,1,0:T(8,128)(2,1)} custom-call(bf16[8,12288]{1,0:T(8,128)(2,1)} %q_ref.1, bf16[8,512]{1,0:T(8,128)(2,1)} %lat_ref.1, bf16[8,64]{1,0:T(8,128)(2,1)} %rope_ref.1), custom_call_target="tpu_custom_call" | custom-call | flops 1000000 | bytes 500000 | tf_op jit(solution)/shard_map/pallas_call | solution.py:67
  1.7 10.0 %all-to-all-start = ((bf16[8,8,2176]{2,1,0:T(8,128)(2,1)}), bf16[8,8,2176]{2,1,0:T(8,128)(2,1)S(1)}, u32[]{:S(2)}, u32[]{:S(2)}) async-start(bf16[8,8,2176]{2,1,0:T(8,128)(2,1)} %shard_map.64), calls=%async_computation | async-start | bytes 557056 | tf_op jit(solution)/shard_map/all_to_all | solution.py:367
  11.6 0.7 pad_add_fusion.info_ref
  12.4 0.6 shard_map.65.floor_ref
  13.0 9.4 %all-to-all-done = bf16[8,8,2176]{2,1,0:T(8,128)(2,1)S(1)} async-done(((bf16[8,8,2176]{2,1,0:T(8,128)(2,1)}), bf16[8,8,2176]{2,1,0:T(8,128)(2,1)S(1)}, u32[]{:S(2)}, u32[]{:S(2)}) %all-to-all-start) | async-done | bytes 278560 | tf_op jit(solution)/shard_map/all_to_all | solution.py:367
  22.4 0.0 copy-start
  22.4 0.0 copy-start.1
  22.4 0.9 %shard_map.66 = (bf16[64,1536]{1,0:T(8,128)(2,1)S(1)}, bf16[8,288,128]{2,1,0:T(8,128)(2,1)}) custom-call(bf16[64,2176]{1,0:T(8,128)(2,1)S(1)} %bitcast.6, bf16[256,128]{1,0:T(8,128)(2,1)S(1)} %shard_map.65.floor_ref), custom_call_target="tpu_custom_call" | custom-call | flops 4000000000 | bytes 1000000 | tf_op jit(solution)/shard_map/pallas_call | solution.py:102
  23.4 7.1 %all-to-all-start.1 = ((bf16[8,288,128]{2,1,0:T(8,128)(2,1)}), bf16[8,288,128]{2,1,0:T(8,128)(2,1)S(1)}, u32[]{:S(2)}, u32[]{:S(2)}) async-start(bf16[8,288,128]{2,1,0:T(8,128)(2,1)} %get-tuple-element.12), calls=%async_computation.1 | async-start | bytes 1179648 | tf_op jit(solution)/shard_map/all_to_all | solution.py:369
  30.5 3.4 %collective-permute-start = (bf16[64,1536]{1,0:T(8,128)(2,1)S(1)}, bf16[64,1536]{1,0:T(8,128)(2,1)S(1)}, u32[]{:S(2)}, u32[]{:S(2)}) collective-permute-start(bf16[64,1536]{1,0:T(8,128)(2,1)S(1)} %get-tuple-element.11.q0), channel_id=1, source_target_pairs={{0,16},{16,32},{32,48},{48,0},{1,17},{17,33},{33,49},{49,1},{2,18}... | collective-permute-start | bytes 589832 | tf_op jit(solution)/shard_map/ppermute | solution.py:371
  33.9 4.6 %collective-permute-start.1 = (bf16[64,1536]{1,0:T(8,128)(2,1)S(1)}, bf16[64,1536]{1,0:T(8,128)(2,1)S(1)}, u32[]{:S(2)}, u32[]{:S(2)}) collective-permute-start(bf16[64,1536]{1,0:T(8,128)(2,1)S(1)} %get-tuple-element.11.q0), channel_id=1, source_target_pairs={{0,32},{16,48},{32,0},{48,16},{1,33},{17,49},{33,1},{49,17},{2,34}... | collective-permute-start | bytes 589832 | tf_op jit(solution)/shard_map/ppermute | solution.py:371
  38.5 3.3 %collective-permute-start.2 = (bf16[64,1536]{1,0:T(8,128)(2,1)S(1)}, bf16[64,1536]{1,0:T(8,128)(2,1)S(1)}, u32[]{:S(2)}, u32[]{:S(2)}) collective-permute-start(bf16[64,1536]{1,0:T(8,128)(2,1)S(1)} %get-tuple-element.11.q0), channel_id=1, source_target_pairs={{0,48},{16,0},{32,16},{48,32},{1,49},{17,1},{33,17},{49,33},{2,50}... | collective-permute-start | bytes 589832 | tf_op jit(solution)/shard_map/ppermute | solution.py:371
  41.9 4.8 %all-to-all-done.1.kv = bf16[8,288,128]{2,1,0:T(8,128)(2,1)S(1)} async-done(((bf16[8,288,128]{2,1,0:T(8,128)(2,1)}), bf16[8,288,128]{2,1,0:T(8,128)(2,1)S(1)}, u32[]{:S(2)}, u32[]{:S(2)}) %all-to-all-start.1) | async-done | bytes 589856 | tf_op jit(solution)/shard_map/all_to_all | solution.py:369
  46.7 1.9 %collective-permute-start.3 = (bf16[8,288,128]{2,1,0:T(8,128)(2,1)S(1)}, bf16[8,288,128]{2,1,0:T(8,128)(2,1)S(1)}, u32[]{:S(2)}, u32[]{:S(2)}) collective-permute-start(bf16[8,288,128]{2,1,0:T(8,128)(2,1)S(1)} %all-to-all-done.1.kv), channel_id=1, source_target_pairs={{0,8},{8,0},{1,9},{9,1},{2,10},{10,2},{3,11},{11,3},{4,12},{12,4},... | collective-permute-start | bytes 1769480 | tf_op jit(solution)/shard_map/ppermute | solution.py:370
  48.6 0.0 collective-permute-done.q1
  48.6 0.0 collective-permute-done.1.q2
  48.6 0.0 collective-permute-done.2.q3
  48.6 0.0 copy-done
  48.6 0.0 copy-done.1
  48.6 4.0 %shard_map.67 = (bf16[8,256,640]{2,1,0:T(8,128)(2,1)S(1)}, f32[8,256,128]{2,1,0:T(8,128)S(1)}, f32[8,256,128]{2,1,0:T(8,128)S(1)}, f32[8,256,128]{2,1,0:T(8,128)S(1)}) custom-call(s32[1]{0:T(128)} %bitcast.place_ref, bf16[64,1536]{1,0:T(8,128)(2,1)S(1)} %get-tuple-element.11.q0, bf16[64,1536]{1,0:T(8,128)(2,1)S(1)} %collective-permute-done.q1, ...), custom_call_target="tpu_custom_call" | custom-call | flops 6000000000 | bytes 5000000 | tf_op jit(solution)/shard_map/pallas_call | solution.py:244
  52.7 0.0 collective-permute-done.3.kv
  52.7 3.8 %shard_map.68 = bf16[4,64,1152]{2,1,0:T(8,128)(2,1)S(1)} custom-call(s32[1]{0:T(128)} %bitcast.place_ref, bf16[8,256,640]{2,1,0:T(8,128)(2,1)S(1)} %get-tuple-element.13.q_ref, bf16[256,128]{1,0:T(8,128)(2,1)S(1)} %shard_map.65.floor_ref, bf16[8,288,128]{2,1,0:T(8,128)(2,1)S(1)} %collective-permute-done.3.kv, f32[8,256,128]{2,1,0:T(8,128)S(1)} %get-tuple-element.14.sum_ref, ...), custom_call_target="tpu_custom_call" | custom-call | flops 4000000000 | bytes 5000000 | tf_op jit(solution)/shard_map/pallas_call | solution.py:310
  56.5 27.3 %all_to_all.15 = bf16[32,8,1152]{2,1,0:T(8,128)(2,1)S(1)} all-to-all(bf16[32,8,1152]{2,1,0:T(8,128)(2,1)S(1)} %bitcast.5), channel_id=1, replica_groups=mesh['y'=8,'x'=4,'core'=2,'z'=8] {'x','z'}, dimensions={0} | all-to-all | bytes 1179648 | tf_op jit(solution)/shard_map/all_to_all | solution.py:376
  83.8 1.2 %shard_map.69 = bf16[8,8192]{1,0:T(8,128)(2,1)} custom-call(bf16[4,8,8,1152]{3,2,1,0:T(8,128)(2,1)S(1)} %bitcast.4), custom_call_target="tpu_custom_call" | custom-call | flops 1000000 | bytes 800000 | tf_op jit(solution)/shard_map/pallas_call | solution.py:349
Async XLA Ops:
  1.7 20.7 %all-to-all-start = ((bf16[8,8,2176]{2,1,0:T(8,128)(2,1)}), bf16[8,8,2176]{2,1,0:T(8,128)(2,1)S(1)}, u32[]{:S(2)}, u32[]{:S(2)}) async-start(bf16[8,8,2176]{2,1,0:T(8,128)(2,1)} %shard_map.64), calls=%async_computation | async-start | bytes 557056 | tf_op jit(solution)/shard_map/all_to_all | solution.py:367
  22.4 26.2 %copy-start = (bf16[8,512,128]{2,1,0:T(8,128)(2,1)S(1)}, bf16[8,512,128]{2,1,0:T(8,128)(2,1)}, u32[]{:S(2)}) copy-start(bf16[8,512,128]{2,1,0:T(8,128)(2,1)} %w_uk.1) | copy-start | bytes 3145732
  22.4 26.2 %copy-start.1 = (bf16[8,512,128]{2,1,0:T(8,128)(2,1)S(1)}, bf16[8,512,128]{2,1,0:T(8,128)(2,1)}, u32[]{:S(2)}) copy-start(bf16[8,512,128]{2,1,0:T(8,128)(2,1)} %w_uv.3) | copy-start | bytes 3145732
  23.4 23.3 %all-to-all-start.1 = ((bf16[8,288,128]{2,1,0:T(8,128)(2,1)}), bf16[8,288,128]{2,1,0:T(8,128)(2,1)S(1)}, u32[]{:S(2)}, u32[]{:S(2)}) async-start(bf16[8,288,128]{2,1,0:T(8,128)(2,1)} %get-tuple-element.12), calls=%async_computation.1 | async-start | bytes 1179648 | tf_op jit(solution)/shard_map/all_to_all | solution.py:369
  30.5 18.1 %collective-permute-start = (bf16[64,1536]{1,0:T(8,128)(2,1)S(1)}, bf16[64,1536]{1,0:T(8,128)(2,1)S(1)}, u32[]{:S(2)}, u32[]{:S(2)}) collective-permute-start(bf16[64,1536]{1,0:T(8,128)(2,1)S(1)} %get-tuple-element.11.q0), channel_id=1, source_target_pairs={{0,16},{16,32},{32,48},{48,0},{1,17},{17,33},{33,49},{49,1},{2,18}... | collective-permute-start | bytes 589832 | tf_op jit(solution)/shard_map/ppermute | solution.py:371
  33.9 14.7 %collective-permute-start.1 = (bf16[64,1536]{1,0:T(8,128)(2,1)S(1)}, bf16[64,1536]{1,0:T(8,128)(2,1)S(1)}, u32[]{:S(2)}, u32[]{:S(2)}) collective-permute-start(bf16[64,1536]{1,0:T(8,128)(2,1)S(1)} %get-tuple-element.11.q0), channel_id=1, source_target_pairs={{0,32},{16,48},{32,0},{48,16},{1,33},{17,49},{33,1},{49,17},{2,34}... | collective-permute-start | bytes 589832 | tf_op jit(solution)/shard_map/ppermute | solution.py:371
  38.5 10.1 %collective-permute-start.2 = (bf16[64,1536]{1,0:T(8,128)(2,1)S(1)}, bf16[64,1536]{1,0:T(8,128)(2,1)S(1)}, u32[]{:S(2)}, u32[]{:S(2)}) collective-permute-start(bf16[64,1536]{1,0:T(8,128)(2,1)S(1)} %get-tuple-element.11.q0), channel_id=1, source_target_pairs={{0,48},{16,0},{32,16},{48,32},{1,49},{17,1},{33,17},{49,33},{2,50}... | collective-permute-start | bytes 589832 | tf_op jit(solution)/shard_map/ppermute | solution.py:371
  46.7 6.0 %collective-permute-start.3 = (bf16[8,288,128]{2,1,0:T(8,128)(2,1)S(1)}, bf16[8,288,128]{2,1,0:T(8,128)(2,1)S(1)}, u32[]{:S(2)}, u32[]{:S(2)}) collective-permute-start(bf16[8,288,128]{2,1,0:T(8,128)(2,1)S(1)} %all-to-all-done.1.kv), channel_id=1, source_target_pairs={{0,8},{8,0},{1,9},{9,1},{2,10},{10,2},{3,11},{11,3},{4,12},{12,4},... | collective-permute-start | bytes 1769480 | tf_op jit(solution)/shard_map/ppermute | solution.py:370

commit v10 on v8

--- a/solution.py
+++ b/solution.py
@@ -103,26 +103,19 @@
     keys[:, WIDE:] = jnp.where(ones, 1.0, 0.0).astype(jnp.bfloat16)
 
 
-def pair_scores(q_ref, floor, keys, p):
-    rows = NX * SPAN
-    q = jnp.concatenate(
-        [q_ref[2 * p : 2 * p + 2].reshape(2 * rows, WIDE), jnp.concatenate([floor, floor], axis=0)], axis=1
+PART = 256
+
+
+def part_scores(q_ref, floor, keys, h, part):
+    q = jnp.concatenate([q_ref[h], floor], axis=1)
+    return lax.dot_general(
+        q, keys[part * PART : (part + 1) * PART], (((1,), (1,)), ((), ())), preferred_element_type=jnp.float32
     )
-    return lax.dot_general(q, keys[...], (((1,), (1,)), ((), ())), preferred_element_type=jnp.float32)
 
 
 def pair_values(keys, w_uv, p):
     w = jnp.concatenate([w_uv[2 * p], w_uv[2 * p + 1]], axis=1)
     return jnp.dot(keys[:, :DL], w, preferred_element_type=jnp.float32).astype(jnp.bfloat16)
-
-
-def weigh(weight, values):
-    rows = NX * SPAN
-    weight = weight.astype(jnp.bfloat16)
-    return [
-        jnp.dot(weight[i * rows : (i + 1) * rows], values[:, i * DV : (i + 1) * DV], preferred_element_type=jnp.float32)
-        for i in range(2)
-    ]
 
 
 def wide(value, count):
@@ -189,23 +182,28 @@
     fill_queries(0)
     fill_queries(1)
     fill_keys(keys, kv, 0, place_ref[0] // (2 * NX) * 2)
-    ahead = pair_scores(q_ref, floor, keys, 0)
-    for p in range(HEADS // 2):
+    s = [part_scores(q_ref, floor, keys, 0, part) for part in range(2)]
+    for h in range(HEADS):
+        ahead = []
+        if h + 1 < HEADS:
+            ahead.append(part_scores(q_ref, floor, keys, h + 1, 0))
+        top = jnp.max(jnp.maximum(s[0], s[1]), axis=1, keepdims=True)
+        first = jnp.exp2((s[0] - top) * SCALE2)
+        if h + 2 < HEADS:
+            fill_queries(h + 2)
+        if h + 1 < HEADS:
+            ahead.append(part_scores(q_ref, floor, keys, h + 1, 1))
+        second = jnp.exp2((s[1] - top) * SCALE2)
+        if h % 2 == 0:
+            values = pair_values(keys, w_uv, h // 2)
+        total = jnp.sum(first + second, axis=1, keepdims=True)
+        value = values[:, h % 2 * DV : (h % 2 + 1) * DV]
+        sum_ref[h] = jnp.dot(
+            first.astype(jnp.bfloat16), value[:PART], preferred_element_type=jnp.float32
+        ) + jnp.dot(second.astype(jnp.bfloat16), value[PART:], preferred_element_type=jnp.float32)
+        top_ref[h] = jnp.broadcast_to(top, (rows, STAT))
+        total_ref[h] = jnp.broadcast_to(total, (rows, STAT))
         s = ahead
-        values = pair_values(keys, w_uv, p)
-        if p + 1 < HEADS // 2:
-            fill_queries(2 * p + 2)
-            fill_queries(2 * p + 3)
-            ahead = pair_scores(q_ref, floor, keys, p + 1)
-        top = jnp.max(s, axis=1, keepdims=True)
-        weight = jnp.exp2((s - top) * SCALE2)
-        total = jnp.sum(weight, axis=1, keepdims=True)
-        sums = weigh(weight, values)
-        for i in range(2):
-            sum_ref[2 * p + i] = sums[i]
-        pair = slice(2 * p, 2 * p + 2)
-        top_ref[pair] = jnp.broadcast_to(top, (2 * rows, STAT)).reshape(2, rows, STAT)
-        total_ref[pair] = jnp.broadcast_to(total, (2 * rows, STAT)).reshape(2, rows, STAT)
 
 
 def attend_own(place, qs, w_uk, w_uv, kv, floor):
@@ -235,30 +233,31 @@
     fill_keys(keys, kv, NY * SPAN // HALF, None)
     lanes = lax.broadcasted_iota(jnp.int32, (rows, STAT), 1)
     level = jnp.zeros((rows, STAT), jnp.float32)
-    ahead = pair_scores(q_ref, floor, keys, 0)
-    for p in range(HEADS // 2):
+    s = [part_scores(q_ref, floor, keys, 0, part) for part in range(2)]
+    for h in range(HEADS):
+        ahead = []
+        if h + 1 < HEADS:
+            ahead.append(part_scores(q_ref, floor, keys, h + 1, 0))
+        old_top = top_ref[h]
+        top = jnp.maximum(old_top, jnp.max(jnp.maximum(s[0], s[1]), axis=1, keepdims=True))
+        shrink = jnp.exp2((old_top - top) * SCALE2)
+        first = jnp.exp2((s[0] - wide(top, PART // STAT)) * SCALE2)
+        if h + 1 < HEADS:
+            ahead.append(part_scores(q_ref, floor, keys, h + 1, 1))
+        second = jnp.exp2((s[1] - wide(top, PART // STAT)) * SCALE2)
+        if h % 2 == 0:
+            values = pair_values(keys, w_uv, h // 2)
+        total = total_ref[h] * shrink + jnp.sum(first + second, axis=1, keepdims=True)
+        value = values[:, h % 2 * DV : (h % 2 + 1) * DV]
+        sums = jnp.dot(first.astype(jnp.bfloat16), value[:PART], preferred_element_type=jnp.float32) + jnp.dot(
+            second.astype(jnp.bfloat16), value[PART:], preferred_element_type=jnp.float32
+        )
+        out = ((sums + sum_ref[h] * shrink) * (1.0 / total)).astype(jnp.bfloat16)
+        for step in range(NX):
+            to = (x + NX - step) % NX
+            out_ref[to, :, h * DV : (h + 1) * DV] = out[step * SPAN : (step + 1) * SPAN]
+        level = jnp.where(lanes % HEADS == h, top * SCALE2 + jnp.log2(total), level)
         s = ahead
-        values = pair_values(keys, w_uv, p)
-        if p + 1 < HEADS // 2:
-            ahead = pair_scores(q_ref, floor, keys, p + 1)
-        pair = slice(2 * p, 2 * p + 2)
-        old_top = top_ref[pair].reshape(2 * rows, STAT)
-        old_total = total_ref[pair].reshape(2 * rows, STAT)
-        top = jnp.maximum(old_top, jnp.max(s, axis=1, keepdims=True))
-        shrink = jnp.exp2((old_top - top) * SCALE2)
-        weight = jnp.exp2((s - wide(top, NY * SPAN // STAT)) * SCALE2)
-        total = old_total * shrink + jnp.sum(weight, axis=1, keepdims=True)
-        sums = weigh(weight, values)
-        share = 1.0 / total
-        here = top * SCALE2 + jnp.log2(total)
-        for i in range(2):
-            h = 2 * p + i
-            mine = slice(i * rows, (i + 1) * rows)
-            value = ((sums[i] + sum_ref[h] * shrink[mine]) * share[mine]).astype(jnp.bfloat16)
-            for step in range(NX):
-                to = (x + NX - step) % NX
-                out_ref[to, :, h * DV : (h + 1) * DV] = value[step * SPAN : (step + 1) * SPAN]
-            level = jnp.where(lanes % HEADS == h, here[mine], level)
     high = level.astype(jnp.bfloat16)
     rest = level - high.astype(jnp.float32)
     middle = rest.astype(jnp.bfloat16)

time: 85.5 us -> 85.8 us (level)
  transfers between devices with their start and end apart: 6 -> 6, of which waited for: 2 -> 2; matrix products, arithmetic and copies ran while one was open for 1% -> 1% of each run, Pallas kernels for 5% -> 6%
where the time goes in v10:
time: 85.8 us; the launch traced here: 85.3 us
  starting transfers between devices  30.3 us (35%)
  blocking collectives  27.3 us (32%)
  waiting for transfers between devices  14.2 us (17%)
  Pallas kernels  12.6 us (15%)
    all_to_all x1, blocking collectives, on_device(): lax.all_to_all(partial, ('x', 'z'), split_axis=0, concat_axis=0, tiled=True)  27.3 us
    ppermute x3, starting transfers between devices, on_device(): lax.ppermute(q_own, 'x', along_x(step))  11.4 us
    all_to_all x1, starting transfers between devices, on_device(): lax.all_to_all(both, 'z', split_axis=0, concat_axis=0, tiled=True)  9.96 us
    all_to_all x1, waiting for transfers between devices, on_device(): lax.all_to_all(both, 'z', split_axis=0, concat_axis=0, tiled=True)  9.42 us
    all_to_all x1, starting transfers between devices, on_device(): kv_own = lax.all_to_all(kv, 'y', split_axis=0, concat_axis=0, tiled=True)  7.1 us
    all_to_all x1, waiting for transfers between devices, on_device(): kv_own = lax.all_to_all(kv, 'y', split_axis=0, concat_axis=0, tiled=True)  4.8 us
    pallas_call x1, Pallas kernels, attend_own(): pl.pallas_call(own_kernel, out_shape=[jax.ShapeDtypeStruct((HEADS, rows,...  4.19 us
    pallas_call x1, Pallas kernels, attend_other(): pl.pallas_call(other_kernel, out_shape=jax.ShapeDtypeStruct((NX, SPAN, HE...  3.95 us
  transfers between devices with their start and end apart: 6, of which 2 were waited for; matrix products, arithmetic and copies ran while one was open for 1% of the time, Pallas kernels for 6%

profile of v10, /device:TPU:64, one launch (start us, length us, event | category | flops | bytes accessed | tf_op | source)
XLA Modules:
  0.0 85.3 jit_solution(14418433544143185992)
XLA Ops:
  0.0 1.7 %shard_map.64 = bf16[8,8,2176]{2,1,0:T(8,128)(2,1)} custom-call(bf16[8,12288]{1,0:T(8,128)(2,1)} %q_ref.1, bf16[8,512]{1,0:T(8,128)(2,1)} %lat_ref.1, bf16[8,64]{1,0:T(8,128)(2,1)} %rope_ref.1), custom_call_target="tpu_custom_call" | custom-call | flops 1000000 | bytes 500000 | tf_op jit(solution)/shard_map/pallas_call | solution.py:50
  1.7 10.0 %all-to-all-start = ((bf16[8,8,2176]{2,1,0:T(8,128)(2,1)}), bf16[8,8,2176]{2,1,0:T(8,128)(2,1)S(1)}, u32[]{:S(2)}, u32[]{:S(2)}) async-start(bf16[8,8,2176]{2,1,0:T(8,128)(2,1)} %shard_map.64), calls=%async_computation | async-start | bytes 557056 | tf_op jit(solution)/shard_map/all_to_all | solution.py:337
  11.6 0.7 pad_add_fusion.info_ref
  12.4 0.6 shard_map.65.floor_ref
  13.0 9.4 %all-to-all-done = bf16[8,8,2176]{2,1,0:T(8,128)(2,1)S(1)} async-done(((bf16[8,8,2176]{2,1,0:T(8,128)(2,1)}), bf16[8,8,2176]{2,1,0:T(8,128)(2,1)S(1)}, u32[]{:S(2)}, u32[]{:S(2)}) %all-to-all-start) | async-done | bytes 278560 | tf_op jit(solution)/shard_map/all_to_all | solution.py:337
  22.4 0.0 copy-start
  22.4 0.0 copy-start.1
  22.4 0.9 %shard_map.66 = (bf16[64,1536]{1,0:T(8,128)(2,1)S(1)}, bf16[8,288,128]{2,1,0:T(8,128)(2,1)}) custom-call(bf16[64,2176]{1,0:T(8,128)(2,1)S(1)} %bitcast.6, bf16[256,128]{1,0:T(8,128)(2,1)S(1)} %shard_map.65.floor_ref), custom_call_target="tpu_custom_call" | custom-call | flops 4000000000 | bytes 1000000 | tf_op jit(solution)/shard_map/pallas_call | solution.py:74
  23.3 7.1 %all-to-all-start.1 = ((bf16[8,288,128]{2,1,0:T(8,128)(2,1)}), bf16[8,288,128]{2,1,0:T(8,128)(2,1)S(1)}, u32[]{:S(2)}, u32[]{:S(2)}) async-start(bf16[8,288,128]{2,1,0:T(8,128)(2,1)} %get-tuple-element.12), calls=%async_computation.1 | async-start | bytes 1179648 | tf_op jit(solution)/shard_map/all_to_all | solution.py:339
  30.4 3.4 %collective-permute-start = (bf16[64,1536]{1,0:T(8,128)(2,1)S(1)}, bf16[64,1536]{1,0:T(8,128)(2,1)S(1)}, u32[]{:S(2)}, u32[]{:S(2)}) collective-permute-start(bf16[64,1536]{1,0:T(8,128)(2,1)S(1)} %get-tuple-element.11.q0), channel_id=1, source_target_pairs={{0,16},{16,32},{32,48},{48,0},{1,17},{17,33},{33,49},{49,1},{2,18}... | collective-permute-start | bytes 589832 | tf_op jit(solution)/shard_map/ppermute | solution.py:341
  33.8 4.6 %collective-permute-start.1 = (bf16[64,1536]{1,0:T(8,128)(2,1)S(1)}, bf16[64,1536]{1,0:T(8,128)(2,1)S(1)}, u32[]{:S(2)}, u32[]{:S(2)}) collective-permute-start(bf16[64,1536]{1,0:T(8,128)(2,1)S(1)} %get-tuple-element.11.q0), channel_id=1, source_target_pairs={{0,32},{16,48},{32,0},{48,16},{1,33},{17,49},{33,1},{49,17},{2,34}... | collective-permute-start | bytes 589832 | tf_op jit(solution)/shard_map/ppermute | solution.py:341
  38.5 3.3 %collective-permute-start.2 = (bf16[64,1536]{1,0:T(8,128)(2,1)S(1)}, bf16[64,1536]{1,0:T(8,128)(2,1)S(1)}, u32[]{:S(2)}, u32[]{:S(2)}) collective-permute-start(bf16[64,1536]{1,0:T(8,128)(2,1)S(1)} %get-tuple-element.11.q0), channel_id=1, source_target_pairs={{0,48},{16,0},{32,16},{48,32},{1,49},{17,1},{33,17},{49,33},{2,50}... | collective-permute-start | bytes 589832 | tf_op jit(solution)/shard_map/ppermute | solution.py:341
  41.8 4.8 %all-to-all-done.1.kv = bf16[8,288,128]{2,1,0:T(8,128)(2,1)S(1)} async-done(((bf16[8,288,128]{2,1,0:T(8,128)(2,1)}), bf16[8,288,128]{2,1,0:T(8,128)(2,1)S(1)}, u32[]{:S(2)}, u32[]{:S(2)}) %all-to-all-start.1) | async-done | bytes 589856 | tf_op jit(solution)/shard_map/all_to_all | solution.py:339
  46.6 1.9 %collective-permute-start.3 = (bf16[8,288,128]{2,1,0:T(8,128)(2,1)S(1)}, bf16[8,288,128]{2,1,0:T(8,128)(2,1)S(1)}, u32[]{:S(2)}, u32[]{:S(2)}) collective-permute-start(bf16[8,288,128]{2,1,0:T(8,128)(2,1)S(1)} %all-to-all-done.1.kv), channel_id=1, source_target_pairs={{0,8},{8,0},{1,9},{9,1},{2,10},{10,2},{3,11},{11,3},{4,12},{12,4},... | collective-permute-start | bytes 1769480 | tf_op jit(solution)/shard_map/ppermute | solution.py:340
  48.5 0.0 collective-permute-done.q1
  48.5 0.0 collective-permute-done.1.q2
  48.6 0.0 collective-permute-done.2.q3
  48.6 0.0 copy-done
  48.6 0.0 copy-done.1
  48.6 4.2 %shard_map.67 = (bf16[8,256,640]{2,1,0:T(8,128)(2,1)S(1)}, f32[8,256,128]{2,1,0:T(8,128)S(1)}, f32[8,256,128]{2,1,0:T(8,128)S(1)}, f32[8,256,128]{2,1,0:T(8,128)S(1)}) custom-call(s32[1]{0:T(128)} %bitcast.place_ref, bf16[64,1536]{1,0:T(8,128)(2,1)S(1)} %get-tuple-element.11.q0, bf16[64,1536]{1,0:T(8,128)(2,1)S(1)} %collective-permute-done.q1, ...), custom_call_target="tpu_custom_call" | custom-call | flops 6000000000 | bytes 5000000 | tf_op jit(solution)/shard_map/pallas_call | solution.py:213
  52.8 0.0 collective-permute-done.3.kv
  52.8 3.9 %shard_map.68 = bf16[4,64,1152]{2,1,0:T(8,128)(2,1)S(1)} custom-call(s32[1]{0:T(128)} %bitcast.place_ref, bf16[8,256,640]{2,1,0:T(8,128)(2,1)S(1)} %get-tuple-element.13.q_ref, bf16[256,128]{1,0:T(8,128)(2,1)S(1)} %shard_map.65.floor_ref, bf16[8,288,128]{2,1,0:T(8,128)(2,1)S(1)} %collective-permute-done.3.kv, f32[8,256,128]{2,1,0:T(8,128)S(1)} %get-tuple-element.14.sum_ref, ...), custom_call_target="tpu_custom_call" | custom-call | flops 4000000000 | bytes 5000000 | tf_op jit(solution)/shard_map/pallas_call | solution.py:280
  56.7 27.3 %all_to_all.15 = bf16[32,8,1152]{2,1,0:T(8,128)(2,1)S(1)} all-to-all(bf16[32,8,1152]{2,1,0:T(8,128)(2,1)S(1)} %bitcast.5), channel_id=1, replica_groups=mesh['y'=8,'x'=4,'core'=2,'z'=8] {'x','z'}, dimensions={0} | all-to-all | bytes 1179648 | tf_op jit(solution)/shard_map/all_to_all | solution.py:346
  84.1 1.2 %shard_map.69 = bf16[8,8192]{1,0:T(8,128)(2,1)} custom-call(bf16[4,8,8,1152]{3,2,1,0:T(8,128)(2,1)S(1)} %bitcast.4), custom_call_target="tpu_custom_call" | custom-call | flops 1000000 | bytes 800000 | tf_op jit(solution)/shard_map/pallas_call | solution.py:319
Async XLA Ops:
  1.7 20.7 %all-to-all-start = ((bf16[8,8,2176]{2,1,0:T(8,128)(2,1)}), bf16[8,8,2176]{2,1,0:T(8,128)(2,1)S(1)}, u32[]{:S(2)}, u32[]{:S(2)}) async-start(bf16[8,8,2176]{2,1,0:T(8,128)(2,1)} %shard_map.64), calls=%async_computation | async-start | bytes 557056 | tf_op jit(solution)/shard_map/all_to_all | solution.py:337
  22.4 26.2 %copy-start = (bf16[8,512,128]{2,1,0:T(8,128)(2,1)S(1)}, bf16[8,512,128]{2,1,0:T(8,128)(2,1)}, u32[]{:S(2)}) copy-start(bf16[8,512,128]{2,1,0:T(8,128)(2,1)} %w_uk.1) | copy-start | bytes 3145732
  22.4 26.2 %copy-start.1 = (bf16[8,512,128]{2,1,0:T(8,128)(2,1)S(1)}, bf16[8,512,128]{2,1,0:T(8,128)(2,1)}, u32[]{:S(2)}) copy-start(bf16[8,512,128]{2,1,0:T(8,128)(2,1)} %w_uv.3) | copy-start | bytes 3145732
  23.3 23.3 %all-to-all-start.1 = ((bf16[8,288,128]{2,1,0:T(8,128)(2,1)}), bf16[8,288,128]{2,1,0:T(8,128)(2,1)S(1)}, u32[]{:S(2)}, u32[]{:S(2)}) async-start(bf16[8,288,128]{2,1,0:T(8,128)(2,1)} %get-tuple-element.12), calls=%async_computation.1 | async-start | bytes 1179648 | tf_op jit(solution)/shard_map/all_to_all | solution.py:339
  30.4 18.1 %collective-permute-start = (bf16[64,1536]{1,0:T(8,128)(2,1)S(1)}, bf16[64,1536]{1,0:T(8,128)(2,1)S(1)}, u32[]{:S(2)}, u32[]{:S(2)}) collective-permute-start(bf16[64,1536]{1,0:T(8,128)(2,1)S(1)} %get-tuple-element.11.q0), channel_id=1, source_target_pairs={{0,16},{16,32},{32,48},{48,0},{1,17},{17,33},{33,49},{49,1},{2,18}... | collective-permute-start | bytes 589832 | tf_op jit(solution)/shard_map/ppermute | solution.py:341
  33.8 14.7 %collective-permute-start.1 = (bf16[64,1536]{1,0:T(8,128)(2,1)S(1)}, bf16[64,1536]{1,0:T(8,128)(2,1)S(1)}, u32[]{:S(2)}, u32[]{:S(2)}) collective-permute-start(bf16[64,1536]{1,0:T(8,128)(2,1)S(1)} %get-tuple-element.11.q0), channel_id=1, source_target_pairs={{0,32},{16,48},{32,0},{48,16},{1,33},{17,49},{33,1},{49,17},{2,34}... | collective-permute-start | bytes 589832 | tf_op jit(solution)/shard_map/ppermute | solution.py:341
  38.5 10.1 %collective-permute-start.2 = (bf16[64,1536]{1,0:T(8,128)(2,1)S(1)}, bf16[64,1536]{1,0:T(8,128)(2,1)S(1)}, u32[]{:S(2)}, u32[]{:S(2)}) collective-permute-start(bf16[64,1536]{1,0:T(8,128)(2,1)S(1)} %get-tuple-element.11.q0), channel_id=1, source_target_pairs={{0,48},{16,0},{32,16},{48,32},{1,49},{17,1},{33,17},{49,33},{2,50}... | collective-permute-start | bytes 589832 | tf_op jit(solution)/shard_map/ppermute | solution.py:341
  46.6 6.2 %collective-permute-start.3 = (bf16[8,288,128]{2,1,0:T(8,128)(2,1)S(1)}, bf16[8,288,128]{2,1,0:T(8,128)(2,1)S(1)}, u32[]{:S(2)}, u32[]{:S(2)}) collective-permute-start(bf16[8,288,128]{2,1,0:T(8,128)(2,1)S(1)} %all-to-all-done.1.kv), channel_id=1, source_target_pairs={{0,8},{8,0},{1,9},{9,1},{2,10},{10,2},{3,11},{11,3},{4,12},{12,4},... | collective-permute-start | bytes 1769480 | tf_op jit(solution)/shard_map/ppermute | solution.py:340

commit v11 on v8

--- a/solution.py
+++ b/solution.py
@@ -113,16 +113,18 @@
 
 def pair_values(keys, w_uv, p):
     w = jnp.concatenate([w_uv[2 * p], w_uv[2 * p + 1]], axis=1)
-    return jnp.dot(keys[:, :DL], w, preferred_element_type=jnp.float32).astype(jnp.bfloat16)
+    values = jnp.dot(keys[:, :DL], w, preferred_element_type=jnp.float32).astype(jnp.bfloat16)
+    ones = jnp.ones((NY * SPAN, STAT), jnp.bfloat16)
+    return [jnp.concatenate([values[:, i * DV : (i + 1) * DV], ones], axis=1) for i in range(2)]
 
 
 def weigh(weight, values):
     rows = NX * SPAN
     weight = weight.astype(jnp.bfloat16)
-    return [
-        jnp.dot(weight[i * rows : (i + 1) * rows], values[:, i * DV : (i + 1) * DV], preferred_element_type=jnp.float32)
-        for i in range(2)
+    both = [
+        jnp.dot(weight[i * rows : (i + 1) * rows], values[i], preferred_element_type=jnp.float32) for i in range(2)
     ]
+    return [one[:, :DV] for one in both], [one[:, DV:] for one in both]
 
 
 def wide(value, count):
@@ -199,13 +201,12 @@
             ahead = pair_scores(q_ref, floor, keys, p + 1)
         top = jnp.max(s, axis=1, keepdims=True)
         weight = jnp.exp2((s - top) * SCALE2)
-        total = jnp.sum(weight, axis=1, keepdims=True)
-        sums = weigh(weight, values)
+        sums, totals = weigh(weight, values)
         for i in range(2):
             sum_ref[2 * p + i] = sums[i]
+            total_ref[2 * p + i] = totals[i]
         pair = slice(2 * p, 2 * p + 2)
         top_ref[pair] = jnp.broadcast_to(top, (2 * rows, STAT)).reshape(2, rows, STAT)
-        total_ref[pair] = jnp.broadcast_to(total, (2 * rows, STAT)).reshape(2, rows, STAT)
 
 
 def attend_own(place, qs, w_uk, w_uv, kv, floor):
@@ -243,22 +244,19 @@
             ahead = pair_scores(q_ref, floor, keys, p + 1)
         pair = slice(2 * p, 2 * p + 2)
         old_top = top_ref[pair].reshape(2 * rows, STAT)
-        old_total = total_ref[pair].reshape(2 * rows, STAT)
         top = jnp.maximum(old_top, jnp.max(s, axis=1, keepdims=True))
         shrink = jnp.exp2((old_top - top) * SCALE2)
         weight = jnp.exp2((s - wide(top, NY * SPAN // STAT)) * SCALE2)
-        total = old_total * shrink + jnp.sum(weight, axis=1, keepdims=True)
-        sums = weigh(weight, values)
-        share = 1.0 / total
-        here = top * SCALE2 + jnp.log2(total)
+        sums, totals = weigh(weight, values)
         for i in range(2):
             h = 2 * p + i
             mine = slice(i * rows, (i + 1) * rows)
-            value = ((sums[i] + sum_ref[h] * shrink[mine]) * share[mine]).astype(jnp.bfloat16)
+            total = totals[i] + total_ref[h] * shrink[mine]
+            value = ((sums[i] + sum_ref[h] * shrink[mine]) * (1.0 / total)).astype(jnp.bfloat16)
             for step in range(NX):
                 to = (x + NX - step) % NX
                 out_ref[to, :, h * DV : (h + 1) * DV] = value[step * SPAN : (step + 1) * SPAN]
-            level = jnp.where(lanes % HEADS == h, here[mine], level)
+            level = jnp.where(lanes % HEADS == h, top[mine] * SCALE2 + jnp.log2(total), level)
     high = level.astype(jnp.bfloat16)
     rest = level - high.astype(jnp.float32)
     middle = rest.astype(jnp.bfloat16)

time: 85.5 us -> 85.2 us (level)
  no operation moved by 1% of the time
where the time goes in v11:
time: 85.2 us; the launch traced here: 84.7 us
  starting transfers between devices  30.3 us (36%)
  blocking collectives  27.3 us (32%)
  waiting for transfers between devices  14.2 us (17%)
  Pallas kernels  12 us (14%)
    all_to_all x1, blocking collectives, on_device(): lax.all_to_all(partial, ('x', 'z'), split_axis=0, concat_axis=0, tiled=True)  27.3 us
    ppermute x3, starting transfers between devices, on_device(): lax.ppermute(q_own, 'x', along_x(step))  11.4 us
    all_to_all x1, starting transfers between devices, on_device(): lax.all_to_all(both, 'z', split_axis=0, concat_axis=0, tiled=True)  9.96 us
    all_to_all x1, waiting for transfers between devices, on_device(): lax.all_to_all(both, 'z', split_axis=0, concat_axis=0, tiled=True)  9.42 us
    all_to_all x1, starting transfers between devices, on_device(): kv_own = lax.all_to_all(kv, 'y', split_axis=0, concat_axis=0, tiled=True)  7.1 us
    all_to_all x1, waiting for transfers between devices, on_device(): kv_own = lax.all_to_all(kv, 'y', split_axis=0, concat_axis=0, tiled=True)  4.8 us
    pallas_call x1, Pallas kernels, attend_own(): pl.pallas_call(own_kernel, out_shape=[jax.ShapeDtypeStruct((HEADS, rows,...  3.9 us
    pallas_call x1, Pallas kernels, attend_other(): pl.pallas_call(other_kernel, out_shape=jax.ShapeDtypeStruct((NX, SPAN, HE...  3.64 us
  transfers between devices with their start and end apart: 6, of which 2 were waited for; matrix products, arithmetic and copies ran while one was open for 1% of the time, Pallas kernels for 5%

profile of v11, /device:TPU:64, one launch (start us, length us, event | category | flops | bytes accessed | tf_op | source)
XLA Modules:
  0.0 84.7 jit_solution(230786420041403066)
XLA Ops:
  0.0 1.7 %shard_map.64 = bf16[8,8,2176]{2,1,0:T(8,128)(2,1)} custom-call(bf16[8,12288]{1,0:T(8,128)(2,1)} %q_ref.1, bf16[8,512]{1,0:T(8,128)(2,1)} %lat_ref.1, bf16[8,64]{1,0:T(8,128)(2,1)} %rope_ref.1), custom_call_target="tpu_custom_call" | custom-call | flops 1000000 | bytes 500000 | tf_op jit(solution)/shard_map/pallas_call | solution.py:50
  1.7 10.0 %all-to-all-start = ((bf16[8,8,2176]{2,1,0:T(8,128)(2,1)}), bf16[8,8,2176]{2,1,0:T(8,128)(2,1)S(1)}, u32[]{:S(2)}, u32[]{:S(2)}) async-start(bf16[8,8,2176]{2,1,0:T(8,128)(2,1)} %shard_map.64), calls=%async_computation | async-start | bytes 557056 | tf_op jit(solution)/shard_map/all_to_all | solution.py:336
  11.6 0.7 pad_add_fusion.info_ref
  12.4 0.6 shard_map.65.floor_ref
  13.0 9.4 %all-to-all-done = bf16[8,8,2176]{2,1,0:T(8,128)(2,1)S(1)} async-done(((bf16[8,8,2176]{2,1,0:T(8,128)(2,1)}), bf16[8,8,2176]{2,1,0:T(8,128)(2,1)S(1)}, u32[]{:S(2)}, u32[]{:S(2)}) %all-to-all-start) | async-done | bytes 278560 | tf_op jit(solution)/shard_map/all_to_all | solution.py:336
  22.4 0.0 copy-start
  22.4 0.0 copy-start.1
  22.4 0.9 %shard_map.66 = (bf16[64,1536]{1,0:T(8,128)(2,1)S(1)}, bf16[8,288,128]{2,1,0:T(8,128)(2,1)}) custom-call(bf16[64,2176]{1,0:T(8,128)(2,1)S(1)} %bitcast.6, bf16[256,128]{1,0:T(8,128)(2,1)S(1)} %shard_map.65.floor_ref), custom_call_target="tpu_custom_call" | custom-call | flops 4000000000 | bytes 1000000 | tf_op jit(solution)/shard_map/pallas_call | solution.py:74
  23.3 7.1 %all-to-all-start.1 = ((bf16[8,288,128]{2,1,0:T(8,128)(2,1)}), bf16[8,288,128]{2,1,0:T(8,128)(2,1)S(1)}, u32[]{:S(2)}, u32[]{:S(2)}) async-start(bf16[8,288,128]{2,1,0:T(8,128)(2,1)} %get-tuple-element.12), calls=%async_computation.1 | async-start | bytes 1179648 | tf_op jit(solution)/shard_map/all_to_all | solution.py:338
  30.4 3.4 %collective-permute-start = (bf16[64,1536]{1,0:T(8,128)(2,1)S(1)}, bf16[64,1536]{1,0:T(8,128)(2,1)S(1)}, u32[]{:S(2)}, u32[]{:S(2)}) collective-permute-start(bf16[64,1536]{1,0:T(8,128)(2,1)S(1)} %get-tuple-element.11.q0), channel_id=1, source_target_pairs={{0,16},{16,32},{32,48},{48,0},{1,17},{17,33},{33,49},{49,1},{2,18}... | collective-permute-start | bytes 589832 | tf_op jit(solution)/shard_map/ppermute | solution.py:340
  33.8 4.6 %collective-permute-start.1 = (bf16[64,1536]{1,0:T(8,128)(2,1)S(1)}, bf16[64,1536]{1,0:T(8,128)(2,1)S(1)}, u32[]{:S(2)}, u32[]{:S(2)}) collective-permute-start(bf16[64,1536]{1,0:T(8,128)(2,1)S(1)} %get-tuple-element.11.q0), channel_id=1, source_target_pairs={{0,32},{16,48},{32,0},{48,16},{1,33},{17,49},{33,1},{49,17},{2,34}... | collective-permute-start | bytes 589832 | tf_op jit(solution)/shard_map/ppermute | solution.py:340
  38.5 3.3 %collective-permute-start.2 = (bf16[64,1536]{1,0:T(8,128)(2,1)S(1)}, bf16[64,1536]{1,0:T(8,128)(2,1)S(1)}, u32[]{:S(2)}, u32[]{:S(2)}) collective-permute-start(bf16[64,1536]{1,0:T(8,128)(2,1)S(1)} %get-tuple-element.11.q0), channel_id=1, source_target_pairs={{0,48},{16,0},{32,16},{48,32},{1,49},{17,1},{33,17},{49,33},{2,50}... | collective-permute-start | bytes 589832 | tf_op jit(solution)/shard_map/ppermute | solution.py:340
  41.8 4.8 %all-to-all-done.1.kv = bf16[8,288,128]{2,1,0:T(8,128)(2,1)S(1)} async-done(((bf16[8,288,128]{2,1,0:T(8,128)(2,1)}), bf16[8,288,128]{2,1,0:T(8,128)(2,1)S(1)}, u32[]{:S(2)}, u32[]{:S(2)}) %all-to-all-start.1) | async-done | bytes 589856 | tf_op jit(solution)/shard_map/all_to_all | solution.py:338
  46.6 1.9 %collective-permute-start.3 = (bf16[8,288,128]{2,1,0:T(8,128)(2,1)S(1)}, bf16[8,288,128]{2,1,0:T(8,128)(2,1)S(1)}, u32[]{:S(2)}, u32[]{:S(2)}) collective-permute-start(bf16[8,288,128]{2,1,0:T(8,128)(2,1)S(1)} %all-to-all-done.1.kv), channel_id=1, source_target_pairs={{0,8},{8,0},{1,9},{9,1},{2,10},{10,2},{3,11},{11,3},{4,12},{12,4},... | collective-permute-start | bytes 1769480 | tf_op jit(solution)/shard_map/ppermute | solution.py:339
  48.5 0.0 collective-permute-done.q1
  48.5 0.0 collective-permute-done.1.q2
  48.6 0.0 collective-permute-done.2.q3
  48.6 0.0 copy-done
  48.6 0.0 copy-done.1
  48.6 3.9 %shard_map.67 = (bf16[8,256,640]{2,1,0:T(8,128)(2,1)S(1)}, f32[8,256,128]{2,1,0:T(8,128)S(1)}, f32[8,256,128]{2,1,0:T(8,128)S(1)}, f32[8,256,128]{2,1,0:T(8,128)S(1)}) custom-call(s32[1]{0:T(128)} %bitcast.place_ref, bf16[64,1536]{1,0:T(8,128)(2,1)S(1)} %get-tuple-element.11.q0, bf16[64,1536]{1,0:T(8,128)(2,1)S(1)} %collective-permute-done.q1, ...), custom_call_target="tpu_custom_call" | custom-call | flops 6000000000 | bytes 5000000 | tf_op jit(solution)/shard_map/pallas_call | solution.py:216
  52.5 0.0 collective-permute-done.3.kv
  52.5 3.6 %shard_map.68 = bf16[4,64,1152]{2,1,0:T(8,128)(2,1)S(1)} custom-call(s32[1]{0:T(128)} %bitcast.place_ref, bf16[8,256,640]{2,1,0:T(8,128)(2,1)S(1)} %get-tuple-element.13.q_ref, bf16[256,128]{1,0:T(8,128)(2,1)S(1)} %shard_map.65.floor_ref, bf16[8,288,128]{2,1,0:T(8,128)(2,1)S(1)} %collective-permute-done.3.kv, f32[8,256,128]{2,1,0:T(8,128)S(1)} %get-tuple-element.14.sum_ref, ...), custom_call_target="tpu_custom_call" | custom-call | flops 4000000000 | bytes 5000000 | tf_op jit(solution)/shard_map/pallas_call | solution.py:279
  56.1 27.3 %all_to_all.15 = bf16[32,8,1152]{2,1,0:T(8,128)(2,1)S(1)} all-to-all(bf16[32,8,1152]{2,1,0:T(8,128)(2,1)S(1)} %bitcast.5), channel_id=1, replica_groups=mesh['y'=8,'x'=4,'core'=2,'z'=8] {'x','z'}, dimensions={0} | all-to-all | bytes 1179648 | tf_op jit(solution)/shard_map/all_to_all | solution.py:345
  83.5 1.2 %shard_map.69 = bf16[8,8192]{1,0:T(8,128)(2,1)} custom-call(bf16[4,8,8,1152]{3,2,1,0:T(8,128)(2,1)S(1)} %bitcast.4), custom_call_target="tpu_custom_call" | custom-call | flops 1000000 | bytes 800000 | tf_op jit(solution)/shard_map/pallas_call | solution.py:318
Async XLA Ops:
  1.7 20.7 %all-to-all-start = ((bf16[8,8,2176]{2,1,0:T(8,128)(2,1)}), bf16[8,8,2176]{2,1,0:T(8,128)(2,1)S(1)}, u32[]{:S(2)}, u32[]{:S(2)}) async-start(bf16[8,8,2176]{2,1,0:T(8,128)(2,1)} %shard_map.64), calls=%async_computation | async-start | bytes 557056 | tf_op jit(solution)/shard_map/all_to_all | solution.py:336
  22.4 26.2 %copy-start = (bf16[8,512,128]{2,1,0:T(8,128)(2,1)S(1)}, bf16[8,512,128]{2,1,0:T(8,128)(2,1)}, u32[]{:S(2)}) copy-start(bf16[8,512,128]{2,1,0:T(8,128)(2,1)} %w_uk.1) | copy-start | bytes 3145732
  22.4 26.2 %copy-start.1 = (bf16[8,512,128]{2,1,0:T(8,128)(2,1)S(1)}, bf16[8,512,128]{2,1,0:T(8,128)(2,1)}, u32[]{:S(2)}) copy-start(bf16[8,512,128]{2,1,0:T(8,128)(2,1)} %w_uv.3) | copy-start | bytes 3145732
  23.3 23.3 %all-to-all-start.1 = ((bf16[8,288,128]{2,1,0:T(8,128)(2,1)}), bf16[8,288,128]{2,1,0:T(8,128)(2,1)S(1)}, u32[]{:S(2)}, u32[]{:S(2)}) async-start(bf16[8,288,128]{2,1,0:T(8,128)(2,1)} %get-tuple-element.12), calls=%async_computation.1 | async-start | bytes 1179648 | tf_op jit(solution)/shard_map/all_to_all | solution.py:338
  30.4 18.1 %collective-permute-start = (bf16[64,1536]{1,0:T(8,128)(2,1)S(1)}, bf16[64,1536]{1,0:T(8,128)(2,1)S(1)}, u32[]{:S(2)}, u32[]{:S(2)}) collective-permute-start(bf16[64,1536]{1,0:T(8,128)(2,1)S(1)} %get-tuple-element.11.q0), channel_id=1, source_target_pairs={{0,16},{16,32},{32,48},{48,0},{1,17},{17,33},{33,49},{49,1},{2,18}... | collective-permute-start | bytes 589832 | tf_op jit(solution)/shard_map/ppermute | solution.py:340
  33.8 14.7 %collective-permute-start.1 = (bf16[64,1536]{1,0:T(8,128)(2,1)S(1)}, bf16[64,1536]{1,0:T(8,128)(2,1)S(1)}, u32[]{:S(2)}, u32[]{:S(2)}) collective-permute-start(bf16[64,1536]{1,0:T(8,128)(2,1)S(1)} %get-tuple-element.11.q0), channel_id=1, source_target_pairs={{0,32},{16,48},{32,0},{48,16},{1,33},{17,49},{33,1},{49,17},{2,34}... | collective-permute-start | bytes 589832 | tf_op jit(solution)/shard_map/ppermute | solution.py:340
  38.5 10.1 %collective-permute-start.2 = (bf16[64,1536]{1,0:T(8,128)(2,1)S(1)}, bf16[64,1536]{1,0:T(8,128)(2,1)S(1)}, u32[]{:S(2)}, u32[]{:S(2)}) collective-permute-start(bf16[64,1536]{1,0:T(8,128)(2,1)S(1)} %get-tuple-element.11.q0), channel_id=1, source_target_pairs={{0,48},{16,0},{32,16},{48,32},{1,49},{17,1},{33,17},{49,33},{2,50}... | collective-permute-start | bytes 589832 | tf_op jit(solution)/shard_map/ppermute | solution.py:340
  46.6 5.9 %collective-permute-start.3 = (bf16[8,288,128]{2,1,0:T(8,128)(2,1)S(1)}, bf16[8,288,128]{2,1,0:T(8,128)(2,1)S(1)}, u32[]{:S(2)}, u32[]{:S(2)}) collective-permute-start(bf16[8,288,128]{2,1,0:T(8,128)(2,1)S(1)} %all-to-all-done.1.kv), channel_id=1, source_target_pairs={{0,8},{8,0},{1,9},{9,1},{2,10},{10,2},{3,11},{11,3},{4,12},{12,4},... | collective-permute-start | bytes 1769480 | tf_op jit(solution)/shard_map/ppermute | solution.py:339

commit v12 on v11

--- a/solution.py
+++ b/solution.py
@@ -200,7 +200,7 @@
             fill_queries(2 * p + 3)
             ahead = pair_scores(q_ref, floor, keys, p + 1)
         top = jnp.max(s, axis=1, keepdims=True)
-        weight = jnp.exp2((s - top) * SCALE2)
+        weight = jnp.exp2(s * SCALE2 - top * SCALE2)
         sums, totals = weigh(weight, values)
         for i in range(2):
             sum_ref[2 * p + i] = sums[i]
@@ -246,7 +246,7 @@
         old_top = top_ref[pair].reshape(2 * rows, STAT)
         top = jnp.maximum(old_top, jnp.max(s, axis=1, keepdims=True))
         shrink = jnp.exp2((old_top - top) * SCALE2)
-        weight = jnp.exp2((s - wide(top, NY * SPAN // STAT)) * SCALE2)
+        weight = jnp.exp2(s * SCALE2 - wide(top * SCALE2, NY * SPAN // STAT))
         sums, totals = weigh(weight, values)
         for i in range(2):
             h = 2 * p + i

time: 85.2 us -> 85.4 us (level)
  no operation moved by 1% of the time
where the time goes in v12:
time: 85.4 us; the launch traced here: 84.9 us
  starting transfers between devices  30.3 us (35%)
  blocking collectives  27.3 us (32%)
  waiting for transfers between devices  14.2 us (17%)
  Pallas kernels  12.2 us (14%)
    all_to_all x1, blocking collectives, on_device(): lax.all_to_all(partial, ('x', 'z'), split_axis=0, concat_axis=0, tiled=True)  27.3 us
    ppermute x3, starting transfers between devices, on_device(): lax.ppermute(q_own, 'x', along_x(step))  11.4 us
    all_to_all x1, starting transfers between devices, on_device(): lax.all_to_all(both, 'z', split_axis=0, concat_axis=0, tiled=True)  9.96 us
    all_to_all x1, waiting for transfers between devices, on_device(): lax.all_to_all(both, 'z', split_axis=0, concat_axis=0, tiled=True)  9.42 us
    all_to_all x1, starting transfers between devices, on_device(): kv_own = lax.all_to_all(kv, 'y', split_axis=0, concat_axis=0, tiled=True)  7.1 us
    all_to_all x1, waiting for transfers between devices, on_device(): kv_own = lax.all_to_all(kv, 'y', split_axis=0, concat_axis=0, tiled=True)  4.8 us
    pallas_call x1, Pallas kernels, attend_own(): pl.pallas_call(own_kernel, out_shape=[jax.ShapeDtypeStruct((HEADS, rows,...  4.02 us
    pallas_call x1, Pallas kernels, attend_other(): pl.pallas_call(other_kernel, out_shape=jax.ShapeDtypeStruct((NX, SPAN, HE...  3.73 us
  transfers between devices with their start and end apart: 6, of which 2 were waited for; matrix products, arithmetic and copies ran while one was open for 1% of the time, Pallas kernels for 5%

profile of v12, /device:TPU:64, one launch (start us, length us, event | category | flops | bytes accessed | tf_op | source)
XLA Modules:
  0.0 84.9 jit_solution(14812711941292875573)
XLA Ops:
  0.0 1.7 %shard_map.64 = bf16[8,8,2176]{2,1,0:T(8,128)(2,1)} custom-call(bf16[8,12288]{1,0:T(8,128)(2,1)} %q_ref.1, bf16[8,512]{1,0:T(8,128)(2,1)} %lat_ref.1, bf16[8,64]{1,0:T(8,128)(2,1)} %rope_ref.1), custom_call_target="tpu_custom_call" | custom-call | flops 1000000 | bytes 500000 | tf_op jit(solution)/shard_map/pallas_call | solution.py:50
  1.7 10.0 %all-to-all-start = ((bf16[8,8,2176]{2,1,0:T(8,128)(2,1)}), bf16[8,8,2176]{2,1,0:T(8,128)(2,1)S(1)}, u32[]{:S(2)}, u32[]{:S(2)}) async-start(bf16[8,8,2176]{2,1,0:T(8,128)(2,1)} %shard_map.64), calls=%async_computation | async-start | bytes 557056 | tf_op jit(solution)/shard_map/all_to_all | solution.py:336
  11.6 0.7 pad_add_fusion.info_ref
  12.4 0.6 shard_map.65.floor_ref
  13.0 9.4 %all-to-all-done = bf16[8,8,2176]{2,1,0:T(8,128)(2,1)S(1)} async-done(((bf16[8,8,2176]{2,1,0:T(8,128)(2,1)}), bf16[8,8,2176]{2,1,0:T(8,128)(2,1)S(1)}, u32[]{:S(2)}, u32[]{:S(2)}) %all-to-all-start) | async-done | bytes 278560 | tf_op jit(solution)/shard_map/all_to_all | solution.py:336
  22.4 0.0 copy-start
  22.4 0.0 copy-start.1
  22.4 0.9 %shard_map.66 = (bf16[64,1536]{1,0:T(8,128)(2,1)S(1)}, bf16[8,288,128]{2,1,0:T(8,128)(2,1)}) custom-call(bf16[64,2176]{1,0:T(8,128)(2,1)S(1)} %bitcast.6, bf16[256,128]{1,0:T(8,128)(2,1)S(1)} %shard_map.65.floor_ref), custom_call_target="tpu_custom_call" | custom-call | flops 4000000000 | bytes 1000000 | tf_op jit(solution)/shard_map/pallas_call | solution.py:74
  23.3 7.1 %all-to-all-start.1 = ((bf16[8,288,128]{2,1,0:T(8,128)(2,1)}), bf16[8,288,128]{2,1,0:T(8,128)(2,1)S(1)}, u32[]{:S(2)}, u32[]{:S(2)}) async-start(bf16[8,288,128]{2,1,0:T(8,128)(2,1)} %get-tuple-element.12), calls=%async_computation.1 | async-start | bytes 1179648 | tf_op jit(solution)/shard_map/all_to_all | solution.py:338
  30.4 3.4 %collective-permute-start = (bf16[64,1536]{1,0:T(8,128)(2,1)S(1)}, bf16[64,1536]{1,0:T(8,128)(2,1)S(1)}, u32[]{:S(2)}, u32[]{:S(2)}) collective-permute-start(bf16[64,1536]{1,0:T(8,128)(2,1)S(1)} %get-tuple-element.11.q0), channel_id=1, source_target_pairs={{0,16},{16,32},{32,48},{48,0},{1,17},{17,33},{33,49},{49,1},{2,18}... | collective-permute-start | bytes 589832 | tf_op jit(solution)/shard_map/ppermute | solution.py:340
  33.8 4.6 %collective-permute-start.1 = (bf16[64,1536]{1,0:T(8,128)(2,1)S(1)}, bf16[64,1536]{1,0:T(8,128)(2,1)S(1)}, u32[]{:S(2)}, u32[]{:S(2)}) collective-permute-start(bf16[64,1536]{1,0:T(8,128)(2,1)S(1)} %get-tuple-element.11.q0), channel_id=1, source_target_pairs={{0,32},{16,48},{32,0},{48,16},{1,33},{17,49},{33,1},{49,17},{2,34}... | collective-permute-start | bytes 589832 | tf_op jit(solution)/shard_map/ppermute | solution.py:340
  38.5 3.3 %collective-permute-start.2 = (bf16[64,1536]{1,0:T(8,128)(2,1)S(1)}, bf16[64,1536]{1,0:T(8,128)(2,1)S(1)}, u32[]{:S(2)}, u32[]{:S(2)}) collective-permute-start(bf16[64,1536]{1,0:T(8,128)(2,1)S(1)} %get-tuple-element.11.q0), channel_id=1, source_target_pairs={{0,48},{16,0},{32,16},{48,32},{1,49},{17,1},{33,17},{49,33},{2,50}... | collective-permute-start | bytes 589832 | tf_op jit(solution)/shard_map/ppermute | solution.py:340
  41.8 4.8 %all-to-all-done.1.kv = bf16[8,288,128]{2,1,0:T(8,128)(2,1)S(1)} async-done(((bf16[8,288,128]{2,1,0:T(8,128)(2,1)}), bf16[8,288,128]{2,1,0:T(8,128)(2,1)S(1)}, u32[]{:S(2)}, u32[]{:S(2)}) %all-to-all-start.1) | async-done | bytes 589856 | tf_op jit(solution)/shard_map/all_to_all | solution.py:338
  46.6 1.9 %collective-permute-start.3 = (bf16[8,288,128]{2,1,0:T(8,128)(2,1)S(1)}, bf16[8,288,128]{2,1,0:T(8,128)(2,1)S(1)}, u32[]{:S(2)}, u32[]{:S(2)}) collective-permute-start(bf16[8,288,128]{2,1,0:T(8,128)(2,1)S(1)} %all-to-all-done.1.kv), channel_id=1, source_target_pairs={{0,8},{8,0},{1,9},{9,1},{2,10},{10,2},{3,11},{11,3},{4,12},{12,4},... | collective-permute-start | bytes 1769480 | tf_op jit(solution)/shard_map/ppermute | solution.py:339
  48.5 0.0 collective-permute-done.q1
  48.5 0.0 collective-permute-done.1.q2
  48.6 0.0 collective-permute-done.2.q3
  48.6 0.0 copy-done
  48.6 0.0 copy-done.1
  48.6 4.0 %shard_map.67 = (bf16[8,256,640]{2,1,0:T(8,128)(2,1)S(1)}, f32[8,256,128]{2,1,0:T(8,128)S(1)}, f32[8,256,128]{2,1,0:T(8,128)S(1)}, f32[8,256,128]{2,1,0:T(8,128)S(1)}) custom-call(s32[1]{0:T(128)} %bitcast.place_ref, bf16[64,1536]{1,0:T(8,128)(2,1)S(1)} %get-tuple-element.11.q0, bf16[64,1536]{1,0:T(8,128)(2,1)S(1)} %collective-permute-done.q1, ...), custom_call_target="tpu_custom_call" | custom-call | flops 6000000000 | bytes 5000000 | tf_op jit(solution)/shard_map/pallas_call | solution.py:216
  52.6 0.0 collective-permute-done.3.kv
  52.6 3.7 %shard_map.68 = bf16[4,64,1152]{2,1,0:T(8,128)(2,1)S(1)} custom-call(s32[1]{0:T(128)} %bitcast.place_ref, bf16[8,256,640]{2,1,0:T(8,128)(2,1)S(1)} %get-tuple-element.13.q_ref, bf16[256,128]{1,0:T(8,128)(2,1)S(1)} %shard_map.65.floor_ref, bf16[8,288,128]{2,1,0:T(8,128)(2,1)S(1)} %collective-permute-done.3.kv, f32[8,256,128]{2,1,0:T(8,128)S(1)} %get-tuple-element.14.sum_ref, ...), custom_call_target="tpu_custom_call" | custom-call | flops 4000000000 | bytes 5000000 | tf_op jit(solution)/shard_map/pallas_call | solution.py:279
  56.4 27.3 %all_to_all.15 = bf16[32,8,1152]{2,1,0:T(8,128)(2,1)S(1)} all-to-all(bf16[32,8,1152]{2,1,0:T(8,128)(2,1)S(1)} %bitcast.5), channel_id=1, replica_groups=mesh['y'=8,'x'=4,'core'=2,'z'=8] {'x','z'}, dimensions={0} | all-to-all | bytes 1179648 | tf_op jit(solution)/shard_map/all_to_all | solution.py:345
  83.7 1.2 %shard_map.69 = bf16[8,8192]{1,0:T(8,128)(2,1)} custom-call(bf16[4,8,8,1152]{3,2,1,0:T(8,128)(2,1)S(1)} %bitcast.4), custom_call_target="tpu_custom_call" | custom-call | flops 1000000 | bytes 800000 | tf_op jit(solution)/shard_map/pallas_call | solution.py:318
Async XLA Ops:
  1.7 20.7 %all-to-all-start = ((bf16[8,8,2176]{2,1,0:T(8,128)(2,1)}), bf16[8,8,2176]{2,1,0:T(8,128)(2,1)S(1)}, u32[]{:S(2)}, u32[]{:S(2)}) async-start(bf16[8,8,2176]{2,1,0:T(8,128)(2,1)} %shard_map.64), calls=%async_computation | async-start | bytes 557056 | tf_op jit(solution)/shard_map/all_to_all | solution.py:336
  22.4 26.2 %copy-start = (bf16[8,512,128]{2,1,0:T(8,128)(2,1)S(1)}, bf16[8,512,128]{2,1,0:T(8,128)(2,1)}, u32[]{:S(2)}) copy-start(bf16[8,512,128]{2,1,0:T(8,128)(2,1)} %w_uk.1) | copy-start | bytes 3145732
  22.4 26.2 %copy-start.1 = (bf16[8,512,128]{2,1,0:T(8,128)(2,1)S(1)}, bf16[8,512,128]{2,1,0:T(8,128)(2,1)}, u32[]{:S(2)}) copy-start(bf16[8,512,128]{2,1,0:T(8,128)(2,1)} %w_uv.3) | copy-start | bytes 3145732
  23.3 23.3 %all-to-all-start.1 = ((bf16[8,288,128]{2,1,0:T(8,128)(2,1)}), bf16[8,288,128]{2,1,0:T(8,128)(2,1)S(1)}, u32[]{:S(2)}, u32[]{:S(2)}) async-start(bf16[8,288,128]{2,1,0:T(8,128)(2,1)} %get-tuple-element.12), calls=%async_computation.1 | async-start | bytes 1179648 | tf_op jit(solution)/shard_map/all_to_all | solution.py:338
  30.4 18.1 %collective-permute-start = (bf16[64,1536]{1,0:T(8,128)(2,1)S(1)}, bf16[64,1536]{1,0:T(8,128)(2,1)S(1)}, u32[]{:S(2)}, u32[]{:S(2)}) collective-permute-start(bf16[64,1536]{1,0:T(8,128)(2,1)S(1)} %get-tuple-element.11.q0), channel_id=1, source_target_pairs={{0,16},{16,32},{32,48},{48,0},{1,17},{17,33},{33,49},{49,1},{2,18}... | collective-permute-start | bytes 589832 | tf_op jit(solution)/shard_map/ppermute | solution.py:340
  33.8 14.7 %collective-permute-start.1 = (bf16[64,1536]{1,0:T(8,128)(2,1)S(1)}, bf16[64,1536]{1,0:T(8,128)(2,1)S(1)}, u32[]{:S(2)}, u32[]{:S(2)}) collective-permute-start(bf16[64,1536]{1,0:T(8,128)(2,1)S(1)} %get-tuple-element.11.q0), channel_id=1, source_target_pairs={{0,32},{16,48},{32,0},{48,16},{1,33},{17,49},{33,1},{49,17},{2,34}... | collective-permute-start | bytes 589832 | tf_op jit(solution)/shard_map/ppermute | solution.py:340
  38.5 10.1 %collective-permute-start.2 = (bf16[64,1536]{1,0:T(8,128)(2,1)S(1)}, bf16[64,1536]{1,0:T(8,128)(2,1)S(1)}, u32[]{:S(2)}, u32[]{:S(2)}) collective-permute-start(bf16[64,1536]{1,0:T(8,128)(2,1)S(1)} %get-tuple-element.11.q0), channel_id=1, source_target_pairs={{0,48},{16,0},{32,16},{48,32},{1,49},{17,1},{33,17},{49,33},{2,50}... | collective-permute-start | bytes 589832 | tf_op jit(solution)/shard_map/ppermute | solution.py:340
  46.6 6.0 %collective-permute-start.3 = (bf16[8,288,128]{2,1,0:T(8,128)(2,1)S(1)}, bf16[8,288,128]{2,1,0:T(8,128)(2,1)S(1)}, u32[]{:S(2)}, u32[]{:S(2)}) collective-permute-start(bf16[8,288,128]{2,1,0:T(8,128)(2,1)S(1)} %all-to-all-done.1.kv), channel_id=1, source_target_pairs={{0,8},{8,0},{1,9},{9,1},{2,10},{10,2},{3,11},{11,3},{4,12},{12,4},... | collective-permute-start | bytes 1769480 | tf_op jit(solution)/shard_map/ppermute | solution.py:339

commit v13 on v11

--- a/solution.py
+++ b/solution.py
@@ -173,7 +173,7 @@
     )(info)
 
 
-def own_kernel(place_ref, q0, q1, q2, q3, w_uk, w_uv, kv, floor_ref, q_ref, sum_ref, top_ref, total_ref, keys):
+def own_kernel(place_ref, q0, q3, q2, q1, w_uk, w_uv, kv, floor_ref, q_ref, sum_ref, top_ref, total_ref, keys):
     rows = NX * SPAN
     floor = floor_ref[...]
     none = jnp.zeros((rows, WIDE - DL - DR), jnp.bfloat16)
@@ -226,7 +226,7 @@
         scratch_shapes=[pltpu.VMEM((NY * SPAN, WIDE + EXTRA), jnp.bfloat16)],
         compiler_params=pltpu.CompilerParams(vmem_limit_bytes=20 * 1024 * 1024),
         cost_estimate=pl.CostEstimate(flops=6_000_000_000, bytes_accessed=5_000_000, transcendentals=1_000_000),
-    )(place, *qs, w_uk, w_uv, kv, floor)
+    )(place, qs[0], qs[3], qs[2], qs[1], w_uk, w_uv, kv, floor)
 
 
 def other_kernel(place_ref, q_ref, floor_ref, kv, sum_ref, top_ref, total_ref, w_uv, out_ref, keys):
@@ -297,16 +297,27 @@
     shares = [jnp.exp2(level - top) for level in levels]
     whole = functools.reduce(jnp.add, shares)
     shares = [share / whole for share in shares]
+    lane = lax.broadcasted_iota(jnp.int32, (STAT, HEADS * DV), 0)
+    col = lax.broadcasted_iota(jnp.int32, (STAT, HEADS * DV), 1)
+    spread_ones = jnp.where(col // DV == lane, 1.0, 0.0).astype(jnp.bfloat16)
+    share = jnp.concatenate(shares, axis=0)
+    high = share.astype(jnp.bfloat16)
+    rest = share - high.astype(jnp.float32)
+    middle = rest.astype(jnp.bfloat16)
+    low = (rest - middle.astype(jnp.float32)).astype(jnp.bfloat16)
+    pieces = jnp.concatenate([high, middle, low], axis=0)
+    broad = jnp.dot(pieces, spread_ones, preferred_element_type=jnp.float32)
+    count = NX * SPAN
+    broad = broad[:count] + broad[count : 2 * count] + broad[2 * count :]
     tokens = SPAN // NZ
     moves = []
     for z in range(NZ):
-        here = slice(z * tokens, (z + 1) * tokens)
-        for h in range(HEADS):
-            acc = jnp.zeros((tokens, DV), jnp.float32)
-            for x in range(NX):
-                acc = acc + shares[x][here, h : h + 1] * p_ref[x, z, :, h * DV : (h + 1) * DV].astype(jnp.float32)
-            held[:, (z * HEADS + h) * DV : (z * HEADS + h + 1) * DV] = acc.astype(jnp.bfloat16)
+        acc = jnp.zeros((tokens, HEADS * DV), jnp.float32)
+        for x in range(NX):
+            here = slice(x * SPAN + z * tokens, x * SPAN + (z + 1) * tokens)
+            acc = acc + broad[here] * p_ref[x, z, :, : HEADS * DV].astype(jnp.float32)
         cols = slice(z * HEADS * DV, (z + 1) * HEADS * DV)
+        held[:, cols] = acc.astype(jnp.bfloat16)
         moves.append(pltpu.make_async_copy(held.at[:, cols], out_ref.at[:, cols], sems.at[z]))
         moves[-1].start()
     for move in moves:

time: 85.2 us -> 85.3 us (level)
  waiting for transfers between devices: 14.2 us -> 15.4 us
  starting transfers between devices: 30.3 us -> 29.1 us
    all_to_all x1, waiting for transfers between devices: 4.8 us -> 6.01 us  [on_device(): kv_own = lax.all_to_all(kv, 'y', split_axis=0, concat_axis=0, tiled=True)]
    ppermute x3, starting transfers between devices: 11.4 us -> 10.2 us  [on_device(): lax.ppermute(q_own, 'x', along_x(step))]
where the time goes in v13:
time: 85.3 us; the launch traced here: 84.8 us
  starting transfers between devices  29.1 us (34%)
  blocking collectives  27.3 us (32%)
  waiting for transfers between devices  15.4 us (18%)
  Pallas kernels  12.1 us (14%)
    all_to_all x1, blocking collectives, on_device(): lax.all_to_all(partial, ('x', 'z'), split_axis=0, concat_axis=0, tiled=True)  27.3 us
    ppermute x3, starting transfers between devices, on_device(): lax.ppermute(q_own, 'x', along_x(step))  10.2 us
    all_to_all x1, starting transfers between devices, on_device(): lax.all_to_all(both, 'z', split_axis=0, concat_axis=0, tiled=True)  9.96 us
    all_to_all x1, waiting for transfers between devices, on_device(): lax.all_to_all(both, 'z', split_axis=0, concat_axis=0, tiled=True)  9.42 us
    all_to_all x1, starting transfers between devices, on_device(): kv_own = lax.all_to_all(kv, 'y', split_axis=0, concat_axis=0, tiled=True)  7.1 us
    all_to_all x1, waiting for transfers between devices, on_device(): kv_own = lax.all_to_all(kv, 'y', split_axis=0, concat_axis=0, tiled=True)  6.01 us
    pallas_call x1, Pallas kernels, attend_own(): pl.pallas_call(own_kernel, out_shape=[jax.ShapeDtypeStruct((HEADS, rows,...  3.9 us
    pallas_call x1, Pallas kernels, attend_other(): pl.pallas_call(other_kernel, out_shape=jax.ShapeDtypeStruct((NX, SPAN, HE...  3.64 us
  transfers between devices with their start and end apart: 6, of which 2 were waited for; matrix products, arithmetic and copies ran while one was open for 1% of the time, Pallas kernels for 5%

profile of v13, /device:TPU:64, one launch (start us, length us, event | category | flops | bytes accessed | tf_op | source)
XLA Modules:
  0.0 84.8 jit_solution(5340851247330042114)
XLA Ops:
  0.0 1.7 %shard_map.64 = bf16[8,8,2176]{2,1,0:T(8,128)(2,1)} custom-call(bf16[8,12288]{1,0:T(8,128)(2,1)} %q_ref.1, bf16[8,512]{1,0:T(8,128)(2,1)} %lat_ref.1, bf16[8,64]{1,0:T(8,128)(2,1)} %rope_ref.1), custom_call_target="tpu_custom_call" | custom-call | flops 1000000 | bytes 500000 | tf_op jit(solution)/shard_map/pallas_call | solution.py:50
  1.7 10.0 %all-to-all-start = ((bf16[8,8,2176]{2,1,0:T(8,128)(2,1)}), bf16[8,8,2176]{2,1,0:T(8,128)(2,1)S(1)}, u32[]{:S(2)}, u32[]{:S(2)}) async-start(bf16[8,8,2176]{2,1,0:T(8,128)(2,1)} %shard_map.64), calls=%async_computation | async-start | bytes 557056 | tf_op jit(solution)/shard_map/all_to_all | solution.py:347
  11.6 0.7 pad_add_fusion.info_ref
  12.4 0.6 shard_map.65.floor_ref
  13.0 9.4 %all-to-all-done = bf16[8,8,2176]{2,1,0:T(8,128)(2,1)S(1)} async-done(((bf16[8,8,2176]{2,1,0:T(8,128)(2,1)}), bf16[8,8,2176]{2,1,0:T(8,128)(2,1)S(1)}, u32[]{:S(2)}, u32[]{:S(2)}) %all-to-all-start) | async-done | bytes 278560 | tf_op jit(solution)/shard_map/all_to_all | solution.py:347
  22.4 0.0 copy-start
  22.4 0.0 copy-start.1
  22.4 0.9 %shard_map.66 = (bf16[64,1536]{1,0:T(8,128)(2,1)S(1)}, bf16[8,288,128]{2,1,0:T(8,128)(2,1)}) custom-call(bf16[64,2176]{1,0:T(8,128)(2,1)S(1)} %bitcast.6, bf16[256,128]{1,0:T(8,128)(2,1)S(1)} %shard_map.65.floor_ref), custom_call_target="tpu_custom_call" | custom-call | flops 4000000000 | bytes 1000000 | tf_op jit(solution)/shard_map/pallas_call | solution.py:74
  23.3 7.1 %all-to-all-start.1 = ((bf16[8,288,128]{2,1,0:T(8,128)(2,1)}), bf16[8,288,128]{2,1,0:T(8,128)(2,1)S(1)}, u32[]{:S(2)}, u32[]{:S(2)}) async-start(bf16[8,288,128]{2,1,0:T(8,128)(2,1)} %get-tuple-element.12), calls=%async_computation.1 | async-start | bytes 1179648 | tf_op jit(solution)/shard_map/all_to_all | solution.py:349
  30.4 4.7 %collective-permute-start = (bf16[64,1536]{1,0:T(8,128)(2,1)S(1)}, bf16[64,1536]{1,0:T(8,128)(2,1)S(1)}, u32[]{:S(2)}, u32[]{:S(2)}) collective-permute-start(bf16[64,1536]{1,0:T(8,128)(2,1)S(1)} %get-tuple-element.11.q0), channel_id=1, source_target_pairs={{0,48},{16,0},{32,16},{48,32},{1,49},{17,1},{33,17},{49,33},{2,50}... | collective-permute-start | bytes 589832 | tf_op jit(solution)/shard_map/ppermute | solution.py:351
  35.1 2.7 %collective-permute-start.1 = (bf16[64,1536]{1,0:T(8,128)(2,1)S(1)}, bf16[64,1536]{1,0:T(8,128)(2,1)S(1)}, u32[]{:S(2)}, u32[]{:S(2)}) collective-permute-start(bf16[64,1536]{1,0:T(8,128)(2,1)S(1)} %get-tuple-element.11.q0), channel_id=1, source_target_pairs={{0,32},{16,48},{32,0},{48,16},{1,33},{17,49},{33,1},{49,17},{2,34}... | collective-permute-start | bytes 589832 | tf_op jit(solution)/shard_map/ppermute | solution.py:351
  37.8 2.8 %collective-permute-start.2 = (bf16[64,1536]{1,0:T(8,128)(2,1)S(1)}, bf16[64,1536]{1,0:T(8,128)(2,1)S(1)}, u32[]{:S(2)}, u32[]{:S(2)}) collective-permute-start(bf16[64,1536]{1,0:T(8,128)(2,1)S(1)} %get-tuple-element.11.q0), channel_id=1, source_target_pairs={{0,16},{16,32},{32,48},{48,0},{1,17},{17,33},{33,49},{49,1},{2,18}... | collective-permute-start | bytes 589832 | tf_op jit(solution)/shard_map/ppermute | solution.py:351
  40.6 6.0 %all-to-all-done.1.kv = bf16[8,288,128]{2,1,0:T(8,128)(2,1)S(1)} async-done(((bf16[8,288,128]{2,1,0:T(8,128)(2,1)}), bf16[8,288,128]{2,1,0:T(8,128)(2,1)S(1)}, u32[]{:S(2)}, u32[]{:S(2)}) %all-to-all-start.1) | async-done | bytes 589856 | tf_op jit(solution)/shard_map/all_to_all | solution.py:349
  46.6 1.9 %collective-permute-start.3 = (bf16[8,288,128]{2,1,0:T(8,128)(2,1)S(1)}, bf16[8,288,128]{2,1,0:T(8,128)(2,1)S(1)}, u32[]{:S(2)}, u32[]{:S(2)}) collective-permute-start(bf16[8,288,128]{2,1,0:T(8,128)(2,1)S(1)} %all-to-all-done.1.kv), channel_id=1, source_target_pairs={{0,8},{8,0},{1,9},{9,1},{2,10},{10,2},{3,11},{11,3},{4,12},{12,4},... | collective-permute-start | bytes 1769480 | tf_op jit(solution)/shard_map/ppermute | solution.py:350
  48.5 0.0 collective-permute-done.q3
  48.5 0.0 collective-permute-done.1.q2
  48.6 0.0 collective-permute-done.2.q1
  48.6 0.0 copy-done
  48.6 0.0 copy-done.1
  48.6 3.9 %shard_map.67 = (bf16[8,256,640]{2,1,0:T(8,128)(2,1)S(1)}, f32[8,256,128]{2,1,0:T(8,128)S(1)}, f32[8,256,128]{2,1,0:T(8,128)S(1)}, f32[8,256,128]{2,1,0:T(8,128)S(1)}) custom-call(s32[1]{0:T(128)} %bitcast.place_ref, bf16[64,1536]{1,0:T(8,128)(2,1)S(1)} %get-tuple-element.11.q0, bf16[64,1536]{1,0:T(8,128)(2,1)S(1)} %collective-permute-done.q3, ...), custom_call_target="tpu_custom_call" | custom-call | flops 6000000000 | bytes 5000000 | tf_op jit(solution)/shard_map/pallas_call | solution.py:216
  52.5 0.0 collective-permute-done.3.kv
  52.5 3.6 %shard_map.68 = bf16[4,64,1152]{2,1,0:T(8,128)(2,1)S(1)} custom-call(s32[1]{0:T(128)} %bitcast.place_ref, bf16[8,256,640]{2,1,0:T(8,128)(2,1)S(1)} %get-tuple-element.13.q_ref, bf16[256,128]{1,0:T(8,128)(2,1)S(1)} %shard_map.65.floor_ref, bf16[8,288,128]{2,1,0:T(8,128)(2,1)S(1)} %collective-permute-done.3.kv, f32[8,256,128]{2,1,0:T(8,128)S(1)} %get-tuple-element.14.sum_ref, ...), custom_call_target="tpu_custom_call" | custom-call | flops 4000000000 | bytes 5000000 | tf_op jit(solution)/shard_map/pallas_call | solution.py:279
  56.1 27.3 %all_to_all.15 = bf16[32,8,1152]{2,1,0:T(8,128)(2,1)S(1)} all-to-all(bf16[32,8,1152]{2,1,0:T(8,128)(2,1)S(1)} %bitcast.5), channel_id=1, replica_groups=mesh['y'=8,'x'=4,'core'=2,'z'=8] {'x','z'}, dimensions={0} | all-to-all | bytes 1179648 | tf_op jit(solution)/shard_map/all_to_all | solution.py:356
  83.5 1.3 %shard_map.69 = bf16[8,8192]{1,0:T(8,128)(2,1)} custom-call(bf16[4,8,8,1152]{3,2,1,0:T(8,128)(2,1)S(1)} %bitcast.4), custom_call_target="tpu_custom_call" | custom-call | flops 1000000 | bytes 800000 | tf_op jit(solution)/shard_map/pallas_call | solution.py:329
Async XLA Ops:
  1.7 20.7 %all-to-all-start = ((bf16[8,8,2176]{2,1,0:T(8,128)(2,1)}), bf16[8,8,2176]{2,1,0:T(8,128)(2,1)S(1)}, u32[]{:S(2)}, u32[]{:S(2)}) async-start(bf16[8,8,2176]{2,1,0:T(8,128)(2,1)} %shard_map.64), calls=%async_computation | async-start | bytes 557056 | tf_op jit(solution)/shard_map/all_to_all | solution.py:347
  22.4 26.2 %copy-start = (bf16[8,512,128]{2,1,0:T(8,128)(2,1)S(1)}, bf16[8,512,128]{2,1,0:T(8,128)(2,1)}, u32[]{:S(2)}) copy-start(bf16[8,512,128]{2,1,0:T(8,128)(2,1)} %w_uk.1) | copy-start | bytes 3145732
  22.4 26.2 %copy-start.1 = (bf16[8,512,128]{2,1,0:T(8,128)(2,1)S(1)}, bf16[8,512,128]{2,1,0:T(8,128)(2,1)}, u32[]{:S(2)}) copy-start(bf16[8,512,128]{2,1,0:T(8,128)(2,1)} %w_uv.3) | copy-start | bytes 3145732
  23.3 23.3 %all-to-all-start.1 = ((bf16[8,288,128]{2,1,0:T(8,128)(2,1)}), bf16[8,288,128]{2,1,0:T(8,128)(2,1)S(1)}, u32[]{:S(2)}, u32[]{:S(2)}) async-start(bf16[8,288,128]{2,1,0:T(8,128)(2,1)} %get-tuple-element.12), calls=%async_computation.1 | async-start | bytes 1179648 | tf_op jit(solution)/shard_map/all_to_all | solution.py:349
  30.4 18.1 %collective-permute-start = (bf16[64,1536]{1,0:T(8,128)(2,1)S(1)}, bf16[64,1536]{1,0:T(8,128)(2,1)S(1)}, u32[]{:S(2)}, u32[]{:S(2)}) collective-permute-start(bf16[64,1536]{1,0:T(8,128)(2,1)S(1)} %get-tuple-element.11.q0), channel_id=1, source_target_pairs={{0,48},{16,0},{32,16},{48,32},{1,49},{17,1},{33,17},{49,33},{2,50}... | collective-permute-start | bytes 589832 | tf_op jit(solution)/shard_map/ppermute | solution.py:351
  35.1 13.5 %collective-permute-start.1 = (bf16[64,1536]{1,0:T(8,128)(2,1)S(1)}, bf16[64,1536]{1,0:T(8,128)(2,1)S(1)}, u32[]{:S(2)}, u32[]{:S(2)}) collective-permute-start(bf16[64,1536]{1,0:T(8,128)(2,1)S(1)} %get-tuple-element.11.q0), channel_id=1, source_target_pairs={{0,32},{16,48},{32,0},{48,16},{1,33},{17,49},{33,1},{49,17},{2,34}... | collective-permute-start | bytes 589832 | tf_op jit(solution)/shard_map/ppermute | solution.py:351
  37.8 10.8 %collective-permute-start.2 = (bf16[64,1536]{1,0:T(8,128)(2,1)S(1)}, bf16[64,1536]{1,0:T(8,128)(2,1)S(1)}, u32[]{:S(2)}, u32[]{:S(2)}) collective-permute-start(bf16[64,1536]{1,0:T(8,128)(2,1)S(1)} %get-tuple-element.11.q0), channel_id=1, source_target_pairs={{0,16},{16,32},{32,48},{48,0},{1,17},{17,33},{33,49},{49,1},{2,18}... | collective-permute-start | bytes 589832 | tf_op jit(solution)/shard_map/ppermute | solution.py:351
  46.6 5.9 %collective-permute-start.3 = (bf16[8,288,128]{2,1,0:T(8,128)(2,1)S(1)}, bf16[8,288,128]{2,1,0:T(8,128)(2,1)S(1)}, u32[]{:S(2)}, u32[]{:S(2)}) collective-permute-start(bf16[8,288,128]{2,1,0:T(8,128)(2,1)S(1)} %all-to-all-done.1.kv), channel_id=1, source_target_pairs={{0,8},{8,0},{1,9},{9,1},{2,10},{10,2},{3,11},{11,3},{4,12},{12,4},... | collective-permute-start | bytes 1769480 | tf_op jit(solution)/shard_map/ppermute | solution.py:350

commit v14 on v11

--- a/solution.py
+++ b/solution.py
@@ -94,13 +94,17 @@
         keys[b * SPAN : b * SPAN + HALF, DL : DL + DR] = kv[b, PACKED - HALF :, :DR]
         keys[b * SPAN + HALF : (b + 1) * SPAN, DL : DL + DR] = kv[b, PACKED - HALF :, DR:]
     keys[:, DL + DR : WIDE] = jnp.zeros((count, WIDE - DL - DR), jnp.bfloat16)
-    key = lax.broadcasted_iota(jnp.int32, (count, EXTRA), 0)
-    col = lax.broadcasted_iota(jnp.int32, (count, EXTRA), 1)
-    ones = col == key // HALF + first
+    lane = lax.broadcasted_iota(jnp.int32, (HALF, EXTRA), 1)
+    for block in range(count // HALF):
+        ones = jnp.where(lane == block + first, 1.0, 0.0).astype(jnp.bfloat16)
+        keys[block * HALF : (block + 1) * HALF, WIDE:] = ones
     if own_block is not None:
-        in_own = (key // HALF == own_block) | (key // HALF == own_block + 1)
-        ones = ones | (in_own & (col == blocks + key - own_block * HALF))
-    keys[:, WIDE:] = jnp.where(ones, 1.0, 0.0).astype(jnp.bfloat16)
+        row = lax.broadcasted_iota(jnp.int32, (HALF, EXTRA), 0)
+        for half in range(2):
+            block = own_block + half
+            here = (lane == block + first) | (lane == blocks + half * HALF + row)
+            rows = pl.ds(pl.multiple_of(block * HALF, HALF), HALF)
+            keys[rows, WIDE:] = jnp.where(here, 1.0, 0.0).astype(jnp.bfloat16)
 
 
 def pair_scores(q_ref, floor, keys, p):

time: 85.2 us -> 85.3 us (level)
  no operation moved by 1% of the time
where the time goes in v14:
time: 85.3 us; the launch traced here: 84.8 us
  starting transfers between devices  30.3 us (36%)
  blocking collectives  27.3 us (32%)
  waiting for transfers between devices  14.2 us (17%)
  Pallas kernels  12.1 us (14%)
    all_to_all x1, blocking collectives, on_device(): lax.all_to_all(partial, ('x', 'z'), split_axis=0, concat_axis=0, tiled=True)  27.3 us
    ppermute x3, starting transfers between devices, on_device(): lax.ppermute(q_own, 'x', along_x(step))  11.4 us
    all_to_all x1, starting transfers between devices, on_device(): lax.all_to_all(both, 'z', split_axis=0, concat_axis=0, tiled=True)  9.96 us
    all_to_all x1, waiting for transfers between devices, on_device(): lax.all_to_all(both, 'z', split_axis=0, concat_axis=0, tiled=True)  9.42 us
    all_to_all x1, starting transfers between devices, on_device(): kv_own = lax.all_to_all(kv, 'y', split_axis=0, concat_axis=0, tiled=True)  7.1 us
    all_to_all x1, waiting for transfers between devices, on_device(): kv_own = lax.all_to_all(kv, 'y', split_axis=0, concat_axis=0, tiled=True)  4.8 us
    pallas_call x1, Pallas kernels, attend_own(): pl.pallas_call(own_kernel, out_shape=[jax.ShapeDtypeStruct((HEADS, rows,...  3.98 us
    pallas_call x1, Pallas kernels, attend_other(): pl.pallas_call(other_kernel, out_shape=jax.ShapeDtypeStruct((NX, SPAN, HE...  3.63 us
  transfers between devices with their start and end apart: 6, of which 2 were waited for; matrix products, arithmetic and copies ran while one was open for 1% of the time, Pallas kernels for 5%

profile of v14, /device:TPU:64, one launch (start us, length us, event | category | flops | bytes accessed | tf_op | source)
XLA Modules:
  0.0 84.8 jit_solution(8175696965207704823)
XLA Ops:
  0.0 1.7 %shard_map.64 = bf16[8,8,2176]{2,1,0:T(8,128)(2,1)} custom-call(bf16[8,12288]{1,0:T(8,128)(2,1)} %q_ref.1, bf16[8,512]{1,0:T(8,128)(2,1)} %lat_ref.1, bf16[8,64]{1,0:T(8,128)(2,1)} %rope_ref.1), custom_call_target="tpu_custom_call" | custom-call | flops 1000000 | bytes 500000 | tf_op jit(solution)/shard_map/pallas_call | solution.py:50
  1.7 10.0 %all-to-all-start = ((bf16[8,8,2176]{2,1,0:T(8,128)(2,1)}), bf16[8,8,2176]{2,1,0:T(8,128)(2,1)S(1)}, u32[]{:S(2)}, u32[]{:S(2)}) async-start(bf16[8,8,2176]{2,1,0:T(8,128)(2,1)} %shard_map.64), calls=%async_computation | async-start | bytes 557056 | tf_op jit(solution)/shard_map/all_to_all | solution.py:340
  11.6 0.7 pad_add_fusion.info_ref
  12.4 0.6 shard_map.65.floor_ref
  13.0 9.4 %all-to-all-done = bf16[8,8,2176]{2,1,0:T(8,128)(2,1)S(1)} async-done(((bf16[8,8,2176]{2,1,0:T(8,128)(2,1)}), bf16[8,8,2176]{2,1,0:T(8,128)(2,1)S(1)}, u32[]{:S(2)}, u32[]{:S(2)}) %all-to-all-start) | async-done | bytes 278560 | tf_op jit(solution)/shard_map/all_to_all | solution.py:340
  22.4 0.0 copy-start
  22.4 0.0 copy-start.1
  22.4 0.9 %shard_map.66 = (bf16[64,1536]{1,0:T(8,128)(2,1)S(1)}, bf16[8,288,128]{2,1,0:T(8,128)(2,1)}) custom-call(bf16[64,2176]{1,0:T(8,128)(2,1)S(1)} %bitcast.6, bf16[256,128]{1,0:T(8,128)(2,1)S(1)} %shard_map.65.floor_ref), custom_call_target="tpu_custom_call" | custom-call | flops 4000000000 | bytes 1000000 | tf_op jit(solution)/shard_map/pallas_call | solution.py:74
  23.3 7.1 %all-to-all-start.1 = ((bf16[8,288,128]{2,1,0:T(8,128)(2,1)}), bf16[8,288,128]{2,1,0:T(8,128)(2,1)S(1)}, u32[]{:S(2)}, u32[]{:S(2)}) async-start(bf16[8,288,128]{2,1,0:T(8,128)(2,1)} %get-tuple-element.12), calls=%async_computation.1 | async-start | bytes 1179648 | tf_op jit(solution)/shard_map/all_to_all | solution.py:342
  30.4 3.4 %collective-permute-start = (bf16[64,1536]{1,0:T(8,128)(2,1)S(1)}, bf16[64,1536]{1,0:T(8,128)(2,1)S(1)}, u32[]{:S(2)}, u32[]{:S(2)}) collective-permute-start(bf16[64,1536]{1,0:T(8,128)(2,1)S(1)} %get-tuple-element.11.q0), channel_id=1, source_target_pairs={{0,16},{16,32},{32,48},{48,0},{1,17},{17,33},{33,49},{49,1},{2,18}... | collective-permute-start | bytes 589832 | tf_op jit(solution)/shard_map/ppermute | solution.py:344
  33.8 4.6 %collective-permute-start.1 = (bf16[64,1536]{1,0:T(8,128)(2,1)S(1)}, bf16[64,1536]{1,0:T(8,128)(2,1)S(1)}, u32[]{:S(2)}, u32[]{:S(2)}) collective-permute-start(bf16[64,1536]{1,0:T(8,128)(2,1)S(1)} %get-tuple-element.11.q0), channel_id=1, source_target_pairs={{0,32},{16,48},{32,0},{48,16},{1,33},{17,49},{33,1},{49,17},{2,34}... | collective-permute-start | bytes 589832 | tf_op jit(solution)/shard_map/ppermute | solution.py:344
  38.5 3.3 %collective-permute-start.2 = (bf16[64,1536]{1,0:T(8,128)(2,1)S(1)}, bf16[64,1536]{1,0:T(8,128)(2,1)S(1)}, u32[]{:S(2)}, u32[]{:S(2)}) collective-permute-start(bf16[64,1536]{1,0:T(8,128)(2,1)S(1)} %get-tuple-element.11.q0), channel_id=1, source_target_pairs={{0,48},{16,0},{32,16},{48,32},{1,49},{17,1},{33,17},{49,33},{2,50}... | collective-permute-start | bytes 589832 | tf_op jit(solution)/shard_map/ppermute | solution.py:344
  41.8 4.8 %all-to-all-done.1.kv = bf16[8,288,128]{2,1,0:T(8,128)(2,1)S(1)} async-done(((bf16[8,288,128]{2,1,0:T(8,128)(2,1)}), bf16[8,288,128]{2,1,0:T(8,128)(2,1)S(1)}, u32[]{:S(2)}, u32[]{:S(2)}) %all-to-all-start.1) | async-done | bytes 589856 | tf_op jit(solution)/shard_map/all_to_all | solution.py:342
  46.6 1.9 %collective-permute-start.3 = (bf16[8,288,128]{2,1,0:T(8,128)(2,1)S(1)}, bf16[8,288,128]{2,1,0:T(8,128)(2,1)S(1)}, u32[]{:S(2)}, u32[]{:S(2)}) collective-permute-start(bf16[8,288,128]{2,1,0:T(8,128)(2,1)S(1)} %all-to-all-done.1.kv), channel_id=1, source_target_pairs={{0,8},{8,0},{1,9},{9,1},{2,10},{10,2},{3,11},{11,3},{4,12},{12,4},... | collective-permute-start | bytes 1769480 | tf_op jit(solution)/shard_map/ppermute | solution.py:343
  48.5 0.0 collective-permute-done.q1
  48.5 0.0 collective-permute-done.1.q2
  48.6 0.0 collective-permute-done.2.q3
  48.6 0.0 copy-done
  48.6 0.0 copy-done.1
  48.6 4.0 %shard_map.67 = (bf16[8,256,640]{2,1,0:T(8,128)(2,1)S(1)}, f32[8,256,128]{2,1,0:T(8,128)S(1)}, f32[8,256,128]{2,1,0:T(8,128)S(1)}, f32[8,256,128]{2,1,0:T(8,128)S(1)}) custom-call(s32[1]{0:T(128)} %bitcast.place_ref, bf16[64,1536]{1,0:T(8,128)(2,1)S(1)} %get-tuple-element.11.q0, bf16[64,1536]{1,0:T(8,128)(2,1)S(1)} %collective-permute-done.q1, ...), custom_call_target="tpu_custom_call" | custom-call | flops 6000000000 | bytes 5000000 | tf_op jit(solution)/shard_map/pallas_call | solution.py:220
  52.6 0.0 collective-permute-done.3.kv
  52.6 3.6 %shard_map.68 = bf16[4,64,1152]{2,1,0:T(8,128)(2,1)S(1)} custom-call(s32[1]{0:T(128)} %bitcast.place_ref, bf16[8,256,640]{2,1,0:T(8,128)(2,1)S(1)} %get-tuple-element.13.q_ref, bf16[256,128]{1,0:T(8,128)(2,1)S(1)} %shard_map.65.floor_ref, bf16[8,288,128]{2,1,0:T(8,128)(2,1)S(1)} %collective-permute-done.3.kv, f32[8,256,128]{2,1,0:T(8,128)S(1)} %get-tuple-element.14.sum_ref, ...), custom_call_target="tpu_custom_call" | custom-call | flops 4000000000 | bytes 5000000 | tf_op jit(solution)/shard_map/pallas_call | solution.py:283
  56.2 27.3 %all_to_all.15 = bf16[32,8,1152]{2,1,0:T(8,128)(2,1)S(1)} all-to-all(bf16[32,8,1152]{2,1,0:T(8,128)(2,1)S(1)} %bitcast.5), channel_id=1, replica_groups=mesh['y'=8,'x'=4,'core'=2,'z'=8] {'x','z'}, dimensions={0} | all-to-all | bytes 1179648 | tf_op jit(solution)/shard_map/all_to_all | solution.py:349
  83.6 1.2 %shard_map.69 = bf16[8,8192]{1,0:T(8,128)(2,1)} custom-call(bf16[4,8,8,1152]{3,2,1,0:T(8,128)(2,1)S(1)} %bitcast.4), custom_call_target="tpu_custom_call" | custom-call | flops 1000000 | bytes 800000 | tf_op jit(solution)/shard_map/pallas_call | solution.py:322
Async XLA Ops:
  1.7 20.7 %all-to-all-start = ((bf16[8,8,2176]{2,1,0:T(8,128)(2,1)}), bf16[8,8,2176]{2,1,0:T(8,128)(2,1)S(1)}, u32[]{:S(2)}, u32[]{:S(2)}) async-start(bf16[8,8,2176]{2,1,0:T(8,128)(2,1)} %shard_map.64), calls=%async_computation | async-start | bytes 557056 | tf_op jit(solution)/shard_map/all_to_all | solution.py:340
  22.4 26.2 %copy-start = (bf16[8,512,128]{2,1,0:T(8,128)(2,1)S(1)}, bf16[8,512,128]{2,1,0:T(8,128)(2,1)}, u32[]{:S(2)}) copy-start(bf16[8,512,128]{2,1,0:T(8,128)(2,1)} %w_uk.1) | copy-start | bytes 3145732
  22.4 26.2 %copy-start.1 = (bf16[8,512,128]{2,1,0:T(8,128)(2,1)S(1)}, bf16[8,512,128]{2,1,0:T(8,128)(2,1)}, u32[]{:S(2)}) copy-start(bf16[8,512,128]{2,1,0:T(8,128)(2,1)} %w_uv.3) | copy-start | bytes 3145732
  23.3 23.3 %all-to-all-start.1 = ((bf16[8,288,128]{2,1,0:T(8,128)(2,1)}), bf16[8,288,128]{2,1,0:T(8,128)(2,1)S(1)}, u32[]{:S(2)}, u32[]{:S(2)}) async-start(bf16[8,288,128]{2,1,0:T(8,128)(2,1)} %get-tuple-element.12), calls=%async_computation.1 | async-start | bytes 1179648 | tf_op jit(solution)/shard_map/all_to_all | solution.py:342
  30.4 18.1 %collective-permute-start = (bf16[64,1536]{1,0:T(8,128)(2,1)S(1)}, bf16[64,1536]{1,0:T(8,128)(2,1)S(1)}, u32[]{:S(2)}, u32[]{:S(2)}) collective-permute-start(bf16[64,1536]{1,0:T(8,128)(2,1)S(1)} %get-tuple-element.11.q0), channel_id=1, source_target_pairs={{0,16},{16,32},{32,48},{48,0},{1,17},{17,33},{33,49},{49,1},{2,18}... | collective-permute-start | bytes 589832 | tf_op jit(solution)/shard_map/ppermute | solution.py:344
  33.8 14.7 %collective-permute-start.1 = (bf16[64,1536]{1,0:T(8,128)(2,1)S(1)}, bf16[64,1536]{1,0:T(8,128)(2,1)S(1)}, u32[]{:S(2)}, u32[]{:S(2)}) collective-permute-start(bf16[64,1536]{1,0:T(8,128)(2,1)S(1)} %get-tuple-element.11.q0), channel_id=1, source_target_pairs={{0,32},{16,48},{32,0},{48,16},{1,33},{17,49},{33,1},{49,17},{2,34}... | collective-permute-start | bytes 589832 | tf_op jit(solution)/shard_map/ppermute | solution.py:344
  38.5 10.1 %collective-permute-start.2 = (bf16[64,1536]{1,0:T(8,128)(2,1)S(1)}, bf16[64,1536]{1,0:T(8,128)(2,1)S(1)}, u32[]{:S(2)}, u32[]{:S(2)}) collective-permute-start(bf16[64,1536]{1,0:T(8,128)(2,1)S(1)} %get-tuple-element.11.q0), channel_id=1, source_target_pairs={{0,48},{16,0},{32,16},{48,32},{1,49},{17,1},{33,17},{49,33},{2,50}... | collective-permute-start | bytes 589832 | tf_op jit(solution)/shard_map/ppermute | solution.py:344
  46.6 6.0 %collective-permute-start.3 = (bf16[8,288,128]{2,1,0:T(8,128)(2,1)S(1)}, bf16[8,288,128]{2,1,0:T(8,128)(2,1)S(1)}, u32[]{:S(2)}, u32[]{:S(2)}) collective-permute-start(bf16[8,288,128]{2,1,0:T(8,128)(2,1)S(1)} %all-to-all-done.1.kv), channel_id=1, source_target_pairs={{0,8},{8,0},{1,9},{9,1},{2,10},{10,2},{3,11},{11,3},{4,12},{12,4},... | collective-permute-start | bytes 1769480 | tf_op jit(solution)/shard_map/ppermute | solution.py:343

commit v15 on v12

--- a/solution.py
+++ b/solution.py
@@ -106,7 +106,7 @@
 def pair_scores(q_ref, floor, keys, p):
     rows = NX * SPAN
     q = jnp.concatenate(
-        [q_ref[2 * p : 2 * p + 2].reshape(2 * rows, WIDE), jnp.concatenate([floor, floor], axis=0)], axis=1
+        [q_ref[pl.ds(2 * p, 2)].reshape(2 * rows, WIDE), jnp.concatenate([floor, floor], axis=0)], axis=1
     )
     return lax.dot_general(q, keys[...], (((1,), (1,)), ((), ())), preferred_element_type=jnp.float32)
 
@@ -188,25 +188,25 @@
         q_ref[h, :, DL : DL + DR] = q[:, DN:]
         q_ref[h, :, DL + DR : WIDE] = none
 
-    fill_queries(0)
-    fill_queries(1)
+    for h in range(HEADS):
+        fill_queries(h)
     fill_keys(keys, kv, 0, place_ref[0] // (2 * NX) * 2)
-    ahead = pair_scores(q_ref, floor, keys, 0)
-    for p in range(HEADS // 2):
-        s = ahead
-        values = pair_values(keys, w_uv, p)
-        if p + 1 < HEADS // 2:
-            fill_queries(2 * p + 2)
-            fill_queries(2 * p + 3)
-            ahead = pair_scores(q_ref, floor, keys, p + 1)
-        top = jnp.max(s, axis=1, keepdims=True)
-        weight = jnp.exp2(s * SCALE2 - top * SCALE2)
-        sums, totals = weigh(weight, values)
-        for i in range(2):
-            sum_ref[2 * p + i] = sums[i]
-            total_ref[2 * p + i] = totals[i]
-        pair = slice(2 * p, 2 * p + 2)
-        top_ref[pair] = jnp.broadcast_to(top, (2 * rows, STAT)).reshape(2, rows, STAT)
+
+    def step(i, carry):
+        scores = [pair_scores(q_ref, floor, keys, 2 * i + j) for j in range(2)]
+        for j, s in enumerate(scores):
+            p = 2 * i + j
+            values = pair_values(keys, w_uv, p)
+            top = jnp.max(s, axis=1, keepdims=True)
+            weight = jnp.exp2((s - top) * SCALE2)
+            sums, totals = weigh(weight, values)
+            for k in range(2):
+                sum_ref[2 * p + k] = sums[k]
+                total_ref[2 * p + k] = totals[k]
+            top_ref[pl.ds(2 * p, 2)] = jnp.broadcast_to(top, (2 * rows, STAT)).reshape(2, rows, STAT)
+        return carry
+
+    lax.fori_loop(0, HEADS // 4, step, 0)
 
 
 def attend_own(place, qs, w_uk, w_uv, kv, floor):
@@ -235,28 +235,30 @@
     floor = floor_ref[...]
     fill_keys(keys, kv, NY * SPAN // HALF, None)
     lanes = lax.broadcasted_iota(jnp.int32, (rows, STAT), 1)
-    level = jnp.zeros((rows, STAT), jnp.float32)
-    ahead = pair_scores(q_ref, floor, keys, 0)
-    for p in range(HEADS // 2):
-        s = ahead
-        values = pair_values(keys, w_uv, p)
-        if p + 1 < HEADS // 2:
-            ahead = pair_scores(q_ref, floor, keys, p + 1)
-        pair = slice(2 * p, 2 * p + 2)
-        old_top = top_ref[pair].reshape(2 * rows, STAT)
-        top = jnp.maximum(old_top, jnp.max(s, axis=1, keepdims=True))
-        shrink = jnp.exp2((old_top - top) * SCALE2)
-        weight = jnp.exp2(s * SCALE2 - wide(top * SCALE2, NY * SPAN // STAT))
-        sums, totals = weigh(weight, values)
-        for i in range(2):
-            h = 2 * p + i
-            mine = slice(i * rows, (i + 1) * rows)
-            total = totals[i] + total_ref[h] * shrink[mine]
-            value = ((sums[i] + sum_ref[h] * shrink[mine]) * (1.0 / total)).astype(jnp.bfloat16)
-            for step in range(NX):
-                to = (x + NX - step) % NX
-                out_ref[to, :, h * DV : (h + 1) * DV] = value[step * SPAN : (step + 1) * SPAN]
-            level = jnp.where(lanes % HEADS == h, top[mine] * SCALE2 + jnp.log2(total), level)
+
+    def step(i, level):
+        scores = [pair_scores(q_ref, floor, keys, 2 * i + j) for j in range(2)]
+        for j, s in enumerate(scores):
+            p = 2 * i + j
+            values = pair_values(keys, w_uv, p)
+            old_top = top_ref[pl.ds(2 * p, 2)].reshape(2 * rows, STAT)
+            top = jnp.maximum(old_top, jnp.max(s, axis=1, keepdims=True))
+            shrink = jnp.exp2((old_top - top) * SCALE2)
+            weight = jnp.exp2((s - wide(top, NY * SPAN // STAT)) * SCALE2)
+            sums, totals = weigh(weight, values)
+            for k in range(2):
+                h = 2 * p + k
+                mine = slice(k * rows, (k + 1) * rows)
+                total = totals[k] + total_ref[h] * shrink[mine]
+                value = ((sums[k] + sum_ref[h] * shrink[mine]) * (1.0 / total)).astype(jnp.bfloat16)
+                cols = pl.ds(pl.multiple_of(h * DV, DV), DV)
+                for member in range(NX):
+                    to = (x + NX - member) % NX
+                    out_ref[to, :, cols] = value[member * SPAN : (member + 1) * SPAN]
+                level = jnp.where(lanes % HEADS == h, top[mine] * SCALE2 + jnp.log2(total), level)
+        return level
+
+    level = lax.fori_loop(0, HEADS // 4, step, jnp.zeros((rows, STAT), jnp.float32))
     high = level.astype(jnp.bfloat16)
     rest = level - high.astype(jnp.float32)
     middle = rest.astype(jnp.bfloat16)

time: 85.4 us -> 86.6 us (1.014)
  Pallas kernels: 12.2 us -> 13.4 us
  transfers between devices with their start and end apart: 6 -> 6, of which waited for: 2 -> 2; matrix products, arithmetic and copies ran while one was open for 1% -> 1% of each run, Pallas kernels for 5% -> 6%
where the time goes in v15:
time: 86.6 us; the launch traced here: 86.1 us
  starting transfers between devices  30.3 us (35%)
  blocking collectives  27.3 us (32%)
  waiting for transfers between devices  14.2 us (16%)
  Pallas kernels  13.4 us (15%)
    all_to_all x1, blocking collectives, on_device(): lax.all_to_all(partial, ('x', 'z'), split_axis=0, concat_axis=0, tiled=True)  27.3 us
    ppermute x3, starting transfers between devices, on_device(): lax.ppermute(q_own, 'x', along_x(step))  11.4 us
    all_to_all x1, starting transfers between devices, on_device(): lax.all_to_all(both, 'z', split_axis=0, concat_axis=0, tiled=True)  9.96 us
    all_to_all x1, waiting for transfers between devices, on_device(): lax.all_to_all(both, 'z', split_axis=0, concat_axis=0, tiled=True)  9.42 us
    all_to_all x1, starting transfers between devices, on_device(): kv_own = lax.all_to_all(kv, 'y', split_axis=0, concat_axis=0, tiled=True)  7.1 us
    all_to_all x1, waiting for transfers between devices, on_device(): kv_own = lax.all_to_all(kv, 'y', split_axis=0, concat_axis=0, tiled=True)  4.8 us
    pallas_call x1, Pallas kernels, attend_own(): pl.pallas_call(own_kernel, out_shape=[jax.ShapeDtypeStruct((HEADS, rows,...  4.75 us
    pallas_call x1, Pallas kernels, attend_other(): pl.pallas_call(other_kernel, out_shape=jax.ShapeDtypeStruct((NX, SPAN, HE...  4.16 us
  transfers between devices with their start and end apart: 6, of which 2 were waited for; matrix products, arithmetic and copies ran while one was open for 1% of the time, Pallas kernels for 6%

profile of v15, /device:TPU:64, one launch (start us, length us, event | category | flops | bytes accessed | tf_op | source)
XLA Modules:
  0.0 86.1 jit_solution(6510317611211796709)
XLA Ops:
  0.0 1.7 %shard_map.64 = bf16[8,8,2176]{2,1,0:T(8,128)(2,1)} custom-call(bf16[8,12288]{1,0:T(8,128)(2,1)} %q_ref.1, bf16[8,512]{1,0:T(8,128)(2,1)} %lat_ref.1, bf16[8,64]{1,0:T(8,128)(2,1)} %rope_ref.1), custom_call_target="tpu_custom_call" | custom-call | flops 1000000 | bytes 500000 | tf_op jit(solution)/shard_map/pallas_call | solution.py:50
  1.7 10.0 %all-to-all-start = ((bf16[8,8,2176]{2,1,0:T(8,128)(2,1)}), bf16[8,8,2176]{2,1,0:T(8,128)(2,1)S(1)}, u32[]{:S(2)}, u32[]{:S(2)}) async-start(bf16[8,8,2176]{2,1,0:T(8,128)(2,1)} %shard_map.64), calls=%async_computation | async-start | bytes 557056 | tf_op jit(solution)/shard_map/all_to_all | solution.py:338
  11.6 0.7 pad_add_fusion.info_ref
  12.4 0.6 shard_map.65.floor_ref
  13.0 9.4 %all-to-all-done = bf16[8,8,2176]{2,1,0:T(8,128)(2,1)S(1)} async-done(((bf16[8,8,2176]{2,1,0:T(8,128)(2,1)}), bf16[8,8,2176]{2,1,0:T(8,128)(2,1)S(1)}, u32[]{:S(2)}, u32[]{:S(2)}) %all-to-all-start) | async-done | bytes 278560 | tf_op jit(solution)/shard_map/all_to_all | solution.py:338
  22.4 0.0 copy-start
  22.4 0.0 copy-start.1
  22.4 0.9 %shard_map.66 = (bf16[64,1536]{1,0:T(8,128)(2,1)S(1)}, bf16[8,288,128]{2,1,0:T(8,128)(2,1)}) custom-call(bf16[64,2176]{1,0:T(8,128)(2,1)S(1)} %bitcast.6, bf16[256,128]{1,0:T(8,128)(2,1)S(1)} %shard_map.65.floor_ref), custom_call_target="tpu_custom_call" | custom-call | flops 4000000000 | bytes 1000000 | tf_op jit(solution)/shard_map/pallas_call | solution.py:74
  23.3 7.1 %all-to-all-start.1 = ((bf16[8,288,128]{2,1,0:T(8,128)(2,1)}), bf16[8,288,128]{2,1,0:T(8,128)(2,1)S(1)}, u32[]{:S(2)}, u32[]{:S(2)}) async-start(bf16[8,288,128]{2,1,0:T(8,128)(2,1)} %get-tuple-element.12), calls=%async_computation.1 | async-start | bytes 1179648 | tf_op jit(solution)/shard_map/all_to_all | solution.py:340
  30.4 3.4 %collective-permute-start = (bf16[64,1536]{1,0:T(8,128)(2,1)S(1)}, bf16[64,1536]{1,0:T(8,128)(2,1)S(1)}, u32[]{:S(2)}, u32[]{:S(2)}) collective-permute-start(bf16[64,1536]{1,0:T(8,128)(2,1)S(1)} %get-tuple-element.11.q0), channel_id=1, source_target_pairs={{0,16},{16,32},{32,48},{48,0},{1,17},{17,33},{33,49},{49,1},{2,18}... | collective-permute-start | bytes 589832 | tf_op jit(solution)/shard_map/ppermute | solution.py:342
  33.8 4.6 %collective-permute-start.1 = (bf16[64,1536]{1,0:T(8,128)(2,1)S(1)}, bf16[64,1536]{1,0:T(8,128)(2,1)S(1)}, u32[]{:S(2)}, u32[]{:S(2)}) collective-permute-start(bf16[64,1536]{1,0:T(8,128)(2,1)S(1)} %get-tuple-element.11.q0), channel_id=1, source_target_pairs={{0,32},{16,48},{32,0},{48,16},{1,33},{17,49},{33,1},{49,17},{2,34}... | collective-permute-start | bytes 589832 | tf_op jit(solution)/shard_map/ppermute | solution.py:342
  38.5 3.3 %collective-permute-start.2 = (bf16[64,1536]{1,0:T(8,128)(2,1)S(1)}, bf16[64,1536]{1,0:T(8,128)(2,1)S(1)}, u32[]{:S(2)}, u32[]{:S(2)}) collective-permute-start(bf16[64,1536]{1,0:T(8,128)(2,1)S(1)} %get-tuple-element.11.q0), channel_id=1, source_target_pairs={{0,48},{16,0},{32,16},{48,32},{1,49},{17,1},{33,17},{49,33},{2,50}... | collective-permute-start | bytes 589832 | tf_op jit(solution)/shard_map/ppermute | solution.py:342
  41.8 4.8 %all-to-all-done.1.kv = bf16[8,288,128]{2,1,0:T(8,128)(2,1)S(1)} async-done(((bf16[8,288,128]{2,1,0:T(8,128)(2,1)}), bf16[8,288,128]{2,1,0:T(8,128)(2,1)S(1)}, u32[]{:S(2)}, u32[]{:S(2)}) %all-to-all-start.1) | async-done | bytes 589856 | tf_op jit(solution)/shard_map/all_to_all | solution.py:340
  46.6 1.9 %collective-permute-start.3 = (bf16[8,288,128]{2,1,0:T(8,128)(2,1)S(1)}, bf16[8,288,128]{2,1,0:T(8,128)(2,1)S(1)}, u32[]{:S(2)}, u32[]{:S(2)}) collective-permute-start(bf16[8,288,128]{2,1,0:T(8,128)(2,1)S(1)} %all-to-all-done.1.kv), channel_id=1, source_target_pairs={{0,8},{8,0},{1,9},{9,1},{2,10},{10,2},{3,11},{11,3},{4,12},{12,4},... | collective-permute-start | bytes 1769480 | tf_op jit(solution)/shard_map/ppermute | solution.py:341
  48.5 0.0 collective-permute-done.q1
  48.5 0.0 collective-permute-done.1.q2
  48.6 0.0 collective-permute-done.2.q3
  48.6 0.0 copy-done
  48.6 0.0 copy-done.1
  48.6 4.8 %shard_map.67 = (bf16[8,256,640]{2,1,0:T(8,128)(2,1)S(1)}, f32[8,256,128]{2,1,0:T(8,128)S(1)}, f32[8,256,128]{2,1,0:T(8,128)S(1)}, f32[8,256,128]{2,1,0:T(8,128)S(1)}) custom-call(s32[1]{0:T(128)} %bitcast.place_ref, bf16[64,1536]{1,0:T(8,128)(2,1)S(1)} %get-tuple-element.11.q0, bf16[64,1536]{1,0:T(8,128)(2,1)S(1)} %collective-permute-done.q1, ...), custom_call_target="tpu_custom_call" | custom-call | flops 6000000000 | bytes 5000000 | tf_op jit(solution)/shard_map/pallas_call | solution.py:216
  53.3 0.0 collective-permute-done.3.kv
  53.4 4.2 %shard_map.68 = bf16[4,64,1152]{2,1,0:T(8,128)(2,1)S(1)} custom-call(s32[1]{0:T(128)} %bitcast.place_ref, bf16[8,256,640]{2,1,0:T(8,128)(2,1)S(1)} %get-tuple-element.13.q_ref, bf16[256,128]{1,0:T(8,128)(2,1)S(1)} %shard_map.65.floor_ref, bf16[8,288,128]{2,1,0:T(8,128)(2,1)S(1)} %collective-permute-done.3.kv, f32[8,256,128]{2,1,0:T(8,128)S(1)} %get-tuple-element.14.sum_ref, ...), custom_call_target="tpu_custom_call" | custom-call | flops 4000000000 | bytes 5000000 | tf_op jit(solution)/shard_map/pallas_call | solution.py:281
  57.5 27.3 %all_to_all.15 = bf16[32,8,1152]{2,1,0:T(8,128)(2,1)S(1)} all-to-all(bf16[32,8,1152]{2,1,0:T(8,128)(2,1)S(1)} %bitcast.5), channel_id=1, replica_groups=mesh['y'=8,'x'=4,'core'=2,'z'=8] {'x','z'}, dimensions={0} | all-to-all | bytes 1179648 | tf_op jit(solution)/shard_map/all_to_all | solution.py:347
  84.9 1.2 %shard_map.69 = bf16[8,8192]{1,0:T(8,128)(2,1)} custom-call(bf16[4,8,8,1152]{3,2,1,0:T(8,128)(2,1)S(1)} %bitcast.4), custom_call_target="tpu_custom_call" | custom-call | flops 1000000 | bytes 800000 | tf_op jit(solution)/shard_map/pallas_call | solution.py:320
Async XLA Ops:
  1.7 20.7 %all-to-all-start = ((bf16[8,8,2176]{2,1,0:T(8,128)(2,1)}), bf16[8,8,2176]{2,1,0:T(8,128)(2,1)S(1)}, u32[]{:S(2)}, u32[]{:S(2)}) async-start(bf16[8,8,2176]{2,1,0:T(8,128)(2,1)} %shard_map.64), calls=%async_computation | async-start | bytes 557056 | tf_op jit(solution)/shard_map/all_to_all | solution.py:338
  22.4 26.2 %copy-start = (bf16[8,512,128]{2,1,0:T(8,128)(2,1)S(1)}, bf16[8,512,128]{2,1,0:T(8,128)(2,1)}, u32[]{:S(2)}) copy-start(bf16[8,512,128]{2,1,0:T(8,128)(2,1)} %w_uk.1) | copy-start | bytes 3145732
  22.4 26.2 %copy-start.1 = (bf16[8,512,128]{2,1,0:T(8,128)(2,1)S(1)}, bf16[8,512,128]{2,1,0:T(8,128)(2,1)}, u32[]{:S(2)}) copy-start(bf16[8,512,128]{2,1,0:T(8,128)(2,1)} %w_uv.3) | copy-start | bytes 3145732
  23.3 23.3 %all-to-all-start.1 = ((bf16[8,288,128]{2,1,0:T(8,128)(2,1)}), bf16[8,288,128]{2,1,0:T(8,128)(2,1)S(1)}, u32[]{:S(2)}, u32[]{:S(2)}) async-start(bf16[8,288,128]{2,1,0:T(8,128)(2,1)} %get-tuple-element.12), calls=%async_computation.1 | async-start | bytes 1179648 | tf_op jit(solution)/shard_map/all_to_all | solution.py:340
  30.4 18.1 %collective-permute-start = (bf16[64,1536]{1,0:T(8,128)(2,1)S(1)}, bf16[64,1536]{1,0:T(8,128)(2,1)S(1)}, u32[]{:S(2)}, u32[]{:S(2)}) collective-permute-start(bf16[64,1536]{1,0:T(8,128)(2,1)S(1)} %get-tuple-element.11.q0), channel_id=1, source_target_pairs={{0,16},{16,32},{32,48},{48,0},{1,17},{17,33},{33,49},{49,1},{2,18}... | collective-permute-start | bytes 589832 | tf_op jit(solution)/shard_map/ppermute | solution.py:342
  33.8 14.7 %collective-permute-start.1 = (bf16[64,1536]{1,0:T(8,128)(2,1)S(1)}, bf16[64,1536]{1,0:T(8,128)(2,1)S(1)}, u32[]{:S(2)}, u32[]{:S(2)}) collective-permute-start(bf16[64,1536]{1,0:T(8,128)(2,1)S(1)} %get-tuple-element.11.q0), channel_id=1, source_target_pairs={{0,32},{16,48},{32,0},{48,16},{1,33},{17,49},{33,1},{49,17},{2,34}... | collective-permute-start | bytes 589832 | tf_op jit(solution)/shard_map/ppermute | solution.py:342
  38.5 10.1 %collective-permute-start.2 = (bf16[64,1536]{1,0:T(8,128)(2,1)S(1)}, bf16[64,1536]{1,0:T(8,128)(2,1)S(1)}, u32[]{:S(2)}, u32[]{:S(2)}) collective-permute-start(bf16[64,1536]{1,0:T(8,128)(2,1)S(1)} %get-tuple-element.11.q0), channel_id=1, source_target_pairs={{0,48},{16,0},{32,16},{48,32},{1,49},{17,1},{33,17},{49,33},{2,50}... | collective-permute-start | bytes 589832 | tf_op jit(solution)/shard_map/ppermute | solution.py:342
  46.6 6.7 %collective-permute-start.3 = (bf16[8,288,128]{2,1,0:T(8,128)(2,1)S(1)}, bf16[8,288,128]{2,1,0:T(8,128)(2,1)S(1)}, u32[]{:S(2)}, u32[]{:S(2)}) collective-permute-start(bf16[8,288,128]{2,1,0:T(8,128)(2,1)S(1)} %all-to-all-done.1.kv), channel_id=1, source_target_pairs={{0,8},{8,0},{1,9},{9,1},{2,10},{10,2},{3,11},{11,3},{4,12},{12,4},... | collective-permute-start | bytes 1769480 | tf_op jit(solution)/shard_map/ppermute | solution.py:341

commit v16 on v11

--- a/solution.py
+++ b/solution.py
@@ -191,14 +191,19 @@
     fill_queries(0)
     fill_queries(1)
     fill_keys(keys, kv, 0, place_ref[0] // (2 * NX) * 2)
-    ahead = pair_scores(q_ref, floor, keys, 0)
+    ahead = [pair_scores(q_ref, floor, keys, 0)]
+    fill_queries(2)
+    fill_queries(3)
+    ahead.append(pair_scores(q_ref, floor, keys, 1))
+    later = pair_values(keys, w_uv, 0)
     for p in range(HEADS // 2):
-        s = ahead
-        values = pair_values(keys, w_uv, p)
+        s, values = ahead.pop(0), later
+        if p + 2 < HEADS // 2:
+            fill_queries(2 * p + 4)
+            fill_queries(2 * p + 5)
+            ahead.append(pair_scores(q_ref, floor, keys, p + 2))
         if p + 1 < HEADS // 2:
-            fill_queries(2 * p + 2)
-            fill_queries(2 * p + 3)
-            ahead = pair_scores(q_ref, floor, keys, p + 1)
+            later = pair_values(keys, w_uv, p + 1)
         top = jnp.max(s, axis=1, keepdims=True)
         weight = jnp.exp2((s - top) * SCALE2)
         sums, totals = weigh(weight, values)
@@ -236,12 +241,14 @@
     fill_keys(keys, kv, NY * SPAN // HALF, None)
     lanes = lax.broadcasted_iota(jnp.int32, (rows, STAT), 1)
     level = jnp.zeros((rows, STAT), jnp.float32)
-    ahead = pair_scores(q_ref, floor, keys, 0)
+    ahead = [pair_scores(q_ref, floor, keys, p) for p in range(2)]
+    later = pair_values(keys, w_uv, 0)
     for p in range(HEADS // 2):
-        s = ahead
-        values = pair_values(keys, w_uv, p)
+        s, values = ahead.pop(0), later
+        if p + 2 < HEADS // 2:
+            ahead.append(pair_scores(q_ref, floor, keys, p + 2))
         if p + 1 < HEADS // 2:
-            ahead = pair_scores(q_ref, floor, keys, p + 1)
+            later = pair_values(keys, w_uv, p + 1)
         pair = slice(2 * p, 2 * p + 2)
         old_top = top_ref[pair].reshape(2 * rows, STAT)
         top = jnp.maximum(old_top, jnp.max(s, axis=1, keepdims=True))

time: 85.2 us -> 84.7 us (level)
  no operation moved by 1% of the time
where the time goes in v16:
time: 84.7 us; the launch traced here: 84.2 us
  starting transfers between devices  30.3 us (36%)
  blocking collectives  27.3 us (32%)
  waiting for transfers between devices  14.2 us (17%)
  Pallas kernels  11.5 us (14%)
    all_to_all x1, blocking collectives, on_device(): lax.all_to_all(partial, ('x', 'z'), split_axis=0, concat_axis=0, tiled=True)  27.3 us
    ppermute x3, starting transfers between devices, on_device(): lax.ppermute(q_own, 'x', along_x(step))  11.4 us
    all_to_all x1, starting transfers between devices, on_device(): lax.all_to_all(both, 'z', split_axis=0, concat_axis=0, tiled=True)  9.96 us
    all_to_all x1, waiting for transfers between devices, on_device(): lax.all_to_all(both, 'z', split_axis=0, concat_axis=0, tiled=True)  9.42 us
    all_to_all x1, starting transfers between devices, on_device(): kv_own = lax.all_to_all(kv, 'y', split_axis=0, concat_axis=0, tiled=True)  7.1 us
    all_to_all x1, waiting for transfers between devices, on_device(): kv_own = lax.all_to_all(kv, 'y', split_axis=0, concat_axis=0, tiled=True)  4.8 us
    pallas_call x1, Pallas kernels, attend_own(): pl.pallas_call(own_kernel, out_shape=[jax.ShapeDtypeStruct((HEADS, rows,...  3.6 us
    pallas_call x1, Pallas kernels, attend_other(): pl.pallas_call(other_kernel, out_shape=jax.ShapeDtypeStruct((NX, SPAN, HE...  3.45 us
  transfers between devices with their start and end apart: 6, of which 2 were waited for; matrix products, arithmetic and copies ran while one was open for 1% of the time, Pallas kernels for 5%

profile of v16, /device:TPU:64, one launch (start us, length us, event | category | flops | bytes accessed | tf_op | source)
XLA Modules:
  0.0 84.2 jit_solution(1112886810972989783)
XLA Ops:
  0.0 1.7 %shard_map.64 = bf16[8,8,2176]{2,1,0:T(8,128)(2,1)} custom-call(bf16[8,12288]{1,0:T(8,128)(2,1)} %q_ref.1, bf16[8,512]{1,0:T(8,128)(2,1)} %lat_ref.1, bf16[8,64]{1,0:T(8,128)(2,1)} %rope_ref.1), custom_call_target="tpu_custom_call" | custom-call | flops 1000000 | bytes 500000 | tf_op jit(solution)/shard_map/pallas_call | solution.py:50
  1.7 10.0 %all-to-all-start = ((bf16[8,8,2176]{2,1,0:T(8,128)(2,1)}), bf16[8,8,2176]{2,1,0:T(8,128)(2,1)S(1)}, u32[]{:S(2)}, u32[]{:S(2)}) async-start(bf16[8,8,2176]{2,1,0:T(8,128)(2,1)} %shard_map.64), calls=%async_computation | async-start | bytes 557056 | tf_op jit(solution)/shard_map/all_to_all | solution.py:343
  11.6 0.7 pad_add_fusion.info_ref
  12.4 0.6 shard_map.65.floor_ref
  13.0 9.4 %all-to-all-done = bf16[8,8,2176]{2,1,0:T(8,128)(2,1)S(1)} async-done(((bf16[8,8,2176]{2,1,0:T(8,128)(2,1)}), bf16[8,8,2176]{2,1,0:T(8,128)(2,1)S(1)}, u32[]{:S(2)}, u32[]{:S(2)}) %all-to-all-start) | async-done | bytes 278560 | tf_op jit(solution)/shard_map/all_to_all | solution.py:343
  22.4 0.0 copy-start
  22.4 0.0 copy-start.1
  22.4 0.9 %shard_map.66 = (bf16[64,1536]{1,0:T(8,128)(2,1)S(1)}, bf16[8,288,128]{2,1,0:T(8,128)(2,1)}) custom-call(bf16[64,2176]{1,0:T(8,128)(2,1)S(1)} %bitcast.6, bf16[256,128]{1,0:T(8,128)(2,1)S(1)} %shard_map.65.floor_ref), custom_call_target="tpu_custom_call" | custom-call | flops 4000000000 | bytes 1000000 | tf_op jit(solution)/shard_map/pallas_call | solution.py:74
  23.3 7.1 %all-to-all-start.1 = ((bf16[8,288,128]{2,1,0:T(8,128)(2,1)}), bf16[8,288,128]{2,1,0:T(8,128)(2,1)S(1)}, u32[]{:S(2)}, u32[]{:S(2)}) async-start(bf16[8,288,128]{2,1,0:T(8,128)(2,1)} %get-tuple-element.12), calls=%async_computation.1 | async-start | bytes 1179648 | tf_op jit(solution)/shard_map/all_to_all | solution.py:345
  30.4 3.4 %collective-permute-start = (bf16[64,1536]{1,0:T(8,128)(2,1)S(1)}, bf16[64,1536]{1,0:T(8,128)(2,1)S(1)}, u32[]{:S(2)}, u32[]{:S(2)}) collective-permute-start(bf16[64,1536]{1,0:T(8,128)(2,1)S(1)} %get-tuple-element.11.q0), channel_id=1, source_target_pairs={{0,16},{16,32},{32,48},{48,0},{1,17},{17,33},{33,49},{49,1},{2,18}... | collective-permute-start | bytes 589832 | tf_op jit(solution)/shard_map/ppermute | solution.py:347
  33.8 4.6 %collective-permute-start.1 = (bf16[64,1536]{1,0:T(8,128)(2,1)S(1)}, bf16[64,1536]{1,0:T(8,128)(2,1)S(1)}, u32[]{:S(2)}, u32[]{:S(2)}) collective-permute-start(bf16[64,1536]{1,0:T(8,128)(2,1)S(1)} %get-tuple-element.11.q0), channel_id=1, source_target_pairs={{0,32},{16,48},{32,0},{48,16},{1,33},{17,49},{33,1},{49,17},{2,34}... | collective-permute-start | bytes 589832 | tf_op jit(solution)/shard_map/ppermute | solution.py:347
  38.5 3.3 %collective-permute-start.2 = (bf16[64,1536]{1,0:T(8,128)(2,1)S(1)}, bf16[64,1536]{1,0:T(8,128)(2,1)S(1)}, u32[]{:S(2)}, u32[]{:S(2)}) collective-permute-start(bf16[64,1536]{1,0:T(8,128)(2,1)S(1)} %get-tuple-element.11.q0), channel_id=1, source_target_pairs={{0,48},{16,0},{32,16},{48,32},{1,49},{17,1},{33,17},{49,33},{2,50}... | collective-permute-start | bytes 589832 | tf_op jit(solution)/shard_map/ppermute | solution.py:347
  41.8 4.8 %all-to-all-done.1.kv = bf16[8,288,128]{2,1,0:T(8,128)(2,1)S(1)} async-done(((bf16[8,288,128]{2,1,0:T(8,128)(2,1)}), bf16[8,288,128]{2,1,0:T(8,128)(2,1)S(1)}, u32[]{:S(2)}, u32[]{:S(2)}) %all-to-all-start.1) | async-done | bytes 589856 | tf_op jit(solution)/shard_map/all_to_all | solution.py:345
  46.6 1.9 %collective-permute-start.3 = (bf16[8,288,128]{2,1,0:T(8,128)(2,1)S(1)}, bf16[8,288,128]{2,1,0:T(8,128)(2,1)S(1)}, u32[]{:S(2)}, u32[]{:S(2)}) collective-permute-start(bf16[8,288,128]{2,1,0:T(8,128)(2,1)S(1)} %all-to-all-done.1.kv), channel_id=1, source_target_pairs={{0,8},{8,0},{1,9},{9,1},{2,10},{10,2},{3,11},{11,3},{4,12},{12,4},... | collective-permute-start | bytes 1769480 | tf_op jit(solution)/shard_map/ppermute | solution.py:346
  48.5 0.0 collective-permute-done.q1
  48.5 0.0 collective-permute-done.1.q2
  48.6 0.0 collective-permute-done.2.q3
  48.6 0.0 copy-done
  48.6 0.0 copy-done.1
  48.6 3.6 %shard_map.67 = (bf16[8,256,640]{2,1,0:T(8,128)(2,1)S(1)}, f32[8,256,128]{2,1,0:T(8,128)S(1)}, f32[8,256,128]{2,1,0:T(8,128)S(1)}, f32[8,256,128]{2,1,0:T(8,128)S(1)}) custom-call(s32[1]{0:T(128)} %bitcast.place_ref, bf16[64,1536]{1,0:T(8,128)(2,1)S(1)} %get-tuple-element.11.q0, bf16[64,1536]{1,0:T(8,128)(2,1)S(1)} %collective-permute-done.q1, ...), custom_call_target="tpu_custom_call" | custom-call | flops 6000000000 | bytes 5000000 | tf_op jit(solution)/shard_map/pallas_call | solution.py:221
  52.2 0.0 collective-permute-done.3.kv
  52.2 3.5 %shard_map.68 = bf16[4,64,1152]{2,1,0:T(8,128)(2,1)S(1)} custom-call(s32[1]{0:T(128)} %bitcast.place_ref, bf16[8,256,640]{2,1,0:T(8,128)(2,1)S(1)} %get-tuple-element.13.q_ref, bf16[256,128]{1,0:T(8,128)(2,1)S(1)} %shard_map.65.floor_ref, bf16[8,288,128]{2,1,0:T(8,128)(2,1)S(1)} %collective-permute-done.3.kv, f32[8,256,128]{2,1,0:T(8,128)S(1)} %get-tuple-element.14.sum_ref, ...), custom_call_target="tpu_custom_call" | custom-call | flops 4000000000 | bytes 5000000 | tf_op jit(solution)/shard_map/pallas_call | solution.py:286
  55.7 27.3 %all_to_all.15 = bf16[32,8,1152]{2,1,0:T(8,128)(2,1)S(1)} all-to-all(bf16[32,8,1152]{2,1,0:T(8,128)(2,1)S(1)} %bitcast.5), channel_id=1, replica_groups=mesh['y'=8,'x'=4,'core'=2,'z'=8] {'x','z'}, dimensions={0} | all-to-all | bytes 1179648 | tf_op jit(solution)/shard_map/all_to_all | solution.py:352
  83.0 1.2 %shard_map.69 = bf16[8,8192]{1,0:T(8,128)(2,1)} custom-call(bf16[4,8,8,1152]{3,2,1,0:T(8,128)(2,1)S(1)} %bitcast.4), custom_call_target="tpu_custom_call" | custom-call | flops 1000000 | bytes 800000 | tf_op jit(solution)/shard_map/pallas_call | solution.py:325
Async XLA Ops:
  1.7 20.7 %all-to-all-start = ((bf16[8,8,2176]{2,1,0:T(8,128)(2,1)}), bf16[8,8,2176]{2,1,0:T(8,128)(2,1)S(1)}, u32[]{:S(2)}, u32[]{:S(2)}) async-start(bf16[8,8,2176]{2,1,0:T(8,128)(2,1)} %shard_map.64), calls=%async_computation | async-start | bytes 557056 | tf_op jit(solution)/shard_map/all_to_all | solution.py:343
  22.4 26.2 %copy-start = (bf16[8,512,128]{2,1,0:T(8,128)(2,1)S(1)}, bf16[8,512,128]{2,1,0:T(8,128)(2,1)}, u32[]{:S(2)}) copy-start(bf16[8,512,128]{2,1,0:T(8,128)(2,1)} %w_uk.1) | copy-start | bytes 3145732
  22.4 26.2 %copy-start.1 = (bf16[8,512,128]{2,1,0:T(8,128)(2,1)S(1)}, bf16[8,512,128]{2,1,0:T(8,128)(2,1)}, u32[]{:S(2)}) copy-start(bf16[8,512,128]{2,1,0:T(8,128)(2,1)} %w_uv.3) | copy-start | bytes 3145732
  23.3 23.3 %all-to-all-start.1 = ((bf16[8,288,128]{2,1,0:T(8,128)(2,1)}), bf16[8,288,128]{2,1,0:T(8,128)(2,1)S(1)}, u32[]{:S(2)}, u32[]{:S(2)}) async-start(bf16[8,288,128]{2,1,0:T(8,128)(2,1)} %get-tuple-element.12), calls=%async_computation.1 | async-start | bytes 1179648 | tf_op jit(solution)/shard_map/all_to_all | solution.py:345
  30.4 18.1 %collective-permute-start = (bf16[64,1536]{1,0:T(8,128)(2,1)S(1)}, bf16[64,1536]{1,0:T(8,128)(2,1)S(1)}, u32[]{:S(2)}, u32[]{:S(2)}) collective-permute-start(bf16[64,1536]{1,0:T(8,128)(2,1)S(1)} %get-tuple-element.11.q0), channel_id=1, source_target_pairs={{0,16},{16,32},{32,48},{48,0},{1,17},{17,33},{33,49},{49,1},{2,18}... | collective-permute-start | bytes 589832 | tf_op jit(solution)/shard_map/ppermute | solution.py:347
  33.8 14.7 %collective-permute-start.1 = (bf16[64,1536]{1,0:T(8,128)(2,1)S(1)}, bf16[64,1536]{1,0:T(8,128)(2,1)S(1)}, u32[]{:S(2)}, u32[]{:S(2)}) collective-permute-start(bf16[64,1536]{1,0:T(8,128)(2,1)S(1)} %get-tuple-element.11.q0), channel_id=1, source_target_pairs={{0,32},{16,48},{32,0},{48,16},{1,33},{17,49},{33,1},{49,17},{2,34}... | collective-permute-start | bytes 589832 | tf_op jit(solution)/shard_map/ppermute | solution.py:347
  38.5 10.1 %collective-permute-start.2 = (bf16[64,1536]{1,0:T(8,128)(2,1)S(1)}, bf16[64,1536]{1,0:T(8,128)(2,1)S(1)}, u32[]{:S(2)}, u32[]{:S(2)}) collective-permute-start(bf16[64,1536]{1,0:T(8,128)(2,1)S(1)} %get-tuple-element.11.q0), channel_id=1, source_target_pairs={{0,48},{16,0},{32,16},{48,32},{1,49},{17,1},{33,17},{49,33},{2,50}... | collective-permute-start | bytes 589832 | tf_op jit(solution)/shard_map/ppermute | solution.py:347
  46.6 5.6 %collective-permute-start.3 = (bf16[8,288,128]{2,1,0:T(8,128)(2,1)S(1)}, bf16[8,288,128]{2,1,0:T(8,128)(2,1)S(1)}, u32[]{:S(2)}, u32[]{:S(2)}) collective-permute-start(bf16[8,288,128]{2,1,0:T(8,128)(2,1)S(1)} %all-to-all-done.1.kv), channel_id=1, source_target_pairs={{0,8},{8,0},{1,9},{9,1},{2,10},{10,2},{3,11},{11,3},{4,12},{12,4},... | collective-permute-start | bytes 1769480 | tf_op jit(solution)/shard_map/ppermute | solution.py:346

commit v17 on v16

--- a/solution.py
+++ b/solution.py
@@ -195,15 +195,18 @@
     fill_queries(2)
     fill_queries(3)
     ahead.append(pair_scores(q_ref, floor, keys, 1))
-    later = pair_values(keys, w_uv, 0)
+    fill_queries(4)
+    fill_queries(5)
+    ahead.append(pair_scores(q_ref, floor, keys, 2))
+    later = [pair_values(keys, w_uv, p) for p in range(2)]
     for p in range(HEADS // 2):
-        s, values = ahead.pop(0), later
+        s, values = ahead.pop(0), later.pop(0)
+        if p + 3 < HEADS // 2:
+            fill_queries(2 * p + 6)
+            fill_queries(2 * p + 7)
+            ahead.append(pair_scores(q_ref, floor, keys, p + 3))
         if p + 2 < HEADS // 2:
-            fill_queries(2 * p + 4)
-            fill_queries(2 * p + 5)
-            ahead.append(pair_scores(q_ref, floor, keys, p + 2))
-        if p + 1 < HEADS // 2:
-            later = pair_values(keys, w_uv, p + 1)
+            later.append(pair_values(keys, w_uv, p + 2))
         top = jnp.max(s, axis=1, keepdims=True)
         weight = jnp.exp2((s - top) * SCALE2)
         sums, totals = weigh(weight, values)
@@ -241,14 +244,14 @@
     fill_keys(keys, kv, NY * SPAN // HALF, None)
     lanes = lax.broadcasted_iota(jnp.int32, (rows, STAT), 1)
     level = jnp.zeros((rows, STAT), jnp.float32)
-    ahead = [pair_scores(q_ref, floor, keys, p) for p in range(2)]
-    later = pair_values(keys, w_uv, 0)
+    ahead = [pair_scores(q_ref, floor, keys, p) for p in range(3)]
+    later = [pair_values(keys, w_uv, p) for p in range(2)]
     for p in range(HEADS // 2):
-        s, values = ahead.pop(0), later
+        s, values = ahead.pop(0), later.pop(0)
+        if p + 3 < HEADS // 2:
+            ahead.append(pair_scores(q_ref, floor, keys, p + 3))
         if p + 2 < HEADS // 2:
-            ahead.append(pair_scores(q_ref, floor, keys, p + 2))
-        if p + 1 < HEADS // 2:
-            later = pair_values(keys, w_uv, p + 1)
+            later.append(pair_values(keys, w_uv, p + 2))
         pair = slice(2 * p, 2 * p + 2)
         old_top = top_ref[pair].reshape(2 * rows, STAT)
         top = jnp.maximum(old_top, jnp.max(s, axis=1, keepdims=True))

time: 84.7 us -> 84.6 us (level)
  no operation moved by 1% of the time
where the time goes in v17:
time: 84.6 us; the launch traced here: 84.2 us
  starting transfers between devices  30.3 us (36%)
  blocking collectives  27.3 us (32%)
  waiting for transfers between devices  14.2 us (17%)
  Pallas kernels  11.4 us (13%)
    all_to_all x1, blocking collectives, on_device(): lax.all_to_all(partial, ('x', 'z'), split_axis=0, concat_axis=0, tiled=True)  27.3 us
    ppermute x3, starting transfers between devices, on_device(): lax.ppermute(q_own, 'x', along_x(step))  11.4 us
    all_to_all x1, starting transfers between devices, on_device(): lax.all_to_all(both, 'z', split_axis=0, concat_axis=0, tiled=True)  9.96 us
    all_to_all x1, waiting for transfers between devices, on_device(): lax.all_to_all(both, 'z', split_axis=0, concat_axis=0, tiled=True)  9.42 us
    all_to_all x1, starting transfers between devices, on_device(): kv_own = lax.all_to_all(kv, 'y', split_axis=0, concat_axis=0, tiled=True)  7.1 us
    all_to_all x1, waiting for transfers between devices, on_device(): kv_own = lax.all_to_all(kv, 'y', split_axis=0, concat_axis=0, tiled=True)  4.8 us
    pallas_call x1, Pallas kernels, attend_own(): pl.pallas_call(own_kernel, out_shape=[jax.ShapeDtypeStruct((HEADS, rows,...  3.61 us
    pallas_call x1, Pallas kernels, attend_other(): pl.pallas_call(other_kernel, out_shape=jax.ShapeDtypeStruct((NX, SPAN, HE...  3.37 us
  transfers between devices with their start and end apart: 6, of which 2 were waited for; matrix products, arithmetic and copies ran while one was open for 1% of the time, Pallas kernels for 5%

profile of v17, /device:TPU:64, one launch (start us, length us, event | category | flops | bytes accessed | tf_op | source)
XLA Modules:
  0.0 84.2 jit_solution(13030759919213348096)
XLA Ops:
  0.0 1.7 %shard_map.64 = bf16[8,8,2176]{2,1,0:T(8,128)(2,1)} custom-call(bf16[8,12288]{1,0:T(8,128)(2,1)} %q_ref.1, bf16[8,512]{1,0:T(8,128)(2,1)} %lat_ref.1, bf16[8,64]{1,0:T(8,128)(2,1)} %rope_ref.1), custom_call_target="tpu_custom_call" | custom-call | flops 1000000 | bytes 500000 | tf_op jit(solution)/shard_map/pallas_call | solution.py:50
  1.7 10.0 %all-to-all-start = ((bf16[8,8,2176]{2,1,0:T(8,128)(2,1)}), bf16[8,8,2176]{2,1,0:T(8,128)(2,1)S(1)}, u32[]{:S(2)}, u32[]{:S(2)}) async-start(bf16[8,8,2176]{2,1,0:T(8,128)(2,1)} %shard_map.64), calls=%async_computation | async-start | bytes 557056 | tf_op jit(solution)/shard_map/all_to_all | solution.py:346
  11.6 0.7 pad_add_fusion.info_ref
  12.4 0.6 shard_map.65.floor_ref
  13.0 9.4 %all-to-all-done = bf16[8,8,2176]{2,1,0:T(8,128)(2,1)S(1)} async-done(((bf16[8,8,2176]{2,1,0:T(8,128)(2,1)}), bf16[8,8,2176]{2,1,0:T(8,128)(2,1)S(1)}, u32[]{:S(2)}, u32[]{:S(2)}) %all-to-all-start) | async-done | bytes 278560 | tf_op jit(solution)/shard_map/all_to_all | solution.py:346
  22.4 0.0 copy-start
  22.4 0.0 copy-start.1
  22.4 0.9 %shard_map.66 = (bf16[64,1536]{1,0:T(8,128)(2,1)S(1)}, bf16[8,288,128]{2,1,0:T(8,128)(2,1)}) custom-call(bf16[64,2176]{1,0:T(8,128)(2,1)S(1)} %bitcast.6, bf16[256,128]{1,0:T(8,128)(2,1)S(1)} %shard_map.65.floor_ref), custom_call_target="tpu_custom_call" | custom-call | flops 4000000000 | bytes 1000000 | tf_op jit(solution)/shard_map/pallas_call | solution.py:74
  23.3 7.1 %all-to-all-start.1 = ((bf16[8,288,128]{2,1,0:T(8,128)(2,1)}), bf16[8,288,128]{2,1,0:T(8,128)(2,1)S(1)}, u32[]{:S(2)}, u32[]{:S(2)}) async-start(bf16[8,288,128]{2,1,0:T(8,128)(2,1)} %get-tuple-element.12), calls=%async_computation.1 | async-start | bytes 1179648 | tf_op jit(solution)/shard_map/all_to_all | solution.py:348
  30.4 3.4 %collective-permute-start = (bf16[64,1536]{1,0:T(8,128)(2,1)S(1)}, bf16[64,1536]{1,0:T(8,128)(2,1)S(1)}, u32[]{:S(2)}, u32[]{:S(2)}) collective-permute-start(bf16[64,1536]{1,0:T(8,128)(2,1)S(1)} %get-tuple-element.11.q0), channel_id=1, source_target_pairs={{0,16},{16,32},{32,48},{48,0},{1,17},{17,33},{33,49},{49,1},{2,18}... | collective-permute-start | bytes 589832 | tf_op jit(solution)/shard_map/ppermute | solution.py:350
  33.8 4.6 %collective-permute-start.1 = (bf16[64,1536]{1,0:T(8,128)(2,1)S(1)}, bf16[64,1536]{1,0:T(8,128)(2,1)S(1)}, u32[]{:S(2)}, u32[]{:S(2)}) collective-permute-start(bf16[64,1536]{1,0:T(8,128)(2,1)S(1)} %get-tuple-element.11.q0), channel_id=1, source_target_pairs={{0,32},{16,48},{32,0},{48,16},{1,33},{17,49},{33,1},{49,17},{2,34}... | collective-permute-start | bytes 589832 | tf_op jit(solution)/shard_map/ppermute | solution.py:350
  38.5 3.3 %collective-permute-start.2 = (bf16[64,1536]{1,0:T(8,128)(2,1)S(1)}, bf16[64,1536]{1,0:T(8,128)(2,1)S(1)}, u32[]{:S(2)}, u32[]{:S(2)}) collective-permute-start(bf16[64,1536]{1,0:T(8,128)(2,1)S(1)} %get-tuple-element.11.q0), channel_id=1, source_target_pairs={{0,48},{16,0},{32,16},{48,32},{1,49},{17,1},{33,17},{49,33},{2,50}... | collective-permute-start | bytes 589832 | tf_op jit(solution)/shard_map/ppermute | solution.py:350
  41.8 4.8 %all-to-all-done.1.kv = bf16[8,288,128]{2,1,0:T(8,128)(2,1)S(1)} async-done(((bf16[8,288,128]{2,1,0:T(8,128)(2,1)}), bf16[8,288,128]{2,1,0:T(8,128)(2,1)S(1)}, u32[]{:S(2)}, u32[]{:S(2)}) %all-to-all-start.1) | async-done | bytes 589856 | tf_op jit(solution)/shard_map/all_to_all | solution.py:348
  46.6 1.9 %collective-permute-start.3 = (bf16[8,288,128]{2,1,0:T(8,128)(2,1)S(1)}, bf16[8,288,128]{2,1,0:T(8,128)(2,1)S(1)}, u32[]{:S(2)}, u32[]{:S(2)}) collective-permute-start(bf16[8,288,128]{2,1,0:T(8,128)(2,1)S(1)} %all-to-all-done.1.kv), channel_id=1, source_target_pairs={{0,8},{8,0},{1,9},{9,1},{2,10},{10,2},{3,11},{11,3},{4,12},{12,4},... | collective-permute-start | bytes 1769480 | tf_op jit(solution)/shard_map/ppermute | solution.py:349
  48.5 0.0 collective-permute-done.q1
  48.5 0.0 collective-permute-done.1.q2
  48.6 0.0 collective-permute-done.2.q3
  48.6 0.0 copy-done
  48.6 0.0 copy-done.1
  48.6 3.6 %shard_map.67 = (bf16[8,256,640]{2,1,0:T(8,128)(2,1)S(1)}, f32[8,256,128]{2,1,0:T(8,128)S(1)}, f32[8,256,128]{2,1,0:T(8,128)S(1)}, f32[8,256,128]{2,1,0:T(8,128)S(1)}) custom-call(s32[1]{0:T(128)} %bitcast.place_ref, bf16[64,1536]{1,0:T(8,128)(2,1)S(1)} %get-tuple-element.11.q0, bf16[64,1536]{1,0:T(8,128)(2,1)S(1)} %collective-permute-done.q1, ...), custom_call_target="tpu_custom_call" | custom-call | flops 6000000000 | bytes 5000000 | tf_op jit(solution)/shard_map/pallas_call | solution.py:224
  52.2 0.0 collective-permute-done.3.kv
  52.2 3.4 %shard_map.68 = bf16[4,64,1152]{2,1,0:T(8,128)(2,1)S(1)} custom-call(s32[1]{0:T(128)} %bitcast.place_ref, bf16[8,256,640]{2,1,0:T(8,128)(2,1)S(1)} %get-tuple-element.13.q_ref, bf16[256,128]{1,0:T(8,128)(2,1)S(1)} %shard_map.65.floor_ref, bf16[8,288,128]{2,1,0:T(8,128)(2,1)S(1)} %collective-permute-done.3.kv, f32[8,256,128]{2,1,0:T(8,128)S(1)} %get-tuple-element.14.sum_ref, ...), custom_call_target="tpu_custom_call" | custom-call | flops 4000000000 | bytes 5000000 | tf_op jit(solution)/shard_map/pallas_call | solution.py:289
  55.6 27.3 %all_to_all.15 = bf16[32,8,1152]{2,1,0:T(8,128)(2,1)S(1)} all-to-all(bf16[32,8,1152]{2,1,0:T(8,128)(2,1)S(1)} %bitcast.5), channel_id=1, replica_groups=mesh['y'=8,'x'=4,'core'=2,'z'=8] {'x','z'}, dimensions={0} | all-to-all | bytes 1179648 | tf_op jit(solution)/shard_map/all_to_all | solution.py:355
  82.9 1.2 %shard_map.69 = bf16[8,8192]{1,0:T(8,128)(2,1)} custom-call(bf16[4,8,8,1152]{3,2,1,0:T(8,128)(2,1)S(1)} %bitcast.4), custom_call_target="tpu_custom_call" | custom-call | flops 1000000 | bytes 800000 | tf_op jit(solution)/shard_map/pallas_call | solution.py:328
Async XLA Ops:
  1.7 20.7 %all-to-all-start = ((bf16[8,8,2176]{2,1,0:T(8,128)(2,1)}), bf16[8,8,2176]{2,1,0:T(8,128)(2,1)S(1)}, u32[]{:S(2)}, u32[]{:S(2)}) async-start(bf16[8,8,2176]{2,1,0:T(8,128)(2,1)} %shard_map.64), calls=%async_computation | async-start | bytes 557056 | tf_op jit(solution)/shard_map/all_to_all | solution.py:346
  22.4 26.2 %copy-start = (bf16[8,512,128]{2,1,0:T(8,128)(2,1)S(1)}, bf16[8,512,128]{2,1,0:T(8,128)(2,1)}, u32[]{:S(2)}) copy-start(bf16[8,512,128]{2,1,0:T(8,128)(2,1)} %w_uk.1) | copy-start | bytes 3145732
  22.4 26.2 %copy-start.1 = (bf16[8,512,128]{2,1,0:T(8,128)(2,1)S(1)}, bf16[8,512,128]{2,1,0:T(8,128)(2,1)}, u32[]{:S(2)}) copy-start(bf16[8,512,128]{2,1,0:T(8,128)(2,1)} %w_uv.3) | copy-start | bytes 3145732
  23.3 23.3 %all-to-all-start.1 = ((bf16[8,288,128]{2,1,0:T(8,128)(2,1)}), bf16[8,288,128]{2,1,0:T(8,128)(2,1)S(1)}, u32[]{:S(2)}, u32[]{:S(2)}) async-start(bf16[8,288,128]{2,1,0:T(8,128)(2,1)} %get-tuple-element.12), calls=%async_computation.1 | async-start | bytes 1179648 | tf_op jit(solution)/shard_map/all_to_all | solution.py:348
  30.4 18.1 %collective-permute-start = (bf16[64,1536]{1,0:T(8,128)(2,1)S(1)}, bf16[64,1536]{1,0:T(8,128)(2,1)S(1)}, u32[]{:S(2)}, u32[]{:S(2)}) collective-permute-start(bf16[64,1536]{1,0:T(8,128)(2,1)S(1)} %get-tuple-element.11.q0), channel_id=1, source_target_pairs={{0,16},{16,32},{32,48},{48,0},{1,17},{17,33},{33,49},{49,1},{2,18}... | collective-permute-start | bytes 589832 | tf_op jit(solution)/shard_map/ppermute | solution.py:350
  33.8 14.7 %collective-permute-start.1 = (bf16[64,1536]{1,0:T(8,128)(2,1)S(1)}, bf16[64,1536]{1,0:T(8,128)(2,1)S(1)}, u32[]{:S(2)}, u32[]{:S(2)}) collective-permute-start(bf16[64,1536]{1,0:T(8,128)(2,1)S(1)} %get-tuple-element.11.q0), channel_id=1, source_target_pairs={{0,32},{16,48},{32,0},{48,16},{1,33},{17,49},{33,1},{49,17},{2,34}... | collective-permute-start | bytes 589832 | tf_op jit(solution)/shard_map/ppermute | solution.py:350
  38.5 10.1 %collective-permute-start.2 = (bf16[64,1536]{1,0:T(8,128)(2,1)S(1)}, bf16[64,1536]{1,0:T(8,128)(2,1)S(1)}, u32[]{:S(2)}, u32[]{:S(2)}) collective-permute-start(bf16[64,1536]{1,0:T(8,128)(2,1)S(1)} %get-tuple-element.11.q0), channel_id=1, source_target_pairs={{0,48},{16,0},{32,16},{48,32},{1,49},{17,1},{33,17},{49,33},{2,50}... | collective-permute-start | bytes 589832 | tf_op jit(solution)/shard_map/ppermute | solution.py:350
  46.6 5.6 %collective-permute-start.3 = (bf16[8,288,128]{2,1,0:T(8,128)(2,1)S(1)}, bf16[8,288,128]{2,1,0:T(8,128)(2,1)S(1)}, u32[]{:S(2)}, u32[]{:S(2)}) collective-permute-start(bf16[8,288,128]{2,1,0:T(8,128)(2,1)S(1)} %all-to-all-done.1.kv), channel_id=1, source_target_pairs={{0,8},{8,0},{1,9},{9,1},{2,10},{10,2},{3,11},{11,3},{4,12},{12,4},... | collective-permute-start | bytes 1769480 | tf_op jit(solution)/shard_map/ppermute | solution.py:349
